TPU v7x, 32 devices: a whole 2x2x4 slice. The times are simulated.
32 devices in a mesh: group: 4 (over y, x), member: 8 (over z, core).
Axes of the slice: x: 2, y: 2, z: 4, core: 2. Of those that a mesh axis runs over, the one named last changes fastest.
Arguments:
- source_vectors: bfloat16 [32768, 256], P(('group', 'member')), may hold values from -4 to 4
- target_vectors: bfloat16 [32768, 256], P(('group', 'member')), may hold values from -4 to 4
- source_mass: float32 [32768], P(('group', 'member')), may hold values from -1 to 1
- target_mass: float32 [32768], P(('group', 'member')), may hold values from -1 to 1
- candidates: int32 [128, 8], P(('group', 'member')), may hold values from 0 to 127, as said below
Outputs:
- source_potential: float32 [32768], P(('group', 'member'))
- target_potential: float32 [32768], P(('group', 'member'))
Inputs may be any that keep to these rules, and one draw needn't show every extreme that they name: Target block t lies on device t // 4, devices counted group-major (group index times 8 plus member index). Candidates 0 to 6 of a source block lie on devices of its own group; of these 4 * (7) candidates of one device, at most 4 lie on any one device, and in each group one device holds exactly 4 of them for every device of the group. The last candidate of each source block on the device of group g and member m is block g of the device of group g2 and member m, the 4 source blocks of one device taking 4 different g2.
All inputs are finite; a program needn't handle non-finite values.
Results may differ from a plain program's by a relative error of at most 0.0003.
Values may be sent and summed in bfloat16 or wider, within the bound.
No kernel may reach another device: no remote copies, remote signals or barrier semaphores. Data moves between devices by JAX's collectives and lax.ppermute only.
A program may use at most 64 MiB of HBM per device.

v0:
```python
import jax
import jax.numpy as jnp
from jax import lax
from jax.sharding import PartitionSpec as P

ITERS = 2


entropy_strength = 0.3
very_low = -1e30


def log_partition(values, axis):
    largest_score = jnp.max(values, axis=axis, keepdims=True)
    return jnp.squeeze(largest_score, axis) + jnp.log(
        jnp.sum(jnp.exp(values - largest_score), axis=axis)
    )


def slot_layout(lists, per_device, members, capacity):
    owner = lists // per_device
    partner = owner % members
    local_block = lists % per_device
    ordering = jnp.arange(lists.shape[-1], dtype=jnp.int32)
    matching = partner[..., :, None] == partner[..., None, :]
    earlier = ordering[None, :] < ordering[:, None]
    position = jnp.sum(jnp.logical_and(matching, earlier).astype(jnp.int32), axis=-1)
    return (partner * capacity + position, local_block)


def trade_member(values):
    return lax.all_to_all(values, "member", split_axis=0, concat_axis=0, tiled=True)


def trade_group(values):
    return lax.all_to_all(values, "group", split_axis=0, concat_axis=0, tiled=True)


def tile_terms(sources, target_blocks, picks, side, by_rows):
    tile_count, block_rows, width = sources.shape
    batch = 4
    grouped = (
        sources.reshape(tile_count // batch, batch, block_rows, width),
        picks.reshape(tile_count // batch, batch),
        side.reshape(tile_count // batch, batch, block_rows),
    )

    def visit(grouped_part):
        source_portion, pick_part, side_portion = grouped_part
        key_entries = jnp.take(target_blocks, pick_part, axis=0)
        score_matrix = jnp.einsum(
            "umk,ugk->umg", source_portion, key_entries, preferred_element_type=jnp.float32
        )
        if by_rows:
            return log_partition((score_matrix + side_portion[:, None, :]) / entropy_strength, 2)
        return log_partition((score_matrix + side_portion[:, :, None]) / entropy_strength, 1)

    return lax.map(visit, grouped).reshape(tile_count, block_rows)


def owner_update(slot_terms, mirror_terms, incoming, target_marginal):
    output_list = []
    for local_block in range(target_marginal.shape[0]):
        masked = jnp.where((incoming == local_block)[:, None], slot_terms, very_low)
        stacked = jnp.concatenate([masked, mirror_terms[local_block][None, :]], axis=0)
        output_list.append(log_partition(stacked, 0))
    return entropy_strength * target_marginal - entropy_strength * jnp.stack(output_list)


def shards(source_vectors, target_vectors, source_mass, target_mass, candidates):
    members = lax.axis_size("member")
    groups = lax.axis_size("group")
    own_member = lax.axis_index("member")
    source_count, cand_count = candidates.shape
    inside_count = cand_count - 1
    block_rows = source_vectors.shape[0] // source_count
    width = source_vectors.shape[1]
    target_count = target_vectors.shape[0] // block_rows
    capacity = (source_count * inside_count + members - 1) // members
    spots = members * capacity
    source_blocks = source_vectors.reshape(source_count, block_rows, width)
    target_blocks = target_vectors.reshape(target_count, block_rows, width)
    source_marginal = source_mass.reshape(source_count, block_rows)
    target_marginal = target_mass.reshape(target_count, block_rows)
    own_lists = candidates[:, :inside_count]
    own_spots, own_local = slot_layout(
        own_lists.reshape(1, source_count * inside_count), target_count, members, capacity
    )
    own_spots = own_spots[0]
    all_lists = lax.all_gather(own_lists, "member", axis=0, tiled=True)
    their_spots, their_local = slot_layout(
        all_lists.reshape(members, source_count * inside_count), target_count, members, capacity
    )
    wanted_spots = own_member * capacity + jnp.arange(capacity, dtype=jnp.int32)
    hits = their_spots[:, :, None] == wanted_spots[None, None, :]
    incoming = (jnp.sum(jnp.where(hits, their_local[:, :, None] + 1, 0), axis=1) - 1).reshape(spots)
    picks = jnp.maximum(incoming, 0)
    mirror_group = candidates[:, inside_count] // target_count // members
    spot_range = jnp.arange(spots, dtype=jnp.int32)
    group_range = jnp.arange(groups, dtype=jnp.int32)
    source_of = jnp.arange(source_count * inside_count, dtype=jnp.int32) // inside_count
    slot_index = jnp.sum(
        jnp.where(own_spots[:, None] == spot_range[None, :], source_of[:, None], 0), axis=0
    )
    mirror_index = jnp.sum(
        jnp.where(
            mirror_group[:, None] == group_range[None, :],
            jnp.arange(source_count, dtype=jnp.int32)[:, None],
            0,
        ),
        axis=0,
    )
    slot_payload = jnp.take(source_blocks, slot_index, axis=0)
    mirror_payload = jnp.take(source_blocks, mirror_index, axis=0)
    arrived = lax.all_to_all(
        slot_payload.reshape(members, capacity, block_rows, width),
        "member",
        split_axis=0,
        concat_axis=0,
        tiled=True,
    ).reshape(spots, block_rows, width)
    arrived_mirror = lax.all_to_all(
        mirror_payload, "group", split_axis=0, concat_axis=0, tiled=True
    )
    target_current = jnp.zeros((target_count, block_rows), jnp.float32)
    for step in range(ITERS):
        row_slots = tile_terms(
            arrived, target_blocks, picks, jnp.take(target_current, picks, axis=0), True
        )
        row_mirror = tile_terms(arrived_mirror, target_blocks, group_range, target_current, True)
        slot_back = trade_member(row_slots.reshape(members, capacity, block_rows)).reshape(
            spots, block_rows
        )
        mirror_back = trade_group(row_mirror)
        collected_rows = jnp.concatenate(
            [
                jnp.take(slot_back, own_spots, axis=0).reshape(
                    source_count, inside_count, block_rows
                ),
                jnp.take(mirror_back, mirror_group, axis=0)[:, None],
            ],
            axis=1,
        )
        source_current = entropy_strength * source_marginal - entropy_strength * log_partition(
            collected_rows, 1
        )
        slot_sides = trade_member(
            jnp.take(source_current, slot_index, axis=0).reshape(members, capacity, block_rows)
        ).reshape(spots, block_rows)
        mirror_sides = trade_group(jnp.take(source_current, mirror_index, axis=0))
        column_slots = tile_terms(arrived, target_blocks, picks, slot_sides, False)
        column_mirror = tile_terms(arrived_mirror, target_blocks, group_range, mirror_sides, False)
        target_current = owner_update(column_slots, column_mirror, incoming, target_marginal)
    return (
        source_current.reshape(source_count * block_rows),
        target_current.reshape(target_count * block_rows),
    )


def solution(mesh):
    placed = (
        P(("group", "member"), None),
        P(("group", "member"), None),
        P(("group", "member")),
        P(("group", "member")),
        P(("group", "member"), None),
    )
    return jax.shard_map(
        shards,
        mesh=mesh,
        in_specs=placed,
        out_specs=(P(("group", "member")), P(("group", "member"))),
        check_vma=False,
    )
```

profile of v0, /device:TPU:0, one launch (start us, length us, event | category | flops | bytes accessed | tf_op | source)
XLA Modules:
  0.0 281.7 jit_solution(3192375023441504240)
XLA Ops:
  3.3 5.2 %all-to-all-start.2 = ((bf16[4,256,256]{2,1,0:T(8,128)(2,1)}), bf16[4,256,256]{2,1,0:T(8,128)(2,1)S(1)}, u32[]{:S(2)}, u32[]{:S(2)}) async-start(bf16[4,256,256]{2,1,0:T(8,128)(2,1)} %broadcast_select_fusion.1), calls=%async_computation.2 | async-start | bytes 1048576 | tf_op jit(solution)/shard_map/all_to_all | solution.py:122
  10.1 2.7 gather_fusion.4
  13.1 4.6 %broadcast_select_fusion = bf16[8,4,256,256]{3,2,1,0:T(8,128)(2,1)} fusion(bf16[8,4,256,256]{3,2,1,0:T(8,128)(2,1)} %bitcast.144, pred[8,4]{1,0:T(8,128)(4,1)S(1)} %copy.46), kind=kLoop, calls=%fused_computation.85 | loop fusion | flops 2097152 | bytes 8388640 | tf_op jit(solution)/shard_map/jit(_take)/select_n | solution.py:113
  17.7 5.0 %all-to-all-start = ((bf16[8,4,256,256]{3,2,1,0:T(8,128)(2,1)}), bf16[8,4,256,256]{3,2,1,0:T(8,128)(2,1)}, u32[]{:S(2)}, u32[]{:S(2)}) async-start(bf16[8,4,256,256]{3,2,1,0:T(8,128)(2,1)} %broadcast_select_fusion), calls=%async_computation | async-start | bytes 8388608 | tf_op jit(solution)/shard_map/all_to_all | solution.py:115
  22.7 100.0 %all-gather = s32[8,4,7]{2,1,0:T(4,128)S(1)} all-gather(s32[1,4,7]{2,1,0:T(4,128)S(1)} %get-tuple-element.369), channel_id=1, replica_groups=mesh['group'=4,'member'=8] {'member'}, dimensions={0}, use_global_device_ids=true | all-gather | bytes 1008 | tf_op jit(solution)/shard_map/all_gather | solution.py:90
  127.9 4.2 %all-to-all-start.3 = ((f32[4,1,256]{2,1,0:T(1,128)}), f32[4,1,256]{2,1,0:T(1,128)S(1)}, u32[]{:S(2)}, u32[]{:S(2)}) async-start(f32[4,1,256]{2,1,0:T(1,128)} %add.430), calls=%async_computation.3 | async-start | bytes 8192 | tf_op jit(solution)/shard_map/all_to_all | solution.py:36
  132.7 22.6 %while.8 = (s32[]{:T(128)}, f32[8,4,256]{2,1,0:T(4,128)}, bf16[8,4,256,256]{3,2,1,0:T(8,128)(2,1)}, s32[8,4]{1,0:T(8,128)S(1)}, bf16[4,256,256]{2,1,0:T(8,128)(2,1)S(1)}, /*index=5*/f32[8,4,256]{2,1,0:T(4,128)S(1)}, s32[]{:T(128)}) while((s32[]{:T(128)}, f32[8,4,256]{2,1,0:T(4,128)}, bf16[8,4,256,256]{3,2,1,0:T(8,128)(2,1)}, ...), condition=%wide.region_7.10_spmd, body=%wide.region_4.9_spmd.sunk | while | flops 135790624 | bytes 4236445 | solution.py:58
  155.3 3.3 %all-to-all-start.1 = ((f32[8,4,256]{2,1,0:T(4,128)}), f32[8,4,256]{2,1,0:T(4,128)S(1)}, u32[]{:S(2)}, u32[]{:S(2)}) async-start(f32[8,4,256]{2,1,0:T(4,128)} %get-tuple-element.203), calls=%async_computation.1 | async-start | bytes 65536 | tf_op jit(solution)/shard_map/all_to_all | solution.py:32
  159.2 5.1 %all-to-all-done.1 = f32[8,4,256]{2,1,0:T(4,128)S(1)} async-done(((f32[8,4,256]{2,1,0:T(4,128)}), f32[8,4,256]{2,1,0:T(4,128)S(1)}, u32[]{:S(2)}, u32[]{:S(2)}) %all-to-all-start.1) | async-done | bytes 32800 | tf_op jit(solution)/shard_map/all_to_all | solution.py:32
  167.0 4.2 %all-to-all-start.5 = ((f32[4,1,256]{2,1,0:T(1,128)}), f32[4,1,256]{2,1,0:T(1,128)S(1)}, u32[]{:S(2)}, u32[]{:S(2)}) async-start(f32[4,1,256]{2,1,0:T(1,128)} %copy.54), calls=%async_computation.5 | async-start | bytes 8192 | tf_op jit(solution)/shard_map/all_to_all | solution.py:36
  171.9 4.0 %all-to-all-done.5 = f32[4,1,256]{2,1,0:T(1,128)S(1)} async-done(((f32[4,1,256]{2,1,0:T(1,128)}), f32[4,1,256]{2,1,0:T(1,128)S(1)}, u32[]{:S(2)}, u32[]{:S(2)}) %all-to-all-start.5) | async-done | bytes 4128 | tf_op jit(solution)/shard_map/all_to_all | solution.py:36
  175.9 3.3 %all-to-all-start.4 = ((f32[8,4,256]{2,1,0:T(4,128)}), f32[8,4,256]{2,1,0:T(4,128)S(1)}, u32[]{:S(2)}, u32[]{:S(2)}) async-start(f32[8,4,256]{2,1,0:T(4,128)} %reshape.860), calls=%async_computation.4 | async-start | bytes 65536 | tf_op jit(solution)/shard_map/all_to_all | solution.py:32
  179.8 5.1 %all-to-all-done.4 = f32[8,4,256]{2,1,0:T(4,128)S(1)} async-done(((f32[8,4,256]{2,1,0:T(4,128)}), f32[8,4,256]{2,1,0:T(4,128)S(1)}, u32[]{:S(2)}, u32[]{:S(2)}) %all-to-all-start.4) | async-done | bytes 32800 | tf_op jit(solution)/shard_map/all_to_all | solution.py:32
  184.9 18.5 %while.9 = (s32[]{:T(128)}, f32[8,4,256]{2,1,0:T(4,128)S(1)}, bf16[8,4,256,256]{3,2,1,0:T(8,128)(2,1)}, s32[8,4]{1,0:T(8,128)S(1)}, bf16[4,256,256]{2,1,0:T(8,12...) while((s32[]{:T(128)}, f32[8,4,256]{2,1,0:T(4,128)S(1)}, bf16[8,4,256,256]{3,2,1,0:T(8,128)(2,1)}, ...), condition=%wide.region_16.21_spmd, body=%wide.region_13.20_spmd.sunk | while | flops 135790624 | bytes 4235937 | solution.py:58
  187.9 1.5 fusion.94
  192.5 1.5 fusion.94
  197.2 1.5 fusion.94
  201.8 1.5 fusion.94
  205.9 3.2 %all-to-all-start.7 = ((f32[4,1,256]{2,1,0:T(1,128)}), f32[4,1,256]{2,1,0:T(1,128)S(1)}, u32[]{:S(2)}, u32[]{:S(2)}) async-start(f32[4,1,256]{2,1,0:T(1,128)} %add.443), calls=%async_computation.7 | async-start | bytes 8192 | tf_op jit(solution)/shard_map/all_to_all | solution.py:36
  209.8 22.6 %while.10 = (s32[]{:T(128)}, f32[8,4,256]{2,1,0:T(4,128)}, bf16[8,4,256,256]{3,2,1,0:T(8,128)(2,1)}, s32[8,4]{1,0:T(8,128)S(1)}, bf16[4,256,256]{2,1,0:T(8,128)(2,1)S(1)}, /*index=5*/f32[8,4,256]{2,1,0:T(4,128)S(1)}, s32[]{:T(128)}) while((s32[]{:T(128)}, f32[8,4,256]{2,1,0:T(4,128)}, bf16[8,4,256,256]{3,2,1,0:T(8,128)(2,1)}, ...), condition=%wide.region_30.35_spmd, body=%wide.region_27.34_spmd.sunk | while | flops 135790624 | bytes 4236445 | solution.py:58
  232.3 3.3 %all-to-all-start.6 = ((f32[8,4,256]{2,1,0:T(4,128)}), f32[8,4,256]{2,1,0:T(4,128)S(1)}, u32[]{:S(2)}, u32[]{:S(2)}) async-start(f32[8,4,256]{2,1,0:T(4,128)} %get-tuple-element.205), calls=%async_computation.6 | async-start | bytes 65536 | tf_op jit(solution)/shard_map/all_to_all | solution.py:32
  236.3 5.1 %all-to-all-done.6 = f32[8,4,256]{2,1,0:T(4,128)S(1)} async-done(((f32[8,4,256]{2,1,0:T(4,128)}), f32[8,4,256]{2,1,0:T(4,128)S(1)}, u32[]{:S(2)}, u32[]{:S(2)}) %all-to-all-start.6) | async-done | bytes 32800 | tf_op jit(solution)/shard_map/all_to_all | solution.py:32
  244.1 4.2 %all-to-all-start.9 = ((f32[4,1,256]{2,1,0:T(1,128)}), f32[4,1,256]{2,1,0:T(1,128)S(1)}, u32[]{:S(2)}, u32[]{:S(2)}) async-start(f32[4,1,256]{2,1,0:T(1,128)} %copy.65), calls=%async_computation.9 | async-start | bytes 8192 | tf_op jit(solution)/shard_map/all_to_all | solution.py:36
  249.5 3.5 %all-to-all-done.9 = f32[4,1,256]{2,1,0:T(1,128)S(1)} async-done(((f32[4,1,256]{2,1,0:T(1,128)}), f32[4,1,256]{2,1,0:T(1,128)S(1)}, u32[]{:S(2)}, u32[]{:S(2)}) %all-to-all-start.9) | async-done | bytes 4128 | tf_op jit(solution)/shard_map/all_to_all | solution.py:36
  253.0 3.3 %all-to-all-start.8 = ((f32[8,4,256]{2,1,0:T(4,128)}), f32[8,4,256]{2,1,0:T(4,128)S(1)}, u32[]{:S(2)}, u32[]{:S(2)}) async-start(f32[8,4,256]{2,1,0:T(4,128)} %reshape.865), calls=%async_computation.8 | async-start | bytes 65536 | tf_op jit(solution)/shard_map/all_to_all | solution.py:32
  256.9 5.1 %all-to-all-done.8 = f32[8,4,256]{2,1,0:T(4,128)S(1)} async-done(((f32[8,4,256]{2,1,0:T(4,128)}), f32[8,4,256]{2,1,0:T(4,128)S(1)}, u32[]{:S(2)}, u32[]{:S(2)}) %all-to-all-start.8) | async-done | bytes 32800 | tf_op jit(solution)/shard_map/all_to_all | solution.py:32
  262.0 18.6 %while.11 = (s32[]{:T(128)}, f32[8,4,256]{2,1,0:T(4,128)S(1)}, bf16[8,4,256,256]{3,2,1,0:T(8,128)(2,1)}, s32[8,4]{1,0:T(8,128)S(1)}, bf16[4,256,256]{2,1,0:T(8,1...) while((s32[]{:T(128)}, f32[8,4,256]{2,1,0:T(4,128)S(1)}, bf16[8,4,256,256]{3,2,1,0:T(8,128)(2,1)}, ...), condition=%wide.region_38.43_spmd, body=%wide.region_35.42_spmd.sunk | while | flops 135790624 | bytes 4235937 | solution.py:58
  264.9 1.5 fusion.96
  269.6 1.5 fusion.96
  271.9 1.5 fusion.96
  274.2 1.5 fusion.96
  276.6 1.5 fusion.96
  (383 shorter events, 91.2 us)
Async XLA Ops:
  0.6 1.1 copy-start
  3.3 14.4 %all-to-all-start.2 = ((bf16[4,256,256]{2,1,0:T(8,128)(2,1)}), bf16[4,256,256]{2,1,0:T(8,128)(2,1)S(1)}, u32[]{:S(2)}, u32[]{:S(2)}) async-start(bf16[4,256,256]{2,1,0:T(8,128)(2,1)} %broadcast_select_fusion.1), calls=%async_computation.2 | async-start | bytes 1048576 | tf_op jit(solution)/shard_map/all_to_all | solution.py:122
  17.7 107.1 %copy-start.2 = (f32[1024]{0:T(1024)S(1)}, f32[1024]{0:T(1024)}, u32[]{:S(2)}) copy-start(f32[1024]{0:T(1024)} %param.23) | copy-start | bytes 12292
  17.7 107.9 %copy-start.3 = (f32[1024]{0:T(1024)S(1)}, f32[1024]{0:T(1024)}, u32[]{:S(2)}) copy-start(f32[1024]{0:T(1024)} %param.24) | copy-start | bytes 12292
  17.7 107.9 %copy-start.1 = (bf16[1024,256]{1,0:T(8,128)(2,1)S(1)}, bf16[1024,256]{1,0:T(8,128)(2,1)}, u32[]{:S(2)}) copy-start(bf16[1024,256]{1,0:T(8,128)(2,1)} %param.22) | copy-start | bytes 1572868
  17.7 110.2 %all-to-all-start = ((bf16[8,4,256,256]{3,2,1,0:T(8,128)(2,1)}), bf16[8,4,256,256]{3,2,1,0:T(8,128)(2,1)}, u32[]{:S(2)}, u32[]{:S(2)}) async-start(bf16[8,4,256,256]{3,2,1,0:T(8,128)(2,1)} %broadcast_select_fusion), calls=%async_computation | async-start | bytes 8388608 | tf_op jit(solution)/shard_map/all_to_all | solution.py:115
  127.9 27.4 %all-to-all-start.3 = ((f32[4,1,256]{2,1,0:T(1,128)}), f32[4,1,256]{2,1,0:T(1,128)S(1)}, u32[]{:S(2)}, u32[]{:S(2)}) async-start(f32[4,1,256]{2,1,0:T(1,128)} %add.430), calls=%async_computation.3 | async-start | bytes 8192 | tf_op jit(solution)/shard_map/all_to_all | solution.py:36
  155.3 9.0 %all-to-all-start.1 = ((f32[8,4,256]{2,1,0:T(4,128)}), f32[8,4,256]{2,1,0:T(4,128)S(1)}, u32[]{:S(2)}, u32[]{:S(2)}) async-start(f32[8,4,256]{2,1,0:T(4,128)} %get-tuple-element.203), calls=%async_computation.1 | async-start | bytes 65536 | tf_op jit(solution)/shard_map/all_to_all | solution.py:32
  167.0 8.9 %all-to-all-start.5 = ((f32[4,1,256]{2,1,0:T(1,128)}), f32[4,1,256]{2,1,0:T(1,128)S(1)}, u32[]{:S(2)}, u32[]{:S(2)}) async-start(f32[4,1,256]{2,1,0:T(1,128)} %copy.54), calls=%async_computation.5 | async-start | bytes 8192 | tf_op jit(solution)/shard_map/all_to_all | solution.py:36
  175.9 9.0 %all-to-all-start.4 = ((f32[8,4,256]{2,1,0:T(4,128)}), f32[8,4,256]{2,1,0:T(4,128)S(1)}, u32[]{:S(2)}, u32[]{:S(2)}) async-start(f32[8,4,256]{2,1,0:T(4,128)} %reshape.860), calls=%async_computation.4 | async-start | bytes 65536 | tf_op jit(solution)/shard_map/all_to_all | solution.py:32
  205.9 26.4 %all-to-all-start.7 = ((f32[4,1,256]{2,1,0:T(1,128)}), f32[4,1,256]{2,1,0:T(1,128)S(1)}, u32[]{:S(2)}, u32[]{:S(2)}) async-start(f32[4,1,256]{2,1,0:T(1,128)} %add.443), calls=%async_computation.7 | async-start | bytes 8192 | tf_op jit(solution)/shard_map/all_to_all | solution.py:36
  232.3 9.0 %all-to-all-start.6 = ((f32[8,4,256]{2,1,0:T(4,128)}), f32[8,4,256]{2,1,0:T(4,128)S(1)}, u32[]{:S(2)}, u32[]{:S(2)}) async-start(f32[8,4,256]{2,1,0:T(4,128)} %get-tuple-element.205), calls=%async_computation.6 | async-start | bytes 65536 | tf_op jit(solution)/shard_map/all_to_all | solution.py:32
  244.1 8.8 %all-to-all-start.9 = ((f32[4,1,256]{2,1,0:T(1,128)}), f32[4,1,256]{2,1,0:T(1,128)S(1)}, u32[]{:S(2)}, u32[]{:S(2)}) async-start(f32[4,1,256]{2,1,0:T(1,128)} %copy.65), calls=%async_computation.9 | async-start | bytes 8192 | tf_op jit(solution)/shard_map/all_to_all | solution.py:36
  253.0 9.0 %all-to-all-start.8 = ((f32[8,4,256]{2,1,0:T(4,128)}), f32[8,4,256]{2,1,0:T(4,128)S(1)}, u32[]{:S(2)}, u32[]{:S(2)}) async-start(f32[8,4,256]{2,1,0:T(4,128)} %reshape.865), calls=%async_computation.8 | async-start | bytes 65536 | tf_op jit(solution)/shard_map/all_to_all | solution.py:32
where the time goes:
time: 284 us; the launch traced here: 282 us
  blocking collectives  100 us (35%)
  matrix products  46.9 us (17%)
  starting transfers between devices  39.3 us (14%)
  local copies, waits for them, and re-layouts  35.9 us (13%)
  other arithmetic  29.1 us (10%)
  waiting for transfers between devices  27.9 us (10%)
    all_gather x1, blocking collectives, shards(): all_lists = lax.all_gather(own_lists, 'member', axis=0, tiled=True)  100 us
    dot_general x33, matrix products, visit(): jnp.einsum('umk,ugk->umg', source_portion, key_entries, preferred_element...  46.9 us
    all_to_all x4, waiting for transfers between devices, trade_member(): lax.all_to_all(values, 'member', split_axis=0, concat_axis=0, tiled=True)  20.4 us
    gather x33, local copies, waits for them, and re-layouts, visit(): key_entries = jnp.take(target_blocks, pick_part, axis=0)  19.2 us
    all_to_all x4, starting transfers between devices, trade_group(): lax.all_to_all(values, 'group', split_axis=0, concat_axis=0, tiled=True)  15.8 us
    all_to_all x4, starting transfers between devices, trade_member(): lax.all_to_all(values, 'member', split_axis=0, concat_axis=0, tiled=True)  13.4 us
    dynamic_update_slice x32, other arithmetic, tile_terms(): return lax.map(visit, grouped).reshape(tile_count, block_rows)  9.96 us
    all_to_all x4, waiting for transfers between devices, trade_group(): lax.all_to_all(values, 'group', split_axis=0, concat_axis=0, tiled=True)  7.45 us
  transfers between devices with their start and end apart: 10, of which 6 were waited for; matrix products, arithmetic and copies ran while one was open for 23% of the time, Pallas kernels for 0%

commit v1 on v0

--- a/solution.py
+++ b/solution.py
@@ -1,6 +1,10 @@
+import functools
+
 import jax
 import jax.numpy as jnp
 from jax import lax
+from jax.experimental import pallas as pl
+from jax.experimental.pallas import tpu as pltpu
 from jax.sharding import PartitionSpec as P
 
 ITERS = 2
@@ -67,7 +71,7 @@
     return entropy_strength * target_marginal - entropy_strength * jnp.stack(output_list)
 
 
-def shards(source_vectors, target_vectors, source_mass, target_mass, candidates):
+def shards_any(source_vectors, target_vectors, source_mass, target_mass, candidates):
     members = lax.axis_size("member")
     groups = lax.axis_size("group")
     own_member = lax.axis_index("member")
@@ -157,6 +161,327 @@
     )
 
 
+LOG2E = 1.4426950408889634
+TO_LOGIT = LOG2E / entropy_strength
+TO_POTENTIAL = entropy_strength / LOG2E
+TILE_SLOTS = 40
+UNROLL = 4
+SOURCE_SLOTS = 16
+TARGET_SLOTS = 11
+
+
+def merge(parts):
+    top = functools.reduce(jnp.maximum, parts)
+    return top + LOG2E * jnp.log(sum(jnp.exp2(part - top) for part in parts))
+
+
+def swapped(rows, size):
+    pieces = [rows[start : start + size] for start in range(0, rows.shape[0], size)]
+    return jnp.concatenate([pieces[index ^ 1] for index in range(len(pieces))], axis=0)
+
+
+def source_bias(mass_refs, part_refs):
+    own, core, near, cross = (ref[...] for ref in part_refs)
+    core = swapped(core, 4)
+    near = swapped(near, 8)
+    cross = swapped(swapped(cross, 4), 8)
+    mass = jnp.concatenate([ref[0:4] for ref in mass_refs], axis=0)
+    return mass - merge([own, core, near, cross])
+
+
+def target_bias(scalars, columns, partner, mirrors, scratch):
+    group = scalars[2, 1]
+    scratch[...] = jnp.full(scratch.shape, very_low, jnp.float32)
+    for offset, ref in enumerate(mirrors, 1):
+        scratch[pl.ds(group ^ offset, 1), :] = ref[0:1]
+        scratch[pl.ds(4 + (group ^ offset), 1), :] = ref[1:2]
+    theirs = jnp.concatenate([partner[4:8], partner[0:4]], axis=0)
+    mass = jnp.concatenate([columns[12:16], partner[12:16]], axis=0)
+    inside = mass - merge([columns[0:8], theirs, scratch[0:8]])
+    across = [
+        ref[3:4] - merge([ref[2:3], columns[7 + offset : 8 + offset]])
+        for offset, ref in enumerate(mirrors, 1)
+    ]
+    return jnp.concatenate([inside, *across, jnp.zeros((5, inside.shape[1]), jnp.float32)], axis=0)
+
+
+def load_blocks(block_refs, source_buffer, target_buffer, semaphores):
+    copies = []
+    for index in range(4):
+        copies.append((block_refs[index], source_buffer.at[pl.ds(4 * index, 4)]))
+    for index in range(2):
+        copies.append((block_refs[4 + index], target_buffer.at[pl.ds(4 * index, 4)]))
+    for index in range(3):
+        copies.append((block_refs[6 + index], target_buffer.at[pl.ds(8 + index, 1)]))
+    started = []
+    for index, (origin, place) in enumerate(copies):
+        copy = pltpu.make_async_copy(origin, place, semaphores.at[index])
+        copy.start()
+        started.append(copy)
+    return started
+
+
+def run_tiles(scalars, ids, summed, summed_row, kept, kept_row, kept_count, bias, tops, sums):
+    def visit(step, carry):
+        for inner in range(UNROLL):
+            slot = step * UNROLL + inner
+            first = scalars[summed_row, slot]
+            second = scalars[kept_row, slot]
+            score = lax.dot_general(
+                summed[first], kept[second], (((1,), (1,)), ((), ())), preferred_element_type=jnp.float32
+            )
+            logits = score * TO_LOGIT
+            if bias is not None:
+                shift = bias[first]
+                logits = logits + jnp.concatenate([shift, shift], axis=1)
+            top = jnp.max(logits, axis=0, keepdims=True)
+            tops[pl.ds(slot, 1), :] = top
+            sums[pl.ds(slot, 1), :] = jnp.sum(jnp.exp2(logits - top), axis=0, keepdims=True)
+        return carry
+
+    lax.fori_loop(0, (scalars[2, 0] + UNROLL - 1) // UNROLL, visit, 0)
+    id_rows = jnp.concatenate([ids[...], ids[...]], axis=1)
+    top_rows = tops[...]
+    sum_rows = sums[...]
+    best, total = [], []
+    for block in range(kept_count):
+        mine = id_rows == block
+        top = jnp.max(jnp.where(mine, top_rows, very_low), axis=0, keepdims=True)
+        best.append(top)
+        total.append(jnp.sum(jnp.where(mine, sum_rows * jnp.exp2(top_rows - top), 0.0), axis=0, keepdims=True))
+    best = jnp.concatenate(best, axis=0)
+    total = jnp.concatenate(total, axis=0)
+    return jnp.where(total > 0, best + LOG2E * jnp.log(jnp.where(total > 0, total, 1.0)), very_low)
+
+
+def fill_bias(rows, bias):
+    turned = rows.T
+    for slot in range(bias.shape[0]):
+        bias[slot] = jnp.broadcast_to(turned[:, slot : slot + 1], bias.shape[1:])
+
+
+def rows_kernel(first_pass, *refs):
+    scalars, ids = refs[:2]
+    block_refs = refs[2:11]
+    rest = refs[11:]
+    if first_pass:
+        out, source_buffer, target_buffer, tops, sums, semaphores = rest
+        bias = None
+    else:
+        columns, partner, *mirrors = rest[:5]
+        out, source_buffer, target_buffer, tops, sums, semaphores, bias, scratch = rest[5:]
+    started = load_blocks(block_refs, source_buffer, target_buffer, semaphores)
+    if not first_pass:
+        fill_bias(target_bias(scalars, columns, partner, mirrors, scratch), bias)
+    for copy in started:
+        copy.wait()
+    out[...] = run_tiles(
+        scalars, ids, target_buffer, 1, source_buffer, 0, SOURCE_SLOTS, bias, tops, sums
+    )
+
+
+def columns_kernel(last_pass, *refs):
+    scalars, ids = refs[:2]
+    block_refs = refs[2:11]
+    masses, parts, target_mass = refs[11:15], refs[15:19], refs[19]
+    out = refs[20]
+    rest = refs[21:]
+    if last_pass:
+        potential, *rest = rest
+    source_buffer, target_buffer, tops, sums, semaphores, bias = rest
+    started = load_blocks(block_refs, source_buffer, target_buffer, semaphores)
+    rows = source_bias(masses, parts)
+    fill_bias(rows, bias)
+    if last_pass:
+        for block in range(4):
+            for half in range(2):
+                potential[2 * block + half : 2 * block + half + 1, :] = (
+                    TO_POTENTIAL * rows[block : block + 1, 128 * half : 128 * (half + 1)]
+                )
+    for copy in started:
+        copy.wait()
+    out[0:TARGET_SLOTS, :] = run_tiles(
+        scalars, ids, source_buffer, 0, target_buffer, 1, TARGET_SLOTS, bias, tops, sums
+    )
+    out[TARGET_SLOTS : TARGET_SLOTS + 1, :] = jnp.zeros((1, out.shape[1]), jnp.float32)
+    out[12:16, :] = target_mass[0:4]
+
+
+def forward_kernel(scalars, columns, partner, *outs):
+    group = scalars[2, 1]
+    for offset, out in enumerate(outs, 1):
+        block = group ^ offset
+        out[0:1, :] = columns[7 + offset : 8 + offset]
+        out[1:2, :] = partner[7 + offset : 8 + offset]
+        out[2:3, :] = merge([columns[pl.ds(block, 1), :], partner[pl.ds(4 + block, 1), :]])
+        out[3:4, :] = columns[pl.ds(12 + block, 1), :]
+
+
+def finish_kernel(scalars, columns, partner, *rest):
+    *mirrors, out, scratch = rest
+    group = scalars[2, 1]
+    scratch[...] = jnp.full(scratch.shape, very_low, jnp.float32)
+    for offset, ref in enumerate(mirrors, 1):
+        scratch[pl.ds(group ^ offset, 1), :] = ref[7 + offset : 8 + offset]
+    rows = columns[12:16] - merge([columns[0:4], partner[4:8], scratch[0:4]])
+    for block in range(4):
+        for half in range(2):
+            out[2 * block + half : 2 * block + half + 1, :] = (
+                TO_POTENTIAL * rows[block : block + 1, 128 * half : 128 * (half + 1)]
+            )
+
+
+def spaces(*kinds):
+    return [pl.BlockSpec(memory_space=kind) for kind in kinds]
+
+
+SMEM, VMEM = pltpu.SMEM, pltpu.VMEM
+
+
+def call(kernel, inputs, kinds, outs, scratch, flops=0):
+    return pl.pallas_call(
+        kernel,
+        out_shape=[jax.ShapeDtypeStruct(shape, jnp.float32) for shape in outs],
+        in_specs=spaces(*kinds),
+        out_specs=spaces(*(VMEM for _ in outs)),
+        scratch_shapes=scratch,
+        compiler_params=pltpu.CompilerParams(vmem_limit_bytes=32 << 20),
+    )(*inputs)
+
+
+def swap(values, axis, size, bit):
+    return lax.ppermute(values, axis, [(index, index ^ bit) for index in range(size)])
+
+
+def tile_lists(candidates, own_group, own_member, members, per_device):
+    owner = candidates // per_device
+    local = candidates % per_device
+    apart = (owner % members) ^ own_member
+    last = candidates.shape[1] - 1
+    mirror = (owner // members) ^ own_group
+    is_last = jnp.arange(last + 1)[None, :] == last
+    source = jnp.broadcast_to(jnp.arange(SOURCE_SLOTS, dtype=jnp.int32)[:, None], candidates.shape)
+    inside = jnp.logical_and(~is_last, jnp.logical_or(apart == 0, apart == 4))
+    taken = jnp.logical_or(inside, jnp.logical_and(is_last, source < per_device))
+    target = jnp.where(
+        is_last, jnp.where(mirror == 0, local, 7 + mirror), local + jnp.where(apart == 4, per_device, 0)
+    )
+    taken, source, target = (values.reshape(-1) for values in (taken, source, target))
+    order = jnp.arange(taken.shape[0], dtype=jnp.int32)
+    earlier = jnp.logical_and(order[None, :] < order[:, None], taken[None, :])
+    position = jnp.sum(earlier.astype(jnp.int32), axis=1)
+    slots = jnp.arange(TILE_SLOTS, dtype=jnp.int32)
+    hits = jnp.logical_and(position[None, :] == slots[:, None], taken[None, :])
+    count = jnp.sum(taken.astype(jnp.int32))
+    sources = jnp.sum(jnp.where(hits, source[None, :], 0), axis=1)
+    targets = jnp.sum(jnp.where(hits, target[None, :], 0), axis=1)
+    used = slots < count
+    extra = jnp.where(slots == 0, count, jnp.where(slots == 1, own_group, 0))
+    scalars = jnp.stack([sources, targets, extra.astype(jnp.int32)])
+    by_source, by_target = (
+        jnp.broadcast_to(jnp.where(used, ids, -1)[:, None], (TILE_SLOTS, 128))
+        for ids in (sources, targets)
+    )
+    return scalars, by_source, by_target
+
+
+def shards_quad(source_vectors, target_vectors, source_mass, target_mass, candidates):
+    members = lax.axis_size("member")
+    groups = lax.axis_size("group")
+    own_group = lax.axis_index("group")
+    own_member = lax.axis_index("member")
+    per_device, cand_count = candidates.shape
+    block_rows = source_vectors.shape[0] // per_device
+    width = source_vectors.shape[1]
+    blocked = (per_device, block_rows, width)
+    member_swap = lambda values, bit: swap(values, "member", members, bit)
+    group_swap = lambda values, bit: swap(values, "group", groups, bit)
+
+    source_own = source_vectors.reshape(blocked)
+    target_own = target_vectors.reshape(blocked)
+    source_near = member_swap(source_own, 2)
+    target_far = member_swap(target_own, 4)
+    note = jnp.concatenate(
+        [
+            LOG2E * source_mass.reshape(per_device, block_rows),
+            jnp.pad(
+                candidates.astype(jnp.float32).reshape(1, per_device * cand_count),
+                ((0, 3), (0, block_rows - per_device * cand_count)),
+            ),
+        ]
+    )
+    notes = [note] + [member_swap(note, bit) for bit in (1, 2, 3)]
+    mirrors = [
+        group_swap(lax.dynamic_slice_in_dim(target_own, own_group ^ bit, 1, 0), bit) for bit in (1, 2, 3)
+    ]
+    source_core = member_swap(source_own, 1)
+    source_cross = member_swap(source_near, 1)
+    lists = jnp.stack([values[4, : per_device * cand_count] for values in notes])
+    lists = lists.reshape(4 * per_device, cand_count).astype(jnp.int32)
+    scalars, by_source, by_target = tile_lists(lists, own_group, own_member, members, per_device)
+    own_mass = LOG2E * target_mass.reshape(per_device, block_rows)
+    blocks = [source_own, source_core, source_near, source_cross, target_own, target_far, *mirrors]
+
+    buffers = [
+        VMEM((SOURCE_SLOTS, block_rows, width), source_vectors.dtype),
+        VMEM((TARGET_SLOTS, block_rows, width), target_vectors.dtype),
+        VMEM((TILE_SLOTS, block_rows), jnp.float32),
+        VMEM((TILE_SLOTS, block_rows), jnp.float32),
+        pltpu.SemaphoreType.DMA((9,)),
+    ]
+    source_bias_buffer = VMEM((SOURCE_SLOTS, block_rows, 128), jnp.float32)
+    target_bias_buffer = VMEM((TARGET_SLOTS, block_rows, 128), jnp.float32)
+    side = (16, block_rows)
+    start = (SMEM, VMEM) + (pl.ANY,) * 9
+
+    (parts,) = call(
+        functools.partial(rows_kernel, True), [scalars, by_source, *blocks], start, [side], buffers
+    )
+    for step in range(ITERS):
+        last_pass = step == ITERS - 1
+        theirs = [member_swap(parts, bit) for bit in (1, 2, 3)]
+        columns, *potential = call(
+            functools.partial(columns_kernel, last_pass),
+            [scalars, by_target, *blocks, *notes, parts, *theirs, own_mass],
+            start + (VMEM,) * 9,
+            [side, (8, 128)] if last_pass else [side],
+            buffers + [source_bias_buffer],
+        )
+        partner = member_swap(columns, 4)
+        if last_pass:
+            break
+        sent = call(
+            forward_kernel,
+            [scalars, columns, partner],
+            (SMEM, VMEM, VMEM),
+            [(4, block_rows)] * 3,
+            [],
+        )
+        received = [group_swap(values, bit) for bit, values in enumerate(sent, 1)]
+        (parts,) = call(
+            functools.partial(rows_kernel, False),
+            [scalars, by_source, *blocks, columns, partner, *received],
+            start + (VMEM,) * 5,
+            [side],
+            buffers + [target_bias_buffer, VMEM((8, block_rows), jnp.float32)],
+        )
+    received = [group_swap(columns, bit) for bit in (1, 2, 3)]
+    (final,) = call(
+        finish_kernel,
+        [scalars, columns, partner, *received],
+        (SMEM,) + (VMEM,) * 5,
+        [(8, 128)],
+        [VMEM((8, block_rows), jnp.float32)],
+    )
+    return potential[0].reshape(source_mass.shape), final.reshape(target_mass.shape)
+
+
+def shards(source_vectors, target_vectors, source_mass, target_mass, candidates):
+    quad = lax.axis_size("member") == 8 and lax.axis_size("group") == 4 and candidates.shape == (4, 8)
+    plan = shards_quad if quad else shards_any
+    return plan(source_vectors, target_vectors, source_mass, target_mass, candidates)
+
+
 def solution(mesh):
     placed = (
         P(("group", "member"), None),

time: 284 us -> 93.4 us (0.33)
  blocking collectives: 100 us -> 0 us
  matrix products: 46.9 us -> 0 us
  local copies, waits for them, and re-layouts: 35.9 us -> 3.21 us
  Pallas kernels: 0 us -> 28.6 us
  other arithmetic: 29.1 us -> 5.1 us
  starting transfers between devices: 39.3 us -> 26.1 us
    all_gather x1 -> x0, blocking collectives: 100 us -> none  [shards(): all_lists = lax.all_gather(own_lists, 'member', axis=0, tiled=True)]
    dot_general x33 -> x0, matrix products: 46.9 us -> none  [visit(): jnp.einsum('umk,ugk->umg', source_portion, key_entries, preferred_element...]
    all_to_all x10 -> x0, starting transfers between devices: 39.3 us -> none  [the longest x4 15.8 us: trade_group(): lax.all_to_all(values, 'group', split_axis=0, concat_axis=0, tiled=True)]
    ppermute x0 -> x24, waiting for transfers between devices: none -> 29.2 us  [swap(): lax.ppermute(values, axis, [(index, index ^ bit) for index in range(size)])]
    pallas_call x0 -> x6, Pallas kernels: none -> 28.6 us  [call(): pl.pallas_call(kernel, out_shape=[jax.ShapeDtypeStruct(shape, jnp.float32...]
    gather x45 -> x0, local copies, waits for them, and re-layouts: 28.3 us -> none  [the longest x33 19.2 us: visit(): key_entries = jnp.take(target_blocks, pick_part, axis=0)]
    all_to_all x10 -> x0, waiting for transfers between devices: 27.9 us -> none  [the longest x4 20.4 us: trade_member(): lax.all_to_all(values, 'member', split_axis=0, concat_axis=0, tiled=True)]
    ppermute x0 -> x24, starting transfers between devices: none -> 26.1 us  [swap(): lax.ppermute(values, axis, [(index, index ^ bit) for index in range(size)])]
  transfers between devices with their start and end apart: 10 -> 24, of which waited for: 6 -> 13; matrix products, arithmetic and copies ran while one was open for 23% -> 6% of each run, Pallas kernels for 0% -> 0%
where the time goes in v1:
time: 93.4 us; the launch traced here: 93.1 us
  waiting for transfers between devices  29.2 us (31%)
  Pallas kernels  28.6 us (31%)
  starting transfers between devices  26.1 us (28%)
  other arithmetic  5.1 us (5%)
  local copies, waits for them, and re-layouts  3.21 us (3%)
    ppermute x24, waiting for transfers between devices, swap(): lax.ppermute(values, axis, [(index, index ^ bit) for index in range(size)])  29.2 us
    pallas_call x6, Pallas kernels, call(): pl.pallas_call(kernel, out_shape=[jax.ShapeDtypeStruct(shape, jnp.float32...  28.6 us
    ppermute x24, starting transfers between devices, swap(): lax.ppermute(values, axis, [(index, index ^ bit) for index in range(size)])  26.1 us
  transfers between devices with their start and end apart: 24, of which 13 were waited for; matrix products, arithmetic and copies ran while one was open for 6% of the time, Pallas kernels for 0%

profile of v1, /device:TPU:0, one launch (start us, length us, event | category | flops | bytes accessed | tf_op | source)
XLA Modules:
  0.0 93.1 jit_solution(2681068080492641544)
XLA Ops:
  0.6 0.7 broadcast_multiply_fusion.1
  2.2 2.5 %collective-permute-start.2 = (f32[8,256]{1,0:T(8,128)S(1)}, f32[8,256]{1,0:T(8,128)S(1)}, u32[]{:S(2)}, u32[]{:S(2)}) collective-permute-start(f32[8,256]{1,0:T(8,128)S(1)} %select_maximum_fusion.refs_11_), channel_id=1, source_target_pairs={{0,3},{1,2},{2,1},{3,0},{4,7},{5,6},{6,5},{7,4},{8,11},{9,10},{10,... | collective-permute-start | bytes 24584 | tf_op jit(solution)/shard_map/ppermute | solution.py:353
  5.4 1.7 %collective-permute-start.4 = (bf16[4,256,256]{2,1,0:T(8,128)(2,1)}, bf16[4,256,256]{2,1,0:T(8,128)(2,1)S(1)}, u32[]{:S(2)}, u32[]{:S(2)}) collective-permute-start(bf16[4,256,256]{2,1,0:T(8,128)(2,1)} %bitcast.14), channel_id=1, source_target_pairs={{0,2},{1,3},{2,0},{3,1},{4,6},{5,7},{6,4},{7,5},{8,10},{9,11},{10,... | collective-permute-start | bytes 1572872 | tf_op jit(solution)/shard_map/ppermute | solution.py:353
  7.1 0.7 broadcast_multiply_fusion
  7.8 1.1 %constant_dynamic-slice_fusion.2 = (bf16[1,256,256]{2,1,0:T(8,128)(2,1)S(1)}, bf16[1,256,256]{2,1,0:T(8,128)(2,1)S(1)}, bf16[1,256,256]{2,1,0:T(8,128)(2,1)S(1)}) fusion(bf16[4,256,256]{2,1,0:T(8,128)(2,1)} %bitcast.8, s32[]{:T(128)S(6)} %select_n.145, s32[]{:T(128)S(6)} %select_n.144, s32[]{:T(128)S(6)} %select_n.143), kind=kLoop, calls=%fused_computation.47 | loop fusion | bytes 786444 | tf_op jit(solution)/shard_map/dynamic_slice | solution.py:415
  9.4 2.7 %collective-permute-start.6 = (bf16[4,256,256]{2,1,0:T(8,128)(2,1)S(1)}, bf16[4,256,256]{2,1,0:T(8,128)(2,1)S(1)}, u32[]{:S(2)}, u32[]{:S(2)}) collective-permute-start(bf16[4,256,256]{2,1,0:T(8,128)(2,1)S(1)} %bitcast.9), channel_id=1, source_target_pairs={{0,4},{1,5},{2,6},{3,7},{4,0},{5,1},{6,2},{7,3},{8,12},{9,13},{10,... | collective-permute-start | bytes 1572872 | tf_op jit(solution)/shard_map/ppermute | solution.py:353
  12.1 2.5 %collective-permute-start.9 = (bf16[1,256,256]{2,1,0:T(8,128)(2,1)S(1)}, bf16[1,256,256]{2,1,0:T(8,128)(2,1)S(1)}, u32[]{:S(2)}, u32[]{:S(2)}) collective-permute-start(bf16[1,256,256]{2,1,0:T(8,128)(2,1)S(1)} %get-tuple-element.16), channel_id=1, source_target_pairs={{0,24},{8,16},{16,8},{24,0},{1,25},{9,17},{17,9},{25,1},{2,26},{10... | collective-permute-start | bytes 393224 | tf_op jit(solution)/shard_map/ppermute | solution.py:353
  15.7 0.7 convert_reduce_fusion.1
  16.5 11.9 %collective-permute-done.4.refs_4_ = bf16[4,256,256]{2,1,0:T(8,128)(2,1)S(1)} collective-permute-done((bf16[4,256,256]{2,1,0:T(8,128)(2,1)}, bf16[4,256,256]{2,1,0:T(8,128)(2,1)S(1)}, u32[]{:S(2)}, u32[]{:S(2)}) %collective-permute-start.4) | collective-permute-done | bytes 524320 | tf_op jit(solution)/shard_map/ppermute | solution.py:353
  29.2 1.6 %collective-permute-start.7 = (bf16[1,256,256]{2,1,0:T(8,128)(2,1)S(1)}, bf16[1,256,256]{2,1,0:T(8,128)(2,1)S(1)}, u32[]{:S(2)}, u32[]{:S(2)}) collective-permute-start(bf16[1,256,256]{2,1,0:T(8,128)(2,1)S(1)} %get-tuple-element.18), channel_id=1, source_target_pairs={{0,8},{8,0},{16,24},{24,16},{1,9},{9,1},{17,25},{25,17},{2,10},{10... | collective-permute-start | bytes 393224 | tf_op jit(solution)/shard_map/ppermute | solution.py:353
  31.4 3.7 %collective-permute-done.7.refs_8_ = bf16[1,256,256]{2,1,0:T(8,128)(2,1)S(1)} collective-permute-done((bf16[1,256,256]{2,1,0:T(8,128)(2,1)S(1)}, bf16[1,256,256]{2,1,0:T(8,128)(2,1)S(1)}, u32[]{:S(2)}, u32[]{:S(2)}) %collective-permute-start.7) | collective-permute-done | bytes 131104 | tf_op jit(solution)/shard_map/ppermute | solution.py:353
  35.1 0.9 collective-permute-done.6.refs_7_
  36.1 1.0 %copy-done.1 = bf16[1024,256]{1,0:T(8,128)(2,1)S(1)} copy-done((bf16[1024,256]{1,0:T(8,128)(2,1)S(1)}, bf16[1024,256]{1,0:T(8,128)(2,1)}, u32[]{:S(2)}) %copy-start.1) | copy-done | bytes 524312
  37.1 6.1 %shard_map.68.refs_15_ = f32[16,256]{1,0:T(8,128)S(1)} custom-call(s32[3,40]{1,0:T(4,128)S(1)} %pad_add_fusion.refs_0_.scalars, s32[40,128]{1,0:T(8,128)S(1)} %broadcast_in_dim.89.refs_1_, bf16[4,256,256]{2,1,0:T(8,128)(2,1)S(1)} %bitcast.16, bf16[4,256,256]{2,1,0:T(8,128)(2,1)S(1)} %collective-permute-done.3.refs_3_, ...), custom_call_target="tpu_custom_call" | custom-call | tf_op jit(solution)/shard_map/pallas_call | solution.py:342
  43.3 1.3 %collective-permute-start.11 = (f32[16,256]{1,0:T(8,128)S(1)}, f32[16,256]{1,0:T(8,128)S(1)}, u32[]{:S(2)}, u32[]{:S(2)}) collective-permute-start(f32[16,256]{1,0:T(8,128)S(1)} %shard_map.68.refs_15_), channel_id=1, source_target_pairs={{0,2},{1,3},{2,0},{3,1},{4,6},{5,7},{6,4},{7,5},{8,10},{9,11},{10,... | collective-permute-start | bytes 49160 | tf_op jit(solution)/shard_map/ppermute | solution.py:353
  45.8 0.7 collective-permute-done.12.refs_18_
  47.2 6.8 %shard_map.69.columns.refs_11_ = f32[16,256]{1,0:T(8,128)S(1)} custom-call(s32[3,40]{1,0:T(4,128)S(1)} %pad_add_fusion.refs_0_.scalars, s32[40,128]{1,0:T(8,128)S(1)} %broadcast_in_dim.88.refs_1_, bf16[4,256,256]{2,1,0:T(8,128)(2,1)S(1)} %bitcast.17, bf16[4,256,256]{2,1,0:T(8,128)(2,1)S(1)} %collective-permute-done.3.refs_3_, ...), custom_call_target="tpu_custom_call" | custom-call | tf_op jit(solution)/shard_map/pallas_call | solution.py:342
  54.0 1.3 %collective-permute-start.13 = (f32[16,256]{1,0:T(8,128)S(1)}, f32[16,256]{1,0:T(8,128)S(1)}, u32[]{:S(2)}, u32[]{:S(2)}) collective-permute-start(f32[16,256]{1,0:T(8,128)S(1)} %shard_map.69.columns.refs_11_), channel_id=1, source_target_pairs={{0,4},{1,5},{2,6},{3,7},{4,0},{5,1},{6,2},{7,3},{8,12},{9,13},{10,... | collective-permute-start | bytes 49160 | tf_op jit(solution)/shard_map/ppermute | solution.py:353
  55.3 3.4 %collective-permute-done.13.partner.refs_12_ = f32[16,256]{1,0:T(8,128)S(1)} collective-permute-done((f32[16,256]{1,0:T(8,128)S(1)}, f32[16,256]{1,0:T(8,128)S(1)}, u32[]{:S(2)}, u32[]{:S(2)}) %collective-permute-start.13) | collective-permute-done | bytes 16416 | tf_op jit(solution)/shard_map/ppermute | solution.py:353
  59.3 1.6 %collective-permute-start.14 = (f32[4,256]{1,0:T(4,128)S(1)}, f32[4,256]{1,0:T(4,128)S(1)}, u32[]{:S(2)}, u32[]{:S(2)}) collective-permute-start(f32[4,256]{1,0:T(4,128)S(1)} %get-tuple-element.7), channel_id=1, source_target_pairs={{0,8},{8,0},{16,24},{24,16},{1,9},{9,1},{17,25},{25,17},{2,10},{10... | collective-permute-start | bytes 12296 | tf_op jit(solution)/shard_map/ppermute | solution.py:353
  61.4 1.5 %collective-permute-start.16 = (f32[4,256]{1,0:T(4,128)S(1)}, f32[4,256]{1,0:T(4,128)S(1)}, u32[]{:S(2)}, u32[]{:S(2)}) collective-permute-start(f32[4,256]{1,0:T(4,128)S(1)} %get-tuple-element.9), channel_id=1, source_target_pairs={{0,24},{8,16},{16,8},{24,0},{1,25},{9,17},{17,9},{25,1},{2,26},{10... | collective-permute-start | bytes 12296 | tf_op jit(solution)/shard_map/ppermute | solution.py:353
  63.0 1.5 %collective-permute-done.15.refs_14_ = f32[4,256]{1,0:T(4,128)S(1)} collective-permute-done((f32[4,256]{1,0:T(4,128)S(1)}, f32[4,256]{1,0:T(4,128)S(1)}, u32[]{:S(2)}, u32[]{:S(2)}) %collective-permute-start.15) | collective-permute-done | bytes 4128 | tf_op jit(solution)/shard_map/ppermute | solution.py:353
  64.5 1.4 %collective-permute-done.16.refs_15_ = f32[4,256]{1,0:T(4,128)S(1)} collective-permute-done((f32[4,256]{1,0:T(4,128)S(1)}, f32[4,256]{1,0:T(4,128)S(1)}, u32[]{:S(2)}, u32[]{:S(2)}) %collective-permute-start.16) | collective-permute-done | bytes 4128 | tf_op jit(solution)/shard_map/ppermute | solution.py:353
  65.9 6.7 %shard_map.71.refs_15_ = f32[16,256]{1,0:T(8,128)S(1)} custom-call(s32[3,40]{1,0:T(4,128)S(1)} %pad_add_fusion.refs_0_.scalars, s32[40,128]{1,0:T(8,128)S(1)} %broadcast_in_dim.89.refs_1_, bf16[4,256,256]{2,1,0:T(8,128)(2,1)S(1)} %bitcast.18, bf16[4,256,256]{2,1,0:T(8,128)(2,1)S(1)} %collective-permute-done.3.refs_3_, ...), custom_call_target="tpu_custom_call" | custom-call | tf_op jit(solution)/shard_map/pallas_call | solution.py:342
  72.6 1.4 %collective-permute-start.18 = (f32[16,256]{1,0:T(8,128)S(1)}, f32[16,256]{1,0:T(8,128)S(1)}, u32[]{:S(2)}, u32[]{:S(2)}) collective-permute-start(f32[16,256]{1,0:T(8,128)S(1)} %shard_map.71.refs_15_), channel_id=1, source_target_pairs={{0,2},{1,3},{2,0},{3,1},{4,6},{5,7},{6,4},{7,5},{8,10},{9,11},{10,... | collective-permute-start | bytes 49160 | tf_op jit(solution)/shard_map/ppermute | solution.py:353
  74.5 1.3 %collective-permute-done.19.refs_18_ = f32[16,256]{1,0:T(8,128)S(1)} collective-permute-done((f32[16,256]{1,0:T(8,128)S(1)}, f32[16,256]{1,0:T(8,128)S(1)}, u32[]{:S(2)}, u32[]{:S(2)}) %collective-permute-start.19) | collective-permute-done | bytes 16416 | tf_op jit(solution)/shard_map/ppermute | solution.py:353
  76.5 7.3 %shard_map.72 = (f32[16,256]{1,0:T(8,128)S(1)}, f32[8,128]{1,0:T(8,128)}) custom-call(s32[3,40]{1,0:T(4,128)S(1)} %pad_add_fusion.refs_0_.scalars, s32[40,128]{1,0:T(8,128)S(1)} %broadcast_in_dim.88.refs_1_, bf16[4,256,256]{2,1,0:T(8,128)(2,1)S(1)} %bitcast.19, bf16[4,256,256]{2,1,0:T(8,128)(2,1)S(1)} %collective-permute-done.3.refs_3_, ...), custom_call_target="tpu_custom_call" | custom-call | tf_op jit(solution)/shard_map/pallas_call | solution.py:342
  84.3 2.5 %collective-permute-start.22 = (f32[16,256]{1,0:T(8,128)S(1)}, f32[16,256]{1,0:T(8,128)S(1)}, u32[]{:S(2)}, u32[]{:S(2)}) collective-permute-start(f32[16,256]{1,0:T(8,128)S(1)} %get-tuple-element.11.columns), channel_id=1, source_target_pairs={{0,16},{8,24},{16,0},{24,8},{1,17},{9,25},{17,1},{25,9},{2,18},{10... | collective-permute-start | bytes 49160 | tf_op jit(solution)/shard_map/ppermute | solution.py:353
  87.3 1.6 %collective-permute-start.20 = (f32[16,256]{1,0:T(8,128)S(1)}, f32[16,256]{1,0:T(8,128)S(1)}, u32[]{:S(2)}, u32[]{:S(2)}) collective-permute-start(f32[16,256]{1,0:T(8,128)S(1)} %get-tuple-element.11.columns), channel_id=1, source_target_pairs={{0,4},{1,5},{2,6},{3,7},{4,0},{5,1},{6,2},{7,3},{8,12},{9,13},{10,... | collective-permute-start | bytes 49160 | tf_op jit(solution)/shard_map/ppermute | solution.py:353
  88.9 1.6 %collective-permute-done.21.rest_0_ = f32[16,256]{1,0:T(8,128)S(1)} collective-permute-done((f32[16,256]{1,0:T(8,128)S(1)}, f32[16,256]{1,0:T(8,128)S(1)}, u32[]{:S(2)}, u32[]{:S(2)}) %collective-permute-start.21) | collective-permute-done | bytes 16416 | tf_op jit(solution)/shard_map/ppermute | solution.py:353
  90.5 1.4 %collective-permute-done.20.partner = f32[16,256]{1,0:T(8,128)S(1)} collective-permute-done((f32[16,256]{1,0:T(8,128)S(1)}, f32[16,256]{1,0:T(8,128)S(1)}, u32[]{:S(2)}, u32[]{:S(2)}) %collective-permute-start.20) | collective-permute-done | bytes 16416 | tf_op jit(solution)/shard_map/ppermute | solution.py:353
  91.9 1.2 %shard_map.73 = f32[8,128]{1,0:T(8,128)} custom-call(s32[3,40]{1,0:T(4,128)S(1)} %pad_add_fusion.refs_0_.scalars, f32[16,256]{1,0:T(8,128)S(1)} %get-tuple-element.11.columns, f32[16,256]{1,0:T(8,128)S(1)} %collective-permute-done.20.partner, f32[16,256]{1,0:T(8,128)S(1)} %collective-permute-done.21.rest_0_, f32[16,256]{1,0:T(8,128)S(1)} %collective-permute-done.22.rest_1_, ...), custom_call_target="tpu_custom_call" | custom-call | tf_op jit(solution)/shard_map/pallas_call | solution.py:342
  (66 shorter events, 10.0 us)
Async XLA Ops:
  0.6 8.8 %copy-start = (bf16[1024,256]{1,0:T(8,128)(2,1)S(1)}, bf16[1024,256]{1,0:T(8,128)(2,1)}, u32[]{:S(2)}) copy-start(bf16[1024,256]{1,0:T(8,128)(2,1)} %param.6) | copy-start | bytes 1572868
  2.2 7.2 %collective-permute-start.2 = (f32[8,256]{1,0:T(8,128)S(1)}, f32[8,256]{1,0:T(8,128)S(1)}, u32[]{:S(2)}, u32[]{:S(2)}) collective-permute-start(f32[8,256]{1,0:T(8,128)S(1)} %select_maximum_fusion.refs_11_), channel_id=1, source_target_pairs={{0,3},{1,2},{2,1},{3,0},{4,7},{5,6},{6,5},{7,4},{8,11},{9,10},{10,... | collective-permute-start | bytes 24584 | tf_op jit(solution)/shard_map/ppermute | solution.py:353
  4.7 7.4 %collective-permute-start.1 = (f32[8,256]{1,0:T(8,128)S(1)}, f32[8,256]{1,0:T(8,128)S(1)}, u32[]{:S(2)}, u32[]{:S(2)}) collective-permute-start(f32[8,256]{1,0:T(8,128)S(1)} %select_maximum_fusion.refs_11_), channel_id=1, source_target_pairs={{0,2},{1,3},{2,0},{3,1},{4,6},{5,7},{6,4},{7,5},{8,10},{9,11},{10,... | collective-permute-start | bytes 24584 | tf_op jit(solution)/shard_map/ppermute | solution.py:353
  5.3 9.3 %collective-permute-start = (f32[8,256]{1,0:T(8,128)S(1)}, f32[8,256]{1,0:T(8,128)S(1)}, u32[]{:S(2)}, u32[]{:S(2)}) collective-permute-start(f32[8,256]{1,0:T(8,128)S(1)} %select_maximum_fusion.refs_11_), channel_id=1, source_target_pairs={{0,1},{1,0},{2,3},{3,2},{4,5},{5,4},{6,7},{7,6},{8,9},{9,8},{10,11... | collective-permute-start | bytes 24584 | tf_op jit(solution)/shard_map/ppermute | solution.py:353
  5.4 23.0 %collective-permute-start.4 = (bf16[4,256,256]{2,1,0:T(8,128)(2,1)}, bf16[4,256,256]{2,1,0:T(8,128)(2,1)S(1)}, u32[]{:S(2)}, u32[]{:S(2)}) collective-permute-start(bf16[4,256,256]{2,1,0:T(8,128)(2,1)} %bitcast.14), channel_id=1, source_target_pairs={{0,2},{1,3},{2,0},{3,1},{4,6},{5,7},{6,4},{7,5},{8,10},{9,11},{10,... | collective-permute-start | bytes 1572872 | tf_op jit(solution)/shard_map/ppermute | solution.py:353
  7.1 28.0 %collective-permute-start.3 = (bf16[4,256,256]{2,1,0:T(8,128)(2,1)}, bf16[4,256,256]{2,1,0:T(8,128)(2,1)S(1)}, u32[]{:S(2)}, u32[]{:S(2)}) collective-permute-start(bf16[4,256,256]{2,1,0:T(8,128)(2,1)} %bitcast.15), channel_id=1, source_target_pairs={{0,1},{1,0},{2,3},{3,2},{4,5},{5,4},{6,7},{7,6},{8,9},{9,8},{10,11... | collective-permute-start | bytes 1572872 | tf_op jit(solution)/shard_map/ppermute | solution.py:353
  9.4 26.6 %collective-permute-start.6 = (bf16[4,256,256]{2,1,0:T(8,128)(2,1)S(1)}, bf16[4,256,256]{2,1,0:T(8,128)(2,1)S(1)}, u32[]{:S(2)}, u32[]{:S(2)}) collective-permute-start(bf16[4,256,256]{2,1,0:T(8,128)(2,1)S(1)} %bitcast.9), channel_id=1, source_target_pairs={{0,4},{1,5},{2,6},{3,7},{4,0},{5,1},{6,2},{7,3},{8,12},{9,13},{10,... | collective-permute-start | bytes 1572872 | tf_op jit(solution)/shard_map/ppermute | solution.py:353
  12.1 17.0 %collective-permute-start.9 = (bf16[1,256,256]{2,1,0:T(8,128)(2,1)S(1)}, bf16[1,256,256]{2,1,0:T(8,128)(2,1)S(1)}, u32[]{:S(2)}, u32[]{:S(2)}) collective-permute-start(bf16[1,256,256]{2,1,0:T(8,128)(2,1)S(1)} %get-tuple-element.16), channel_id=1, source_target_pairs={{0,24},{8,16},{16,8},{24,0},{1,25},{9,17},{17,9},{25,1},{2,26},{10... | collective-permute-start | bytes 393224 | tf_op jit(solution)/shard_map/ppermute | solution.py:353
  14.6 16.8 %collective-permute-start.8 = (bf16[1,256,256]{2,1,0:T(8,128)(2,1)S(1)}, bf16[1,256,256]{2,1,0:T(8,128)(2,1)S(1)}, u32[]{:S(2)}, u32[]{:S(2)}) collective-permute-start(bf16[1,256,256]{2,1,0:T(8,128)(2,1)S(1)} %get-tuple-element.17), channel_id=1, source_target_pairs={{0,16},{8,24},{16,0},{24,8},{1,17},{9,25},{17,1},{25,9},{2,18},{10... | collective-permute-start | bytes 393224 | tf_op jit(solution)/shard_map/ppermute | solution.py:353
  28.4 7.6 %collective-permute-start.5 = (bf16[4,256,256]{2,1,0:T(8,128)(2,1)S(1)}, bf16[4,256,256]{2,1,0:T(8,128)(2,1)S(1)}, u32[]{:S(2)}, u32[]{:S(2)}) collective-permute-start(bf16[4,256,256]{2,1,0:T(8,128)(2,1)S(1)} %collective-permute-done.4.refs_4_), channel_id=1, source_target_pairs={{0,1},{1,0},{2,3},{3,2},{4,5},{5,4},{6,7},{7,6},{8,9},{9,8},{10,11... | collective-permute-start | bytes 1572872 | tf_op jit(solution)/shard_map/ppermute | solution.py:353
  29.2 6.0 %collective-permute-start.7 = (bf16[1,256,256]{2,1,0:T(8,128)(2,1)S(1)}, bf16[1,256,256]{2,1,0:T(8,128)(2,1)S(1)}, u32[]{:S(2)}, u32[]{:S(2)}) collective-permute-start(bf16[1,256,256]{2,1,0:T(8,128)(2,1)S(1)} %get-tuple-element.18), channel_id=1, source_target_pairs={{0,8},{8,0},{16,24},{24,16},{1,9},{9,1},{17,25},{25,17},{2,10},{10... | collective-permute-start | bytes 393224 | tf_op jit(solution)/shard_map/ppermute | solution.py:353
  36.1 1.0 %copy-start.1 = (bf16[1024,256]{1,0:T(8,128)(2,1)S(1)}, bf16[1024,256]{1,0:T(8,128)(2,1)}, u32[]{:S(2)}) copy-start(bf16[1024,256]{1,0:T(8,128)(2,1)} %param.5) | copy-start | bytes 1572868
  37.1 10.1 %copy-start.2 = (bf16[1024,256]{1,0:T(8,128)(2,1)S(1)}, bf16[1024,256]{1,0:T(8,128)(2,1)}, u32[]{:S(2)}) copy-start(bf16[1024,256]{1,0:T(8,128)(2,1)} %param.5) | copy-start | bytes 1572868
  43.3 3.3 %collective-permute-start.12 = (f32[16,256]{1,0:T(8,128)S(1)}, f32[16,256]{1,0:T(8,128)S(1)}, u32[]{:S(2)}, u32[]{:S(2)}) collective-permute-start(f32[16,256]{1,0:T(8,128)S(1)} %shard_map.68.refs_15_), channel_id=1, source_target_pairs={{0,3},{1,2},{2,1},{3,0},{4,7},{5,6},{6,5},{7,4},{8,11},{9,10},{10,... | collective-permute-start | bytes 49160 | tf_op jit(solution)/shard_map/ppermute | solution.py:353
  43.3 3.8 %collective-permute-start.11 = (f32[16,256]{1,0:T(8,128)S(1)}, f32[16,256]{1,0:T(8,128)S(1)}, u32[]{:S(2)}, u32[]{:S(2)}) collective-permute-start(f32[16,256]{1,0:T(8,128)S(1)} %shard_map.68.refs_15_), channel_id=1, source_target_pairs={{0,2},{1,3},{2,0},{3,1},{4,6},{5,7},{6,4},{7,5},{8,10},{9,11},{10,... | collective-permute-start | bytes 49160 | tf_op jit(solution)/shard_map/ppermute | solution.py:353
  44.7 2.5 %collective-permute-start.10 = (f32[16,256]{1,0:T(8,128)S(1)}, f32[16,256]{1,0:T(8,128)S(1)}, u32[]{:S(2)}, u32[]{:S(2)}) collective-permute-start(f32[16,256]{1,0:T(8,128)S(1)} %shard_map.68.refs_15_), channel_id=1, source_target_pairs={{0,1},{1,0},{2,3},{3,2},{4,5},{5,4},{6,7},{7,6},{8,9},{9,8},{10,11... | collective-permute-start | bytes 49160 | tf_op jit(solution)/shard_map/ppermute | solution.py:353
  54.0 4.7 %collective-permute-start.13 = (f32[16,256]{1,0:T(8,128)S(1)}, f32[16,256]{1,0:T(8,128)S(1)}, u32[]{:S(2)}, u32[]{:S(2)}) collective-permute-start(f32[16,256]{1,0:T(8,128)S(1)} %shard_map.69.columns.refs_11_), channel_id=1, source_target_pairs={{0,4},{1,5},{2,6},{3,7},{4,0},{5,1},{6,2},{7,3},{8,12},{9,13},{10,... | collective-permute-start | bytes 49160 | tf_op jit(solution)/shard_map/ppermute | solution.py:353
  59.3 3.7 %collective-permute-start.14 = (f32[4,256]{1,0:T(4,128)S(1)}, f32[4,256]{1,0:T(4,128)S(1)}, u32[]{:S(2)}, u32[]{:S(2)}) collective-permute-start(f32[4,256]{1,0:T(4,128)S(1)} %get-tuple-element.7), channel_id=1, source_target_pairs={{0,8},{8,0},{16,24},{24,16},{1,9},{9,1},{17,25},{25,17},{2,10},{10... | collective-permute-start | bytes 12296 | tf_op jit(solution)/shard_map/ppermute | solution.py:353
  60.9 3.6 %collective-permute-start.15 = (f32[4,256]{1,0:T(4,128)S(1)}, f32[4,256]{1,0:T(4,128)S(1)}, u32[]{:S(2)}, u32[]{:S(2)}) collective-permute-start(f32[4,256]{1,0:T(4,128)S(1)} %get-tuple-element.8), channel_id=1, source_target_pairs={{0,16},{8,24},{16,0},{24,8},{1,17},{9,25},{17,1},{25,9},{2,18},{10... | collective-permute-start | bytes 12296 | tf_op jit(solution)/shard_map/ppermute | solution.py:353
  61.4 4.5 %collective-permute-start.16 = (f32[4,256]{1,0:T(4,128)S(1)}, f32[4,256]{1,0:T(4,128)S(1)}, u32[]{:S(2)}, u32[]{:S(2)}) collective-permute-start(f32[4,256]{1,0:T(4,128)S(1)} %get-tuple-element.9), channel_id=1, source_target_pairs={{0,24},{8,16},{16,8},{24,0},{1,25},{9,17},{17,9},{25,1},{2,26},{10... | collective-permute-start | bytes 12296 | tf_op jit(solution)/shard_map/ppermute | solution.py:353
  72.6 3.3 %collective-permute-start.19 = (f32[16,256]{1,0:T(8,128)S(1)}, f32[16,256]{1,0:T(8,128)S(1)}, u32[]{:S(2)}, u32[]{:S(2)}) collective-permute-start(f32[16,256]{1,0:T(8,128)S(1)} %shard_map.71.refs_15_), channel_id=1, source_target_pairs={{0,3},{1,2},{2,1},{3,0},{4,7},{5,6},{6,5},{7,4},{8,11},{9,10},{10,... | collective-permute-start | bytes 49160 | tf_op jit(solution)/shard_map/ppermute | solution.py:353
  72.6 3.8 %collective-permute-start.18 = (f32[16,256]{1,0:T(8,128)S(1)}, f32[16,256]{1,0:T(8,128)S(1)}, u32[]{:S(2)}, u32[]{:S(2)}) collective-permute-start(f32[16,256]{1,0:T(8,128)S(1)} %shard_map.71.refs_15_), channel_id=1, source_target_pairs={{0,2},{1,3},{2,0},{3,1},{4,6},{5,7},{6,4},{7,5},{8,10},{9,11},{10,... | collective-permute-start | bytes 49160 | tf_op jit(solution)/shard_map/ppermute | solution.py:353
  74.0 2.4 %collective-permute-start.17 = (f32[16,256]{1,0:T(8,128)S(1)}, f32[16,256]{1,0:T(8,128)S(1)}, u32[]{:S(2)}, u32[]{:S(2)}) collective-permute-start(f32[16,256]{1,0:T(8,128)S(1)} %shard_map.71.refs_15_), channel_id=1, source_target_pairs={{0,1},{1,0},{2,3},{3,2},{4,5},{5,4},{6,7},{7,6},{8,9},{9,8},{10,11... | collective-permute-start | bytes 49160 | tf_op jit(solution)/shard_map/ppermute | solution.py:353
  83.7 5.2 %collective-permute-start.23 = (f32[16,256]{1,0:T(8,128)S(1)}, f32[16,256]{1,0:T(8,128)S(1)}, u32[]{:S(2)}, u32[]{:S(2)}) collective-permute-start(f32[16,256]{1,0:T(8,128)S(1)} %get-tuple-element.11.columns), channel_id=1, source_target_pairs={{0,24},{8,16},{16,8},{24,0},{1,25},{9,17},{17,9},{25,1},{2,26},{10... | collective-permute-start | bytes 49160 | tf_op jit(solution)/shard_map/ppermute | solution.py:353
  84.3 4.6 %collective-permute-start.22 = (f32[16,256]{1,0:T(8,128)S(1)}, f32[16,256]{1,0:T(8,128)S(1)}, u32[]{:S(2)}, u32[]{:S(2)}) collective-permute-start(f32[16,256]{1,0:T(8,128)S(1)} %get-tuple-element.11.columns), channel_id=1, source_target_pairs={{0,16},{8,24},{16,0},{24,8},{1,17},{9,25},{17,1},{25,9},{2,18},{10... | collective-permute-start | bytes 49160 | tf_op jit(solution)/shard_map/ppermute | solution.py:353
  86.8 3.7 %collective-permute-start.21 = (f32[16,256]{1,0:T(8,128)S(1)}, f32[16,256]{1,0:T(8,128)S(1)}, u32[]{:S(2)}, u32[]{:S(2)}) collective-permute-start(f32[16,256]{1,0:T(8,128)S(1)} %get-tuple-element.11.columns), channel_id=1, source_target_pairs={{0,8},{8,0},{16,24},{24,16},{1,9},{9,1},{17,25},{25,17},{2,10},{10... | collective-permute-start | bytes 49160 | tf_op jit(solution)/shard_map/ppermute | solution.py:353
  87.3 4.6 %collective-permute-start.20 = (f32[16,256]{1,0:T(8,128)S(1)}, f32[16,256]{1,0:T(8,128)S(1)}, u32[]{:S(2)}, u32[]{:S(2)}) collective-permute-start(f32[16,256]{1,0:T(8,128)S(1)} %get-tuple-element.11.columns), channel_id=1, source_target_pairs={{0,4},{1,5},{2,6},{3,7},{4,0},{5,1},{6,2},{7,3},{8,12},{9,13},{10,... | collective-permute-start | bytes 49160 | tf_op jit(solution)/shard_map/ppermute | solution.py:353

commit v2 on v0

--- a/solution.py
+++ b/solution.py
@@ -1,6 +1,10 @@
+import functools
+
 import jax
 import jax.numpy as jnp
 from jax import lax
+from jax.experimental import pallas as pl
+from jax.experimental.pallas import tpu as pltpu
 from jax.sharding import PartitionSpec as P
 
 ITERS = 2
@@ -67,7 +71,7 @@
     return entropy_strength * target_marginal - entropy_strength * jnp.stack(output_list)
 
 
-def shards(source_vectors, target_vectors, source_mass, target_mass, candidates):
+def shards_any(source_vectors, target_vectors, source_mass, target_mass, candidates):
     members = lax.axis_size("member")
     groups = lax.axis_size("group")
     own_member = lax.axis_index("member")
@@ -157,6 +161,423 @@
     )
 
 
+LOG2E = 1.4426950408889634
+TO_LOGIT = LOG2E / entropy_strength
+TO_POTENTIAL = entropy_strength / LOG2E
+CAPACITY = 4
+SOURCE_SLOTS = 16
+TARGET_SLOTS = 12
+FAR = 8
+SECTIONS = ((0, 12), (12, 8), (20, 8), (28, 8))
+TILE_SLOTS = 40
+SMALL, LARGE = 2.0**-100, 2.0**100
+
+
+def merge(parts):
+    top = functools.reduce(jnp.maximum, parts)
+    return top + LOG2E * jnp.log(sum(jnp.exp2(part - top) for part in parts))
+
+
+def swapped(rows, size):
+    pieces = [rows[start : start + size] for start in range(0, rows.shape[0], size)]
+    return jnp.concatenate([pieces[index ^ 1] for index in range(len(pieces))], axis=0)
+
+
+def source_bias(note_refs, part_refs):
+    own, core, near, cross = (ref[...] for ref in part_refs)
+    core = swapped(core, 4)
+    near = swapped(near, 8)
+    cross = swapped(swapped(cross, 4), 8)
+    mass = jnp.concatenate([ref[0:4] for ref in note_refs], axis=0)
+    return mass - merge([own, core, near, cross])
+
+
+def target_bias(scalars, columns, partner, mirrors, scratch):
+    group = scalars[4, 0]
+    scratch[...] = jnp.full(scratch.shape, very_low, jnp.float32)
+    for offset, ref in enumerate(mirrors, 1):
+        scratch[pl.ds(group ^ offset, 1), :] = ref[0:1]
+        scratch[pl.ds(4 + (group ^ offset), 1), :] = ref[1:2]
+    own = columns[12:16] - merge([columns[0:4], partner[8:12], scratch[0:4]])
+    far = partner[12:16] - merge([columns[8:12], partner[0:4], scratch[4:8]])
+    across = [
+        ref[3:4] - merge([ref[2:3], columns[3 + offset : 4 + offset]])
+        for offset, ref in enumerate(mirrors, 1)
+    ]
+    blank = jnp.zeros((1, own.shape[1]), jnp.float32)
+    return jnp.concatenate([own, *across, blank, far, *([blank] * 4)], axis=0)
+
+
+def spread(rows, bias):
+    high = rows.astype(jnp.bfloat16)
+    rest = rows - high.astype(jnp.float32)
+    middle = rest.astype(jnp.bfloat16)
+    low = (rest - middle.astype(jnp.float32)).astype(jnp.bfloat16)
+    parts = jnp.concatenate([high, middle, low], axis=0)
+    count = rows.shape[0]
+    shape = (3 * count, count * 128)
+    slot = lax.broadcasted_iota(jnp.int32, shape, 0) & (count - 1)
+    place = lax.broadcasted_iota(jnp.int32, shape, 1) >> 7
+    chosen = jnp.where(slot == place, 1.0, 0.0).astype(jnp.bfloat16)
+    turned = lax.dot_general(
+        parts, chosen, (((0,), (0,)), ((), ())), preferred_element_type=jnp.float32
+    )
+    for index in range(bias.shape[0]):
+        bias[index] = turned[:, 128 * index : 128 * (index + 1)]
+
+
+def score(summed, kept):
+    product = lax.dot_general(summed, kept, (((1,), (1,)), ((), ())), preferred_element_type=jnp.float32)
+    return product * TO_LOGIT
+
+
+def wide(values):
+    return jnp.concatenate([values, values], axis=1)
+
+
+def sides(section, by_rows, sources, targets):
+    late_source, late_target = section in (1, 3), section in (2, 3)
+    source = (sources[late_source], 0, 8 if late_source else 0)
+    target = (targets[late_target], 1, FAR if late_target else 0)
+    return (target, source) if by_rows else (source, target)
+
+
+def exact_pass(scalars, ids, by_rows, sections, sources, targets, bias, tops, sums, unrolled):
+    for section in sections:
+        first, count = SECTIONS[section]
+        (summed, summed_row, summed_base), (kept, kept_row, _) = sides(section, by_rows, sources, targets)
+
+        def visit(slot, carry=0):
+            block = scalars[summed_row, slot]
+            logits = score(summed[block], kept[scalars[kept_row, slot]])
+            if bias is not None:
+                logits = logits + wide(bias[summed_base + block])
+            top = jnp.max(logits, axis=0, keepdims=True)
+            tops[pl.ds(slot, 1), :] = top
+            sums[pl.ds(slot, 1), :] = jnp.sum(jnp.exp2(logits - top), axis=0, keepdims=True)
+            return carry
+
+        if unrolled:
+            for slot in range(first, first + count):
+                visit(slot)
+        else:
+            lax.fori_loop(first, first + count, visit, 0)
+    first, last = SECTIONS[sections[0]][0], sum(SECTIONS[sections[-1]])
+    low, high = first // 8 * 8, (last + 7) // 8 * 8
+    id_rows = wide(ids[low:high])
+    if low < first or last < high:
+        slot = low + lax.broadcasted_iota(jnp.int32, id_rows.shape, 0)
+        id_rows = jnp.where(jnp.logical_and(slot >= first, slot < last), id_rows, -1)
+    top_rows, sum_rows = tops[low:high], sums[low:high]
+    best, total = [], []
+    for block in range(SOURCE_SLOTS if by_rows else TARGET_SLOTS):
+        mine = id_rows == block
+        top = jnp.max(jnp.where(mine, top_rows, very_low), axis=0, keepdims=True)
+        best.append(top)
+        total.append(
+            jnp.sum(jnp.where(mine, sum_rows * jnp.exp2(top_rows - top), 0.0), axis=0, keepdims=True)
+        )
+    best = jnp.concatenate(best, axis=0)
+    total = jnp.concatenate(total, axis=0)
+    return jnp.where(total > 0, best + LOG2E * jnp.log(jnp.where(total > 0, total, 1.0)), very_low)
+
+
+def fast_pass(scalars, ids, present, by_rows, sources, targets, bias, reference, total, tops, sums, out):
+    total[...] = jnp.zeros(total.shape, jnp.float32)
+    for section, (first, count) in enumerate(SECTIONS):
+        (summed, summed_row, summed_base), (kept, kept_row, kept_base) = sides(
+            section, by_rows, sources, targets
+        )
+        for slot in range(first, first + count):
+            block, partner = scalars[summed_row, slot], scalars[kept_row, slot]
+            logits = score(summed[block], kept[partner]) + wide(bias[summed_base + block])
+            if reference is not None:
+                logits = logits + reference[pl.ds(kept_base + partner, 1), :]
+            terms = jnp.exp2(logits)
+            place = scalars[2 + kept_row, slot]
+            total[place] = total[place] + jnp.sum(terms.reshape(-1, 8, terms.shape[1]), axis=0)
+    count = SOURCE_SLOTS if by_rows else TARGET_SLOTS
+    sums_of = jnp.concatenate(
+        [jnp.sum(total[block], axis=0, keepdims=True) for block in range(count)], axis=0
+    )
+    here = wide(present[0:count]) > 0
+    result = LOG2E * jnp.log(jnp.where(here, sums_of, 1.0))
+    if reference is not None:
+        result = result - reference[0:count]
+    out[0:count, :] = jnp.where(here, result, very_low)
+    fine = jnp.logical_and(sums_of > SMALL, sums_of < LARGE)
+    worst = jnp.min(jnp.where(jnp.logical_or(fine, jnp.logical_not(here)), 1.0, 0.0))
+
+    @pl.when(worst < 0.5)
+    def _():
+        out[0:count, :] = exact_pass(
+            scalars, ids, by_rows, (0, 1, 2, 3), sources, targets, bias, tops, sums, False
+        )
+
+
+def early_kernel(
+    scalars, ids, own, core, target, mirror_1, mirror_2, mirror_3, out, sources, targets, tops, sums
+):
+    sources[0:4] = own[...]
+    sources[4:8] = core[...]
+    targets[0:4] = target[...]
+    for index, mirror in enumerate((mirror_1, mirror_2, mirror_3)):
+        targets[4 + index : 5 + index] = mirror[...]
+    out[...] = exact_pass(
+        scalars, ids, True, (0,), (sources, None), (targets, None), None, tops, sums, True
+    )
+
+
+def first_kernel(
+    scalars, ids, early, sources, near, cross, targets, far, out, late_sources, tops, sums
+):
+    late_sources[0:4] = near[...]
+    late_sources[4:8] = cross[...]
+    late = exact_pass(
+        scalars, ids, True, (1, 2, 3), (sources, late_sources), (targets, far), None, tops, sums, True
+    )
+    out[...] = merge([early[...], late])
+
+
+def columns_kernel(last_pass, *refs):
+    scalars, ids, present = refs[:3]
+    sources, targets = refs[3:5], refs[5:7]
+    notes, parts, target_mass = refs[7:11], refs[11:15], refs[15]
+    rest = refs[16:]
+    reference = None
+    if last_pass:
+        reference, *rest = rest
+    out, second, total, tops, sums, bias = rest
+    rows = source_bias(notes, parts)
+    spread(rows, bias)
+    if last_pass:
+        for block in range(4):
+            for half in range(2):
+                second[2 * block + half : 2 * block + half + 1, :] = (
+                    TO_POTENTIAL * rows[block : block + 1, 128 * half : 128 * (half + 1)]
+                )
+    else:
+        second[...] = rows
+    fast_pass(
+        scalars, ids, present, False, sources, targets, bias, reference, total, tops, sums, out
+    )
+    out[12:16, :] = target_mass[0:4]
+
+
+def rows_kernel(*refs):
+    scalars, ids, present = refs[:3]
+    sources, targets = refs[3:5], refs[5:7]
+    reference, columns, partner, *mirrors = refs[7:13]
+    out, second, total, tops, sums, bias, scratch = refs[13:]
+    rows = target_bias(scalars, columns, partner, mirrors, scratch)
+    spread(rows, bias)
+    second[...] = rows
+    fast_pass(
+        scalars, ids, present, True, sources, targets, bias, reference, total, tops, sums, out
+    )
+
+
+def forward_kernel(scalars, columns, partner, *outs):
+    group = scalars[4, 0]
+    for offset, out in enumerate(outs, 1):
+        block = group ^ offset
+        out[0:1, :] = columns[3 + offset : 4 + offset]
+        out[1:2, :] = partner[3 + offset : 4 + offset]
+        out[2:3, :] = merge([columns[pl.ds(block, 1), :], partner[pl.ds(FAR + block, 1), :]])
+        out[3:4, :] = columns[pl.ds(12 + block, 1), :]
+
+
+def finish_kernel(scalars, columns, partner, *rest):
+    *mirrors, out, scratch = rest
+    group = scalars[4, 0]
+    scratch[...] = jnp.full(scratch.shape, very_low, jnp.float32)
+    for offset, ref in enumerate(mirrors, 1):
+        scratch[pl.ds(group ^ offset, 1), :] = ref[3 + offset : 4 + offset]
+    rows = columns[12:16] - merge([columns[0:4], partner[8:12], scratch[0:4]])
+    for block in range(4):
+        for half in range(2):
+            out[2 * block + half : 2 * block + half + 1, :] = (
+                TO_POTENTIAL * rows[block : block + 1, 128 * half : 128 * (half + 1)]
+            )
+
+
+SMEM, VMEM = pltpu.SMEM, pltpu.VMEM
+
+
+def call(kernel, inputs, outs, scratch=()):
+    whole = pl.BlockSpec(memory_space=VMEM)
+    return pl.pallas_call(
+        kernel,
+        out_shape=outs,
+        in_specs=[pl.BlockSpec(memory_space=SMEM)] + [whole] * (len(inputs) - 1),
+        out_specs=[whole] * len(outs),
+        scratch_shapes=list(scratch),
+        compiler_params=pltpu.CompilerParams(vmem_limit_bytes=32 << 20),
+    )(*inputs)
+
+
+def swap(values, axis, size, bit):
+    return lax.ppermute(values, axis, [(index, index ^ bit) for index in range(size)])
+
+
+def tile_lists(candidates, own_group, own_member, members, per_device):
+    owner = candidates // per_device
+    local = candidates % per_device
+    apart = (owner % members) ^ own_member
+    last = candidates.shape[1] - 1
+    mirror = (owner // members) ^ own_group
+    is_last = jnp.arange(last + 1)[None, :] == last
+    source = jnp.broadcast_to(jnp.arange(SOURCE_SLOTS, dtype=jnp.int32)[:, None], candidates.shape)
+    own_mirror = jnp.logical_and(is_last, source < per_device)
+    near = jnp.logical_and(~is_last, apart == 0)
+    far = jnp.logical_and(~is_last, apart == 4)
+    late = source >= 2 * per_device
+    target = jnp.where(jnp.logical_and(is_last, mirror > 0), 3 + mirror, local)
+    members_of = (
+        jnp.logical_or(jnp.logical_and(near, ~late), own_mirror),
+        jnp.logical_and(near, late),
+        jnp.logical_and(far, ~late),
+        jnp.logical_and(far, late),
+    )
+    source, target = source.reshape(1, -1), target.reshape(1, -1)
+    order = jnp.arange(source.shape[1], dtype=jnp.int32)
+    before = order[None, :] < order[:, None]
+    place = jnp.full(order.shape, -1, jnp.int32)
+    for (first, _), taken in zip(SECTIONS, members_of):
+        taken = taken.reshape(-1)
+        earlier = jnp.sum(jnp.logical_and(before, taken[None, :]).astype(jnp.int32), axis=1)
+        place = jnp.where(taken, first + earlier, place)
+    slots = jnp.arange(TILE_SLOTS, dtype=jnp.int32)
+    hits = place[None, :] == slots[:, None]
+    used = jnp.any(hits, axis=1)
+    sources = jnp.sum(jnp.where(hits, source, 0), axis=1)
+    targets = jnp.sum(jnp.where(hits, target, 0), axis=1)
+    late_slot = jnp.logical_or(jnp.logical_and(slots >= 12, slots < 20), slots >= 28)
+    source_ids = jnp.where(used, sources, -1)
+    target_ids = jnp.where(used, jnp.where(slots >= 20, FAR + targets, targets), -1)
+    scalars = jnp.stack(
+        [
+            jnp.where(jnp.logical_and(late_slot, used), sources - 8, sources),
+            targets,
+            jnp.where(used, source_ids, SOURCE_SLOTS),
+            jnp.where(used, target_ids, TARGET_SLOTS),
+            jnp.broadcast_to(own_group, slots.shape).astype(jnp.int32),
+        ]
+    )
+    lists = []
+    for ids in (source_ids, target_ids):
+        rows = jnp.any(ids[None, :] == jnp.arange(16)[:, None], axis=1).astype(jnp.float32)
+        lists.append(jnp.broadcast_to(ids[:, None], (TILE_SLOTS, 128)))
+        lists.append(jnp.broadcast_to(rows[:, None], (16, 128)))
+    return scalars, *lists
+
+
+def shards_quad(source_vectors, target_vectors, source_mass, target_mass, candidates):
+    members = lax.axis_size("member")
+    groups = lax.axis_size("group")
+    own_group = lax.axis_index("group")
+    own_member = lax.axis_index("member")
+    per_device, cand_count = candidates.shape
+    block_rows = source_vectors.shape[0] // per_device
+    width = source_vectors.shape[1]
+    blocked = (per_device, block_rows, width)
+    member_swap = lambda values, bit: swap(values, "member", members, bit)
+    group_swap = lambda values, bit: swap(values, "group", groups, bit)
+
+    source_own = source_vectors.reshape(blocked)
+    target_own = target_vectors.reshape(blocked)
+    target_far = member_swap(target_own, 4)
+    source_near = member_swap(source_own, 2)
+    source_core = member_swap(source_own, 1)
+    source_cross = member_swap(source_near, 1)
+    source_mass_late, candidates_late, target_late, _ = lax.optimization_barrier(
+        (source_mass, candidates, target_own, source_core)
+    )
+    note = jnp.concatenate(
+        [
+            LOG2E * source_mass_late.reshape(per_device, block_rows),
+            jnp.pad(
+                candidates_late.astype(jnp.float32).reshape(1, per_device * cand_count),
+                ((0, 3), (0, block_rows - per_device * cand_count)),
+            ),
+        ]
+    )
+    notes = [note] + [member_swap(note, bit) for bit in (1, 2, 3)]
+    mirrors = [
+        group_swap(lax.dynamic_slice_in_dim(target_late, own_group ^ bit, 1, 0), bit) for bit in (1, 2, 3)
+    ]
+    named = jnp.stack([values[4, : per_device * cand_count] for values in notes])
+    named = named.reshape(SOURCE_SLOTS, cand_count).astype(jnp.int32)
+    scalars, by_source, has_source, by_target, has_target = tile_lists(
+        named, own_group, own_member, members, per_device
+    )
+    own_mass = LOG2E * target_mass.reshape(per_device, block_rows)
+
+    side = jax.ShapeDtypeStruct((16, block_rows), jnp.float32)
+    flat = jax.ShapeDtypeStruct((8, 128), jnp.float32)
+    stacked = lambda count: jax.ShapeDtypeStruct((count, block_rows, width), source_vectors.dtype)
+    tile_rows = [VMEM((TILE_SLOTS, block_rows), jnp.float32)] * 2
+    pass_buffers = [
+        VMEM((SOURCE_SLOTS + 1, 8, block_rows), jnp.float32),
+        *tile_rows,
+        VMEM((SOURCE_SLOTS, block_rows, 128), jnp.float32),
+    ]
+
+    early, sources, targets = call(
+        early_kernel,
+        [scalars, by_source, source_own, source_core, target_own, *mirrors],
+        [side, stacked(8), stacked(7)],
+        tile_rows,
+    )
+    parts, late_sources = call(
+        first_kernel,
+        [scalars, by_source, early, sources, source_near, source_cross, targets, target_far],
+        [side, stacked(8)],
+        tile_rows,
+    )
+    blocks = [sources, late_sources, targets, target_far]
+    reference = []
+    for step in range(ITERS):
+        last_pass = step == ITERS - 1
+        theirs = [member_swap(parts, bit) for bit in (1, 2, 3)]
+        columns, potential = call(
+            functools.partial(columns_kernel, last_pass),
+            [scalars, by_target, has_target, *blocks, *notes, parts, *theirs, own_mass, *reference],
+            [side, flat if last_pass else side],
+            pass_buffers,
+        )
+        partner = member_swap(columns, 4)
+        if last_pass:
+            break
+        sent = call(
+            forward_kernel,
+            [scalars, columns, partner],
+            [jax.ShapeDtypeStruct((4, block_rows), jnp.float32)] * 3,
+        )
+        received = [group_swap(values, bit) for bit, values in enumerate(sent, 1)]
+        parts, target_rows = call(
+            rows_kernel,
+            [scalars, by_source, has_source, *blocks, potential, columns, partner, *received],
+            [side, side],
+            [*pass_buffers, VMEM((8, block_rows), jnp.float32)],
+        )
+        reference = [target_rows]
+    received = [group_swap(columns, bit) for bit in (1, 2, 3)]
+    (final,) = call(
+        finish_kernel,
+        [scalars, columns, partner, *received],
+        [flat],
+        [VMEM((8, block_rows), jnp.float32)],
+    )
+    return potential.reshape(source_mass.shape), final.reshape(target_mass.shape)
+
+
+def shards(source_vectors, target_vectors, source_mass, target_mass, candidates):
+    quad = lax.axis_size("member") == 8 and lax.axis_size("group") == 4 and candidates.shape == (4, 8)
+    plan = shards_quad if quad else shards_any
+    return plan(source_vectors, target_vectors, source_mass, target_mass, candidates)
+
+
 def solution(mesh):
     placed = (
         P(("group", "member"), None),

time: 284 us -> 94.5 us (0.33)
  blocking collectives: 100 us -> 0 us
  matrix products: 46.9 us -> 0 us
  local copies, waits for them, and re-layouts: 35.9 us -> 3.42 us
  Pallas kernels: 0 us -> 27.4 us
  other arithmetic: 29.1 us -> 2.9 us
  starting transfers between devices: 39.3 us -> 27.3 us
  waiting for transfers between devices: 27.9 us -> 32.3 us
    all_gather x1 -> x0, blocking collectives: 100 us -> none  [shards(): all_lists = lax.all_gather(own_lists, 'member', axis=0, tiled=True)]
    dot_general x33 -> x0, matrix products: 46.9 us -> none  [visit(): jnp.einsum('umk,ugk->umg', source_portion, key_entries, preferred_element...]
    all_to_all x10 -> x0, starting transfers between devices: 39.3 us -> none  [the longest x4 15.8 us: trade_group(): lax.all_to_all(values, 'group', split_axis=0, concat_axis=0, tiled=True)]
    ppermute x0 -> x24, waiting for transfers between devices: none -> 32.3 us  [swap(): lax.ppermute(values, axis, [(index, index ^ bit) for index in range(size)])]
    gather x45 -> x0, local copies, waits for them, and re-layouts: 28.3 us -> none  [the longest x33 19.2 us: visit(): key_entries = jnp.take(target_blocks, pick_part, axis=0)]
    all_to_all x10 -> x0, waiting for transfers between devices: 27.9 us -> none  [the longest x4 20.4 us: trade_member(): lax.all_to_all(values, 'member', split_axis=0, concat_axis=0, tiled=True)]
    pallas_call x0 -> x7, Pallas kernels: none -> 27.4 us  [call(): pl.pallas_call(kernel, out_shape=outs, in_specs=[pl.BlockSpec(memory_spac...]
    ppermute x0 -> x24, starting transfers between devices: none -> 27.3 us  [swap(): lax.ppermute(values, axis, [(index, index ^ bit) for index in range(size)])]
  transfers between devices with their start and end apart: 10 -> 24, of which waited for: 6 -> 11; matrix products, arithmetic and copies ran while one was open for 23% -> 5% of each run, Pallas kernels for 0% -> 2%
where the time goes in v2:
time: 94.5 us; the launch traced here: 94.2 us
  waiting for transfers between devices  32.3 us (34%)
  Pallas kernels  27.4 us (29%)
  starting transfers between devices  27.3 us (29%)
  local copies, waits for them, and re-layouts  3.42 us (4%)
  other arithmetic  2.9 us (3%)
    ppermute x24, waiting for transfers between devices, swap(): lax.ppermute(values, axis, [(index, index ^ bit) for index in range(size)])  32.3 us
    pallas_call x7, Pallas kernels, call(): pl.pallas_call(kernel, out_shape=outs, in_specs=[pl.BlockSpec(memory_spac...  27.4 us
    ppermute x24, starting transfers between devices, swap(): lax.ppermute(values, axis, [(index, index ^ bit) for index in range(size)])  27.3 us
  transfers between devices with their start and end apart: 24, of which 11 were waited for; matrix products, arithmetic and copies ran while one was open for 5% of the time, Pallas kernels for 2%

profile of v2, /device:TPU:0, one launch (start us, length us, event | category | flops | bytes accessed | tf_op | source)
XLA Modules:
  0.0 94.2 jit_solution(15779115419686843338)
XLA Ops:
  1.2 2.7 %collective-permute-start.7 = (bf16[4,256,256]{2,1,0:T(8,128)(2,1)}, bf16[4,256,256]{2,1,0:T(8,128)(2,1)S(1)}, u32[]{:S(2)}, u32[]{:S(2)}) collective-permute-start(bf16[4,256,256]{2,1,0:T(8,128)(2,1)} %bitcast.25), channel_id=1, source_target_pairs={{0,2},{1,3},{2,0},{3,1},{4,6},{5,7},{6,4},{7,5},{8,10},{9,11},{10,... | collective-permute-start | bytes 1572872 | tf_op jit(solution)/shard_map/ppermute | solution.py:420
  3.8 2.6 %collective-permute-start.9 = (bf16[4,256,256]{2,1,0:T(8,128)(2,1)}, bf16[4,256,256]{2,1,0:T(8,128)(2,1)S(1)}, u32[]{:S(2)}, u32[]{:S(2)}) collective-permute-start(bf16[4,256,256]{2,1,0:T(8,128)(2,1)} %bitcast.21), channel_id=1, source_target_pairs={{0,4},{1,5},{2,6},{3,7},{4,0},{5,1},{6,2},{7,3},{8,12},{9,13},{10,... | collective-permute-start | bytes 1572872 | tf_op jit(solution)/shard_map/ppermute | solution.py:420
  7.0 0.7 broadcast_multiply_fusion
  8.8 0.7 broadcast_multiply_fusion.1
  10.1 1.3 %collective-permute-start.3 = (f32[8,256]{1,0:T(8,128)S(1)}, f32[8,256]{1,0:T(8,128)S(1)}, u32[]{:S(2)}, u32[]{:S(2)}) collective-permute-start(f32[8,256]{1,0:T(8,128)S(1)} %select_maximum_fusion.refs_7_), channel_id=1, source_target_pairs={{0,3},{1,2},{2,1},{3,0},{4,7},{5,6},{6,5},{7,4},{8,11},{9,10},{10,... | collective-permute-start | bytes 24584 | tf_op jit(solution)/shard_map/ppermute | solution.py:420
  11.5 1.1 %constant_dynamic-slice_fusion.2 = (bf16[1,256,256]{2,1,0:T(8,128)(2,1)S(1)}, bf16[1,256,256]{2,1,0:T(8,128)(2,1)S(1)}, bf16[1,256,256]{2,1,0:T(8,128)(2,1)S(1)}) fusion(bf16[4,256,256]{2,1,0:T(8,128)(2,1)} %bitcast.22, s32[]{:T(128)S(6)} %select_n.239, s32[]{:T(128)S(6)} %select_n.238, s32[]{:T(128)S(6)} %select_n.237), kind=kLoop, calls=%fused_computation.46 | loop fusion | bytes 786444 | tf_op jit(solution)/shard_map/dynamic_slice | solution.py:507
  12.5 1.6 %collective-permute-start.4 = (bf16[1,256,256]{2,1,0:T(8,128)(2,1)S(1)}, bf16[1,256,256]{2,1,0:T(8,128)(2,1)S(1)}, u32[]{:S(2)}, u32[]{:S(2)}) collective-permute-start(bf16[1,256,256]{2,1,0:T(8,128)(2,1)S(1)} %get-tuple-element.44), channel_id=1, source_target_pairs={{0,8},{8,0},{16,24},{24,16},{1,9},{9,1},{17,25},{25,17},{2,10},{10... | collective-permute-start | bytes 393224 | tf_op jit(solution)/shard_map/ppermute | solution.py:420
  14.1 13.8 %collective-permute-done.2.refs_9_ = f32[8,256]{1,0:T(8,128)S(1)} collective-permute-done((f32[8,256]{1,0:T(8,128)S(1)}, f32[8,256]{1,0:T(8,128)S(1)}, u32[]{:S(2)}, u32[]{:S(2)}) %collective-permute-start.2) | collective-permute-done | bytes 8224 | tf_op jit(solution)/shard_map/ppermute | solution.py:420
  27.9 1.7 %collective-permute-start.5 = (bf16[1,256,256]{2,1,0:T(8,128)(2,1)S(1)}, bf16[1,256,256]{2,1,0:T(8,128)(2,1)S(1)}, u32[]{:S(2)}, u32[]{:S(2)}) collective-permute-start(bf16[1,256,256]{2,1,0:T(8,128)(2,1)S(1)} %get-tuple-element.43), channel_id=1, source_target_pairs={{0,16},{8,24},{16,0},{24,8},{1,17},{9,25},{17,1},{25,9},{2,18},{10... | collective-permute-start | bytes 393224 | tf_op jit(solution)/shard_map/ppermute | solution.py:420
  29.6 1.4 %collective-permute-start.6 = (bf16[1,256,256]{2,1,0:T(8,128)(2,1)S(1)}, bf16[1,256,256]{2,1,0:T(8,128)(2,1)S(1)}, u32[]{:S(2)}, u32[]{:S(2)}) collective-permute-start(bf16[1,256,256]{2,1,0:T(8,128)(2,1)S(1)} %get-tuple-element.42), channel_id=1, source_target_pairs={{0,24},{8,16},{16,8},{24,0},{1,25},{9,17},{17,9},{25,1},{2,26},{10... | collective-permute-start | bytes 393224 | tf_op jit(solution)/shard_map/ppermute | solution.py:420
  31.8 4.1 %collective-permute-done.5.mirror_2 = bf16[1,256,256]{2,1,0:T(8,128)(2,1)S(1)} collective-permute-done((bf16[1,256,256]{2,1,0:T(8,128)(2,1)S(1)}, bf16[1,256,256]{2,1,0:T(8,128)(2,1)S(1)}, u32[]{:S(2)}, u32[]{:S(2)}) %collective-permute-start.5) | collective-permute-done | bytes 131104 | tf_op jit(solution)/shard_map/ppermute | solution.py:420
  36.0 1.0 %copy-done.1 = bf16[1024,256]{1,0:T(8,128)(2,1)S(1)} copy-done((bf16[1024,256]{1,0:T(8,128)(2,1)S(1)}, bf16[1024,256]{1,0:T(8,128)(2,1)}, u32[]{:S(2)}) %copy-start.1) | copy-done | bytes 524312
  37.0 1.9 %shard_map.68 = (f32[16,256]{1,0:T(8,128)S(1)}, bf16[8,256,256]{2,1,0:T(8,128)(2,1)S(1)}, bf16[7,256,256]{2,1,0:T(8,128)(2,1)S(1)}) custom-call(s32[5,40]{1,0:T(8,128)S(1)} %stack.14.scalars.refs_0_, s32[40,128]{1,0:T(8,128)S(1)} %broadcast_in_dim.107.ids.refs_1_, bf16[4,256,256]{2,1,0:T(8,128)(2,1)S(1)} %bitcast.26, ...), custom_call_target="tpu_custom_call" | custom-call | tf_op jit(solution)/shard_map/pallas_call | solution.py:409
  39.0 2.9 %shard_map.69 = (f32[16,256]{1,0:T(8,128)S(1)}, bf16[8,256,256]{2,1,0:T(8,128)(2,1)S(1)}) custom-call(s32[5,40]{1,0:T(8,128)S(1)} %stack.14.scalars.refs_0_, s32[40,128]{1,0:T(8,128)S(1)} %broadcast_in_dim.107.ids.refs_1_, f32[16,256]{1,0:T(8,128)S(1)} %get-tuple-element.23.early, bf16[8,256,256]{2,1,0:T(8,128)(2,1)S(1)} %get-tuple-element.22.sources.refs_3_, ...), custom_call_target="tpu_custom_call" | custom-call | tf_op jit(solution)/shard_map/pallas_call | solution.py:409
  42.0 1.8 %collective-permute-start.11 = (f32[16,256]{1,0:T(8,128)S(1)}, f32[16,256]{1,0:T(8,128)S(1)}, u32[]{:S(2)}, u32[]{:S(2)}) collective-permute-start(f32[16,256]{1,0:T(8,128)S(1)} %get-tuple-element.26.refs_11_), channel_id=1, source_target_pairs={{0,2},{1,3},{2,0},{3,1},{4,6},{5,7},{6,4},{7,5},{8,10},{9,11},{10,... | collective-permute-start | bytes 49160 | tf_op jit(solution)/shard_map/ppermute | solution.py:420
  44.0 1.8 %collective-permute-done.11.refs_13_ = f32[16,256]{1,0:T(8,128)S(1)} collective-permute-done((f32[16,256]{1,0:T(8,128)S(1)}, f32[16,256]{1,0:T(8,128)S(1)}, u32[]{:S(2)}, u32[]{:S(2)}) %collective-permute-start.11) | collective-permute-done | bytes 16416 | tf_op jit(solution)/shard_map/ppermute | solution.py:420
  45.8 1.2 %collective-permute-done.12.refs_14_ = f32[16,256]{1,0:T(8,128)S(1)} collective-permute-done((f32[16,256]{1,0:T(8,128)S(1)}, f32[16,256]{1,0:T(8,128)S(1)}, u32[]{:S(2)}, u32[]{:S(2)}) %collective-permute-start.12) | collective-permute-done | bytes 16416 | tf_op jit(solution)/shard_map/ppermute | solution.py:420
  47.1 2.6 %shard_map.70 = (f32[16,256]{1,0:T(8,128)S(1)}, f32[16,256]{1,0:T(8,128)S(1)}) custom-call(s32[5,40]{1,0:T(8,128)S(1)} %stack.14.scalars.refs_0_, s32[40,128]{1,0:T(8,128)S(1)} %broadcast_in_dim.105.refs_1_, f32[16,128]{1,0:T(8,128)S(1)} %broadcast_in_dim.106.refs_2_, bf16[8,256,256]{2,1,0:T(8,128)(2,1)S(1)} %get-tuple-element.22.sources.refs_3_, ...), custom_call_target="tpu_custom_call" | custom-call | tf_op jit(solution)/shard_map/pallas_call | solution.py:409
  49.7 1.6 %collective-permute-start.13 = (f32[16,256]{1,0:T(8,128)S(1)}, f32[16,256]{1,0:T(8,128)S(1)}, u32[]{:S(2)}, u32[]{:S(2)}) collective-permute-start(f32[16,256]{1,0:T(8,128)S(1)} %get-tuple-element.28.columns.refs_8_), channel_id=1, source_target_pairs={{0,4},{1,5},{2,6},{3,7},{4,0},{5,1},{6,2},{7,3},{8,12},{9,13},{10,... | collective-permute-start | bytes 49160 | tf_op jit(solution)/shard_map/ppermute | solution.py:420
  51.3 3.2 %collective-permute-done.13.partner.refs_9_ = f32[16,256]{1,0:T(8,128)S(1)} collective-permute-done((f32[16,256]{1,0:T(8,128)S(1)}, f32[16,256]{1,0:T(8,128)S(1)}, u32[]{:S(2)}, u32[]{:S(2)}) %collective-permute-start.13) | collective-permute-done | bytes 16416 | tf_op jit(solution)/shard_map/ppermute | solution.py:420
  55.2 1.5 %collective-permute-start.14 = (f32[4,256]{1,0:T(4,128)S(1)}, f32[4,256]{1,0:T(4,128)S(1)}, u32[]{:S(2)}, u32[]{:S(2)}) collective-permute-start(f32[4,256]{1,0:T(4,128)S(1)} %get-tuple-element.29), channel_id=1, source_target_pairs={{0,8},{8,0},{16,24},{24,16},{1,9},{9,1},{17,25},{25,17},{2,10},{10... | collective-permute-start | bytes 12296 | tf_op jit(solution)/shard_map/ppermute | solution.py:420
  56.8 1.5 %collective-permute-start.15 = (f32[4,256]{1,0:T(4,128)S(1)}, f32[4,256]{1,0:T(4,128)S(1)}, u32[]{:S(2)}, u32[]{:S(2)}) collective-permute-start(f32[4,256]{1,0:T(4,128)S(1)} %get-tuple-element.30), channel_id=1, source_target_pairs={{0,16},{8,24},{16,0},{24,8},{1,17},{9,25},{17,1},{25,9},{2,18},{10... | collective-permute-start | bytes 12296 | tf_op jit(solution)/shard_map/ppermute | solution.py:420
  58.9 1.5 %collective-permute-done.15.refs_11_ = f32[4,256]{1,0:T(4,128)S(1)} collective-permute-done((f32[4,256]{1,0:T(4,128)S(1)}, f32[4,256]{1,0:T(4,128)S(1)}, u32[]{:S(2)}, u32[]{:S(2)}) %collective-permute-start.15) | collective-permute-done | bytes 4128 | tf_op jit(solution)/shard_map/ppermute | solution.py:420
  60.4 2.4 %collective-permute-done.16.refs_12_ = f32[4,256]{1,0:T(4,128)S(1)} collective-permute-done((f32[4,256]{1,0:T(4,128)S(1)}, f32[4,256]{1,0:T(4,128)S(1)}, u32[]{:S(2)}, u32[]{:S(2)}) %collective-permute-start.16) | collective-permute-done | bytes 4128 | tf_op jit(solution)/shard_map/ppermute | solution.py:420
  62.9 14.3 %shard_map.72 = (f32[16,256]{1,0:T(8,128)S(1)}, f32[16,256]{1,0:T(8,128)S(1)}) custom-call(s32[5,40]{1,0:T(8,128)S(1)} %stack.14.scalars.refs_0_, s32[40,128]{1,0:T(8,128)S(1)} %broadcast_in_dim.107.ids.refs_1_, f32[16,128]{1,0:T(8,128)S(1)} %broadcast_in_dim.108.refs_2_, bf16[8,256,256]{2,1,0:T(8,128)(2,1)S(1)} %get-tuple-element.22.sources.refs_3_, ...), custom_call_target="tpu_custom_call" | custom-call | tf_op jit(solution)/shard_map/pallas_call | solution.py:409
  77.8 1.3 %collective-permute-start.19 = (f32[16,256]{1,0:T(8,128)S(1)}, f32[16,256]{1,0:T(8,128)S(1)}, u32[]{:S(2)}, u32[]{:S(2)}) collective-permute-start(f32[16,256]{1,0:T(8,128)S(1)} %get-tuple-element.32.refs_11_), channel_id=1, source_target_pairs={{0,3},{1,2},{2,1},{3,0},{4,7},{5,6},{6,5},{7,4},{8,11},{9,10},{10,... | collective-permute-start | bytes 49160 | tf_op jit(solution)/shard_map/ppermute | solution.py:420
  79.1 2.1 %collective-permute-done.18.refs_13_ = f32[16,256]{1,0:T(8,128)S(1)} collective-permute-done((f32[16,256]{1,0:T(8,128)S(1)}, f32[16,256]{1,0:T(8,128)S(1)}, u32[]{:S(2)}, u32[]{:S(2)}) %collective-permute-start.18) | collective-permute-done | bytes 16416 | tf_op jit(solution)/shard_map/ppermute | solution.py:420
  81.2 3.7 %shard_map.73 = (f32[16,256]{1,0:T(8,128)S(1)}, f32[8,128]{1,0:T(8,128)}) custom-call(s32[5,40]{1,0:T(8,128)S(1)} %stack.14.scalars.refs_0_, s32[40,128]{1,0:T(8,128)S(1)} %broadcast_in_dim.105.refs_1_, f32[16,128]{1,0:T(8,128)S(1)} %broadcast_in_dim.106.refs_2_, bf16[8,256,256]{2,1,0:T(8,128)(2,1)S(1)} %get-tuple-element.22.sources.refs_3_, ...), custom_call_target="tpu_custom_call" | custom-call | tf_op jit(solution)/shard_map/pallas_call | solution.py:409
  84.9 2.3 %collective-permute-start.20 = (f32[16,256]{1,0:T(8,128)S(1)}, f32[16,256]{1,0:T(8,128)S(1)}, u32[]{:S(2)}, u32[]{:S(2)}) collective-permute-start(f32[16,256]{1,0:T(8,128)S(1)} %get-tuple-element.35.columns), channel_id=1, source_target_pairs={{0,4},{1,5},{2,6},{3,7},{4,0},{5,1},{6,2},{7,3},{8,12},{9,13},{10,... | collective-permute-start | bytes 49160 | tf_op jit(solution)/shard_map/ppermute | solution.py:420
  88.3 2.4 %collective-permute-start.23 = (f32[16,256]{1,0:T(8,128)S(1)}, f32[16,256]{1,0:T(8,128)S(1)}, u32[]{:S(2)}, u32[]{:S(2)}) collective-permute-start(f32[16,256]{1,0:T(8,128)S(1)} %get-tuple-element.35.columns), channel_id=1, source_target_pairs={{0,24},{8,16},{16,8},{24,0},{1,25},{9,17},{17,9},{25,1},{2,26},{10... | collective-permute-start | bytes 49160 | tf_op jit(solution)/shard_map/ppermute | solution.py:420
  91.6 1.4 %collective-permute-done.23.rest_2_ = f32[16,256]{1,0:T(8,128)S(1)} collective-permute-done((f32[16,256]{1,0:T(8,128)S(1)}, f32[16,256]{1,0:T(8,128)S(1)}, u32[]{:S(2)}, u32[]{:S(2)}) %collective-permute-start.23) | collective-permute-done | bytes 16416 | tf_op jit(solution)/shard_map/ppermute | solution.py:420
  93.0 1.2 %shard_map.74 = f32[8,128]{1,0:T(8,128)} custom-call(s32[5,40]{1,0:T(8,128)S(1)} %stack.14.scalars.refs_0_, f32[16,256]{1,0:T(8,128)S(1)} %get-tuple-element.35.columns, f32[16,256]{1,0:T(8,128)S(1)} %collective-permute-done.20.partner, f32[16,256]{1,0:T(8,128)S(1)} %collective-permute-done.21.rest_0_, f32[16,256]{1,0:T(8,128)S(1)} %collective-permute-done.22.rest_1_, ...), custom_call_target="tpu_custom_call" | custom-call | tf_op jit(solution)/shard_map/pallas_call | solution.py:409
  (77 shorter events, 7.7 us)
Async XLA Ops:
  0.6 35.3 %copy-start = (bf16[1024,256]{1,0:T(8,128)(2,1)S(1)}, bf16[1024,256]{1,0:T(8,128)(2,1)}, u32[]{:S(2)}) copy-start(bf16[1024,256]{1,0:T(8,128)(2,1)} %param.6) | copy-start | bytes 1572868
  0.6 7.4 %collective-permute-start = (bf16[4,256,256]{2,1,0:T(8,128)(2,1)}, bf16[4,256,256]{2,1,0:T(8,128)(2,1)S(1)}, u32[]{:S(2)}, u32[]{:S(2)}) collective-permute-start(bf16[4,256,256]{2,1,0:T(8,128)(2,1)} %bitcast.24), channel_id=1, source_target_pairs={{0,1},{1,0},{2,3},{3,2},{4,5},{5,4},{6,7},{7,6},{8,9},{9,8},{10,11... | collective-permute-start | bytes 1572872 | tf_op jit(solution)/shard_map/ppermute | solution.py:420
  1.2 28.5 %collective-permute-start.7 = (bf16[4,256,256]{2,1,0:T(8,128)(2,1)}, bf16[4,256,256]{2,1,0:T(8,128)(2,1)S(1)}, u32[]{:S(2)}, u32[]{:S(2)}) collective-permute-start(bf16[4,256,256]{2,1,0:T(8,128)(2,1)} %bitcast.25), channel_id=1, source_target_pairs={{0,2},{1,3},{2,0},{3,1},{4,6},{5,7},{6,4},{7,5},{8,10},{9,11},{10,... | collective-permute-start | bytes 1572872 | tf_op jit(solution)/shard_map/ppermute | solution.py:420
  3.8 35.1 %collective-permute-start.9 = (bf16[4,256,256]{2,1,0:T(8,128)(2,1)}, bf16[4,256,256]{2,1,0:T(8,128)(2,1)S(1)}, u32[]{:S(2)}, u32[]{:S(2)}) collective-permute-start(bf16[4,256,256]{2,1,0:T(8,128)(2,1)} %bitcast.21), channel_id=1, source_target_pairs={{0,4},{1,5},{2,6},{3,7},{4,0},{5,1},{6,2},{7,3},{8,12},{9,13},{10,... | collective-permute-start | bytes 1572872 | tf_op jit(solution)/shard_map/ppermute | solution.py:420
  9.5 3.0 %collective-permute-start.1 = (f32[8,256]{1,0:T(8,128)S(1)}, f32[8,256]{1,0:T(8,128)S(1)}, u32[]{:S(2)}, u32[]{:S(2)}) collective-permute-start(f32[8,256]{1,0:T(8,128)S(1)} %select_maximum_fusion.refs_7_), channel_id=1, source_target_pairs={{0,1},{1,0},{2,3},{3,2},{4,5},{5,4},{6,7},{7,6},{8,9},{9,8},{10,11... | collective-permute-start | bytes 24584 | tf_op jit(solution)/shard_map/ppermute | solution.py:420
  9.6 18.3 %collective-permute-start.2 = (f32[8,256]{1,0:T(8,128)S(1)}, f32[8,256]{1,0:T(8,128)S(1)}, u32[]{:S(2)}, u32[]{:S(2)}) collective-permute-start(f32[8,256]{1,0:T(8,128)S(1)} %select_maximum_fusion.refs_7_), channel_id=1, source_target_pairs={{0,2},{1,3},{2,0},{3,1},{4,6},{5,7},{6,4},{7,5},{8,10},{9,11},{10,... | collective-permute-start | bytes 24584 | tf_op jit(solution)/shard_map/ppermute | solution.py:420
  10.1 21.0 %collective-permute-start.3 = (f32[8,256]{1,0:T(8,128)S(1)}, f32[8,256]{1,0:T(8,128)S(1)}, u32[]{:S(2)}, u32[]{:S(2)}) collective-permute-start(f32[8,256]{1,0:T(8,128)S(1)} %select_maximum_fusion.refs_7_), channel_id=1, source_target_pairs={{0,3},{1,2},{2,1},{3,0},{4,7},{5,6},{6,5},{7,4},{8,11},{9,10},{10,... | collective-permute-start | bytes 24584 | tf_op jit(solution)/shard_map/ppermute | solution.py:420
  12.5 19.3 %collective-permute-start.4 = (bf16[1,256,256]{2,1,0:T(8,128)(2,1)S(1)}, bf16[1,256,256]{2,1,0:T(8,128)(2,1)S(1)}, u32[]{:S(2)}, u32[]{:S(2)}) collective-permute-start(bf16[1,256,256]{2,1,0:T(8,128)(2,1)S(1)} %get-tuple-element.44), channel_id=1, source_target_pairs={{0,8},{8,0},{16,24},{24,16},{1,9},{9,1},{17,25},{25,17},{2,10},{10... | collective-permute-start | bytes 393224 | tf_op jit(solution)/shard_map/ppermute | solution.py:420
  27.9 8.0 %collective-permute-start.5 = (bf16[1,256,256]{2,1,0:T(8,128)(2,1)S(1)}, bf16[1,256,256]{2,1,0:T(8,128)(2,1)S(1)}, u32[]{:S(2)}, u32[]{:S(2)}) collective-permute-start(bf16[1,256,256]{2,1,0:T(8,128)(2,1)S(1)} %get-tuple-element.43), channel_id=1, source_target_pairs={{0,16},{8,24},{16,0},{24,8},{1,17},{9,25},{17,1},{25,9},{2,18},{10... | collective-permute-start | bytes 393224 | tf_op jit(solution)/shard_map/ppermute | solution.py:420
  29.6 6.3 %collective-permute-start.6 = (bf16[1,256,256]{2,1,0:T(8,128)(2,1)S(1)}, bf16[1,256,256]{2,1,0:T(8,128)(2,1)S(1)}, u32[]{:S(2)}, u32[]{:S(2)}) collective-permute-start(bf16[1,256,256]{2,1,0:T(8,128)(2,1)S(1)} %get-tuple-element.42), channel_id=1, source_target_pairs={{0,24},{8,16},{16,8},{24,0},{1,25},{9,17},{17,9},{25,1},{2,26},{10... | collective-permute-start | bytes 393224 | tf_op jit(solution)/shard_map/ppermute | solution.py:420
  31.1 7.9 %collective-permute-start.8 = (bf16[4,256,256]{2,1,0:T(8,128)(2,1)S(1)}, bf16[4,256,256]{2,1,0:T(8,128)(2,1)S(1)}, u32[]{:S(2)}, u32[]{:S(2)}) collective-permute-start(bf16[4,256,256]{2,1,0:T(8,128)(2,1)S(1)} %collective-permute-done.7.near), channel_id=1, source_target_pairs={{0,1},{1,0},{2,3},{3,2},{4,5},{5,4},{6,7},{7,6},{8,9},{9,8},{10,11... | collective-permute-start | bytes 1572872 | tf_op jit(solution)/shard_map/ppermute | solution.py:420
  36.0 1.0 %copy-start.1 = (bf16[1024,256]{1,0:T(8,128)(2,1)S(1)}, bf16[1024,256]{1,0:T(8,128)(2,1)}, u32[]{:S(2)}) copy-start(bf16[1024,256]{1,0:T(8,128)(2,1)} %param.5) | copy-start | bytes 1572868
  41.9 2.1 %collective-permute-start.10 = (f32[16,256]{1,0:T(8,128)S(1)}, f32[16,256]{1,0:T(8,128)S(1)}, u32[]{:S(2)}, u32[]{:S(2)}) collective-permute-start(f32[16,256]{1,0:T(8,128)S(1)} %get-tuple-element.26.refs_11_), channel_id=1, source_target_pairs={{0,1},{1,0},{2,3},{3,2},{4,5},{5,4},{6,7},{7,6},{8,9},{9,8},{10,11... | collective-permute-start | bytes 49160 | tf_op jit(solution)/shard_map/ppermute | solution.py:420
  42.0 3.8 %collective-permute-start.11 = (f32[16,256]{1,0:T(8,128)S(1)}, f32[16,256]{1,0:T(8,128)S(1)}, u32[]{:S(2)}, u32[]{:S(2)}) collective-permute-start(f32[16,256]{1,0:T(8,128)S(1)} %get-tuple-element.26.refs_11_), channel_id=1, source_target_pairs={{0,2},{1,3},{2,0},{3,1},{4,6},{5,7},{6,4},{7,5},{8,10},{9,11},{10,... | collective-permute-start | bytes 49160 | tf_op jit(solution)/shard_map/ppermute | solution.py:420
  43.8 3.2 %collective-permute-start.12 = (f32[16,256]{1,0:T(8,128)S(1)}, f32[16,256]{1,0:T(8,128)S(1)}, u32[]{:S(2)}, u32[]{:S(2)}) collective-permute-start(f32[16,256]{1,0:T(8,128)S(1)} %get-tuple-element.26.refs_11_), channel_id=1, source_target_pairs={{0,3},{1,2},{2,1},{3,0},{4,7},{5,6},{6,5},{7,4},{8,11},{9,10},{10,... | collective-permute-start | bytes 49160 | tf_op jit(solution)/shard_map/ppermute | solution.py:420
  49.7 4.9 %collective-permute-start.13 = (f32[16,256]{1,0:T(8,128)S(1)}, f32[16,256]{1,0:T(8,128)S(1)}, u32[]{:S(2)}, u32[]{:S(2)}) collective-permute-start(f32[16,256]{1,0:T(8,128)S(1)} %get-tuple-element.28.columns.refs_8_), channel_id=1, source_target_pairs={{0,4},{1,5},{2,6},{3,7},{4,0},{5,1},{6,2},{7,3},{8,12},{9,13},{10,... | collective-permute-start | bytes 49160 | tf_op jit(solution)/shard_map/ppermute | solution.py:420
  55.2 3.7 %collective-permute-start.14 = (f32[4,256]{1,0:T(4,128)S(1)}, f32[4,256]{1,0:T(4,128)S(1)}, u32[]{:S(2)}, u32[]{:S(2)}) collective-permute-start(f32[4,256]{1,0:T(4,128)S(1)} %get-tuple-element.29), channel_id=1, source_target_pairs={{0,8},{8,0},{16,24},{24,16},{1,9},{9,1},{17,25},{25,17},{2,10},{10... | collective-permute-start | bytes 12296 | tf_op jit(solution)/shard_map/ppermute | solution.py:420
  56.8 3.6 %collective-permute-start.15 = (f32[4,256]{1,0:T(4,128)S(1)}, f32[4,256]{1,0:T(4,128)S(1)}, u32[]{:S(2)}, u32[]{:S(2)}) collective-permute-start(f32[4,256]{1,0:T(4,128)S(1)} %get-tuple-element.30), channel_id=1, source_target_pairs={{0,16},{8,24},{16,0},{24,8},{1,17},{9,25},{17,1},{25,9},{2,18},{10... | collective-permute-start | bytes 12296 | tf_op jit(solution)/shard_map/ppermute | solution.py:420
  58.3 4.5 %collective-permute-start.16 = (f32[4,256]{1,0:T(4,128)S(1)}, f32[4,256]{1,0:T(4,128)S(1)}, u32[]{:S(2)}, u32[]{:S(2)}) collective-permute-start(f32[4,256]{1,0:T(4,128)S(1)} %get-tuple-element.31), channel_id=1, source_target_pairs={{0,24},{8,16},{16,8},{24,0},{1,25},{9,17},{17,9},{25,1},{2,26},{10... | collective-permute-start | bytes 12296 | tf_op jit(solution)/shard_map/ppermute | solution.py:420
  77.2 1.9 %collective-permute-start.17 = (f32[16,256]{1,0:T(8,128)S(1)}, f32[16,256]{1,0:T(8,128)S(1)}, u32[]{:S(2)}, u32[]{:S(2)}) collective-permute-start(f32[16,256]{1,0:T(8,128)S(1)} %get-tuple-element.32.refs_11_), channel_id=1, source_target_pairs={{0,1},{1,0},{2,3},{3,2},{4,5},{5,4},{6,7},{7,6},{8,9},{9,8},{10,11... | collective-permute-start | bytes 49160 | tf_op jit(solution)/shard_map/ppermute | solution.py:420
  77.3 3.9 %collective-permute-start.18 = (f32[16,256]{1,0:T(8,128)S(1)}, f32[16,256]{1,0:T(8,128)S(1)}, u32[]{:S(2)}, u32[]{:S(2)}) collective-permute-start(f32[16,256]{1,0:T(8,128)S(1)} %get-tuple-element.32.refs_11_), channel_id=1, source_target_pairs={{0,2},{1,3},{2,0},{3,1},{4,6},{5,7},{6,4},{7,5},{8,10},{9,11},{10,... | collective-permute-start | bytes 49160 | tf_op jit(solution)/shard_map/ppermute | solution.py:420
  77.8 3.3 %collective-permute-start.19 = (f32[16,256]{1,0:T(8,128)S(1)}, f32[16,256]{1,0:T(8,128)S(1)}, u32[]{:S(2)}, u32[]{:S(2)}) collective-permute-start(f32[16,256]{1,0:T(8,128)S(1)} %get-tuple-element.32.refs_11_), channel_id=1, source_target_pairs={{0,3},{1,2},{2,1},{3,0},{4,7},{5,6},{6,5},{7,4},{8,11},{9,10},{10,... | collective-permute-start | bytes 49160 | tf_op jit(solution)/shard_map/ppermute | solution.py:420
  84.9 5.8 %collective-permute-start.20 = (f32[16,256]{1,0:T(8,128)S(1)}, f32[16,256]{1,0:T(8,128)S(1)}, u32[]{:S(2)}, u32[]{:S(2)}) collective-permute-start(f32[16,256]{1,0:T(8,128)S(1)} %get-tuple-element.35.columns), channel_id=1, source_target_pairs={{0,4},{1,5},{2,6},{3,7},{4,0},{5,1},{6,2},{7,3},{8,12},{9,13},{10,... | collective-permute-start | bytes 49160 | tf_op jit(solution)/shard_map/ppermute | solution.py:420
  87.3 3.7 %collective-permute-start.21 = (f32[16,256]{1,0:T(8,128)S(1)}, f32[16,256]{1,0:T(8,128)S(1)}, u32[]{:S(2)}, u32[]{:S(2)}) collective-permute-start(f32[16,256]{1,0:T(8,128)S(1)} %get-tuple-element.35.columns), channel_id=1, source_target_pairs={{0,8},{8,0},{16,24},{24,16},{1,9},{9,1},{17,25},{25,17},{2,10},{10... | collective-permute-start | bytes 49160 | tf_op jit(solution)/shard_map/ppermute | solution.py:420
  87.8 3.7 %collective-permute-start.22 = (f32[16,256]{1,0:T(8,128)S(1)}, f32[16,256]{1,0:T(8,128)S(1)}, u32[]{:S(2)}, u32[]{:S(2)}) collective-permute-start(f32[16,256]{1,0:T(8,128)S(1)} %get-tuple-element.35.columns), channel_id=1, source_target_pairs={{0,16},{8,24},{16,0},{24,8},{1,17},{9,25},{17,1},{25,9},{2,18},{10... | collective-permute-start | bytes 49160 | tf_op jit(solution)/shard_map/ppermute | solution.py:420
  88.3 4.6 %collective-permute-start.23 = (f32[16,256]{1,0:T(8,128)S(1)}, f32[16,256]{1,0:T(8,128)S(1)}, u32[]{:S(2)}, u32[]{:S(2)}) collective-permute-start(f32[16,256]{1,0:T(8,128)S(1)} %get-tuple-element.35.columns), channel_id=1, source_target_pairs={{0,24},{8,16},{16,8},{24,0},{1,25},{9,17},{17,9},{25,1},{2,26},{10... | collective-permute-start | bytes 49160 | tf_op jit(solution)/shard_map/ppermute | solution.py:420

commit v3 on v2

--- a/solution.py
+++ b/solution.py
@@ -183,12 +183,12 @@
     return jnp.concatenate([pieces[index ^ 1] for index in range(len(pieces))], axis=0)
 
 
-def source_bias(note_refs, part_refs):
-    own, core, near, cross = (ref[...] for ref in part_refs)
+def source_bias(mass_refs, part_refs):
+    own, core, near, cross = (ref[0:16] for ref in part_refs)
     core = swapped(core, 4)
     near = swapped(near, 8)
     cross = swapped(swapped(cross, 4), 8)
-    mass = jnp.concatenate([ref[0:4] for ref in note_refs], axis=0)
+    mass = jnp.concatenate([ref[16:20] for ref in mass_refs], axis=0)
     return mass - merge([own, core, near, cross])
 
 
@@ -315,40 +315,39 @@
         )
 
 
-def early_kernel(
-    scalars, ids, own, core, target, mirror_1, mirror_2, mirror_3, out, sources, targets, tops, sums
-):
+def early_kernel(scalars, ids, own, core, target, mirrors, out, sources, targets, tops, sums):
     sources[0:4] = own[...]
     sources[4:8] = core[...]
     targets[0:4] = target[...]
-    for index, mirror in enumerate((mirror_1, mirror_2, mirror_3)):
-        targets[4 + index : 5 + index] = mirror[...]
+    for offset in (1, 2, 3):
+        targets[3 + offset] = mirrors[scalars[4, 0] ^ offset]
     out[...] = exact_pass(
         scalars, ids, True, (0,), (sources, None), (targets, None), None, tops, sums, True
     )
 
 
 def first_kernel(
-    scalars, ids, early, sources, near, cross, targets, far, out, late_sources, tops, sums
+    scalars, ids, early, mass, sources, near, cross, targets, far, out, late_sources, tops, sums
 ):
     late_sources[0:4] = near[...]
     late_sources[4:8] = cross[...]
     late = exact_pass(
         scalars, ids, True, (1, 2, 3), (sources, late_sources), (targets, far), None, tops, sums, True
     )
-    out[...] = merge([early[...], late])
+    out[0:16, :] = merge([early[...], late])
+    out[16:20, :] = mass[...]
+    out[20:24, :] = jnp.zeros((4, out.shape[1]), jnp.float32)
 
 
 def columns_kernel(last_pass, *refs):
     scalars, ids, present = refs[:3]
     sources, targets = refs[3:5], refs[5:7]
-    notes, parts, target_mass = refs[7:11], refs[11:15], refs[15]
-    rest = refs[16:]
-    reference = None
+    masses, target_mass, rest = refs[7:11], refs[11], refs[12:]
+    parts, reference = masses, None
     if last_pass:
-        reference, *rest = rest
+        parts, (reference, *rest) = rest[:4], rest[4:]
     out, second, total, tops, sums, bias = rest
-    rows = source_bias(notes, parts)
+    rows = source_bias(masses, parts)
     spread(rows, bias)
     if last_pass:
         for block in range(4):
@@ -486,31 +485,16 @@
 
     source_own = source_vectors.reshape(blocked)
     target_own = target_vectors.reshape(blocked)
+    named = [candidates] + [member_swap(candidates, bit) for bit in (1, 2, 3)]
     target_far = member_swap(target_own, 4)
     source_near = member_swap(source_own, 2)
-    source_core = member_swap(source_own, 1)
-    source_cross = member_swap(source_near, 1)
-    source_mass_late, candidates_late, target_late, _ = lax.optimization_barrier(
-        (source_mass, candidates, target_own, source_core)
-    )
-    note = jnp.concatenate(
-        [
-            LOG2E * source_mass_late.reshape(per_device, block_rows),
-            jnp.pad(
-                candidates_late.astype(jnp.float32).reshape(1, per_device * cand_count),
-                ((0, 3), (0, block_rows - per_device * cand_count)),
-            ),
-        ]
-    )
-    notes = [note] + [member_swap(note, bit) for bit in (1, 2, 3)]
-    mirrors = [
-        group_swap(lax.dynamic_slice_in_dim(target_late, own_group ^ bit, 1, 0), bit) for bit in (1, 2, 3)
-    ]
-    named = jnp.stack([values[4, : per_device * cand_count] for values in notes])
-    named = named.reshape(SOURCE_SLOTS, cand_count).astype(jnp.int32)
+    source_late, target_late, *named = lax.optimization_barrier((source_own, target_own, *named))
+    mirrors = lax.all_to_all(target_late, "group", split_axis=0, concat_axis=0, tiled=True)
+    source_core = member_swap(source_late, 1)
     scalars, by_source, has_source, by_target, has_target = tile_lists(
-        named, own_group, own_member, members, per_device
-    )
+        jnp.concatenate(named), own_group, own_member, members, per_device
+    )
+    own_source_mass = LOG2E * source_mass.reshape(per_device, block_rows)
     own_mass = LOG2E * target_mass.reshape(per_device, block_rows)
 
     side = jax.ShapeDtypeStruct((16, block_rows), jnp.float32)
@@ -525,24 +509,37 @@
 
     early, sources, targets = call(
         early_kernel,
-        [scalars, by_source, source_own, source_core, target_own, *mirrors],
+        [scalars, by_source, source_own, source_core, target_own, mirrors],
         [side, stacked(8), stacked(7)],
         tile_rows,
     )
+    source_near, early = lax.optimization_barrier((source_near, early))
+    source_cross = member_swap(source_near, 1)
     parts, late_sources = call(
         first_kernel,
-        [scalars, by_source, early, sources, source_near, source_cross, targets, target_far],
-        [side, stacked(8)],
+        [
+            scalars,
+            by_source,
+            early,
+            own_source_mass,
+            sources,
+            source_near,
+            source_cross,
+            targets,
+            target_far,
+        ],
+        [jax.ShapeDtypeStruct((24, block_rows), jnp.float32), stacked(8)],
         tile_rows,
     )
     blocks = [sources, late_sources, targets, target_far]
-    reference = []
+    masses, extra = [], []
     for step in range(ITERS):
         last_pass = step == ITERS - 1
-        theirs = [member_swap(parts, bit) for bit in (1, 2, 3)]
+        parts = [parts] + [member_swap(parts, bit) for bit in (1, 2, 3)]
+        masses = masses or parts
         columns, potential = call(
             functools.partial(columns_kernel, last_pass),
-            [scalars, by_target, has_target, *blocks, *notes, parts, *theirs, own_mass, *reference],
+            [scalars, by_target, has_target, *blocks, *masses, own_mass, *(parts + extra if last_pass else [])],
             [side, flat if last_pass else side],
             pass_buffers,
         )
@@ -561,7 +558,7 @@
             [side, side],
             [*pass_buffers, VMEM((8, block_rows), jnp.float32)],
         )
-        reference = [target_rows]
+        extra = [target_rows]
     received = [group_swap(columns, bit) for bit in (1, 2, 3)]
     (final,) = call(
         finish_kernel,

time: 94.5 us -> 86.9 us (0.920)
  waiting for transfers between devices: 32.3 us -> 25.2 us
  other arithmetic: 2.9 us -> 0.82 us
  local copies, waits for them, and re-layouts: 3.42 us -> 5.27 us
    ppermute x24 -> x21, waiting for transfers between devices: 32.3 us -> 17.3 us  [swap(): lax.ppermute(values, axis, [(index, index ^ bit) for index in range(size)])]
    all_to_all x0 -> x1, waiting for transfers between devices: none -> 7.93 us  [shards_quad(): lax.all_to_all(target_late, 'group', split_axis=0, concat_axis=0, tiled=T...]
    ppermute x24 -> x21, starting transfers between devices: 27.3 us -> 22.6 us  [swap(): lax.ppermute(values, axis, [(index, index ^ bit) for index in range(size)])]
    all_to_all x0 -> x1, starting transfers between devices: none -> 3.86 us  [shards_quad(): lax.all_to_all(target_late, 'group', split_axis=0, concat_axis=0, tiled=T...]
    unnamed x4 -> x22, local copies, waits for them, and re-layouts: 1.05 us -> 4.05 us
    dynamic_slice x1 -> x0, local copies, waits for them, and re-layouts: 1.06 us -> none  [shards_quad(): lax.dynamic_slice_in_dim(target_late, own_group ^ bit, 1, 0)]
  transfers between devices with their start and end apart: 24 -> 22, of which waited for: 11 -> 12; matrix products, arithmetic and copies ran while one was open for 5% -> 2% of each run, Pallas kernels for 2% -> 2%
where the time goes in v3:
time: 86.9 us; the launch traced here: 86.6 us
  Pallas kernels  27.9 us (32%)
  starting transfers between devices  26.5 us (30%)
  waiting for transfers between devices  25.2 us (29%)
  local copies, waits for them, and re-layouts  5.27 us (6%)
  between operations  0.93 us (1%)
    pallas_call x7, Pallas kernels, call(): pl.pallas_call(kernel, out_shape=outs, in_specs=[pl.BlockSpec(memory_spac...  27.9 us
    ppermute x21, starting transfers between devices, swap(): lax.ppermute(values, axis, [(index, index ^ bit) for index in range(size)])  22.6 us
    ppermute x21, waiting for transfers between devices, swap(): lax.ppermute(values, axis, [(index, index ^ bit) for index in range(size)])  17.3 us
    all_to_all x1, waiting for transfers between devices, shards_quad(): lax.all_to_all(target_late, 'group', split_axis=0, concat_axis=0, tiled=T...  7.93 us
    unnamed x22, local copies, waits for them, and re-layouts  4.05 us
    all_to_all x1, starting transfers between devices, shards_quad(): lax.all_to_all(target_late, 'group', split_axis=0, concat_axis=0, tiled=T...  3.86 us
  transfers between devices with their start and end apart: 22, of which 12 were waited for; matrix products, arithmetic and copies ran while one was open for 2% of the time, Pallas kernels for 2%

profile of v3, /device:TPU:0, one launch (start us, length us, event | category | flops | bytes accessed | tf_op | source)
XLA Modules:
  0.0 86.6 jit_solution(1677420624092868486)
XLA Ops:
  1.1 2.7 %collective-permute-start.1 = (s32[4,8]{1,0:T(4,128)}, s32[4,8]{1,0:T(4,128)S(1)}, u32[]{:S(2)}, u32[]{:S(2)}) collective-permute-start(s32[4,8]{1,0:T(4,128)} %param.9), channel_id=1, source_target_pairs={{0,2},{1,3},{2,0},{3,1},{4,6},{5,7},{6,4},{7,5},{8,10},{9,11},{10,... | collective-permute-start | bytes 392 | tf_op jit(solution)/shard_map/ppermute | solution.py:419
  3.9 1.7 %collective-permute-start.4 = (bf16[4,256,256]{2,1,0:T(8,128)(2,1)}, bf16[4,256,256]{2,1,0:T(8,128)(2,1)}, u32[]{:S(2)}, u32[]{:S(2)}) collective-permute-start(bf16[4,256,256]{2,1,0:T(8,128)(2,1)} %bitcast.24), channel_id=1, source_target_pairs={{0,2},{1,3},{2,0},{3,1},{4,6},{5,7},{6,4},{7,5},{8,10},{9,11},{10,... | collective-permute-start | bytes 1572872 | tf_op jit(solution)/shard_map/ppermute | solution.py:419
  5.6 2.6 %collective-permute-start.6 = (bf16[4,256,256]{2,1,0:T(8,128)(2,1)}, bf16[4,256,256]{2,1,0:T(8,128)(2,1)S(1)}, u32[]{:S(2)}, u32[]{:S(2)}) collective-permute-start(bf16[4,256,256]{2,1,0:T(8,128)(2,1)} %bitcast.21), channel_id=1, source_target_pairs={{0,4},{1,5},{2,6},{3,7},{4,0},{5,1},{6,2},{7,3},{8,12},{9,13},{10,... | collective-permute-start | bytes 1572872 | tf_op jit(solution)/shard_map/ppermute | solution.py:419
  9.9 3.9 %all-to-all-start = ((bf16[4,256,256]{2,1,0:T(8,128)(2,1)}), bf16[4,256,256]{2,1,0:T(8,128)(2,1)S(1)}, u32[]{:S(2)}, u32[]{:S(2)}) async-start(bf16[4,256,256]{2,1,0:T(8,128)(2,1)} %bitcast.22), calls=%async_computation | async-start | bytes 1048576 | tf_op jit(solution)/shard_map/all_to_all | solution.py:492
  14.3 7.9 %all-to-all-done.mirrors = bf16[4,256,256]{2,1,0:T(8,128)(2,1)S(1)} async-done(((bf16[4,256,256]{2,1,0:T(8,128)(2,1)}), bf16[4,256,256]{2,1,0:T(8,128)(2,1)S(1)}, u32[]{:S(2)}, u32[]{:S(2)}) %all-to-all-start) | async-done | bytes 524320 | tf_op jit(solution)/shard_map/all_to_all | solution.py:492
  22.3 0.8 copy-done.2
  23.1 1.0 %copy-done.1 = bf16[1024,256]{1,0:T(8,128)(2,1)S(1)} copy-done((bf16[1024,256]{1,0:T(8,128)(2,1)S(1)}, bf16[1024,256]{1,0:T(8,128)(2,1)}, u32[]{:S(2)}) %copy-start.1) | copy-done | bytes 524312
  24.2 1.0 %copy-done.3 = bf16[4,256,256]{2,1,0:T(8,128)(2,1)S(1)} copy-done((bf16[4,256,256]{2,1,0:T(8,128)(2,1)S(1)}, bf16[4,256,256]{2,1,0:T(8,128)(2,1)}, u32[]{:S(2)}) %copy-start.3) | copy-done | bytes 524312
  25.2 1.8 %shard_map.68 = (f32[16,256]{1,0:T(8,128)S(1)}, bf16[8,256,256]{2,1,0:T(8,128)(2,1)S(1)}, bf16[7,256,256]{2,1,0:T(8,128)(2,1)S(1)}) custom-call(s32[5,40]{1,0:T(8,128)S(1)} %stack.10.scalars.refs_0_, s32[40,128]{1,0:T(8,128)S(1)} %broadcast_in_dim.107.ids.refs_1_, bf16[4,256,256]{2,1,0:T(8,128)(2,1)S(1)} %bitcast.26, bf16[4,256,256]{2,1,0:T(8,128)(2,1)S(1)} %copy-done.3, ...), custom_call_target="tpu_custom_call" | custom-call | tf_op jit(solution)/shard_map/pallas_call | solution.py:408
  27.7 1.8 %collective-permute-done.4.near = bf16[4,256,256]{2,1,0:T(8,128)(2,1)} collective-permute-done((bf16[4,256,256]{2,1,0:T(8,128)(2,1)}, bf16[4,256,256]{2,1,0:T(8,128)(2,1)}, u32[]{:S(2)}, u32[]{:S(2)}) %collective-permute-start.4) | collective-permute-done | bytes 524320 | tf_op jit(solution)/shard_map/ppermute | solution.py:419
  29.6 2.3 %collective-permute-done.6.far.refs_6_ = bf16[4,256,256]{2,1,0:T(8,128)(2,1)S(1)} collective-permute-done((bf16[4,256,256]{2,1,0:T(8,128)(2,1)}, bf16[4,256,256]{2,1,0:T(8,128)(2,1)S(1)}, u32[]{:S(2)}, u32[]{:S(2)}) %collective-permute-start.6) | collective-permute-done | bytes 524320 | tf_op jit(solution)/shard_map/ppermute | solution.py:419
  31.9 3.3 %shard_map.69 = (f32[24,256]{1,0:T(8,128)S(1)}, bf16[8,256,256]{2,1,0:T(8,128)(2,1)S(1)}) custom-call(s32[5,40]{1,0:T(8,128)S(1)} %stack.10.scalars.refs_0_, s32[40,128]{1,0:T(8,128)S(1)} %copy-done.5, f32[16,256]{1,0:T(8,128)S(1)} %copy-done.7, f32[4,256]{1,0:T(4,128)S(1)} %mul.11.mass, bf16[8,256,256]{2,1,0:T(8,128)(2,1)S(1)} %get-tuple-element.30.sources.refs_3_, ...), custom_call_target="tpu_custom_call" | custom-call | tf_op jit(solution)/shard_map/pallas_call | solution.py:408
  35.8 1.3 %collective-permute-start.9 = (f32[24,256]{1,0:T(8,128)S(1)}, f32[24,256]{1,0:T(8,128)S(1)}, u32[]{:S(2)}, u32[]{:S(2)}) collective-permute-start(f32[24,256]{1,0:T(8,128)S(1)} %get-tuple-element.36.refs_7_), channel_id=1, source_target_pairs={{0,3},{1,2},{2,1},{3,0},{4,7},{5,6},{6,5},{7,4},{8,11},{9,10},{10,... | collective-permute-start | bytes 73736 | tf_op jit(solution)/shard_map/ppermute | solution.py:419
  37.3 2.1 %collective-permute-done.8.refs_9_ = f32[24,256]{1,0:T(8,128)S(1)} collective-permute-done((f32[24,256]{1,0:T(8,128)S(1)}, f32[24,256]{1,0:T(8,128)S(1)}, u32[]{:S(2)}, u32[]{:S(2)}) %collective-permute-start.8) | collective-permute-done | bytes 24608 | tf_op jit(solution)/shard_map/ppermute | solution.py:419
  39.5 2.8 %shard_map.70 = (f32[16,256]{1,0:T(8,128)S(1)}, f32[16,256]{1,0:T(8,128)S(1)}) custom-call(s32[5,40]{1,0:T(8,128)S(1)} %stack.10.scalars.refs_0_, s32[40,128]{1,0:T(8,128)S(1)} %broadcast_in_dim.105.refs_1_, f32[16,128]{1,0:T(8,128)S(1)} %broadcast_in_dim.106.refs_2_, bf16[8,256,256]{2,1,0:T(8,128)(2,1)S(1)} %get-tuple-element.30.sources.refs_3_, ...), custom_call_target="tpu_custom_call" | custom-call | tf_op jit(solution)/shard_map/pallas_call | solution.py:408
  42.3 2.4 %collective-permute-start.10 = (f32[16,256]{1,0:T(8,128)S(1)}, f32[16,256]{1,0:T(8,128)S(1)}, u32[]{:S(2)}, u32[]{:S(2)}) collective-permute-start(f32[16,256]{1,0:T(8,128)S(1)} %get-tuple-element.38.columns.refs_8_), channel_id=1, source_target_pairs={{0,4},{1,5},{2,6},{3,7},{4,0},{5,1},{6,2},{7,3},{8,12},{9,13},{10,... | collective-permute-start | bytes 49160 | tf_op jit(solution)/shard_map/ppermute | solution.py:419
  44.6 2.4 %collective-permute-done.10.partner.refs_9_ = f32[16,256]{1,0:T(8,128)S(1)} collective-permute-done((f32[16,256]{1,0:T(8,128)S(1)}, f32[16,256]{1,0:T(8,128)S(1)}, u32[]{:S(2)}, u32[]{:S(2)}) %collective-permute-start.10) | collective-permute-done | bytes 16416 | tf_op jit(solution)/shard_map/ppermute | solution.py:419
  47.1 0.6 shard_map.71
  47.7 1.6 %collective-permute-start.11 = (f32[4,256]{1,0:T(4,128)S(1)}, f32[4,256]{1,0:T(4,128)S(1)}, u32[]{:S(2)}, u32[]{:S(2)}) collective-permute-start(f32[4,256]{1,0:T(4,128)S(1)} %get-tuple-element.39), channel_id=1, source_target_pairs={{0,8},{8,0},{16,24},{24,16},{1,9},{9,1},{17,25},{25,17},{2,10},{10... | collective-permute-start | bytes 12296 | tf_op jit(solution)/shard_map/ppermute | solution.py:419
  49.3 1.5 %collective-permute-start.12 = (f32[4,256]{1,0:T(4,128)S(1)}, f32[4,256]{1,0:T(4,128)S(1)}, u32[]{:S(2)}, u32[]{:S(2)}) collective-permute-start(f32[4,256]{1,0:T(4,128)S(1)} %get-tuple-element.40), channel_id=1, source_target_pairs={{0,16},{8,24},{16,0},{24,8},{1,17},{9,25},{17,1},{25,9},{2,18},{10... | collective-permute-start | bytes 12296 | tf_op jit(solution)/shard_map/ppermute | solution.py:419
  51.4 1.5 %collective-permute-done.12.refs_11_ = f32[4,256]{1,0:T(4,128)S(1)} collective-permute-done((f32[4,256]{1,0:T(4,128)S(1)}, f32[4,256]{1,0:T(4,128)S(1)}, u32[]{:S(2)}, u32[]{:S(2)}) %collective-permute-start.12) | collective-permute-done | bytes 4128 | tf_op jit(solution)/shard_map/ppermute | solution.py:419
  52.9 2.4 %collective-permute-done.13.refs_12_ = f32[4,256]{1,0:T(4,128)S(1)} collective-permute-done((f32[4,256]{1,0:T(4,128)S(1)}, f32[4,256]{1,0:T(4,128)S(1)}, u32[]{:S(2)}, u32[]{:S(2)}) %collective-permute-start.13) | collective-permute-done | bytes 4128 | tf_op jit(solution)/shard_map/ppermute | solution.py:419
  55.4 14.3 %shard_map.72 = (f32[16,256]{1,0:T(8,128)S(1)}, f32[16,256]{1,0:T(8,128)S(1)}) custom-call(s32[5,40]{1,0:T(8,128)S(1)} %stack.10.scalars.refs_0_, s32[40,128]{1,0:T(8,128)S(1)} %copy-done.5, f32[16,128]{1,0:T(8,128)S(1)} %broadcast_in_dim.108.refs_2_, bf16[8,256,256]{2,1,0:T(8,128)(2,1)S(1)} %get-tuple-element.30.sources.refs_3_, ...), custom_call_target="tpu_custom_call" | custom-call | tf_op jit(solution)/shard_map/pallas_call | solution.py:408
  69.8 1.3 %collective-permute-start.15 = (f32[16,256]{1,0:T(8,128)S(1)}, f32[16,256]{1,0:T(8,128)S(1)}, u32[]{:S(2)}, u32[]{:S(2)}) collective-permute-start(f32[16,256]{1,0:T(8,128)S(1)} %get-tuple-element.42.refs_12_), channel_id=1, source_target_pairs={{0,2},{1,3},{2,0},{3,1},{4,6},{5,7},{6,4},{7,5},{8,10},{9,11},{10,... | collective-permute-start | bytes 49160 | tf_op jit(solution)/shard_map/ppermute | solution.py:419
  71.0 0.6 collective-permute-start.16
  71.6 1.9 %collective-permute-done.15.refs_14_ = f32[16,256]{1,0:T(8,128)S(1)} collective-permute-done((f32[16,256]{1,0:T(8,128)S(1)}, f32[16,256]{1,0:T(8,128)S(1)}, u32[]{:S(2)}, u32[]{:S(2)}) %collective-permute-start.15) | collective-permute-done | bytes 16416 | tf_op jit(solution)/shard_map/ppermute | solution.py:419
  73.6 0.6 collective-permute-done.16.refs_15_
  74.2 3.8 %shard_map.73 = (f32[16,256]{1,0:T(8,128)S(1)}, f32[8,128]{1,0:T(8,128)}) custom-call(s32[5,40]{1,0:T(8,128)S(1)} %stack.10.scalars.refs_0_, s32[40,128]{1,0:T(8,128)S(1)} %broadcast_in_dim.105.refs_1_, f32[16,128]{1,0:T(8,128)S(1)} %broadcast_in_dim.106.refs_2_, bf16[8,256,256]{2,1,0:T(8,128)(2,1)S(1)} %get-tuple-element.30.sources.refs_3_, ...), custom_call_target="tpu_custom_call" | custom-call | tf_op jit(solution)/shard_map/pallas_call | solution.py:408
  78.0 1.7 %collective-permute-start.17 = (f32[16,256]{1,0:T(8,128)S(1)}, f32[16,256]{1,0:T(8,128)S(1)}, u32[]{:S(2)}, u32[]{:S(2)}) collective-permute-start(f32[16,256]{1,0:T(8,128)S(1)} %get-tuple-element.45.columns), channel_id=1, source_target_pairs={{0,4},{1,5},{2,6},{3,7},{4,0},{5,1},{6,2},{7,3},{8,12},{9,13},{10,... | collective-permute-start | bytes 49160 | tf_op jit(solution)/shard_map/ppermute | solution.py:419
  80.7 2.4 %collective-permute-start.20 = (f32[16,256]{1,0:T(8,128)S(1)}, f32[16,256]{1,0:T(8,128)S(1)}, u32[]{:S(2)}, u32[]{:S(2)}) collective-permute-start(f32[16,256]{1,0:T(8,128)S(1)} %get-tuple-element.45.columns), channel_id=1, source_target_pairs={{0,24},{8,16},{16,8},{24,0},{1,25},{9,17},{17,9},{25,1},{2,26},{10... | collective-permute-start | bytes 49160 | tf_op jit(solution)/shard_map/ppermute | solution.py:419
  84.0 1.4 %collective-permute-done.20.rest_2_ = f32[16,256]{1,0:T(8,128)S(1)} collective-permute-done((f32[16,256]{1,0:T(8,128)S(1)}, f32[16,256]{1,0:T(8,128)S(1)}, u32[]{:S(2)}, u32[]{:S(2)}) %collective-permute-start.20) | collective-permute-done | bytes 16416 | tf_op jit(solution)/shard_map/ppermute | solution.py:419
  85.4 1.2 %shard_map.74 = f32[8,128]{1,0:T(8,128)} custom-call(s32[5,40]{1,0:T(8,128)S(1)} %stack.10.scalars.refs_0_, f32[16,256]{1,0:T(8,128)S(1)} %get-tuple-element.45.columns, f32[16,256]{1,0:T(8,128)S(1)} %collective-permute-done.17.partner, f32[16,256]{1,0:T(8,128)S(1)} %collective-permute-done.18.rest_0_, f32[16,256]{1,0:T(8,128)S(1)} %collective-permute-done.19.rest_1_, ...), custom_call_target="tpu_custom_call" | custom-call | tf_op jit(solution)/shard_map/pallas_call | solution.py:408
  (84 shorter events, 6.9 us)
Async XLA Ops:
  0.6 8.5 %collective-permute-start = (s32[4,8]{1,0:T(4,128)}, s32[4,8]{1,0:T(4,128)S(1)}, u32[]{:S(2)}, u32[]{:S(2)}) collective-permute-start(s32[4,8]{1,0:T(4,128)} %param.9), channel_id=1, source_target_pairs={{0,1},{1,0},{2,3},{3,2},{4,5},{5,4},{6,7},{7,6},{8,9},{9,8},{10,11... | collective-permute-start | bytes 392 | tf_op jit(solution)/shard_map/ppermute | solution.py:419
  1.1 8.0 %collective-permute-start.1 = (s32[4,8]{1,0:T(4,128)}, s32[4,8]{1,0:T(4,128)S(1)}, u32[]{:S(2)}, u32[]{:S(2)}) collective-permute-start(s32[4,8]{1,0:T(4,128)} %param.9), channel_id=1, source_target_pairs={{0,2},{1,3},{2,0},{3,1},{4,6},{5,7},{6,4},{7,5},{8,10},{9,11},{10,... | collective-permute-start | bytes 392 | tf_op jit(solution)/shard_map/ppermute | solution.py:419
  3.8 5.3 %collective-permute-start.2 = (s32[4,8]{1,0:T(4,128)}, s32[4,8]{1,0:T(4,128)S(1)}, u32[]{:S(2)}, u32[]{:S(2)}) collective-permute-start(s32[4,8]{1,0:T(4,128)} %param.9), channel_id=1, source_target_pairs={{0,3},{1,2},{2,1},{3,0},{4,7},{5,6},{6,5},{7,4},{8,11},{9,10},{10,... | collective-permute-start | bytes 392 | tf_op jit(solution)/shard_map/ppermute | solution.py:419
  3.9 25.7 %collective-permute-start.4 = (bf16[4,256,256]{2,1,0:T(8,128)(2,1)}, bf16[4,256,256]{2,1,0:T(8,128)(2,1)}, u32[]{:S(2)}, u32[]{:S(2)}) collective-permute-start(bf16[4,256,256]{2,1,0:T(8,128)(2,1)} %bitcast.24), channel_id=1, source_target_pairs={{0,2},{1,3},{2,0},{3,1},{4,6},{5,7},{6,4},{7,5},{8,10},{9,11},{10,... | collective-permute-start | bytes 1572872 | tf_op jit(solution)/shard_map/ppermute | solution.py:419
  5.6 26.3 %collective-permute-start.6 = (bf16[4,256,256]{2,1,0:T(8,128)(2,1)}, bf16[4,256,256]{2,1,0:T(8,128)(2,1)S(1)}, u32[]{:S(2)}, u32[]{:S(2)}) collective-permute-start(bf16[4,256,256]{2,1,0:T(8,128)(2,1)} %bitcast.21), channel_id=1, source_target_pairs={{0,4},{1,5},{2,6},{3,7},{4,0},{5,1},{6,2},{7,3},{8,12},{9,13},{10,... | collective-permute-start | bytes 1572872 | tf_op jit(solution)/shard_map/ppermute | solution.py:419
  9.0 0.7 copy-start.10
  9.8 13.4 %copy-start = (bf16[1024,256]{1,0:T(8,128)(2,1)S(1)}, bf16[1024,256]{1,0:T(8,128)(2,1)}, u32[]{:S(2)}) copy-start(bf16[1024,256]{1,0:T(8,128)(2,1)} %param.6) | copy-start | bytes 1572868
  9.8 12.5 %collective-permute-start.3 = (bf16[4,256,256]{2,1,0:T(8,128)(2,1)}, bf16[4,256,256]{2,1,0:T(8,128)(2,1)S(1)}, u32[]{:S(2)}, u32[]{:S(2)}) collective-permute-start(bf16[4,256,256]{2,1,0:T(8,128)(2,1)} %bitcast.25), channel_id=1, source_target_pairs={{0,1},{1,0},{2,3},{3,2},{4,5},{5,4},{6,7},{7,6},{8,9},{9,8},{10,11... | collective-permute-start | bytes 1572872 | tf_op jit(solution)/shard_map/ppermute | solution.py:419
  9.9 12.4 %all-to-all-start = ((bf16[4,256,256]{2,1,0:T(8,128)(2,1)}), bf16[4,256,256]{2,1,0:T(8,128)(2,1)S(1)}, u32[]{:S(2)}, u32[]{:S(2)}) async-start(bf16[4,256,256]{2,1,0:T(8,128)(2,1)} %bitcast.22), calls=%async_computation | async-start | bytes 1048576 | tf_op jit(solution)/shard_map/all_to_all | solution.py:492
  22.3 0.8 copy-start.2
  23.1 1.0 %copy-start.1 = (bf16[1024,256]{1,0:T(8,128)(2,1)S(1)}, bf16[1024,256]{1,0:T(8,128)(2,1)}, u32[]{:S(2)}) copy-start(bf16[1024,256]{1,0:T(8,128)(2,1)} %param.5) | copy-start | bytes 1572868
  24.2 1.0 %copy-start.3 = (bf16[4,256,256]{2,1,0:T(8,128)(2,1)S(1)}, bf16[4,256,256]{2,1,0:T(8,128)(2,1)}, u32[]{:S(2)}) copy-start(bf16[4,256,256]{2,1,0:T(8,128)(2,1)} %copy-done.2) | copy-start | bytes 1572868
  25.2 1.9 %copy-start.4 = (s32[40,128]{1,0:T(8,128)}, s32[40,128]{1,0:T(8,128)S(1)}, u32[]{:S(2)}) copy-start(s32[40,128]{1,0:T(8,128)S(1)} %broadcast_in_dim.107.ids.refs_1_) | copy-start | bytes 61444
  25.2 4.3 %copy-start.8 = (f32[1024]{0:T(1024)S(1)}, f32[1024]{0:T(1024)}, u32[]{:S(2)}) copy-start(f32[1024]{0:T(1024)} %param.7) | copy-start | bytes 12292
  25.2 4.3 %copy-start.9 = (f32[1024]{0:T(1024)S(1)}, f32[1024]{0:T(1024)}, u32[]{:S(2)}) copy-start(f32[1024]{0:T(1024)} %param.8) | copy-start | bytes 12292
  29.5 2.4 %copy-start.5 = (s32[40,128]{1,0:T(8,128)S(1)}, s32[40,128]{1,0:T(8,128)}, u32[]{:S(2)}) copy-start(s32[40,128]{1,0:T(8,128)} %copy-done.4) | copy-start | bytes 61444
  29.5 2.4 %copy-start.7 = (f32[16,256]{1,0:T(8,128)S(1)}, f32[16,256]{1,0:T(8,128)}, u32[]{:S(2)}) copy-start(f32[16,256]{1,0:T(8,128)} %copy-done.6) | copy-start | bytes 49156
  29.5 2.4 %collective-permute-start.5 = (bf16[4,256,256]{2,1,0:T(8,128)(2,1)}, bf16[4,256,256]{2,1,0:T(8,128)(2,1)S(1)}, u32[]{:S(2)}, u32[]{:S(2)}) collective-permute-start(bf16[4,256,256]{2,1,0:T(8,128)(2,1)} %collective-permute-done.4.near), channel_id=1, source_target_pairs={{0,1},{1,0},{2,3},{3,2},{4,5},{5,4},{6,7},{7,6},{8,9},{9,8},{10,11... | collective-permute-start | bytes 1572872 | tf_op jit(solution)/shard_map/ppermute | solution.py:419
  35.2 2.1 %collective-permute-start.7 = (f32[24,256]{1,0:T(8,128)S(1)}, f32[24,256]{1,0:T(8,128)S(1)}, u32[]{:S(2)}, u32[]{:S(2)}) collective-permute-start(f32[24,256]{1,0:T(8,128)S(1)} %get-tuple-element.36.refs_7_), channel_id=1, source_target_pairs={{0,1},{1,0},{2,3},{3,2},{4,5},{5,4},{6,7},{7,6},{8,9},{9,8},{10,11... | collective-permute-start | bytes 73736 | tf_op jit(solution)/shard_map/ppermute | solution.py:419
  35.3 4.1 %collective-permute-start.8 = (f32[24,256]{1,0:T(8,128)S(1)}, f32[24,256]{1,0:T(8,128)S(1)}, u32[]{:S(2)}, u32[]{:S(2)}) collective-permute-start(f32[24,256]{1,0:T(8,128)S(1)} %get-tuple-element.36.refs_7_), channel_id=1, source_target_pairs={{0,2},{1,3},{2,0},{3,1},{4,6},{5,7},{6,4},{7,5},{8,10},{9,11},{10,... | collective-permute-start | bytes 73736 | tf_op jit(solution)/shard_map/ppermute | solution.py:419
  35.8 3.5 %collective-permute-start.9 = (f32[24,256]{1,0:T(8,128)S(1)}, f32[24,256]{1,0:T(8,128)S(1)}, u32[]{:S(2)}, u32[]{:S(2)}) collective-permute-start(f32[24,256]{1,0:T(8,128)S(1)} %get-tuple-element.36.refs_7_), channel_id=1, source_target_pairs={{0,3},{1,2},{2,1},{3,0},{4,7},{5,6},{6,5},{7,4},{8,11},{9,10},{10,... | collective-permute-start | bytes 73736 | tf_op jit(solution)/shard_map/ppermute | solution.py:419
  42.3 4.8 %collective-permute-start.10 = (f32[16,256]{1,0:T(8,128)S(1)}, f32[16,256]{1,0:T(8,128)S(1)}, u32[]{:S(2)}, u32[]{:S(2)}) collective-permute-start(f32[16,256]{1,0:T(8,128)S(1)} %get-tuple-element.38.columns.refs_8_), channel_id=1, source_target_pairs={{0,4},{1,5},{2,6},{3,7},{4,0},{5,1},{6,2},{7,3},{8,12},{9,13},{10,... | collective-permute-start | bytes 49160 | tf_op jit(solution)/shard_map/ppermute | solution.py:419
  47.7 3.7 %collective-permute-start.11 = (f32[4,256]{1,0:T(4,128)S(1)}, f32[4,256]{1,0:T(4,128)S(1)}, u32[]{:S(2)}, u32[]{:S(2)}) collective-permute-start(f32[4,256]{1,0:T(4,128)S(1)} %get-tuple-element.39), channel_id=1, source_target_pairs={{0,8},{8,0},{16,24},{24,16},{1,9},{9,1},{17,25},{25,17},{2,10},{10... | collective-permute-start | bytes 12296 | tf_op jit(solution)/shard_map/ppermute | solution.py:419
  49.3 3.6 %collective-permute-start.12 = (f32[4,256]{1,0:T(4,128)S(1)}, f32[4,256]{1,0:T(4,128)S(1)}, u32[]{:S(2)}, u32[]{:S(2)}) collective-permute-start(f32[4,256]{1,0:T(4,128)S(1)} %get-tuple-element.40), channel_id=1, source_target_pairs={{0,16},{8,24},{16,0},{24,8},{1,17},{9,25},{17,1},{25,9},{2,18},{10... | collective-permute-start | bytes 12296 | tf_op jit(solution)/shard_map/ppermute | solution.py:419
  50.8 4.5 %collective-permute-start.13 = (f32[4,256]{1,0:T(4,128)S(1)}, f32[4,256]{1,0:T(4,128)S(1)}, u32[]{:S(2)}, u32[]{:S(2)}) collective-permute-start(f32[4,256]{1,0:T(4,128)S(1)} %get-tuple-element.41), channel_id=1, source_target_pairs={{0,24},{8,16},{16,8},{24,0},{1,25},{9,17},{17,9},{25,1},{2,26},{10... | collective-permute-start | bytes 12296 | tf_op jit(solution)/shard_map/ppermute | solution.py:419
  69.7 1.9 %collective-permute-start.14 = (f32[16,256]{1,0:T(8,128)S(1)}, f32[16,256]{1,0:T(8,128)S(1)}, u32[]{:S(2)}, u32[]{:S(2)}) collective-permute-start(f32[16,256]{1,0:T(8,128)S(1)} %get-tuple-element.42.refs_12_), channel_id=1, source_target_pairs={{0,1},{1,0},{2,3},{3,2},{4,5},{5,4},{6,7},{7,6},{8,9},{9,8},{10,11... | collective-permute-start | bytes 49160 | tf_op jit(solution)/shard_map/ppermute | solution.py:419
  69.8 3.8 %collective-permute-start.15 = (f32[16,256]{1,0:T(8,128)S(1)}, f32[16,256]{1,0:T(8,128)S(1)}, u32[]{:S(2)}, u32[]{:S(2)}) collective-permute-start(f32[16,256]{1,0:T(8,128)S(1)} %get-tuple-element.42.refs_12_), channel_id=1, source_target_pairs={{0,2},{1,3},{2,0},{3,1},{4,6},{5,7},{6,4},{7,5},{8,10},{9,11},{10,... | collective-permute-start | bytes 49160 | tf_op jit(solution)/shard_map/ppermute | solution.py:419
  71.0 3.2 %collective-permute-start.16 = (f32[16,256]{1,0:T(8,128)S(1)}, f32[16,256]{1,0:T(8,128)S(1)}, u32[]{:S(2)}, u32[]{:S(2)}) collective-permute-start(f32[16,256]{1,0:T(8,128)S(1)} %get-tuple-element.42.refs_12_), channel_id=1, source_target_pairs={{0,3},{1,2},{2,1},{3,0},{4,7},{5,6},{6,5},{7,4},{8,11},{9,10},{10,... | collective-permute-start | bytes 49160 | tf_op jit(solution)/shard_map/ppermute | solution.py:419
  78.0 5.2 %collective-permute-start.17 = (f32[16,256]{1,0:T(8,128)S(1)}, f32[16,256]{1,0:T(8,128)S(1)}, u32[]{:S(2)}, u32[]{:S(2)}) collective-permute-start(f32[16,256]{1,0:T(8,128)S(1)} %get-tuple-element.45.columns), channel_id=1, source_target_pairs={{0,4},{1,5},{2,6},{3,7},{4,0},{5,1},{6,2},{7,3},{8,12},{9,13},{10,... | collective-permute-start | bytes 49160 | tf_op jit(solution)/shard_map/ppermute | solution.py:419
  79.7 3.7 %collective-permute-start.18 = (f32[16,256]{1,0:T(8,128)S(1)}, f32[16,256]{1,0:T(8,128)S(1)}, u32[]{:S(2)}, u32[]{:S(2)}) collective-permute-start(f32[16,256]{1,0:T(8,128)S(1)} %get-tuple-element.45.columns), channel_id=1, source_target_pairs={{0,8},{8,0},{16,24},{24,16},{1,9},{9,1},{17,25},{25,17},{2,10},{10... | collective-permute-start | bytes 49160 | tf_op jit(solution)/shard_map/ppermute | solution.py:419
  80.2 3.7 %collective-permute-start.19 = (f32[16,256]{1,0:T(8,128)S(1)}, f32[16,256]{1,0:T(8,128)S(1)}, u32[]{:S(2)}, u32[]{:S(2)}) collective-permute-start(f32[16,256]{1,0:T(8,128)S(1)} %get-tuple-element.45.columns), channel_id=1, source_target_pairs={{0,16},{8,24},{16,0},{24,8},{1,17},{9,25},{17,1},{25,9},{2,18},{10... | collective-permute-start | bytes 49160 | tf_op jit(solution)/shard_map/ppermute | solution.py:419
  80.7 4.6 %collective-permute-start.20 = (f32[16,256]{1,0:T(8,128)S(1)}, f32[16,256]{1,0:T(8,128)S(1)}, u32[]{:S(2)}, u32[]{:S(2)}) collective-permute-start(f32[16,256]{1,0:T(8,128)S(1)} %get-tuple-element.45.columns), channel_id=1, source_target_pairs={{0,24},{8,16},{16,8},{24,0},{1,25},{9,17},{17,9},{25,1},{2,26},{10... | collective-permute-start | bytes 49160 | tf_op jit(solution)/shard_map/ppermute | solution.py:419
  (1 other events, 0.6 us)

commit v4 on v3

--- a/solution.py
+++ b/solution.py
@@ -282,17 +282,15 @@
     return jnp.where(total > 0, best + LOG2E * jnp.log(jnp.where(total > 0, total, 1.0)), very_low)
 
 
-def fast_pass(scalars, ids, present, by_rows, sources, targets, bias, reference, total, tops, sums, out):
+def fast_pass(scalars, ids, present, by_rows, sections, sources, targets, bias, shift, total, tops, sums):
     total[...] = jnp.zeros(total.shape, jnp.float32)
-    for section, (first, count) in enumerate(SECTIONS):
-        (summed, summed_row, summed_base), (kept, kept_row, kept_base) = sides(
-            section, by_rows, sources, targets
-        )
+    for section in sections:
+        first, count = SECTIONS[section]
+        (summed, summed_row, summed_base), (kept, kept_row, _) = sides(section, by_rows, sources, targets)
         for slot in range(first, first + count):
-            block, partner = scalars[summed_row, slot], scalars[kept_row, slot]
-            logits = score(summed[block], kept[partner]) + wide(bias[summed_base + block])
-            if reference is not None:
-                logits = logits + reference[pl.ds(kept_base + partner, 1), :]
+            block = scalars[summed_row, slot]
+            logits = score(summed[block], kept[scalars[kept_row, slot]])
+            logits = logits + (shift if bias is None else wide(bias[summed_base + block]))
             terms = jnp.exp2(logits)
             place = scalars[2 + kept_row, slot]
             total[place] = total[place] + jnp.sum(terms.reshape(-1, 8, terms.shape[1]), axis=0)
@@ -302,17 +300,34 @@
     )
     here = wide(present[0:count]) > 0
     result = LOG2E * jnp.log(jnp.where(here, sums_of, 1.0))
-    if reference is not None:
-        result = result - reference[0:count]
-    out[0:count, :] = jnp.where(here, result, very_low)
+    if shift is not None:
+        result = result - shift
     fine = jnp.logical_and(sums_of > SMALL, sums_of < LARGE)
     worst = jnp.min(jnp.where(jnp.logical_or(fine, jnp.logical_not(here)), 1.0, 0.0))
-
-    @pl.when(worst < 0.5)
+    return jnp.where(here, result, very_low), worst > 0.5
+
+
+def guarded_pass(scalars, ids, present, by_rows, sections, sources, targets, rows, shift, work, write):
+    total, tops, sums, *bias = work
+    bias = bias[0] if bias else None
+    if bias is not None:
+        spread(rows if shift is None else rows + shift, bias)
+    result, fine = fast_pass(
+        scalars, ids, present, by_rows, sections, sources, targets, bias, shift, total, tops, sums
+    )
+    write(result)
+
+    @pl.when(jnp.logical_not(fine))
     def _():
-        out[0:count, :] = exact_pass(
-            scalars, ids, by_rows, (0, 1, 2, 3), sources, targets, bias, tops, sums, False
-        )
+        if shift is not None and bias is not None:
+            spread(rows, bias)
+        write(exact_pass(scalars, ids, by_rows, sections, sources, targets, bias, tops, sums, False))
+
+
+def middle(pieces):
+    top = functools.reduce(jnp.maximum, [jnp.max(piece, axis=(0, 1), keepdims=True) for piece in pieces])
+    bottom = functools.reduce(jnp.minimum, [jnp.min(piece, axis=(0, 1), keepdims=True) for piece in pieces])
+    return 0.5 * (top + bottom)
 
 
 def early_kernel(scalars, ids, own, core, target, mirrors, out, sources, targets, tops, sums):
@@ -327,28 +342,43 @@
 
 
 def first_kernel(
-    scalars, ids, early, mass, sources, near, cross, targets, far, out, late_sources, tops, sums
+    scalars, ids, present, early, mass, sources, near, cross, targets, far, out, late_sources, *work
 ):
-    late_sources[0:4] = near[...]
-    late_sources[4:8] = cross[...]
-    late = exact_pass(
-        scalars, ids, True, (1, 2, 3), (sources, late_sources), (targets, far), None, tops, sums, True
-    )
-    out[0:16, :] = merge([early[...], late])
+    late_sources[0:4] = near[0 : mass.shape[1] * 4].reshape(late_sources[0:4].shape)
+    late_sources[4:8] = cross[0 : mass.shape[1] * 4].reshape(late_sources[4:8].shape)
     out[16:20, :] = mass[...]
     out[20:24, :] = jnp.zeros((4, out.shape[1]), jnp.float32)
+    begun = early[...]
+    shift = -jnp.max(begun, axis=(0, 1), keepdims=True)
+
+    def write(late):
+        out[0:16, :] = merge([begun, late])
+
+    guarded_pass(
+        scalars,
+        ids,
+        present,
+        True,
+        (1, 2, 3),
+        (sources, late_sources),
+        (targets, far),
+        None,
+        shift,
+        work,
+        write,
+    )
 
 
 def columns_kernel(last_pass, *refs):
     scalars, ids, present = refs[:3]
     sources, targets = refs[3:5], refs[5:7]
     masses, target_mass, rest = refs[7:11], refs[11], refs[12:]
-    parts, reference = masses, None
+    parts, shift = masses, None
     if last_pass:
-        parts, (reference, *rest) = rest[:4], rest[4:]
-    out, second, total, tops, sums, bias = rest
+        parts, (shift, *rest) = rest[:4], rest[4:]
+        shift = shift[0:1, 0:1]
+    out, second, *work = rest
     rows = source_bias(masses, parts)
-    spread(rows, bias)
     if last_pass:
         for block in range(4):
             for half in range(2):
@@ -356,23 +386,30 @@
                     TO_POTENTIAL * rows[block : block + 1, 128 * half : 128 * (half + 1)]
                 )
     else:
-        second[...] = rows
-    fast_pass(
-        scalars, ids, present, False, sources, targets, bias, reference, total, tops, sums, out
-    )
+        second[...] = jnp.broadcast_to(middle([rows]), second.shape)
     out[12:16, :] = target_mass[0:4]
+
+    def write(result):
+        out[0:TARGET_SLOTS, :] = result
+
+    guarded_pass(
+        scalars, ids, present, False, (0, 1, 2, 3), sources, targets, rows, shift, work, write
+    )
 
 
 def rows_kernel(*refs):
     scalars, ids, present = refs[:3]
     sources, targets = refs[3:5], refs[5:7]
-    reference, columns, partner, *mirrors = refs[7:13]
-    out, second, total, tops, sums, bias, scratch = refs[13:]
+    shift, columns, partner, *mirrors = refs[7:13]
+    out, second, *work, scratch = refs[13:]
     rows = target_bias(scalars, columns, partner, mirrors, scratch)
-    spread(rows, bias)
-    second[...] = rows
-    fast_pass(
-        scalars, ids, present, True, sources, targets, bias, reference, total, tops, sums, out
+    second[...] = jnp.broadcast_to(middle([rows[0:7], rows[8:12]]), second.shape)
+
+    def write(result):
+        out[...] = result
+
+    guarded_pass(
+        scalars, ids, present, True, (0, 1, 2, 3), sources, targets, rows, shift[0:1, 0:1], work, write
     )
 
 
@@ -419,14 +456,16 @@
     return lax.ppermute(values, axis, [(index, index ^ bit) for index in range(size)])
 
 
-def tile_lists(candidates, own_group, own_member, members, per_device):
+def tile_lists(candidates, own_group, own_member, members, per_device, slot_count):
     owner = candidates // per_device
     local = candidates % per_device
     apart = (owner % members) ^ own_member
     last = candidates.shape[1] - 1
     mirror = (owner // members) ^ own_group
     is_last = jnp.arange(last + 1)[None, :] == last
-    source = jnp.broadcast_to(jnp.arange(SOURCE_SLOTS, dtype=jnp.int32)[:, None], candidates.shape)
+    source = jnp.broadcast_to(
+        jnp.arange(candidates.shape[0], dtype=jnp.int32)[:, None], candidates.shape
+    )
     own_mirror = jnp.logical_and(is_last, source < per_device)
     near = jnp.logical_and(~is_last, apart == 0)
     far = jnp.logical_and(~is_last, apart == 4)
@@ -443,10 +482,12 @@
     before = order[None, :] < order[:, None]
     place = jnp.full(order.shape, -1, jnp.int32)
     for (first, _), taken in zip(SECTIONS, members_of):
+        if first >= 12 and slot_count == 16:
+            break
         taken = taken.reshape(-1)
         earlier = jnp.sum(jnp.logical_and(before, taken[None, :]).astype(jnp.int32), axis=1)
         place = jnp.where(taken, first + earlier, place)
-    slots = jnp.arange(TILE_SLOTS, dtype=jnp.int32)
+    slots = jnp.arange(slot_count, dtype=jnp.int32)
     hits = place[None, :] == slots[:, None]
     used = jnp.any(hits, axis=1)
     sources = jnp.sum(jnp.where(hits, source, 0), axis=1)
@@ -465,9 +506,10 @@
     )
     lists = []
     for ids in (source_ids, target_ids):
-        rows = jnp.any(ids[None, :] == jnp.arange(16)[:, None], axis=1).astype(jnp.float32)
-        lists.append(jnp.broadcast_to(ids[:, None], (TILE_SLOTS, 128)))
-        lists.append(jnp.broadcast_to(rows[:, None], (16, 128)))
+        lists.append(jnp.broadcast_to(ids[:, None], (slot_count, 128)))
+        for counted in (ids, jnp.where(slots >= 12, ids, -1)):
+            rows = jnp.any(counted[None, :] == jnp.arange(16)[:, None], axis=1).astype(jnp.float32)
+            lists.append(jnp.broadcast_to(rows[:, None], (16, 128)))
     return scalars, *lists
 
 
@@ -485,15 +527,17 @@
 
     source_own = source_vectors.reshape(blocked)
     target_own = target_vectors.reshape(blocked)
-    named = [candidates] + [member_swap(candidates, bit) for bit in (1, 2, 3)]
     target_far = member_swap(target_own, 4)
-    source_near = member_swap(source_own, 2)
-    source_late, target_late, *named = lax.optimization_barrier((source_own, target_own, *named))
+    named = jnp.concatenate([candidates, member_swap(candidates, 1)])
+    note = jnp.pad(
+        named.astype(source_vectors.dtype).reshape(1, named.size), ((0, 15), (0, width - named.size))
+    )
+    source_near = member_swap(jnp.concatenate([source_vectors, note]), 2)
+    source_late, target_late, named = lax.optimization_barrier((source_own, target_own, named))
     mirrors = lax.all_to_all(target_late, "group", split_axis=0, concat_axis=0, tiled=True)
     source_core = member_swap(source_late, 1)
-    scalars, by_source, has_source, by_target, has_target = tile_lists(
-        jnp.concatenate(named), own_group, own_member, members, per_device
-    )
+    place = (own_group, own_member, members, per_device)
+    early_scalars, early_by_source, *_ = tile_lists(named, *place, 16)
     own_source_mass = LOG2E * source_mass.reshape(per_device, block_rows)
     own_mass = LOG2E * target_mass.reshape(per_device, block_rows)
 
@@ -509,17 +553,22 @@
 
     early, sources, targets = call(
         early_kernel,
-        [scalars, by_source, source_own, source_core, target_own, mirrors],
+        [early_scalars, early_by_source, source_own, source_core, target_own, mirrors],
         [side, stacked(8), stacked(7)],
         tile_rows,
     )
     source_near, early = lax.optimization_barrier((source_near, early))
     source_cross = member_swap(source_near, 1)
+    theirs = source_near[per_device * block_rows, : named.size].astype(jnp.int32).reshape(named.shape)
+    scalars, by_source, has_source, has_late_source, by_target, has_target, _ = tile_lists(
+        jnp.concatenate([named, theirs]), *place, TILE_SLOTS
+    )
     parts, late_sources = call(
         first_kernel,
         [
             scalars,
             by_source,
+            has_late_source,
             early,
             own_source_mass,
             sources,
@@ -529,7 +578,7 @@
             target_far,
         ],
         [jax.ShapeDtypeStruct((24, block_rows), jnp.float32), stacked(8)],
-        tile_rows,
+        pass_buffers[:3],
     )
     blocks = [sources, late_sources, targets, target_far]
     masses, extra = [], []
@@ -540,7 +589,7 @@
         columns, potential = call(
             functools.partial(columns_kernel, last_pass),
             [scalars, by_target, has_target, *blocks, *masses, own_mass, *(parts + extra if last_pass else [])],
-            [side, flat if last_pass else side],
+            [side, flat],
             pass_buffers,
         )
         partner = member_swap(columns, 4)
@@ -552,13 +601,13 @@
             [jax.ShapeDtypeStruct((4, block_rows), jnp.float32)] * 3,
         )
         received = [group_swap(values, bit) for bit, values in enumerate(sent, 1)]
-        parts, target_rows = call(
+        parts, shift = call(
             rows_kernel,
             [scalars, by_source, has_source, *blocks, potential, columns, partner, *received],
-            [side, side],
+            [side, flat],
             [*pass_buffers, VMEM((8, block_rows), jnp.float32)],
         )
-        extra = [target_rows]
+        extra = [shift]
     received = [group_swap(columns, bit) for bit in (1, 2, 3)]
     (final,) = call(
         finish_kernel,

time: 86.9 us -> 108 us (1.24)
  other arithmetic: 0.82 us -> 7.86 us
  Pallas kernels: 27.9 us -> 34.1 us
  waiting for transfers between devices: 25.2 us -> 29.6 us
  local copies, waits for them, and re-layouts: 5.27 us -> 9.24 us
    ppermute x21 -> x19, waiting for transfers between devices: 17.3 us -> 23.8 us  [swap(): lax.ppermute(values, axis, [(index, index ^ bit) for index in range(size)])]
    pallas_call x7, Pallas kernels: 27.9 us -> 34.1 us  [call(): pl.pallas_call(kernel, out_shape=outs, in_specs=[pl.BlockSpec(memory_spac...]
    all_to_all x1, waiting for transfers between devices: 7.93 us -> 5.74 us  [shards_quad(): lax.all_to_all(target_late, 'group', split_axis=0, concat_axis=0, tiled=T...]
    broadcast_in_dim x9 -> x12, local copies, waits for them, and re-layouts: 0.67 us -> 2.43 us  [the longest x8 2.15 us: tile_lists(): jnp.broadcast_to(jnp.arange(candidates.shape[0], dtype=jnp.int32)[:, None...]
    concatenate x1 -> x3, other arithmetic: 0.01 us -> 1.54 us  [the longest x1 0.84 us: shards_quad(): source_near = member_swap(jnp.concatenate([source_vectors, note]), 2)]
    unnamed x22 -> x14, local copies, waits for them, and re-layouts: 4.05 us -> 4.21 us
    ppermute x21 -> x19, starting transfers between devices: 22.6 us -> 22.5 us  [swap(): lax.ppermute(values, axis, [(index, index ^ bit) for index in range(size)])]
  transfers between devices with their start and end apart: 22 -> 20, of which waited for: 12 -> 11; matrix products, arithmetic and copies ran while one was open for 2% -> 12% of each run, Pallas kernels for 2% -> 2%
where the time goes in v4:
time: 108 us
  Pallas kernels  34.1 us (32%)
  waiting for transfers between devices  29.6 us (27%)
  starting transfers between devices  26.2 us (24%)
  local copies, waits for them, and re-layouts  9.24 us (9%)
  other arithmetic  7.86 us (7%)
    pallas_call x7, Pallas kernels, call(): pl.pallas_call(kernel, out_shape=outs, in_specs=[pl.BlockSpec(memory_spac...  34.1 us
    ppermute x19, waiting for transfers between devices, swap(): lax.ppermute(values, axis, [(index, index ^ bit) for index in range(size)])  23.8 us
    ppermute x19, starting transfers between devices, swap(): lax.ppermute(values, axis, [(index, index ^ bit) for index in range(size)])  22.5 us
    all_to_all x1, waiting for transfers between devices, shards_quad(): lax.all_to_all(target_late, 'group', split_axis=0, concat_axis=0, tiled=T...  5.74 us
    unnamed x14, local copies, waits for them, and re-layouts  4.21 us
    all_to_all x1, starting transfers between devices, shards_quad(): lax.all_to_all(target_late, 'group', split_axis=0, concat_axis=0, tiled=T...  3.72 us
  transfers between devices with their start and end apart: 20, of which 11 were waited for; matrix products, arithmetic and copies ran while one was open for 12% of the time, Pallas kernels for 2%

profile of v4, /device:TPU:0, one launch (start us, length us, event | category | flops | bytes accessed | tf_op | source)
XLA Modules:
  0.0 107.8 jit_solution(13766643574266050999)
XLA Ops:
  1.2 3.7 %collective-permute-start.4 = (bf16[4,256,256]{2,1,0:T(8,128)(2,1)}, bf16[4,256,256]{2,1,0:T(8,128)(2,1)S(1)}, u32[]{:S(2)}, u32[]{:S(2)}) collective-permute-start(bf16[4,256,256]{2,1,0:T(8,128)(2,1)} %bitcast.38), channel_id=1, source_target_pairs={{0,4},{1,5},{2,6},{3,7},{4,0},{5,1},{6,2},{7,3},{8,12},{9,13},{10,... | collective-permute-start | bytes 1572872 | tf_op jit(solution)/shard_map/ppermute | solution.py:456
  11.7 3.7 %all-to-all-start = ((bf16[4,256,256]{2,1,0:T(8,128)(2,1)}), bf16[4,256,256]{2,1,0:T(8,128)(2,1)S(1)}, u32[]{:S(2)}, u32[]{:S(2)}) async-start(bf16[4,256,256]{2,1,0:T(8,128)(2,1)} %bitcast.39), calls=%async_computation | async-start | bytes 1048576 | tf_op jit(solution)/shard_map/all_to_all | solution.py:537
  15.5 0.8 fusion.1
  16.4 1.6 %collective-permute-start.1 = (bf16[1040,256]{1,0:T(8,128)(2,1)}, bf16[1040,256]{1,0:T(8,128)(2,1)}, u32[]{:S(2)}, u32[]{:S(2)}) collective-permute-start(bf16[1040,256]{1,0:T(8,128)(2,1)} %fusion.1), channel_id=1, source_target_pairs={{0,2},{1,3},{2,0},{3,1},{4,6},{5,7},{6,4},{7,5},{8,10},{9,11},{10,... | collective-permute-start | bytes 1597448 | tf_op jit(solution)/shard_map/ppermute | solution.py:456
  18.2 5.7 %all-to-all-done.mirrors = bf16[4,256,256]{2,1,0:T(8,128)(2,1)S(1)} async-done(((bf16[4,256,256]{2,1,0:T(8,128)(2,1)}), bf16[4,256,256]{2,1,0:T(8,128)(2,1)S(1)}, u32[]{:S(2)}, u32[]{:S(2)}) %all-to-all-start) | async-done | bytes 524320 | tf_op jit(solution)/shard_map/all_to_all | solution.py:537
  24.0 0.8 copy-done.3
  24.8 1.0 copy-done.2
  25.9 1.0 copy-done.4
  26.9 1.9 %shard_map.68 = (f32[16,256]{1,0:T(8,128)S(1)}, bf16[8,256,256]{2,1,0:T(8,128)(2,1)S(1)}, bf16[7,256,256]{2,1,0:T(8,128)(2,1)S(1)}) custom-call(s32[5,16]{1,0:T(8,128)S(1)} %stack.9.scalars, s32[16,128]{1,0:T(8,128)S(1)} %broadcast_in_dim.169.ids, bf16[4,256,256]{2,1,0:T(8,128)(2,1)S(1)} %bitcast.42, bf16[4,256,256]{2,1,0:T(8,128)(2,1)S(1)} %copy-done.4, ...), custom_call_target="tpu_custom_call" | custom-call | tf_op jit(solution)/shard_map/pallas_call | solution.py:445
  29.4 10.9 %collective-permute-done.1.near = bf16[1040,256]{1,0:T(8,128)(2,1)} collective-permute-done((bf16[1040,256]{1,0:T(8,128)(2,1)}, bf16[1040,256]{1,0:T(8,128)(2,1)}, u32[]{:S(2)}, u32[]{:S(2)}) %collective-permute-start.1) | collective-permute-done | bytes 532512 | tf_op jit(solution)/shard_map/ppermute | solution.py:456
  43.8 0.8 select_reduce_fusion
  45.0 0.7 copy-done.6
  45.7 9.7 %shard_map.69 = (f32[24,256]{1,0:T(8,128)S(1)}, bf16[8,256,256]{2,1,0:T(8,128)(2,1)S(1)}) custom-call(s32[5,40]{1,0:T(8,128)S(1)} %stack.21.scalars.refs_0_, s32[40,128]{1,0:T(8,128)S(1)} %broadcast_in_dim.186.ids.refs_1_, f32[16,128]{1,0:T(8,128)S(1)} %broadcast_in_dim.187.present, f32[16,256]{1,0:T(8,128)S(1)} %copy-done.6, f32[4,256]{1,0:T(4,128)S(1)} %mul.11.mass, ...), custom_call_target="tpu_custom_call" | custom-call | tf_op jit(solution)/shard_map/pallas_call | solution.py:445
  56.0 1.4 %collective-permute-start.7 = (f32[24,256]{1,0:T(8,128)S(1)}, f32[24,256]{1,0:T(8,128)S(1)}, u32[]{:S(2)}, u32[]{:S(2)}) collective-permute-start(f32[24,256]{1,0:T(8,128)S(1)} %get-tuple-element.30.refs_7_), channel_id=1, source_target_pairs={{0,3},{1,2},{2,1},{3,0},{4,7},{5,6},{6,5},{7,4},{8,11},{9,10},{10,... | collective-permute-start | bytes 73736 | tf_op jit(solution)/shard_map/ppermute | solution.py:456
  57.5 2.3 %collective-permute-done.6.refs_9_ = f32[24,256]{1,0:T(8,128)S(1)} collective-permute-done((f32[24,256]{1,0:T(8,128)S(1)}, f32[24,256]{1,0:T(8,128)S(1)}, u32[]{:S(2)}, u32[]{:S(2)}) %collective-permute-start.6) | collective-permute-done | bytes 24608 | tf_op jit(solution)/shard_map/ppermute | solution.py:456
  59.9 2.8 %shard_map.70 = (f32[16,256]{1,0:T(8,128)S(1)}, f32[8,128]{1,0:T(8,128)S(1)}) custom-call(s32[5,40]{1,0:T(8,128)S(1)} %stack.21.scalars.refs_0_, s32[40,128]{1,0:T(8,128)S(1)} %broadcast_in_dim.184.refs_1_, f32[16,128]{1,0:T(8,128)S(1)} %broadcast_in_dim.185.refs_2_, bf16[8,256,256]{2,1,0:T(8,128)(2,1)S(1)} %get-tuple-element.26.sources.refs_3_, ...), custom_call_target="tpu_custom_call" | custom-call | tf_op jit(solution)/shard_map/pallas_call | solution.py:445
  62.7 3.3 %collective-permute-start.8 = (f32[16,256]{1,0:T(8,128)S(1)}, f32[16,256]{1,0:T(8,128)S(1)}, u32[]{:S(2)}, u32[]{:S(2)}) collective-permute-start(f32[16,256]{1,0:T(8,128)S(1)} %get-tuple-element.32.columns.refs_8_), channel_id=1, source_target_pairs={{0,4},{1,5},{2,6},{3,7},{4,0},{5,1},{6,2},{7,3},{8,12},{9,13},{10,... | collective-permute-start | bytes 49160 | tf_op jit(solution)/shard_map/ppermute | solution.py:456
  66.0 1.9 %collective-permute-done.8.partner.refs_9_ = f32[16,256]{1,0:T(8,128)S(1)} collective-permute-done((f32[16,256]{1,0:T(8,128)S(1)}, f32[16,256]{1,0:T(8,128)S(1)}, u32[]{:S(2)}, u32[]{:S(2)}) %collective-permute-start.8) | collective-permute-done | bytes 16416 | tf_op jit(solution)/shard_map/ppermute | solution.py:456
  68.5 1.7 %collective-permute-start.10 = (f32[4,256]{1,0:T(4,128)S(1)}, f32[4,256]{1,0:T(4,128)S(1)}, u32[]{:S(2)}, u32[]{:S(2)}) collective-permute-start(f32[4,256]{1,0:T(4,128)S(1)} %get-tuple-element.34), channel_id=1, source_target_pairs={{0,16},{8,24},{16,0},{24,8},{1,17},{9,25},{17,1},{25,9},{2,18},{10... | collective-permute-start | bytes 12296 | tf_op jit(solution)/shard_map/ppermute | solution.py:456
  70.1 1.4 %collective-permute-start.11 = (f32[4,256]{1,0:T(4,128)S(1)}, f32[4,256]{1,0:T(4,128)S(1)}, u32[]{:S(2)}, u32[]{:S(2)}) collective-permute-start(f32[4,256]{1,0:T(4,128)S(1)} %get-tuple-element.35), channel_id=1, source_target_pairs={{0,24},{8,16},{16,8},{24,0},{1,25},{9,17},{17,9},{25,1},{2,26},{10... | collective-permute-start | bytes 12296 | tf_op jit(solution)/shard_map/ppermute | solution.py:456
  72.1 2.5 %collective-permute-done.11.refs_12_ = f32[4,256]{1,0:T(4,128)S(1)} collective-permute-done((f32[4,256]{1,0:T(4,128)S(1)}, f32[4,256]{1,0:T(4,128)S(1)}, u32[]{:S(2)}, u32[]{:S(2)}) %collective-permute-start.11) | collective-permute-done | bytes 4128 | tf_op jit(solution)/shard_map/ppermute | solution.py:456
  75.2 14.4 %shard_map.72 = (f32[16,256]{1,0:T(8,128)S(1)}, f32[8,128]{1,0:T(8,128)S(1)}) custom-call(s32[5,40]{1,0:T(8,128)S(1)} %stack.21.scalars.refs_0_, s32[40,128]{1,0:T(8,128)S(1)} %broadcast_in_dim.186.ids.refs_1_, f32[16,128]{1,0:T(8,128)S(1)} %broadcast_in_dim.188.refs_2_, bf16[8,256,256]{2,1,0:T(8,128)(2,1)S(1)} %get-tuple-element.26.sources.refs_3_, ...), custom_call_target="tpu_custom_call" | custom-call | tf_op jit(solution)/shard_map/pallas_call | solution.py:445
  89.8 1.3 %collective-permute-start.13 = (f32[16,256]{1,0:T(8,128)S(1)}, f32[16,256]{1,0:T(8,128)S(1)}, u32[]{:S(2)}, u32[]{:S(2)}) collective-permute-start(f32[16,256]{1,0:T(8,128)S(1)} %get-tuple-element.36.refs_12_), channel_id=1, source_target_pairs={{0,2},{1,3},{2,0},{3,1},{4,6},{5,7},{6,4},{7,5},{8,10},{9,11},{10,... | collective-permute-start | bytes 49160 | tf_op jit(solution)/shard_map/ppermute | solution.py:456
  91.6 1.9 %collective-permute-done.13.refs_14_ = f32[16,256]{1,0:T(8,128)S(1)} collective-permute-done((f32[16,256]{1,0:T(8,128)S(1)}, f32[16,256]{1,0:T(8,128)S(1)}, u32[]{:S(2)}, u32[]{:S(2)}) %collective-permute-start.13) | collective-permute-done | bytes 16416 | tf_op jit(solution)/shard_map/ppermute | solution.py:456
  94.3 3.4 %shard_map.73 = (f32[16,256]{1,0:T(8,128)S(1)}, f32[8,128]{1,0:T(8,128)}) custom-call(s32[5,40]{1,0:T(8,128)S(1)} %stack.21.scalars.refs_0_, s32[40,128]{1,0:T(8,128)S(1)} %broadcast_in_dim.184.refs_1_, f32[16,128]{1,0:T(8,128)S(1)} %broadcast_in_dim.185.refs_2_, bf16[8,256,256]{2,1,0:T(8,128)(2,1)S(1)} %get-tuple-element.26.sources.refs_3_, ...), custom_call_target="tpu_custom_call" | custom-call | tf_op jit(solution)/shard_map/pallas_call | solution.py:445
  97.6 2.2 %collective-permute-start.15 = (f32[16,256]{1,0:T(8,128)S(1)}, f32[16,256]{1,0:T(8,128)S(1)}, u32[]{:S(2)}, u32[]{:S(2)}) collective-permute-start(f32[16,256]{1,0:T(8,128)S(1)} %get-tuple-element.39.columns), channel_id=1, source_target_pairs={{0,4},{1,5},{2,6},{3,7},{4,0},{5,1},{6,2},{7,3},{8,12},{9,13},{10,... | collective-permute-start | bytes 49160 | tf_op jit(solution)/shard_map/ppermute | solution.py:456
  99.9 0.9 collective-permute-start.16
  100.8 1.1 %collective-permute-start.17 = (f32[16,256]{1,0:T(8,128)S(1)}, f32[16,256]{1,0:T(8,128)S(1)}, u32[]{:S(2)}, u32[]{:S(2)}) collective-permute-start(f32[16,256]{1,0:T(8,128)S(1)} %get-tuple-element.39.columns), channel_id=1, source_target_pairs={{0,16},{8,24},{16,0},{24,8},{1,17},{9,25},{17,1},{25,9},{2,18},{10... | collective-permute-start | bytes 49160 | tf_op jit(solution)/shard_map/ppermute | solution.py:456
  101.9 1.5 %collective-permute-start.18 = (f32[16,256]{1,0:T(8,128)S(1)}, f32[16,256]{1,0:T(8,128)S(1)}, u32[]{:S(2)}, u32[]{:S(2)}) collective-permute-start(f32[16,256]{1,0:T(8,128)S(1)} %get-tuple-element.39.columns), channel_id=1, source_target_pairs={{0,24},{8,16},{16,8},{24,0},{1,25},{9,17},{17,9},{25,1},{2,26},{10... | collective-permute-start | bytes 49160 | tf_op jit(solution)/shard_map/ppermute | solution.py:456
  103.6 0.9 collective-permute-done.17.rest_1_
  104.5 2.0 %collective-permute-done.18.rest_2_ = f32[16,256]{1,0:T(8,128)S(1)} collective-permute-done((f32[16,256]{1,0:T(8,128)S(1)}, f32[16,256]{1,0:T(8,128)S(1)}, u32[]{:S(2)}, u32[]{:S(2)}) %collective-permute-start.18) | collective-permute-done | bytes 16416 | tf_op jit(solution)/shard_map/ppermute | solution.py:456
  106.5 1.2 %shard_map.74 = f32[8,128]{1,0:T(8,128)} custom-call(s32[5,40]{1,0:T(8,128)S(1)} %stack.21.scalars.refs_0_, f32[16,256]{1,0:T(8,128)S(1)} %get-tuple-element.39.columns, f32[16,256]{1,0:T(8,128)S(1)} %collective-permute-done.15.partner, f32[16,256]{1,0:T(8,128)S(1)} %collective-permute-done.16.rest_0_, f32[16,256]{1,0:T(8,128)S(1)} %collective-permute-done.17.rest_1_, ...), custom_call_target="tpu_custom_call" | custom-call | tf_op jit(solution)/shard_map/pallas_call | solution.py:445
  (97 shorter events, 16.4 us)
Async XLA Ops:
  0.6 14.9 %copy-start.1 = (bf16[1024,256]{1,0:T(8,128)(2,1)S(1)}, bf16[1024,256]{1,0:T(8,128)(2,1)}, u32[]{:S(2)}) copy-start(bf16[1024,256]{1,0:T(8,128)(2,1)} %param.5) | copy-start | bytes 1572868
  0.6 9.8 %collective-permute-start = (s32[4,8]{1,0:T(4,128)}, s32[4,8]{1,0:T(4,128)S(1)}, u32[]{:S(2)}, u32[]{:S(2)}) collective-permute-start(s32[4,8]{1,0:T(4,128)} %param.9), channel_id=1, source_target_pairs={{0,1},{1,0},{2,3},{3,2},{4,5},{5,4},{6,7},{7,6},{8,9},{9,8},{10,11... | collective-permute-start | bytes 392 | tf_op jit(solution)/shard_map/ppermute | solution.py:456
  1.2 43.6 %collective-permute-start.4 = (bf16[4,256,256]{2,1,0:T(8,128)(2,1)}, bf16[4,256,256]{2,1,0:T(8,128)(2,1)S(1)}, u32[]{:S(2)}, u32[]{:S(2)}) collective-permute-start(bf16[4,256,256]{2,1,0:T(8,128)(2,1)} %bitcast.38), channel_id=1, source_target_pairs={{0,4},{1,5},{2,6},{3,7},{4,0},{5,1},{6,2},{7,3},{8,12},{9,13},{10,... | collective-permute-start | bytes 1572872 | tf_op jit(solution)/shard_map/ppermute | solution.py:456
  11.5 13.3 %copy-start = (bf16[1024,256]{1,0:T(8,128)(2,1)S(1)}, bf16[1024,256]{1,0:T(8,128)(2,1)}, u32[]{:S(2)}) copy-start(bf16[1024,256]{1,0:T(8,128)(2,1)} %param.6) | copy-start | bytes 1572868
  11.5 12.5 %collective-permute-start.2 = (bf16[4,256,256]{2,1,0:T(8,128)(2,1)}, bf16[4,256,256]{2,1,0:T(8,128)(2,1)S(1)}, u32[]{:S(2)}, u32[]{:S(2)}) collective-permute-start(bf16[4,256,256]{2,1,0:T(8,128)(2,1)} %bitcast.41), channel_id=1, source_target_pairs={{0,1},{1,0},{2,3},{3,2},{4,5},{5,4},{6,7},{7,6},{8,9},{9,8},{10,11... | collective-permute-start | bytes 1572872 | tf_op jit(solution)/shard_map/ppermute | solution.py:456
  11.7 12.3 %all-to-all-start = ((bf16[4,256,256]{2,1,0:T(8,128)(2,1)}), bf16[4,256,256]{2,1,0:T(8,128)(2,1)S(1)}, u32[]{:S(2)}, u32[]{:S(2)}) async-start(bf16[4,256,256]{2,1,0:T(8,128)(2,1)} %bitcast.39), calls=%async_computation | async-start | bytes 1048576 | tf_op jit(solution)/shard_map/all_to_all | solution.py:537
  16.4 23.9 %collective-permute-start.1 = (bf16[1040,256]{1,0:T(8,128)(2,1)}, bf16[1040,256]{1,0:T(8,128)(2,1)}, u32[]{:S(2)}, u32[]{:S(2)}) collective-permute-start(bf16[1040,256]{1,0:T(8,128)(2,1)} %fusion.1), channel_id=1, source_target_pairs={{0,2},{1,3},{2,0},{3,1},{4,6},{5,7},{6,4},{7,5},{8,10},{9,11},{10,... | collective-permute-start | bytes 1597448 | tf_op jit(solution)/shard_map/ppermute | solution.py:456
  24.0 0.8 copy-start.3
  24.8 1.0 copy-start.2
  25.9 1.0 copy-start.4
  28.8 0.6 copy-start.5
  40.3 4.5 %collective-permute-start.3 = (bf16[1040,256]{1,0:T(8,128)(2,1)}, bf16[1040,256]{1,0:T(8,128)(2,1)S(1)}, u32[]{:S(2)}, u32[]{:S(2)}) collective-permute-start(bf16[1040,256]{1,0:T(8,128)(2,1)} %collective-permute-done.1.near), channel_id=1, source_target_pairs={{0,1},{1,0},{2,3},{3,2},{4,5},{5,4},{6,7},{7,6},{8,9},{9,8},{10,11... | collective-permute-start | bytes 1597448 | tf_op jit(solution)/shard_map/ppermute | solution.py:456
  45.0 0.7 copy-start.6
  55.4 2.1 %collective-permute-start.5 = (f32[24,256]{1,0:T(8,128)S(1)}, f32[24,256]{1,0:T(8,128)S(1)}, u32[]{:S(2)}, u32[]{:S(2)}) collective-permute-start(f32[24,256]{1,0:T(8,128)S(1)} %get-tuple-element.30.refs_7_), channel_id=1, source_target_pairs={{0,1},{1,0},{2,3},{3,2},{4,5},{5,4},{6,7},{7,6},{8,9},{9,8},{10,11... | collective-permute-start | bytes 73736 | tf_op jit(solution)/shard_map/ppermute | solution.py:456
  55.9 3.8 %collective-permute-start.6 = (f32[24,256]{1,0:T(8,128)S(1)}, f32[24,256]{1,0:T(8,128)S(1)}, u32[]{:S(2)}, u32[]{:S(2)}) collective-permute-start(f32[24,256]{1,0:T(8,128)S(1)} %get-tuple-element.30.refs_7_), channel_id=1, source_target_pairs={{0,2},{1,3},{2,0},{3,1},{4,6},{5,7},{6,4},{7,5},{8,10},{9,11},{10,... | collective-permute-start | bytes 73736 | tf_op jit(solution)/shard_map/ppermute | solution.py:456
  56.0 3.8 %collective-permute-start.7 = (f32[24,256]{1,0:T(8,128)S(1)}, f32[24,256]{1,0:T(8,128)S(1)}, u32[]{:S(2)}, u32[]{:S(2)}) collective-permute-start(f32[24,256]{1,0:T(8,128)S(1)} %get-tuple-element.30.refs_7_), channel_id=1, source_target_pairs={{0,3},{1,2},{2,1},{3,0},{4,7},{5,6},{6,5},{7,4},{8,11},{9,10},{10,... | collective-permute-start | bytes 73736 | tf_op jit(solution)/shard_map/ppermute | solution.py:456
  62.7 5.1 %collective-permute-start.8 = (f32[16,256]{1,0:T(8,128)S(1)}, f32[16,256]{1,0:T(8,128)S(1)}, u32[]{:S(2)}, u32[]{:S(2)}) collective-permute-start(f32[16,256]{1,0:T(8,128)S(1)} %get-tuple-element.32.columns.refs_8_), channel_id=1, source_target_pairs={{0,4},{1,5},{2,6},{3,7},{4,0},{5,1},{6,2},{7,3},{8,12},{9,13},{10,... | collective-permute-start | bytes 49160 | tf_op jit(solution)/shard_map/ppermute | solution.py:456
  68.5 3.7 %collective-permute-start.10 = (f32[4,256]{1,0:T(4,128)S(1)}, f32[4,256]{1,0:T(4,128)S(1)}, u32[]{:S(2)}, u32[]{:S(2)}) collective-permute-start(f32[4,256]{1,0:T(4,128)S(1)} %get-tuple-element.34), channel_id=1, source_target_pairs={{0,16},{8,24},{16,0},{24,8},{1,17},{9,25},{17,1},{25,9},{2,18},{10... | collective-permute-start | bytes 12296 | tf_op jit(solution)/shard_map/ppermute | solution.py:456
  70.1 4.5 %collective-permute-start.11 = (f32[4,256]{1,0:T(4,128)S(1)}, f32[4,256]{1,0:T(4,128)S(1)}, u32[]{:S(2)}, u32[]{:S(2)}) collective-permute-start(f32[4,256]{1,0:T(4,128)S(1)} %get-tuple-element.35), channel_id=1, source_target_pairs={{0,24},{8,16},{16,8},{24,0},{1,25},{9,17},{17,9},{25,1},{2,26},{10... | collective-permute-start | bytes 12296 | tf_op jit(solution)/shard_map/ppermute | solution.py:456
  71.6 3.6 %collective-permute-start.9 = (f32[4,256]{1,0:T(4,128)S(1)}, f32[4,256]{1,0:T(4,128)S(1)}, u32[]{:S(2)}, u32[]{:S(2)}) collective-permute-start(f32[4,256]{1,0:T(4,128)S(1)} %get-tuple-element.33), channel_id=1, source_target_pairs={{0,8},{8,0},{16,24},{24,16},{1,9},{9,1},{17,25},{25,17},{2,10},{10... | collective-permute-start | bytes 12296 | tf_op jit(solution)/shard_map/ppermute | solution.py:456
  89.7 1.9 %collective-permute-start.12 = (f32[16,256]{1,0:T(8,128)S(1)}, f32[16,256]{1,0:T(8,128)S(1)}, u32[]{:S(2)}, u32[]{:S(2)}) collective-permute-start(f32[16,256]{1,0:T(8,128)S(1)} %get-tuple-element.36.refs_12_), channel_id=1, source_target_pairs={{0,1},{1,0},{2,3},{3,2},{4,5},{5,4},{6,7},{7,6},{8,9},{9,8},{10,11... | collective-permute-start | bytes 49160 | tf_op jit(solution)/shard_map/ppermute | solution.py:456
  89.8 3.8 %collective-permute-start.13 = (f32[16,256]{1,0:T(8,128)S(1)}, f32[16,256]{1,0:T(8,128)S(1)}, u32[]{:S(2)}, u32[]{:S(2)}) collective-permute-start(f32[16,256]{1,0:T(8,128)S(1)} %get-tuple-element.36.refs_12_), channel_id=1, source_target_pairs={{0,2},{1,3},{2,0},{3,1},{4,6},{5,7},{6,4},{7,5},{8,10},{9,11},{10,... | collective-permute-start | bytes 49160 | tf_op jit(solution)/shard_map/ppermute | solution.py:456
  91.1 3.2 %collective-permute-start.14 = (f32[16,256]{1,0:T(8,128)S(1)}, f32[16,256]{1,0:T(8,128)S(1)}, u32[]{:S(2)}, u32[]{:S(2)}) collective-permute-start(f32[16,256]{1,0:T(8,128)S(1)} %get-tuple-element.36.refs_12_), channel_id=1, source_target_pairs={{0,3},{1,2},{2,1},{3,0},{4,7},{5,6},{6,5},{7,4},{8,11},{9,10},{10,... | collective-permute-start | bytes 49160 | tf_op jit(solution)/shard_map/ppermute | solution.py:456
  97.6 5.7 %collective-permute-start.15 = (f32[16,256]{1,0:T(8,128)S(1)}, f32[16,256]{1,0:T(8,128)S(1)}, u32[]{:S(2)}, u32[]{:S(2)}) collective-permute-start(f32[16,256]{1,0:T(8,128)S(1)} %get-tuple-element.39.columns), channel_id=1, source_target_pairs={{0,4},{1,5},{2,6},{3,7},{4,0},{5,1},{6,2},{7,3},{8,12},{9,13},{10,... | collective-permute-start | bytes 49160 | tf_op jit(solution)/shard_map/ppermute | solution.py:456
  99.9 3.7 %collective-permute-start.16 = (f32[16,256]{1,0:T(8,128)S(1)}, f32[16,256]{1,0:T(8,128)S(1)}, u32[]{:S(2)}, u32[]{:S(2)}) collective-permute-start(f32[16,256]{1,0:T(8,128)S(1)} %get-tuple-element.39.columns), channel_id=1, source_target_pairs={{0,8},{8,0},{16,24},{24,16},{1,9},{9,1},{17,25},{25,17},{2,10},{10... | collective-permute-start | bytes 49160 | tf_op jit(solution)/shard_map/ppermute | solution.py:456
  100.8 3.7 %collective-permute-start.17 = (f32[16,256]{1,0:T(8,128)S(1)}, f32[16,256]{1,0:T(8,128)S(1)}, u32[]{:S(2)}, u32[]{:S(2)}) collective-permute-start(f32[16,256]{1,0:T(8,128)S(1)} %get-tuple-element.39.columns), channel_id=1, source_target_pairs={{0,16},{8,24},{16,0},{24,8},{1,17},{9,25},{17,1},{25,9},{2,18},{10... | collective-permute-start | bytes 49160 | tf_op jit(solution)/shard_map/ppermute | solution.py:456
  101.9 4.6 %collective-permute-start.18 = (f32[16,256]{1,0:T(8,128)S(1)}, f32[16,256]{1,0:T(8,128)S(1)}, u32[]{:S(2)}, u32[]{:S(2)}) collective-permute-start(f32[16,256]{1,0:T(8,128)S(1)} %get-tuple-element.39.columns), channel_id=1, source_target_pairs={{0,24},{8,16},{16,8},{24,0},{1,25},{9,17},{17,9},{25,1},{2,26},{10... | collective-permute-start | bytes 49160 | tf_op jit(solution)/shard_map/ppermute | solution.py:456

commit v5 on v4

--- a/solution.py
+++ b/solution.py
@@ -242,7 +242,7 @@
     return (target, source) if by_rows else (source, target)
 
 
-def exact_pass(scalars, ids, by_rows, sections, sources, targets, bias, tops, sums, unrolled):
+def exact_pass(scalars, by_rows, sections, sources, targets, bias, tops, sums, ids, unrolled):
     for section in sections:
         first, count = SECTIONS[section]
         (summed, summed_row, summed_base), (kept, kept_row, _) = sides(section, by_rows, sources, targets)
@@ -255,6 +255,7 @@
             top = jnp.max(logits, axis=0, keepdims=True)
             tops[pl.ds(slot, 1), :] = top
             sums[pl.ds(slot, 1), :] = jnp.sum(jnp.exp2(logits - top), axis=0, keepdims=True)
+            ids[pl.ds(slot, 1), :] = jnp.full((1, ids.shape[1]), scalars[2 + kept_row, slot], jnp.int32)
             return carry
 
         if unrolled:
@@ -264,7 +265,7 @@
             lax.fori_loop(first, first + count, visit, 0)
     first, last = SECTIONS[sections[0]][0], sum(SECTIONS[sections[-1]])
     low, high = first // 8 * 8, (last + 7) // 8 * 8
-    id_rows = wide(ids[low:high])
+    id_rows = ids[low:high]
     if low < first or last < high:
         slot = low + lax.broadcasted_iota(jnp.int32, id_rows.shape, 0)
         id_rows = jnp.where(jnp.logical_and(slot >= first, slot < last), id_rows, -1)
@@ -282,8 +283,9 @@
     return jnp.where(total > 0, best + LOG2E * jnp.log(jnp.where(total > 0, total, 1.0)), very_low)
 
 
-def fast_pass(scalars, ids, present, by_rows, sections, sources, targets, bias, shift, total, tops, sums):
+def fast_pass(scalars, by_rows, sections, sources, targets, bias, shift, total, present):
     total[...] = jnp.zeros(total.shape, jnp.float32)
+    present[...] = jnp.zeros(present.shape, jnp.float32)
     for section in sections:
         first, count = SECTIONS[section]
         (summed, summed_row, summed_base), (kept, kept_row, _) = sides(section, by_rows, sources, targets)
@@ -293,12 +295,13 @@
             logits = logits + (shift if bias is None else wide(bias[summed_base + block]))
             terms = jnp.exp2(logits)
             place = scalars[2 + kept_row, slot]
+            present[pl.ds(place, 1), :] = jnp.ones((1, present.shape[1]), jnp.float32)
             total[place] = total[place] + jnp.sum(terms.reshape(-1, 8, terms.shape[1]), axis=0)
     count = SOURCE_SLOTS if by_rows else TARGET_SLOTS
     sums_of = jnp.concatenate(
         [jnp.sum(total[block], axis=0, keepdims=True) for block in range(count)], axis=0
     )
-    here = wide(present[0:count]) > 0
+    here = present[0:count] > 0
     result = LOG2E * jnp.log(jnp.where(here, sums_of, 1.0))
     if shift is not None:
         result = result - shift
@@ -307,13 +310,13 @@
     return jnp.where(here, result, very_low), worst > 0.5
 
 
-def guarded_pass(scalars, ids, present, by_rows, sections, sources, targets, rows, shift, work, write):
-    total, tops, sums, *bias = work
+def guarded_pass(scalars, by_rows, sections, sources, targets, rows, shift, work, write):
+    total, present, tops, sums, ids, *bias = work
     bias = bias[0] if bias else None
     if bias is not None:
         spread(rows if shift is None else rows + shift, bias)
     result, fine = fast_pass(
-        scalars, ids, present, by_rows, sections, sources, targets, bias, shift, total, tops, sums
+        scalars, by_rows, sections, sources, targets, bias, shift, total, present
     )
     write(result)
 
@@ -321,7 +324,7 @@
     def _():
         if shift is not None and bias is not None:
             spread(rows, bias)
-        write(exact_pass(scalars, ids, by_rows, sections, sources, targets, bias, tops, sums, False))
+        write(exact_pass(scalars, by_rows, sections, sources, targets, bias, tops, sums, ids, False))
 
 
 def middle(pieces):
@@ -330,22 +333,22 @@
     return 0.5 * (top + bottom)
 
 
-def early_kernel(scalars, ids, own, core, target, mirrors, out, sources, targets, tops, sums):
+def early_kernel(scalars, own, core, target, mirrors, out, sources, targets, tops, sums, ids):
     sources[0:4] = own[...]
     sources[4:8] = core[...]
     targets[0:4] = target[...]
     for offset in (1, 2, 3):
         targets[3 + offset] = mirrors[scalars[4, 0] ^ offset]
     out[...] = exact_pass(
-        scalars, ids, True, (0,), (sources, None), (targets, None), None, tops, sums, True
+        scalars, True, (0,), (sources, None), (targets, None), None, tops, sums, ids, True
     )
 
 
 def first_kernel(
-    scalars, ids, present, early, mass, sources, near, cross, targets, far, out, late_sources, *work
+    scalars, early, mass, sources, near, cross, targets, far, out, late_sources, *work
 ):
-    late_sources[0:4] = near[0 : mass.shape[1] * 4].reshape(late_sources[0:4].shape)
-    late_sources[4:8] = cross[0 : mass.shape[1] * 4].reshape(late_sources[4:8].shape)
+    late_sources[0:4] = near[...]
+    late_sources[4:8] = cross[...]
     out[16:20, :] = mass[...]
     out[20:24, :] = jnp.zeros((4, out.shape[1]), jnp.float32)
     begun = early[...]
@@ -356,8 +359,6 @@
 
     guarded_pass(
         scalars,
-        ids,
-        present,
         True,
         (1, 2, 3),
         (sources, late_sources),
@@ -370,9 +371,8 @@
 
 
 def columns_kernel(last_pass, *refs):
-    scalars, ids, present = refs[:3]
-    sources, targets = refs[3:5], refs[5:7]
-    masses, target_mass, rest = refs[7:11], refs[11], refs[12:]
+    scalars, sources, targets = refs[0], refs[1:3], refs[3:5]
+    masses, target_mass, rest = refs[5:9], refs[9], refs[10:]
     parts, shift = masses, None
     if last_pass:
         parts, (shift, *rest) = rest[:4], rest[4:]
@@ -392,16 +392,13 @@
     def write(result):
         out[0:TARGET_SLOTS, :] = result
 
-    guarded_pass(
-        scalars, ids, present, False, (0, 1, 2, 3), sources, targets, rows, shift, work, write
-    )
+    guarded_pass(scalars, False, (0, 1, 2, 3), sources, targets, rows, shift, work, write)
 
 
 def rows_kernel(*refs):
-    scalars, ids, present = refs[:3]
-    sources, targets = refs[3:5], refs[5:7]
-    shift, columns, partner, *mirrors = refs[7:13]
-    out, second, *work, scratch = refs[13:]
+    scalars, sources, targets = refs[0], refs[1:3], refs[3:5]
+    shift, columns, partner, *mirrors = refs[5:11]
+    out, second, *work, scratch = refs[11:]
     rows = target_bias(scalars, columns, partner, mirrors, scratch)
     second[...] = jnp.broadcast_to(middle([rows[0:7], rows[8:12]]), second.shape)
 
@@ -409,7 +406,7 @@
         out[...] = result
 
     guarded_pass(
-        scalars, ids, present, True, (0, 1, 2, 3), sources, targets, rows, shift[0:1, 0:1], work, write
+        scalars, True, (0, 1, 2, 3), sources, targets, rows, shift[0:1, 0:1], work, write
     )
 
 
@@ -493,24 +490,15 @@
     sources = jnp.sum(jnp.where(hits, source, 0), axis=1)
     targets = jnp.sum(jnp.where(hits, target, 0), axis=1)
     late_slot = jnp.logical_or(jnp.logical_and(slots >= 12, slots < 20), slots >= 28)
-    source_ids = jnp.where(used, sources, -1)
-    target_ids = jnp.where(used, jnp.where(slots >= 20, FAR + targets, targets), -1)
-    scalars = jnp.stack(
+    return jnp.stack(
         [
             jnp.where(jnp.logical_and(late_slot, used), sources - 8, sources),
             targets,
-            jnp.where(used, source_ids, SOURCE_SLOTS),
-            jnp.where(used, target_ids, TARGET_SLOTS),
+            jnp.where(used, sources, SOURCE_SLOTS),
+            jnp.where(used, jnp.where(slots >= 20, FAR + targets, targets), TARGET_SLOTS),
             jnp.broadcast_to(own_group, slots.shape).astype(jnp.int32),
         ]
     )
-    lists = []
-    for ids in (source_ids, target_ids):
-        lists.append(jnp.broadcast_to(ids[:, None], (slot_count, 128)))
-        for counted in (ids, jnp.where(slots >= 12, ids, -1)):
-            rows = jnp.any(counted[None, :] == jnp.arange(16)[:, None], axis=1).astype(jnp.float32)
-            lists.append(jnp.broadcast_to(rows[:, None], (16, 128)))
-    return scalars, *lists
 
 
 def shards_quad(source_vectors, target_vectors, source_mass, target_mass, candidates):
@@ -529,46 +517,40 @@
     target_own = target_vectors.reshape(blocked)
     target_far = member_swap(target_own, 4)
     named = jnp.concatenate([candidates, member_swap(candidates, 1)])
-    note = jnp.pad(
-        named.astype(source_vectors.dtype).reshape(1, named.size), ((0, 15), (0, width - named.size))
-    )
-    source_near = member_swap(jnp.concatenate([source_vectors, note]), 2)
+    source_near = member_swap(source_own, 2)
+    theirs = member_swap(named, 2)
     source_late, target_late, named = lax.optimization_barrier((source_own, target_own, named))
     mirrors = lax.all_to_all(target_late, "group", split_axis=0, concat_axis=0, tiled=True)
     source_core = member_swap(source_late, 1)
     place = (own_group, own_member, members, per_device)
-    early_scalars, early_by_source, *_ = tile_lists(named, *place, 16)
+    early_scalars = tile_lists(named, *place, 16)
     own_source_mass = LOG2E * source_mass.reshape(per_device, block_rows)
     own_mass = LOG2E * target_mass.reshape(per_device, block_rows)
 
     side = jax.ShapeDtypeStruct((16, block_rows), jnp.float32)
     flat = jax.ShapeDtypeStruct((8, 128), jnp.float32)
     stacked = lambda count: jax.ShapeDtypeStruct((count, block_rows, width), source_vectors.dtype)
-    tile_rows = [VMEM((TILE_SLOTS, block_rows), jnp.float32)] * 2
+    tile_rows = [VMEM((TILE_SLOTS, block_rows), kind) for kind in (jnp.float32, jnp.float32, jnp.int32)]
     pass_buffers = [
         VMEM((SOURCE_SLOTS + 1, 8, block_rows), jnp.float32),
+        VMEM((24, block_rows), jnp.float32),
         *tile_rows,
         VMEM((SOURCE_SLOTS, block_rows, 128), jnp.float32),
     ]
 
     early, sources, targets = call(
         early_kernel,
-        [early_scalars, early_by_source, source_own, source_core, target_own, mirrors],
+        [early_scalars, source_own, source_core, target_own, mirrors],
         [side, stacked(8), stacked(7)],
         tile_rows,
     )
-    source_near, early = lax.optimization_barrier((source_near, early))
+    source_near, theirs, early = lax.optimization_barrier((source_near, theirs, early))
     source_cross = member_swap(source_near, 1)
-    theirs = source_near[per_device * block_rows, : named.size].astype(jnp.int32).reshape(named.shape)
-    scalars, by_source, has_source, has_late_source, by_target, has_target, _ = tile_lists(
-        jnp.concatenate([named, theirs]), *place, TILE_SLOTS
-    )
+    scalars = tile_lists(jnp.concatenate([named, theirs]), *place, TILE_SLOTS)
     parts, late_sources = call(
         first_kernel,
         [
             scalars,
-            by_source,
-            has_late_source,
             early,
             own_source_mass,
             sources,
@@ -578,7 +560,7 @@
             target_far,
         ],
         [jax.ShapeDtypeStruct((24, block_rows), jnp.float32), stacked(8)],
-        pass_buffers[:3],
+        pass_buffers[:5],
     )
     blocks = [sources, late_sources, targets, target_far]
     masses, extra = [], []
@@ -588,7 +570,7 @@
         masses = masses or parts
         columns, potential = call(
             functools.partial(columns_kernel, last_pass),
-            [scalars, by_target, has_target, *blocks, *masses, own_mass, *(parts + extra if last_pass else [])],
+            [scalars, *blocks, *masses, own_mass, *(parts + extra if last_pass else [])],
             [side, flat],
             pass_buffers,
         )
@@ -603,7 +585,7 @@
         received = [group_swap(values, bit) for bit, values in enumerate(sent, 1)]
         parts, shift = call(
             rows_kernel,
-            [scalars, by_source, has_source, *blocks, potential, columns, partner, *received],
+            [scalars, *blocks, potential, columns, partner, *received],
             [side, flat],
             [*pass_buffers, VMEM((8, block_rows), jnp.float32)],
         )

time: 108 us -> 99 us (0.917)
  waiting for transfers between devices: 29.6 us -> 23.6 us
  other arithmetic: 7.86 us -> 1.92 us
  local copies, waits for them, and re-layouts: 9.24 us -> 13.2 us
  starting transfers between devices: 26.2 us -> 23.6 us
    ppermute x19 -> x20, waiting for transfers between devices: 23.8 us -> 15.2 us  [swap(): lax.ppermute(values, axis, [(index, index ^ bit) for index in range(size)])]
    unnamed x14 -> x32, local copies, waits for them, and re-layouts: 4.21 us -> 9.24 us
    ppermute x19 -> x20, starting transfers between devices: 22.5 us -> 19.7 us  [swap(): lax.ppermute(values, axis, [(index, index ^ bit) for index in range(size)])]
    all_to_all x1, waiting for transfers between devices: 5.74 us -> 8.4 us  [shards_quad(): lax.all_to_all(target_late, 'group', split_axis=0, concat_axis=0, tiled=T...]
  transfers between devices with their start and end apart: 20 -> 21, of which waited for: 11 -> 11; matrix products, arithmetic and copies ran while one was open for 12% -> 6% of each run, Pallas kernels for 2% -> 2%
where the time goes in v5:
time: 99 us; the launch traced here: 98.4 us
  Pallas kernels  35.1 us (35%)
  starting transfers between devices  23.6 us (24%)
  waiting for transfers between devices  23.6 us (24%)
  local copies, waits for them, and re-layouts  13.2 us (13%)
  other arithmetic  1.92 us (2%)
    pallas_call x7, Pallas kernels, call(): pl.pallas_call(kernel, out_shape=outs, in_specs=[pl.BlockSpec(memory_spac...  35.1 us
    ppermute x20, starting transfers between devices, swap(): lax.ppermute(values, axis, [(index, index ^ bit) for index in range(size)])  19.7 us
    ppermute x20, waiting for transfers between devices, swap(): lax.ppermute(values, axis, [(index, index ^ bit) for index in range(size)])  15.2 us
    unnamed x32, local copies, waits for them, and re-layouts  9.24 us
    all_to_all x1, waiting for transfers between devices, shards_quad(): lax.all_to_all(target_late, 'group', split_axis=0, concat_axis=0, tiled=T...  8.4 us
    all_to_all x1, starting transfers between devices, shards_quad(): lax.all_to_all(target_late, 'group', split_axis=0, concat_axis=0, tiled=T...  3.85 us
    broadcast_in_dim x8, local copies, waits for them, and re-layouts, tile_lists(): jnp.broadcast_to(jnp.arange(candidates.shape[0], dtype=jnp.int32)[:, None...  2.15 us
  transfers between devices with their start and end apart: 21, of which 11 were waited for; matrix products, arithmetic and copies ran while one was open for 6% of the time, Pallas kernels for 2%

profile of v5, /device:TPU:0, one launch (start us, length us, event | category | flops | bytes accessed | tf_op | source)
XLA Modules:
  0.0 98.4 jit_solution(7392462723033326168)
XLA Ops:
  1.1 2.7 %collective-permute-start.1 = (bf16[4,256,256]{2,1,0:T(8,128)(2,1)}, bf16[4,256,256]{2,1,0:T(8,128)(2,1)}, u32[]{:S(2)}, u32[]{:S(2)}) collective-permute-start(bf16[4,256,256]{2,1,0:T(8,128)(2,1)} %bitcast.29), channel_id=1, source_target_pairs={{0,2},{1,3},{2,0},{3,1},{4,6},{5,7},{6,4},{7,5},{8,10},{9,11},{10,... | collective-permute-start | bytes 1572872 | tf_op jit(solution)/shard_map/ppermute | solution.py:453
  3.8 2.6 %collective-permute-start.5 = (bf16[4,256,256]{2,1,0:T(8,128)(2,1)}, bf16[4,256,256]{2,1,0:T(8,128)(2,1)S(1)}, u32[]{:S(2)}, u32[]{:S(2)}) collective-permute-start(bf16[4,256,256]{2,1,0:T(8,128)(2,1)} %bitcast.26), channel_id=1, source_target_pairs={{0,4},{1,5},{2,6},{3,7},{4,0},{5,1},{6,2},{7,3},{8,12},{9,13},{10,... | collective-permute-start | bytes 1572872 | tf_op jit(solution)/shard_map/ppermute | solution.py:453
  8.0 0.7 broadcast_in_dim.117
  11.7 3.9 %all-to-all-start = ((bf16[4,256,256]{2,1,0:T(8,128)(2,1)}), bf16[4,256,256]{2,1,0:T(8,128)(2,1)S(1)}, u32[]{:S(2)}, u32[]{:S(2)}) async-start(bf16[4,256,256]{2,1,0:T(8,128)(2,1)} %bitcast.27), calls=%async_computation | async-start | bytes 1048576 | tf_op jit(solution)/shard_map/all_to_all | solution.py:523
  15.8 8.4 %all-to-all-done.mirrors = bf16[4,256,256]{2,1,0:T(8,128)(2,1)S(1)} async-done(((bf16[4,256,256]{2,1,0:T(8,128)(2,1)}), bf16[4,256,256]{2,1,0:T(8,128)(2,1)S(1)}, u32[]{:S(2)}, u32[]{:S(2)}) %all-to-all-start) | async-done | bytes 524320 | tf_op jit(solution)/shard_map/all_to_all | solution.py:523
  24.2 0.8 copy-done.4
  25.0 1.0 %copy-done.3 = bf16[1024,256]{1,0:T(8,128)(2,1)S(1)} copy-done((bf16[1024,256]{1,0:T(8,128)(2,1)S(1)}, bf16[1024,256]{1,0:T(8,128)(2,1)}, u32[]{:S(2)}) %copy-start.3) | copy-done | bytes 524312
  26.1 1.0 %copy-done.5 = bf16[4,256,256]{2,1,0:T(8,128)(2,1)S(1)} copy-done((bf16[4,256,256]{2,1,0:T(8,128)(2,1)S(1)}, bf16[4,256,256]{2,1,0:T(8,128)(2,1)}, u32[]{:S(2)}) %copy-start.5) | copy-done | bytes 524312
  27.1 1.9 %shard_map.68 = (f32[16,256]{1,0:T(8,128)S(1)}, bf16[8,256,256]{2,1,0:T(8,128)(2,1)S(1)}, bf16[7,256,256]{2,1,0:T(8,128)(2,1)S(1)}) custom-call(s32[5,16]{1,0:T(8,128)S(1)} %stack.9.scalars, bf16[4,256,256]{2,1,0:T(8,128)(2,1)S(1)} %bitcast.31, bf16[4,256,256]{2,1,0:T(8,128)(2,1)S(1)} %copy-done.5, bf16[4,256,256]{2,1,0:T(8,128)(2,1)S(1)} %bitcast.28, ...), custom_call_target="tpu_custom_call" | custom-call | tf_op jit(solution)/shard_map/pallas_call | solution.py:442
  29.6 0.7 pad_add_fusion
  32.9 0.7 copy-done.12
  33.8 0.8 copy-done.1
  34.6 1.0 %copy-done.2 = bf16[4,256,256]{2,1,0:T(8,128)(2,1)S(1)} copy-done((bf16[4,256,256]{2,1,0:T(8,128)(2,1)S(1)}, bf16[4,256,256]{2,1,0:T(8,128)(2,1)}, u32[]{:S(2)}) %copy-start.2) | copy-done | bytes 524312
  35.6 0.7 copy-done.7
  36.3 10.4 %shard_map.69 = (f32[24,256]{1,0:T(8,128)}, bf16[8,256,256]{2,1,0:T(8,128)(2,1)S(1)}) custom-call(s32[5,40]{1,0:T(8,128)S(1)} %stack.21.scalars.refs_0_, f32[16,256]{1,0:T(8,128)S(1)} %copy-done.7, f32[4,256]{1,0:T(4,128)S(1)} %mul.11.mass, bf16[8,256,256]{2,1,0:T(8,128)(2,1)S(1)} %get-tuple-element.27.sources.refs_1_, ...), custom_call_target="tpu_custom_call" | custom-call | tf_op jit(solution)/shard_map/pallas_call | solution.py:442
  47.2 1.6 %collective-permute-start.7 = (f32[24,256]{1,0:T(8,128)}, f32[24,256]{1,0:T(8,128)}, u32[]{:S(2)}, u32[]{:S(2)}) collective-permute-start(f32[24,256]{1,0:T(8,128)} %get-tuple-element.32.refs_5_), channel_id=1, source_target_pairs={{0,2},{1,3},{2,0},{3,1},{4,6},{5,7},{6,4},{7,5},{8,10},{9,11},{10,... | collective-permute-start | bytes 73736 | tf_op jit(solution)/shard_map/ppermute | solution.py:453
  48.8 2.5 %collective-permute-done.7.refs_7_ = f32[24,256]{1,0:T(8,128)} collective-permute-done((f32[24,256]{1,0:T(8,128)}, f32[24,256]{1,0:T(8,128)}, u32[]{:S(2)}, u32[]{:S(2)}) %collective-permute-start.7) | collective-permute-done | bytes 24608 | tf_op jit(solution)/shard_map/ppermute | solution.py:453
  51.3 1.2 %collective-permute-done.8.refs_8_ = f32[24,256]{1,0:T(8,128)} collective-permute-done((f32[24,256]{1,0:T(8,128)}, f32[24,256]{1,0:T(8,128)}, u32[]{:S(2)}, u32[]{:S(2)}) %collective-permute-start.8) | collective-permute-done | bytes 24608 | tf_op jit(solution)/shard_map/ppermute | solution.py:453
  52.5 3.0 %shard_map.70 = (f32[16,256]{1,0:T(8,128)S(1)}, f32[8,128]{1,0:T(8,128)S(1)}) custom-call(s32[5,40]{1,0:T(8,128)S(1)} %stack.21.scalars.refs_0_, bf16[8,256,256]{2,1,0:T(8,128)(2,1)S(1)} %get-tuple-element.27.sources.refs_1_, bf16[8,256,256]{2,1,0:T(8,128)(2,1)S(1)} %get-tuple-element.31.refs_2_, bf16[7,256,256]{2,1,0:T(8,128)(2,1)S(1)} %get-tuple-element.30.targets.refs_3_, ...), custom_call_target="tpu_custom_call" | custom-call | tf_op jit(solution)/shard_map/pallas_call | solution.py:442
  56.0 4.4 %collective-permute-done.9.partner.refs_7_ = f32[16,256]{1,0:T(8,128)S(1)} collective-permute-done((f32[16,256]{1,0:T(8,128)S(1)}, f32[16,256]{1,0:T(8,128)S(1)}, u32[]{:S(2)}, u32[]{:S(2)}) %collective-permute-start.9) | collective-permute-done | bytes 16416 | tf_op jit(solution)/shard_map/ppermute | solution.py:453
  61.0 1.5 %collective-permute-start.10 = (f32[4,256]{1,0:T(4,128)S(1)}, f32[4,256]{1,0:T(4,128)S(1)}, u32[]{:S(2)}, u32[]{:S(2)}) collective-permute-start(f32[4,256]{1,0:T(4,128)S(1)} %get-tuple-element.35), channel_id=1, source_target_pairs={{0,8},{8,0},{16,24},{24,16},{1,9},{9,1},{17,25},{25,17},{2,10},{10... | collective-permute-start | bytes 12296 | tf_op jit(solution)/shard_map/ppermute | solution.py:453
  63.0 1.5 %collective-permute-start.12 = (f32[4,256]{1,0:T(4,128)S(1)}, f32[4,256]{1,0:T(4,128)S(1)}, u32[]{:S(2)}, u32[]{:S(2)}) collective-permute-start(f32[4,256]{1,0:T(4,128)S(1)} %get-tuple-element.37), channel_id=1, source_target_pairs={{0,24},{8,16},{16,8},{24,0},{1,25},{9,17},{17,9},{25,1},{2,26},{10... | collective-permute-start | bytes 12296 | tf_op jit(solution)/shard_map/ppermute | solution.py:453
  64.6 1.4 %collective-permute-done.11.refs_9_ = f32[4,256]{1,0:T(4,128)S(1)} collective-permute-done((f32[4,256]{1,0:T(4,128)S(1)}, f32[4,256]{1,0:T(4,128)S(1)}, u32[]{:S(2)}, u32[]{:S(2)}) %collective-permute-start.11) | collective-permute-done | bytes 4128 | tf_op jit(solution)/shard_map/ppermute | solution.py:453
  66.1 1.5 %collective-permute-done.12.refs_10_ = f32[4,256]{1,0:T(4,128)S(1)} collective-permute-done((f32[4,256]{1,0:T(4,128)S(1)}, f32[4,256]{1,0:T(4,128)S(1)}, u32[]{:S(2)}, u32[]{:S(2)}) %collective-permute-start.12) | collective-permute-done | bytes 4128 | tf_op jit(solution)/shard_map/ppermute | solution.py:453
  67.5 14.5 %shard_map.72 = (f32[16,256]{1,0:T(8,128)S(1)}, f32[8,128]{1,0:T(8,128)S(1)}) custom-call(s32[5,40]{1,0:T(8,128)S(1)} %stack.21.scalars.refs_0_, bf16[8,256,256]{2,1,0:T(8,128)(2,1)S(1)} %get-tuple-element.27.sources.refs_1_, bf16[8,256,256]{2,1,0:T(8,128)(2,1)S(1)} %get-tuple-element.31.refs_2_, bf16[7,256,256]{2,1,0:T(8,128)(2,1)S(1)} %get-tuple-element.30.targets.refs_3_, ...), custom_call_target="tpu_custom_call" | custom-call | tf_op jit(solution)/shard_map/pallas_call | solution.py:442
  82.6 1.4 %collective-permute-start.15 = (f32[16,256]{1,0:T(8,128)S(1)}, f32[16,256]{1,0:T(8,128)S(1)}, u32[]{:S(2)}, u32[]{:S(2)}) collective-permute-start(f32[16,256]{1,0:T(8,128)S(1)} %get-tuple-element.38.refs_10_), channel_id=1, source_target_pairs={{0,3},{1,2},{2,1},{3,0},{4,7},{5,6},{6,5},{7,4},{8,11},{9,10},{10,... | collective-permute-start | bytes 49160 | tf_op jit(solution)/shard_map/ppermute | solution.py:453
  84.0 1.9 %collective-permute-done.14.refs_12_ = f32[16,256]{1,0:T(8,128)S(1)} collective-permute-done((f32[16,256]{1,0:T(8,128)S(1)}, f32[16,256]{1,0:T(8,128)S(1)}, u32[]{:S(2)}, u32[]{:S(2)}) %collective-permute-start.14) | collective-permute-done | bytes 16416 | tf_op jit(solution)/shard_map/ppermute | solution.py:453
  85.9 3.6 %shard_map.73 = (f32[16,256]{1,0:T(8,128)S(1)}, f32[8,128]{1,0:T(8,128)}) custom-call(s32[5,40]{1,0:T(8,128)S(1)} %stack.21.scalars.refs_0_, bf16[8,256,256]{2,1,0:T(8,128)(2,1)S(1)} %get-tuple-element.27.sources.refs_1_, bf16[8,256,256]{2,1,0:T(8,128)(2,1)S(1)} %get-tuple-element.31.refs_2_, bf16[7,256,256]{2,1,0:T(8,128)(2,1)S(1)} %get-tuple-element.30.targets.refs_3_, ...), custom_call_target="tpu_custom_call" | custom-call | tf_op jit(solution)/shard_map/pallas_call | solution.py:442
  89.5 1.9 %collective-permute-start.16 = (f32[16,256]{1,0:T(8,128)S(1)}, f32[16,256]{1,0:T(8,128)S(1)}, u32[]{:S(2)}, u32[]{:S(2)}) collective-permute-start(f32[16,256]{1,0:T(8,128)S(1)} %get-tuple-element.41.columns), channel_id=1, source_target_pairs={{0,4},{1,5},{2,6},{3,7},{4,0},{5,1},{6,2},{7,3},{8,12},{9,13},{10,... | collective-permute-start | bytes 49160 | tf_op jit(solution)/shard_map/ppermute | solution.py:453
  92.5 2.5 %collective-permute-start.19 = (f32[16,256]{1,0:T(8,128)S(1)}, f32[16,256]{1,0:T(8,128)S(1)}, u32[]{:S(2)}, u32[]{:S(2)}) collective-permute-start(f32[16,256]{1,0:T(8,128)S(1)} %get-tuple-element.41.columns), channel_id=1, source_target_pairs={{0,24},{8,16},{16,8},{24,0},{1,25},{9,17},{17,9},{25,1},{2,26},{10... | collective-permute-start | bytes 49160 | tf_op jit(solution)/shard_map/ppermute | solution.py:453
  95.7 1.4 %collective-permute-done.19.rest_2_ = f32[16,256]{1,0:T(8,128)S(1)} collective-permute-done((f32[16,256]{1,0:T(8,128)S(1)}, f32[16,256]{1,0:T(8,128)S(1)}, u32[]{:S(2)}, u32[]{:S(2)}) %collective-permute-start.19) | collective-permute-done | bytes 16416 | tf_op jit(solution)/shard_map/ppermute | solution.py:453
  97.1 1.2 %shard_map.74 = f32[8,128]{1,0:T(8,128)} custom-call(s32[5,40]{1,0:T(8,128)S(1)} %stack.21.scalars.refs_0_, f32[16,256]{1,0:T(8,128)S(1)} %get-tuple-element.41.columns, f32[16,256]{1,0:T(8,128)S(1)} %collective-permute-done.16.partner, f32[16,256]{1,0:T(8,128)S(1)} %collective-permute-done.17.rest_0_, f32[16,256]{1,0:T(8,128)S(1)} %collective-permute-done.18.rest_1_, ...), custom_call_target="tpu_custom_call" | custom-call | tf_op jit(solution)/shard_map/pallas_call | solution.py:442
  (99 shorter events, 13.4 us)
Async XLA Ops:
  0.6 9.5 %collective-permute-start = (s32[4,8]{1,0:T(4,128)}, s32[4,8]{1,0:T(4,128)S(1)}, u32[]{:S(2)}, u32[]{:S(2)}) collective-permute-start(s32[4,8]{1,0:T(4,128)} %param.9), channel_id=1, source_target_pairs={{0,1},{1,0},{2,3},{3,2},{4,5},{5,4},{6,7},{7,6},{8,9},{9,8},{10,11... | collective-permute-start | bytes 392 | tf_op jit(solution)/shard_map/ppermute | solution.py:453
  1.1 28.4 %collective-permute-start.1 = (bf16[4,256,256]{2,1,0:T(8,128)(2,1)}, bf16[4,256,256]{2,1,0:T(8,128)(2,1)}, u32[]{:S(2)}, u32[]{:S(2)}) collective-permute-start(bf16[4,256,256]{2,1,0:T(8,128)(2,1)} %bitcast.29), channel_id=1, source_target_pairs={{0,2},{1,3},{2,0},{3,1},{4,6},{5,7},{6,4},{7,5},{8,10},{9,11},{10,... | collective-permute-start | bytes 1572872 | tf_op jit(solution)/shard_map/ppermute | solution.py:453
  3.8 30.0 %collective-permute-start.5 = (bf16[4,256,256]{2,1,0:T(8,128)(2,1)}, bf16[4,256,256]{2,1,0:T(8,128)(2,1)S(1)}, u32[]{:S(2)}, u32[]{:S(2)}) collective-permute-start(bf16[4,256,256]{2,1,0:T(8,128)(2,1)} %bitcast.26), channel_id=1, source_target_pairs={{0,4},{1,5},{2,6},{3,7},{4,0},{5,1},{6,2},{7,3},{8,12},{9,13},{10,... | collective-permute-start | bytes 1572872 | tf_op jit(solution)/shard_map/ppermute | solution.py:453
  8.0 1.4 %copy-start.10 = (f32[1024]{0:T(1024)S(1)}, f32[1024]{0:T(1024)}, u32[]{:S(2)}) copy-start(f32[1024]{0:T(1024)} %param.7) | copy-start | bytes 12292
  10.1 0.7 copy-start.14
  10.8 18.8 %collective-permute-start.2 = (s32[8,8]{1,0:T(8,128)S(1)}, s32[8,8]{1,0:T(8,128)}, u32[]{:S(2)}, u32[]{:S(2)}) collective-permute-start(s32[8,8]{1,0:T(8,128)S(1)} %pad_add_fusion.1), channel_id=1, source_target_pairs={{0,2},{1,3},{2,0},{3,1},{4,6},{5,7},{6,4},{7,5},{8,10},{9,11},{10,... | collective-permute-start | bytes 776 | tf_op jit(solution)/shard_map/ppermute | solution.py:453
  11.5 12.7 %collective-permute-start.3 = (bf16[4,256,256]{2,1,0:T(8,128)(2,1)}, bf16[4,256,256]{2,1,0:T(8,128)(2,1)S(1)}, u32[]{:S(2)}, u32[]{:S(2)}) collective-permute-start(bf16[4,256,256]{2,1,0:T(8,128)(2,1)} %bitcast.30), channel_id=1, source_target_pairs={{0,1},{1,0},{2,3},{3,2},{4,5},{5,4},{6,7},{7,6},{8,9},{9,8},{10,11... | collective-permute-start | bytes 1572872 | tf_op jit(solution)/shard_map/ppermute | solution.py:453
  11.7 13.3 %copy-start = (bf16[1024,256]{1,0:T(8,128)(2,1)S(1)}, bf16[1024,256]{1,0:T(8,128)(2,1)}, u32[]{:S(2)}) copy-start(bf16[1024,256]{1,0:T(8,128)(2,1)} %param.6) | copy-start | bytes 1572868
  11.7 12.5 %all-to-all-start = ((bf16[4,256,256]{2,1,0:T(8,128)(2,1)}), bf16[4,256,256]{2,1,0:T(8,128)(2,1)S(1)}, u32[]{:S(2)}, u32[]{:S(2)}) async-start(bf16[4,256,256]{2,1,0:T(8,128)(2,1)} %bitcast.27), calls=%async_computation | async-start | bytes 1048576 | tf_op jit(solution)/shard_map/all_to_all | solution.py:523
  24.2 0.8 copy-start.4
  25.0 1.0 %copy-start.3 = (bf16[1024,256]{1,0:T(8,128)(2,1)S(1)}, bf16[1024,256]{1,0:T(8,128)(2,1)}, u32[]{:S(2)}) copy-start(bf16[1024,256]{1,0:T(8,128)(2,1)} %param.5) | copy-start | bytes 1572868
  26.1 1.0 %copy-start.5 = (bf16[4,256,256]{2,1,0:T(8,128)(2,1)S(1)}, bf16[4,256,256]{2,1,0:T(8,128)(2,1)}, u32[]{:S(2)}) copy-start(bf16[4,256,256]{2,1,0:T(8,128)(2,1)} %copy-done.4) | copy-start | bytes 1572868
  29.6 4.2 %collective-permute-start.4 = (bf16[4,256,256]{2,1,0:T(8,128)(2,1)}, bf16[4,256,256]{2,1,0:T(8,128)(2,1)S(1)}, u32[]{:S(2)}, u32[]{:S(2)}) collective-permute-start(bf16[4,256,256]{2,1,0:T(8,128)(2,1)} %collective-permute-done.1.near), channel_id=1, source_target_pairs={{0,1},{1,0},{2,3},{3,2},{4,5},{5,4},{6,7},{7,6},{8,9},{9,8},{10,11... | collective-permute-start | bytes 1572872 | tf_op jit(solution)/shard_map/ppermute | solution.py:453
  32.9 0.7 copy-start.12
  33.8 0.8 copy-start.1
  34.6 1.0 %copy-start.2 = (bf16[4,256,256]{2,1,0:T(8,128)(2,1)S(1)}, bf16[4,256,256]{2,1,0:T(8,128)(2,1)}, u32[]{:S(2)}) copy-start(bf16[4,256,256]{2,1,0:T(8,128)(2,1)} %copy-done.1) | copy-start | bytes 1572868
  35.6 0.7 copy-start.7
  36.3 12.5 %copy-start.11 = (f32[1024]{0:T(1024)S(1)}, f32[1024]{0:T(1024)}, u32[]{:S(2)}) copy-start(f32[1024]{0:T(1024)} %param.8) | copy-start | bytes 12292
  46.7 2.1 %collective-permute-start.6 = (f32[24,256]{1,0:T(8,128)}, f32[24,256]{1,0:T(8,128)}, u32[]{:S(2)}, u32[]{:S(2)}) collective-permute-start(f32[24,256]{1,0:T(8,128)} %get-tuple-element.32.refs_5_), channel_id=1, source_target_pairs={{0,1},{1,0},{2,3},{3,2},{4,5},{5,4},{6,7},{7,6},{8,9},{9,8},{10,11... | collective-permute-start | bytes 73736 | tf_op jit(solution)/shard_map/ppermute | solution.py:453
  47.2 4.1 %collective-permute-start.7 = (f32[24,256]{1,0:T(8,128)}, f32[24,256]{1,0:T(8,128)}, u32[]{:S(2)}, u32[]{:S(2)}) collective-permute-start(f32[24,256]{1,0:T(8,128)} %get-tuple-element.32.refs_5_), channel_id=1, source_target_pairs={{0,2},{1,3},{2,0},{3,1},{4,6},{5,7},{6,4},{7,5},{8,10},{9,11},{10,... | collective-permute-start | bytes 73736 | tf_op jit(solution)/shard_map/ppermute | solution.py:453
  48.8 3.7 %collective-permute-start.8 = (f32[24,256]{1,0:T(8,128)}, f32[24,256]{1,0:T(8,128)}, u32[]{:S(2)}, u32[]{:S(2)}) collective-permute-start(f32[24,256]{1,0:T(8,128)} %get-tuple-element.32.refs_5_), channel_id=1, source_target_pairs={{0,3},{1,2},{2,1},{3,0},{4,7},{5,6},{6,5},{7,4},{8,11},{9,10},{10,... | collective-permute-start | bytes 73736 | tf_op jit(solution)/shard_map/ppermute | solution.py:453
  55.5 4.9 %collective-permute-start.9 = (f32[16,256]{1,0:T(8,128)S(1)}, f32[16,256]{1,0:T(8,128)S(1)}, u32[]{:S(2)}, u32[]{:S(2)}) collective-permute-start(f32[16,256]{1,0:T(8,128)S(1)} %get-tuple-element.34.columns.refs_6_), channel_id=1, source_target_pairs={{0,4},{1,5},{2,6},{3,7},{4,0},{5,1},{6,2},{7,3},{8,12},{9,13},{10,... | collective-permute-start | bytes 49160 | tf_op jit(solution)/shard_map/ppermute | solution.py:453
  61.0 3.7 %collective-permute-start.10 = (f32[4,256]{1,0:T(4,128)S(1)}, f32[4,256]{1,0:T(4,128)S(1)}, u32[]{:S(2)}, u32[]{:S(2)}) collective-permute-start(f32[4,256]{1,0:T(4,128)S(1)} %get-tuple-element.35), channel_id=1, source_target_pairs={{0,8},{8,0},{16,24},{24,16},{1,9},{9,1},{17,25},{25,17},{2,10},{10... | collective-permute-start | bytes 12296 | tf_op jit(solution)/shard_map/ppermute | solution.py:453
  62.5 3.6 %collective-permute-start.11 = (f32[4,256]{1,0:T(4,128)S(1)}, f32[4,256]{1,0:T(4,128)S(1)}, u32[]{:S(2)}, u32[]{:S(2)}) collective-permute-start(f32[4,256]{1,0:T(4,128)S(1)} %get-tuple-element.36), channel_id=1, source_target_pairs={{0,16},{8,24},{16,0},{24,8},{1,17},{9,25},{17,1},{25,9},{2,18},{10... | collective-permute-start | bytes 12296 | tf_op jit(solution)/shard_map/ppermute | solution.py:453
  63.0 4.5 %collective-permute-start.12 = (f32[4,256]{1,0:T(4,128)S(1)}, f32[4,256]{1,0:T(4,128)S(1)}, u32[]{:S(2)}, u32[]{:S(2)}) collective-permute-start(f32[4,256]{1,0:T(4,128)S(1)} %get-tuple-element.37), channel_id=1, source_target_pairs={{0,24},{8,16},{16,8},{24,0},{1,25},{9,17},{17,9},{25,1},{2,26},{10... | collective-permute-start | bytes 12296 | tf_op jit(solution)/shard_map/ppermute | solution.py:453
  82.1 1.9 %collective-permute-start.13 = (f32[16,256]{1,0:T(8,128)S(1)}, f32[16,256]{1,0:T(8,128)S(1)}, u32[]{:S(2)}, u32[]{:S(2)}) collective-permute-start(f32[16,256]{1,0:T(8,128)S(1)} %get-tuple-element.38.refs_10_), channel_id=1, source_target_pairs={{0,1},{1,0},{2,3},{3,2},{4,5},{5,4},{6,7},{7,6},{8,9},{9,8},{10,11... | collective-permute-start | bytes 49160 | tf_op jit(solution)/shard_map/ppermute | solution.py:453
  82.1 3.8 %collective-permute-start.14 = (f32[16,256]{1,0:T(8,128)S(1)}, f32[16,256]{1,0:T(8,128)S(1)}, u32[]{:S(2)}, u32[]{:S(2)}) collective-permute-start(f32[16,256]{1,0:T(8,128)S(1)} %get-tuple-element.38.refs_10_), channel_id=1, source_target_pairs={{0,2},{1,3},{2,0},{3,1},{4,6},{5,7},{6,4},{7,5},{8,10},{9,11},{10,... | collective-permute-start | bytes 49160 | tf_op jit(solution)/shard_map/ppermute | solution.py:453
  82.6 3.3 %collective-permute-start.15 = (f32[16,256]{1,0:T(8,128)S(1)}, f32[16,256]{1,0:T(8,128)S(1)}, u32[]{:S(2)}, u32[]{:S(2)}) collective-permute-start(f32[16,256]{1,0:T(8,128)S(1)} %get-tuple-element.38.refs_10_), channel_id=1, source_target_pairs={{0,3},{1,2},{2,1},{3,0},{4,7},{5,6},{6,5},{7,4},{8,11},{9,10},{10,... | collective-permute-start | bytes 49160 | tf_op jit(solution)/shard_map/ppermute | solution.py:453
  89.5 5.4 %collective-permute-start.16 = (f32[16,256]{1,0:T(8,128)S(1)}, f32[16,256]{1,0:T(8,128)S(1)}, u32[]{:S(2)}, u32[]{:S(2)}) collective-permute-start(f32[16,256]{1,0:T(8,128)S(1)} %get-tuple-element.41.columns), channel_id=1, source_target_pairs={{0,4},{1,5},{2,6},{3,7},{4,0},{5,1},{6,2},{7,3},{8,12},{9,13},{10,... | collective-permute-start | bytes 49160 | tf_op jit(solution)/shard_map/ppermute | solution.py:453
  91.5 3.7 %collective-permute-start.17 = (f32[16,256]{1,0:T(8,128)S(1)}, f32[16,256]{1,0:T(8,128)S(1)}, u32[]{:S(2)}, u32[]{:S(2)}) collective-permute-start(f32[16,256]{1,0:T(8,128)S(1)} %get-tuple-element.41.columns), channel_id=1, source_target_pairs={{0,8},{8,0},{16,24},{24,16},{1,9},{9,1},{17,25},{25,17},{2,10},{10... | collective-permute-start | bytes 49160 | tf_op jit(solution)/shard_map/ppermute | solution.py:453
  92.0 3.7 %collective-permute-start.18 = (f32[16,256]{1,0:T(8,128)S(1)}, f32[16,256]{1,0:T(8,128)S(1)}, u32[]{:S(2)}, u32[]{:S(2)}) collective-permute-start(f32[16,256]{1,0:T(8,128)S(1)} %get-tuple-element.41.columns), channel_id=1, source_target_pairs={{0,16},{8,24},{16,0},{24,8},{1,17},{9,25},{17,1},{25,9},{2,18},{10... | collective-permute-start | bytes 49160 | tf_op jit(solution)/shard_map/ppermute | solution.py:453
  92.5 4.6 %collective-permute-start.19 = (f32[16,256]{1,0:T(8,128)S(1)}, f32[16,256]{1,0:T(8,128)S(1)}, u32[]{:S(2)}, u32[]{:S(2)}) collective-permute-start(f32[16,256]{1,0:T(8,128)S(1)} %get-tuple-element.41.columns), channel_id=1, source_target_pairs={{0,24},{8,16},{16,8},{24,0},{1,25},{9,17},{17,9},{25,1},{2,26},{10... | collective-permute-start | bytes 49160 | tf_op jit(solution)/shard_map/ppermute | solution.py:453
  (5 other events, 3.2 us)

commit v6 on v5

--- a/solution.py
+++ b/solution.py
@@ -164,13 +164,27 @@
 LOG2E = 1.4426950408889634
 TO_LOGIT = LOG2E / entropy_strength
 TO_POTENTIAL = entropy_strength / LOG2E
-CAPACITY = 4
 SOURCE_SLOTS = 16
 TARGET_SLOTS = 12
 FAR = 8
-SECTIONS = ((0, 12), (12, 8), (20, 8), (28, 8))
+CAPACITY = 4
+SECTIONS = (
+    (0, 0, 0),
+    (1, 0, 4),
+    (0, 2, 8),
+    (2, 0, 12),
+    (0, 1, 16),
+    (1, 1, 20),
+    (2, 1, 24),
+    (3, 0, 28),
+    (3, 1, 32),
+)
+EARLY, LATE = SECTIONS[:3], SECTIONS[3:]
+LATE_SLOT = 12
 TILE_SLOTS = 40
-SMALL, LARGE = 2.0**-100, 2.0**100
+NO_SLOT = 36
+GROUP_AT = 39
+SMALL, LARGE, LARGEST = 2.0**-100, 2.0**100, 2.0**110
 
 
 def merge(parts):
@@ -193,7 +207,7 @@
 
 
 def target_bias(scalars, columns, partner, mirrors, scratch):
-    group = scalars[4, 0]
+    group = scalars[0, GROUP_AT]
     scratch[...] = jnp.full(scratch.shape, very_low, jnp.float32)
     for offset, ref in enumerate(mirrors, 1):
         scratch[pl.ds(group ^ offset, 1), :] = ref[0:1]
@@ -208,21 +222,24 @@
     return jnp.concatenate([own, *across, blank, far, *([blank] * 4)], axis=0)
 
 
-def spread(rows, bias):
+def in_parts(rows):
     high = rows.astype(jnp.bfloat16)
     rest = rows - high.astype(jnp.float32)
     middle = rest.astype(jnp.bfloat16)
     low = (rest - middle.astype(jnp.float32)).astype(jnp.bfloat16)
-    parts = jnp.concatenate([high, middle, low], axis=0)
+    return jnp.concatenate([high, middle, low], axis=0)
+
+
+def spread(rows, bias):
     count = rows.shape[0]
     shape = (3 * count, count * 128)
     slot = lax.broadcasted_iota(jnp.int32, shape, 0) & (count - 1)
     place = lax.broadcasted_iota(jnp.int32, shape, 1) >> 7
     chosen = jnp.where(slot == place, 1.0, 0.0).astype(jnp.bfloat16)
     turned = lax.dot_general(
-        parts, chosen, (((0,), (0,)), ((), ())), preferred_element_type=jnp.float32
-    )
-    for index in range(bias.shape[0]):
+        in_parts(rows), chosen, (((0,), (0,)), ((), ())), preferred_element_type=jnp.float32
+    )
+    for index in range(count):
         bias[index] = turned[:, 128 * index : 128 * (index + 1)]
 
 
@@ -235,96 +252,98 @@
     return jnp.concatenate([values, values], axis=1)
 
 
-def sides(section, by_rows, sources, targets):
-    late_source, late_target = section in (1, 3), section in (2, 3)
-    source = (sources[late_source], 0, 8 if late_source else 0)
-    target = (targets[late_target], 1, FAR if late_target else 0)
-    return (target, source) if by_rows else (source, target)
-
-
-def exact_pass(scalars, by_rows, sections, sources, targets, bias, tops, sums, ids, unrolled):
-    for section in sections:
-        first, count = SECTIONS[section]
-        (summed, summed_row, summed_base), (kept, kept_row, _) = sides(section, by_rows, sources, targets)
-
-        def visit(slot, carry=0):
-            block = scalars[summed_row, slot]
-            logits = score(summed[block], kept[scalars[kept_row, slot]])
-            if bias is not None:
-                logits = logits + wide(bias[summed_base + block])
-            top = jnp.max(logits, axis=0, keepdims=True)
-            tops[pl.ds(slot, 1), :] = top
-            sums[pl.ds(slot, 1), :] = jnp.sum(jnp.exp2(logits - top), axis=0, keepdims=True)
-            ids[pl.ds(slot, 1), :] = jnp.full((1, ids.shape[1]), scalars[2 + kept_row, slot], jnp.int32)
-            return carry
-
-        if unrolled:
-            for slot in range(first, first + count):
-                visit(slot)
-        else:
-            lax.fori_loop(first, first + count, visit, 0)
-    first, last = SECTIONS[sections[0]][0], sum(SECTIONS[sections[-1]])
-    low, high = first // 8 * 8, (last + 7) // 8 * 8
-    id_rows = ids[low:high]
-    if low < first or last < high:
-        slot = low + lax.broadcasted_iota(jnp.int32, id_rows.shape, 0)
-        id_rows = jnp.where(jnp.logical_and(slot >= first, slot < last), id_rows, -1)
-    top_rows, sum_rows = tops[low:high], sums[low:high]
+def exact_pass(lists, by_rows, sections, sources, targets, tops, sums, ids):
+    summed_row, kept_row = (1, 0) if by_rows else (0, 1)
+    ids[...] = jnp.full(ids.shape, -1, jnp.int32)
+    for source, target, first in sections:
+        pair = (sources[source], targets[target])
+        for slot in range(first, first + CAPACITY):
+            blocks = [array[lists[row, slot]] for row, array in enumerate(pair)]
+            exact_tile(lists, by_rows, slot, blocks, None, tops, sums, ids)
+    return merge_tiles(by_rows, tops, sums, ids)
+
+
+def exact_tile(lists, by_rows, slot, blocks, bias, tops, sums, ids):
+    summed, kept = blocks[::-1] if by_rows else blocks
+    logits = score(summed, kept)
+    if bias is not None:
+        count = bias.shape[0] - 1
+        logits = logits + wide(bias[jnp.minimum(lists[3 if by_rows else 2, slot], count)])
+    top = jnp.max(logits, axis=0, keepdims=True)
+    tops[pl.ds(slot, 1), :] = top
+    sums[pl.ds(slot, 1), :] = jnp.sum(jnp.exp2(logits - top), axis=0, keepdims=True)
+    ids[pl.ds(slot, 1), :] = jnp.full((1, ids.shape[1]), lists[2 if by_rows else 3, slot], jnp.int32)
+
+
+def merge_tiles(by_rows, tops, sums, ids):
     best, total = [], []
     for block in range(SOURCE_SLOTS if by_rows else TARGET_SLOTS):
-        mine = id_rows == block
-        top = jnp.max(jnp.where(mine, top_rows, very_low), axis=0, keepdims=True)
+        mine = ids[...] == block
+        top = jnp.max(jnp.where(mine, tops[...], very_low), axis=0, keepdims=True)
         best.append(top)
         total.append(
-            jnp.sum(jnp.where(mine, sum_rows * jnp.exp2(top_rows - top), 0.0), axis=0, keepdims=True)
+            jnp.sum(jnp.where(mine, sums[...] * jnp.exp2(tops[...] - top), 0.0), axis=0, keepdims=True)
         )
     best = jnp.concatenate(best, axis=0)
     total = jnp.concatenate(total, axis=0)
     return jnp.where(total > 0, best + LOG2E * jnp.log(jnp.where(total > 0, total, 1.0)), very_low)
 
 
-def fast_pass(scalars, by_rows, sections, sources, targets, bias, shift, total, present):
+def exact_loop(lists, by_rows, first, sources, targets, bias, shift, work):
+    tops, sums, ids, packed, semaphore = work
+    for index, blocks in enumerate((*sources, *targets)):
+        copy = pltpu.make_async_copy(blocks, packed.at[pl.ds(4 * index, 4)], semaphore)
+        copy.start()
+        copy.wait()
+    ids[...] = jnp.full(ids.shape, -1, jnp.int32)
+
+    def visit(slot, carry):
+        blocks = packed[lists[4, slot]], packed[lists[5, slot]]
+        exact_tile(lists, by_rows, slot, blocks, bias, tops, sums, ids)
+        return carry
+
+    lax.fori_loop(first, NO_SLOT, visit, 0)
+    result = merge_tiles(by_rows, tops, sums, ids)
+    return result if bias is None or shift is None else result - shift
+
+
+def guarded_pass(lists, present, by_rows, sections, sources, targets, bias, shift, total, work, write):
+    summed_row, kept_row = (1, 0) if by_rows else (0, 1)
     total[...] = jnp.zeros(total.shape, jnp.float32)
-    present[...] = jnp.zeros(present.shape, jnp.float32)
-    for section in sections:
-        first, count = SECTIONS[section]
-        (summed, summed_row, summed_base), (kept, kept_row, _) = sides(section, by_rows, sources, targets)
-        for slot in range(first, first + count):
-            block = scalars[summed_row, slot]
-            logits = score(summed[block], kept[scalars[kept_row, slot]])
-            logits = logits + (shift if bias is None else wide(bias[summed_base + block]))
+    for source, target, first in sections:
+        pair = (sources[source], targets[target])
+        summed, kept = pair[summed_row], pair[kept_row]
+        for slot in range(first, first + CAPACITY):
+            block = lists[summed_row, slot]
+            logits = score(summed[block], kept[lists[kept_row, slot]])
+            if bias is None:
+                logits = logits + shift
+            else:
+                if not by_rows:
+                    place = 4 * source + block
+                elif target == 2:
+                    place = lists[3, slot]
+                else:
+                    place = FAR * target + block
+                logits = logits + wide(bias[place])
             terms = jnp.exp2(logits)
-            place = scalars[2 + kept_row, slot]
-            present[pl.ds(place, 1), :] = jnp.ones((1, present.shape[1]), jnp.float32)
+            place = lists[2 + kept_row, slot]
             total[place] = total[place] + jnp.sum(terms.reshape(-1, 8, terms.shape[1]), axis=0)
     count = SOURCE_SLOTS if by_rows else TARGET_SLOTS
     sums_of = jnp.concatenate(
         [jnp.sum(total[block], axis=0, keepdims=True) for block in range(count)], axis=0
     )
-    here = present[0:count] > 0
+    here = wide(present[0:count]) > 0
     result = LOG2E * jnp.log(jnp.where(here, sums_of, 1.0))
     if shift is not None:
         result = result - shift
+    write(jnp.where(here, result, very_low))
     fine = jnp.logical_and(sums_of > SMALL, sums_of < LARGE)
     worst = jnp.min(jnp.where(jnp.logical_or(fine, jnp.logical_not(here)), 1.0, 0.0))
-    return jnp.where(here, result, very_low), worst > 0.5
-
-
-def guarded_pass(scalars, by_rows, sections, sources, targets, rows, shift, work, write):
-    total, present, tops, sums, ids, *bias = work
-    bias = bias[0] if bias else None
-    if bias is not None:
-        spread(rows if shift is None else rows + shift, bias)
-    result, fine = fast_pass(
-        scalars, by_rows, sections, sources, targets, bias, shift, total, present
-    )
-    write(result)
-
-    @pl.when(jnp.logical_not(fine))
+
+    @pl.when(worst < 0.5)
     def _():
-        if shift is not None and bias is not None:
-            spread(rows, bias)
-        write(exact_pass(scalars, by_rows, sections, sources, targets, bias, tops, sums, ids, False))
+        write(exact_loop(lists, by_rows, sections[0][2], sources, targets, bias, shift, work))
 
 
 def middle(pieces):
@@ -333,52 +352,37 @@
     return 0.5 * (top + bottom)
 
 
-def early_kernel(scalars, own, core, target, mirrors, out, sources, targets, tops, sums, ids):
-    sources[0:4] = own[...]
-    sources[4:8] = core[...]
-    targets[0:4] = target[...]
-    for offset in (1, 2, 3):
-        targets[3 + offset] = mirrors[scalars[4, 0] ^ offset]
-    out[...] = exact_pass(
-        scalars, True, (0,), (sources, None), (targets, None), None, tops, sums, ids, True
-    )
-
-
-def first_kernel(
-    scalars, early, mass, sources, near, cross, targets, far, out, late_sources, *work
-):
-    late_sources[0:4] = near[...]
-    late_sources[4:8] = cross[...]
+def early_kernel(lists, own, core, target, mirrors, out, reference, tops, sums, ids):
+    result = exact_pass(lists, True, EARLY, (own, core), (target, None, mirrors), tops, sums, ids)
+    out[...] = result
+    largest = jnp.max(result, axis=(0, 1), keepdims=True)
+    reference[...] = jnp.broadcast_to(-largest, reference.shape)
+
+
+def first_kernel(lists, present, *refs):
+    sources, targets = refs[0:4], refs[4:7]
+    reference, early, mass, out, total, *work = refs[7:]
     out[16:20, :] = mass[...]
     out[20:24, :] = jnp.zeros((4, out.shape[1]), jnp.float32)
-    begun = early[...]
-    shift = -jnp.max(begun, axis=(0, 1), keepdims=True)
-
-    def write(late):
-        out[0:16, :] = merge([begun, late])
+
+    def write(result):
+        out[0:16, :] = merge([early[...], result])
 
     guarded_pass(
-        scalars,
-        True,
-        (1, 2, 3),
-        (sources, late_sources),
-        (targets, far),
-        None,
-        shift,
-        work,
-        write,
-    )
-
-
-def columns_kernel(last_pass, *refs):
-    scalars, sources, targets = refs[0], refs[1:3], refs[3:5]
-    masses, target_mass, rest = refs[5:9], refs[9], refs[10:]
+        lists, present, True, LATE, sources, targets, None, reference[0:1, 0:1], total, work, write
+    )
+
+
+def columns_kernel(last_pass, lists, present, *refs):
+    sources, targets = refs[0:4], refs[4:7]
+    masses, target_mass, rest = refs[7:11], refs[11], refs[12:]
     parts, shift = masses, None
     if last_pass:
         parts, (shift, *rest) = rest[:4], rest[4:]
         shift = shift[0:1, 0:1]
-    out, second, *work = rest
+    out, second, bias, total, *work = rest
     rows = source_bias(masses, parts)
+    spread(rows + shift if last_pass else rows, bias)
     if last_pass:
         for block in range(4):
             for half in range(2):
@@ -392,26 +396,28 @@
     def write(result):
         out[0:TARGET_SLOTS, :] = result
 
-    guarded_pass(scalars, False, (0, 1, 2, 3), sources, targets, rows, shift, work, write)
-
-
-def rows_kernel(*refs):
-    scalars, sources, targets = refs[0], refs[1:3], refs[3:5]
-    shift, columns, partner, *mirrors = refs[5:11]
-    out, second, *work, scratch = refs[11:]
-    rows = target_bias(scalars, columns, partner, mirrors, scratch)
+    guarded_pass(
+        lists, present, False, SECTIONS, sources, targets, bias, shift, total, work, write
+    )
+
+
+def rows_kernel(lists, present, *refs):
+    sources, targets = refs[0:4], refs[4:7]
+    shift, columns, partner, *mirrors = refs[7:13]
+    out, second, bias, total, *work, scratch = refs[13:]
+    rows = target_bias(lists, columns, partner, mirrors, scratch)
+    shift = shift[0:1, 0:1]
+    spread(rows + shift, bias)
     second[...] = jnp.broadcast_to(middle([rows[0:7], rows[8:12]]), second.shape)
 
     def write(result):
         out[...] = result
 
-    guarded_pass(
-        scalars, True, (0, 1, 2, 3), sources, targets, rows, shift[0:1, 0:1], work, write
-    )
+    guarded_pass(lists, present, True, SECTIONS, sources, targets, bias, shift, total, work, write)
 
 
 def forward_kernel(scalars, columns, partner, *outs):
-    group = scalars[4, 0]
+    group = scalars[0, GROUP_AT]
     for offset, out in enumerate(outs, 1):
         block = group ^ offset
         out[0:1, :] = columns[3 + offset : 4 + offset]
@@ -422,7 +428,7 @@
 
 def finish_kernel(scalars, columns, partner, *rest):
     *mirrors, out, scratch = rest
-    group = scalars[4, 0]
+    group = scalars[0, GROUP_AT]
     scratch[...] = jnp.full(scratch.shape, very_low, jnp.float32)
     for offset, ref in enumerate(mirrors, 1):
         scratch[pl.ds(group ^ offset, 1), :] = ref[3 + offset : 4 + offset]
@@ -439,13 +445,14 @@
 
 def call(kernel, inputs, outs, scratch=()):
     whole = pl.BlockSpec(memory_space=VMEM)
+    scalar = pl.BlockSpec(memory_space=SMEM)
     return pl.pallas_call(
         kernel,
         out_shape=outs,
-        in_specs=[pl.BlockSpec(memory_space=SMEM)] + [whole] * (len(inputs) - 1),
+        in_specs=[scalar] + [whole] * (len(inputs) - 1),
         out_specs=[whole] * len(outs),
         scratch_shapes=list(scratch),
-        compiler_params=pltpu.CompilerParams(vmem_limit_bytes=32 << 20),
+        compiler_params=pltpu.CompilerParams(vmem_limit_bytes=16 << 20),
     )(*inputs)
 
 
@@ -453,52 +460,60 @@
     return lax.ppermute(values, axis, [(index, index ^ bit) for index in range(size)])
 
 
-def tile_lists(candidates, own_group, own_member, members, per_device, slot_count):
-    owner = candidates // per_device
-    local = candidates % per_device
-    apart = (owner % members) ^ own_member
-    last = candidates.shape[1] - 1
-    mirror = (owner // members) ^ own_group
-    is_last = jnp.arange(last + 1)[None, :] == last
-    source = jnp.broadcast_to(
-        jnp.arange(candidates.shape[0], dtype=jnp.int32)[:, None], candidates.shape
-    )
-    own_mirror = jnp.logical_and(is_last, source < per_device)
-    near = jnp.logical_and(~is_last, apart == 0)
+def tile_lists(table, group, member):
+    count = table.shape[1]
+    row = jnp.arange(table.shape[0], dtype=jnp.int32)[:, None]
+    source = row >> 2
+    pick = jnp.arange(count, dtype=jnp.int32)[None, :]
+    is_last = pick == count - 1
+    apart = ((table >> 2) & 7) ^ member
     far = jnp.logical_and(~is_last, apart == 4)
-    late = source >= 2 * per_device
-    target = jnp.where(jnp.logical_and(is_last, mirror > 0), 3 + mirror, local)
-    members_of = (
-        jnp.logical_or(jnp.logical_and(near, ~late), own_mirror),
-        jnp.logical_and(near, late),
-        jnp.logical_and(far, ~late),
-        jnp.logical_and(far, late),
-    )
-    source, target = source.reshape(1, -1), target.reshape(1, -1)
-    order = jnp.arange(source.shape[1], dtype=jnp.int32)
-    before = order[None, :] < order[:, None]
-    place = jnp.full(order.shape, -1, jnp.int32)
-    for (first, _), taken in zip(SECTIONS, members_of):
-        if first >= 12 and slot_count == 16:
-            break
-        taken = taken.reshape(-1)
-        earlier = jnp.sum(jnp.logical_and(before, taken[None, :]).astype(jnp.int32), axis=1)
-        place = jnp.where(taken, first + earlier, place)
-    slots = jnp.arange(slot_count, dtype=jnp.int32)
+    other = table >> 5
+    starts = {(source, target): first for source, target, first in SECTIONS}
+
+    def first_of(target):
+        return functools.reduce(
+            lambda value, index: jnp.where(source == index, starts[index, target], value),
+            range(1, 4),
+            jnp.full(source.shape, starts[0, target], jnp.int32),
+        )
+
+    section = jnp.where(apart == 0, first_of(0), jnp.where(apart == 4, first_of(1), -1))
+    section = jnp.where(is_last, jnp.where(source == 0, starts[0, 2], -1), section)
+    local = table & 3
+    block = jnp.where(is_last, other, local)
+    slot = jnp.where(is_last, jnp.where(other == group, local, 3 + (other ^ group)), local)
+    slot = slot + jnp.where(far, FAR, 0)
+    array = jnp.where(is_last, 6, jnp.where(far, 5, 4))
+    code = (row & 3) + 4 * block + 16 * row + 512 * slot + 16384 * (4 * array + block)
+    section, code = section.reshape(-1), code.reshape(-1)
+    order = jnp.arange(section.shape[0], dtype=jnp.int32)
+    earlier = jnp.logical_and(order[None, :] < order[:, None], section[None, :] == section[:, None])
+    place = jnp.where(section >= 0, section + jnp.sum(earlier.astype(jnp.int32), axis=1), -1)
+    slots = jnp.arange(TILE_SLOTS, dtype=jnp.int32)
     hits = place[None, :] == slots[:, None]
-    used = jnp.any(hits, axis=1)
-    sources = jnp.sum(jnp.where(hits, source, 0), axis=1)
-    targets = jnp.sum(jnp.where(hits, target, 0), axis=1)
-    late_slot = jnp.logical_or(jnp.logical_and(slots >= 12, slots < 20), slots >= 28)
-    return jnp.stack(
+    found = jnp.sum(jnp.where(hits, code[None, :] + 1, 0), axis=1)
+    found = jnp.where(found > 0, found - 1, SOURCE_SLOTS * 16 + TARGET_SLOTS * 512 + 16 * 16384)
+    source_slots, target_slots = (found >> 4) & 31, (found >> 9) & 31
+    blocks = jnp.minimum(source_slots, SOURCE_SLOTS - 1), found >> 14
+    lists = jnp.stack(
         [
-            jnp.where(jnp.logical_and(late_slot, used), sources - 8, sources),
-            targets,
-            jnp.where(used, sources, SOURCE_SLOTS),
-            jnp.where(used, jnp.where(slots >= 20, FAR + targets, targets), TARGET_SLOTS),
-            jnp.broadcast_to(own_group, slots.shape).astype(jnp.int32),
+            jnp.where(slots == GROUP_AT, group, found & 3),
+            (found >> 2) & 3,
+            source_slots,
+            target_slots,
+            *blocks,
         ]
     )
+    late_slots = jnp.where(slots >= LATE_SLOT, source_slots, SOURCE_SLOTS)
+    rows = jnp.arange(16, dtype=jnp.int32)
+    present = [
+        jnp.broadcast_to(
+            jnp.any(taken[None, :] == rows[:, None], axis=1).astype(jnp.float32)[:, None], (16, 128)
+        )
+        for taken in (source_slots, target_slots, late_slots)
+    ]
+    return lists, *present
 
 
 def shards_quad(source_vectors, target_vectors, source_mass, target_mass, candidates):
@@ -516,53 +531,43 @@
     source_own = source_vectors.reshape(blocked)
     target_own = target_vectors.reshape(blocked)
     target_far = member_swap(target_own, 4)
-    named = jnp.concatenate([candidates, member_swap(candidates, 1)])
     source_near = member_swap(source_own, 2)
-    theirs = member_swap(named, 2)
+    named = jnp.concatenate([candidates, member_swap(candidates, 2)])
     source_late, target_late, named = lax.optimization_barrier((source_own, target_own, named))
+    source_core = member_swap(source_late, 1)
+    named_core = member_swap(named, 1)
     mirrors = lax.all_to_all(target_late, "group", split_axis=0, concat_axis=0, tiled=True)
-    source_core = member_swap(source_late, 1)
-    place = (own_group, own_member, members, per_device)
-    early_scalars = tile_lists(named, *place, 16)
+    lists, has_source, has_target, has_late = tile_lists(
+        jnp.concatenate([named[0:4], named_core[0:4], named[4:8], named_core[4:8]]),
+        own_group.astype(jnp.int32),
+        own_member.astype(jnp.int32),
+    )
     own_source_mass = LOG2E * source_mass.reshape(per_device, block_rows)
     own_mass = LOG2E * target_mass.reshape(per_device, block_rows)
 
     side = jax.ShapeDtypeStruct((16, block_rows), jnp.float32)
     flat = jax.ShapeDtypeStruct((8, 128), jnp.float32)
-    stacked = lambda count: jax.ShapeDtypeStruct((count, block_rows, width), source_vectors.dtype)
     tile_rows = [VMEM((TILE_SLOTS, block_rows), kind) for kind in (jnp.float32, jnp.float32, jnp.int32)]
     pass_buffers = [
         VMEM((SOURCE_SLOTS + 1, 8, block_rows), jnp.float32),
-        VMEM((24, block_rows), jnp.float32),
         *tile_rows,
-        VMEM((SOURCE_SLOTS, block_rows, 128), jnp.float32),
+        VMEM((28, block_rows, width), source_vectors.dtype),
+        pltpu.SemaphoreType.DMA,
     ]
-
-    early, sources, targets = call(
-        early_kernel,
-        [early_scalars, source_own, source_core, target_own, mirrors],
-        [side, stacked(8), stacked(7)],
-        tile_rows,
-    )
-    source_near, theirs, early = lax.optimization_barrier((source_near, theirs, early))
+    bias_buffer = VMEM((SOURCE_SLOTS, block_rows, 128), jnp.float32)
+
+    early, reference = call(
+        early_kernel, [lists, source_own, source_core, target_own, mirrors], [side, flat], tile_rows
+    )
+    source_near, early = lax.optimization_barrier((source_near, early))
     source_cross = member_swap(source_near, 1)
-    scalars = tile_lists(jnp.concatenate([named, theirs]), *place, TILE_SLOTS)
-    parts, late_sources = call(
+    blocks = [source_own, source_core, source_near, source_cross, target_own, target_far, mirrors]
+    (parts,) = call(
         first_kernel,
-        [
-            scalars,
-            early,
-            own_source_mass,
-            sources,
-            source_near,
-            source_cross,
-            targets,
-            target_far,
-        ],
-        [jax.ShapeDtypeStruct((24, block_rows), jnp.float32), stacked(8)],
-        pass_buffers[:5],
-    )
-    blocks = [sources, late_sources, targets, target_far]
+        [lists, has_late, *blocks, reference, early, own_source_mass],
+        [jax.ShapeDtypeStruct((24, block_rows), jnp.float32)],
+        pass_buffers,
+    )
     masses, extra = [], []
     for step in range(ITERS):
         last_pass = step == ITERS - 1
@@ -570,30 +575,30 @@
         masses = masses or parts
         columns, potential = call(
             functools.partial(columns_kernel, last_pass),
-            [scalars, *blocks, *masses, own_mass, *(parts + extra if last_pass else [])],
+            [lists, has_target, *blocks, *masses, own_mass, *(parts + extra if last_pass else [])],
             [side, flat],
-            pass_buffers,
+            [bias_buffer, *pass_buffers],
         )
         partner = member_swap(columns, 4)
         if last_pass:
             break
         sent = call(
             forward_kernel,
-            [scalars, columns, partner],
+            [lists, columns, partner],
             [jax.ShapeDtypeStruct((4, block_rows), jnp.float32)] * 3,
         )
         received = [group_swap(values, bit) for bit, values in enumerate(sent, 1)]
         parts, shift = call(
             rows_kernel,
-            [scalars, *blocks, potential, columns, partner, *received],
+            [lists, has_source, *blocks, potential, columns, partner, *received],
             [side, flat],
-            [*pass_buffers, VMEM((8, block_rows), jnp.float32)],
+            [bias_buffer, *pass_buffers, VMEM((8, block_rows), jnp.float32)],
         )
         extra = [shift]
     received = [group_swap(columns, bit) for bit in (1, 2, 3)]
     (final,) = call(
         finish_kernel,
-        [scalars, columns, partner, *received],
+        [lists, columns, partner, *received],
         [flat],
         [VMEM((8, block_rows), jnp.float32)],
     )

time: 99 us -> 92.4 us (0.933)
  local copies, waits for them, and re-layouts: 13.2 us -> 2.55 us
  waiting for transfers between devices: 23.6 us -> 29.3 us
  other arithmetic: 1.92 us -> 0.81 us
    unnamed x32 -> x10, local copies, waits for them, and re-layouts: 9.24 us -> 1.27 us
    ppermute x20, waiting for transfers between devices: 15.2 us -> 21.8 us  [swap(): lax.ppermute(values, axis, [(index, index ^ bit) for index in range(size)])]
    broadcast_in_dim x11 -> x7, local copies, waits for them, and re-layouts: 2.98 us -> 0.47 us  [the longest x4 0.26 us: tile_lists(): jnp.where(is_last, jnp.where(source == 0, starts[0, 2], -1), section)]
  transfers between devices with their start and end apart: 21 -> 21, of which waited for: 11 -> 12; matrix products, arithmetic and copies ran while one was open for 6% -> 2% of each run, Pallas kernels for 2% -> 2%
where the time goes in v6:
time: 92.4 us; the launch traced here: 91.9 us
  Pallas kernels  34.6 us (37%)
  waiting for transfers between devices  29.3 us (32%)
  starting transfers between devices  23.8 us (26%)
  local copies, waits for them, and re-layouts  2.55 us (3%)
    pallas_call x7, Pallas kernels, call(): pl.pallas_call(kernel, out_shape=outs, in_specs=[scalar] + [whole] * (len...  34.6 us
    ppermute x20, waiting for transfers between devices, swap(): lax.ppermute(values, axis, [(index, index ^ bit) for index in range(size)])  21.8 us
    ppermute x20, starting transfers between devices, swap(): lax.ppermute(values, axis, [(index, index ^ bit) for index in range(size)])  20 us
    all_to_all x1, waiting for transfers between devices, shards_quad(): lax.all_to_all(target_late, 'group', split_axis=0, concat_axis=0, tiled=T...  7.42 us
    all_to_all x1, starting transfers between devices, shards_quad(): lax.all_to_all(target_late, 'group', split_axis=0, concat_axis=0, tiled=T...  3.86 us
  transfers between devices with their start and end apart: 21, of which 12 were waited for; matrix products, arithmetic and copies ran while one was open for 2% of the time, Pallas kernels for 2%

profile of v6, /device:TPU:0, one launch (start us, length us, event | category | flops | bytes accessed | tf_op | source)
XLA Modules:
  0.0 91.9 jit_solution(9896194905835493269)
XLA Ops:
  0.6 3.1 %collective-permute-start = (s32[4,8]{1,0:T(4,128)}, s32[4,8]{1,0:T(4,128)S(1)}, u32[]{:S(2)}, u32[]{:S(2)}) collective-permute-start(s32[4,8]{1,0:T(4,128)} %param.9), channel_id=1, source_target_pairs={{0,2},{1,3},{2,0},{3,1},{4,6},{5,7},{6,4},{7,5},{8,10},{9,11},{10,... | collective-permute-start | bytes 392 | tf_op jit(solution)/shard_map/ppermute | solution.py:460
  3.8 3.0 %collective-permute-start.5 = (bf16[4,256,256]{2,1,0:T(8,128)(2,1)}, bf16[4,256,256]{2,1,0:T(8,128)(2,1)S(1)}, u32[]{:S(2)}, u32[]{:S(2)}) collective-permute-start(bf16[4,256,256]{2,1,0:T(8,128)(2,1)} %bitcast.15), channel_id=1, source_target_pairs={{0,4},{1,5},{2,6},{3,7},{4,0},{5,1},{6,2},{7,3},{8,12},{9,13},{10,... | collective-permute-start | bytes 1572872 | tf_op jit(solution)/shard_map/ppermute | solution.py:460
  7.4 0.6 copy-done.4
  8.1 3.9 %all-to-all-start = ((bf16[4,256,256]{2,1,0:T(8,128)(2,1)}), bf16[4,256,256]{2,1,0:T(8,128)(2,1)S(1)}, u32[]{:S(2)}, u32[]{:S(2)}) async-start(bf16[4,256,256]{2,1,0:T(8,128)(2,1)} %bitcast.16), calls=%async_computation | async-start | bytes 1048576 | tf_op jit(solution)/shard_map/all_to_all | solution.py:539
  13.2 7.4 %all-to-all-done.mirrors.refs_6_ = bf16[4,256,256]{2,1,0:T(8,128)(2,1)S(1)} async-done(((bf16[4,256,256]{2,1,0:T(8,128)(2,1)}), bf16[4,256,256]{2,1,0:T(8,128)(2,1)S(1)}, u32[]{:S(2)}, u32[]{:S(2)}) %all-to-all-start) | async-done | bytes 524320 | tf_op jit(solution)/shard_map/all_to_all | solution.py:539
  20.6 2.0 %shard_map.68 = (f32[16,256]{1,0:T(8,128)S(1)}, f32[8,128]{1,0:T(8,128)S(1)}) custom-call(s32[6,40]{1,0:T(8,128)S(1)} %stack.2.lists.scalars, bf16[4,256,256]{2,1,0:T(8,128)(2,1)S(1)} %bitcast.24, bf16[4,256,256]{2,1,0:T(8,128)(2,1)S(1)} %collective-permute-done.2.core.refs_1_, bf16[4,256,256]{2,1,0:T(8,128)(2,1)S(1)} %bitcast.17, ...), custom_call_target="tpu_custom_call" | custom-call | tf_op jit(solution)/shard_map/pallas_call | solution.py:449
  22.6 5.9 %collective-permute-done.3.refs_2_ = bf16[4,256,256]{2,1,0:T(8,128)(2,1)S(1)} collective-permute-done((bf16[4,256,256]{2,1,0:T(8,128)(2,1)}, bf16[4,256,256]{2,1,0:T(8,128)(2,1)S(1)}, u32[]{:S(2)}, u32[]{:S(2)}) %collective-permute-start.3) | collective-permute-done | bytes 524320 | tf_op jit(solution)/shard_map/ppermute | solution.py:460
  28.6 0.7 copy-done.3
  29.4 1.2 %collective-permute-done.4.refs_3_ = bf16[4,256,256]{2,1,0:T(8,128)(2,1)} collective-permute-done((bf16[4,256,256]{2,1,0:T(8,128)(2,1)S(1)}, bf16[4,256,256]{2,1,0:T(8,128)(2,1)}, u32[]{:S(2)}, u32[]{:S(2)}) %collective-permute-start.4) | collective-permute-done | bytes 524320 | tf_op jit(solution)/shard_map/ppermute | solution.py:460
  30.7 10.0 %shard_map.69.refs_7_ = f32[24,256]{1,0:T(8,128)S(1)} custom-call(s32[6,40]{1,0:T(8,128)S(1)} %stack.2.lists.scalars, f32[16,128]{1,0:T(8,128)S(1)} %broadcast_in_dim.190.present, bf16[4,256,256]{2,1,0:T(8,128)(2,1)S(1)} %bitcast.25, bf16[4,256,256]{2,1,0:T(8,128)(2,1)S(1)} %collective-permute-done.2.core.refs_1_, ...), custom_call_target="tpu_custom_call" | custom-call | tf_op jit(solution)/shard_map/pallas_call | solution.py:449
  40.7 1.8 %collective-permute-start.7 = (f32[24,256]{1,0:T(8,128)S(1)}, f32[24,256]{1,0:T(8,128)S(1)}, u32[]{:S(2)}, u32[]{:S(2)}) collective-permute-start(f32[24,256]{1,0:T(8,128)S(1)} %shard_map.69.refs_7_), channel_id=1, source_target_pairs={{0,2},{1,3},{2,0},{3,1},{4,6},{5,7},{6,4},{7,5},{8,10},{9,11},{10,... | collective-permute-start | bytes 73736 | tf_op jit(solution)/shard_map/ppermute | solution.py:460
  42.7 1.3 %collective-permute-done.8.refs_10_ = f32[24,256]{1,0:T(8,128)S(1)} collective-permute-done((f32[24,256]{1,0:T(8,128)S(1)}, f32[24,256]{1,0:T(8,128)S(1)}, u32[]{:S(2)}, u32[]{:S(2)}) %collective-permute-start.8) | collective-permute-done | bytes 24608 | tf_op jit(solution)/shard_map/ppermute | solution.py:460
  44.0 0.8 collective-permute-done.7.refs_9_
  44.8 3.0 %shard_map.70 = (f32[16,256]{1,0:T(8,128)S(1)}, f32[8,128]{1,0:T(8,128)S(1)}) custom-call(s32[6,40]{1,0:T(8,128)S(1)} %stack.2.lists.scalars, f32[16,128]{1,0:T(8,128)S(1)} %broadcast_in_dim.188.present, bf16[4,256,256]{2,1,0:T(8,128)(2,1)S(1)} %bitcast.26, bf16[4,256,256]{2,1,0:T(8,128)(2,1)S(1)} %collective-permute-done.2.core.refs_1_, ...), custom_call_target="tpu_custom_call" | custom-call | tf_op jit(solution)/shard_map/pallas_call | solution.py:449
  47.8 1.3 %collective-permute-start.9 = (f32[16,256]{1,0:T(8,128)S(1)}, f32[16,256]{1,0:T(8,128)S(1)}, u32[]{:S(2)}, u32[]{:S(2)}) collective-permute-start(f32[16,256]{1,0:T(8,128)S(1)} %get-tuple-element.26.columns.refs_8_), channel_id=1, source_target_pairs={{0,4},{1,5},{2,6},{3,7},{4,0},{5,1},{6,2},{7,3},{8,12},{9,13},{10,... | collective-permute-start | bytes 49160 | tf_op jit(solution)/shard_map/ppermute | solution.py:460
  49.1 3.4 %collective-permute-done.9.partner.refs_9_ = f32[16,256]{1,0:T(8,128)S(1)} collective-permute-done((f32[16,256]{1,0:T(8,128)S(1)}, f32[16,256]{1,0:T(8,128)S(1)}, u32[]{:S(2)}, u32[]{:S(2)}) %collective-permute-start.9) | collective-permute-done | bytes 16416 | tf_op jit(solution)/shard_map/ppermute | solution.py:460
  52.5 0.6 shard_map.71
  53.2 1.6 %collective-permute-start.10 = (f32[4,256]{1,0:T(4,128)S(1)}, f32[4,256]{1,0:T(4,128)S(1)}, u32[]{:S(2)}, u32[]{:S(2)}) collective-permute-start(f32[4,256]{1,0:T(4,128)S(1)} %get-tuple-element.27), channel_id=1, source_target_pairs={{0,8},{8,0},{16,24},{24,16},{1,9},{9,1},{17,25},{25,17},{2,10},{10... | collective-permute-start | bytes 12296 | tf_op jit(solution)/shard_map/ppermute | solution.py:460
  54.7 1.5 %collective-permute-start.11 = (f32[4,256]{1,0:T(4,128)S(1)}, f32[4,256]{1,0:T(4,128)S(1)}, u32[]{:S(2)}, u32[]{:S(2)}) collective-permute-start(f32[4,256]{1,0:T(4,128)S(1)} %get-tuple-element.28), channel_id=1, source_target_pairs={{0,16},{8,24},{16,0},{24,8},{1,17},{9,25},{17,1},{25,9},{2,18},{10... | collective-permute-start | bytes 12296 | tf_op jit(solution)/shard_map/ppermute | solution.py:460
  56.8 1.5 %collective-permute-done.11.refs_11_ = f32[4,256]{1,0:T(4,128)S(1)} collective-permute-done((f32[4,256]{1,0:T(4,128)S(1)}, f32[4,256]{1,0:T(4,128)S(1)}, u32[]{:S(2)}, u32[]{:S(2)}) %collective-permute-start.11) | collective-permute-done | bytes 4128 | tf_op jit(solution)/shard_map/ppermute | solution.py:460
  58.3 2.4 %collective-permute-done.12.refs_12_ = f32[4,256]{1,0:T(4,128)S(1)} collective-permute-done((f32[4,256]{1,0:T(4,128)S(1)}, f32[4,256]{1,0:T(4,128)S(1)}, u32[]{:S(2)}, u32[]{:S(2)}) %collective-permute-start.12) | collective-permute-done | bytes 4128 | tf_op jit(solution)/shard_map/ppermute | solution.py:460
  60.8 14.2 %shard_map.72 = (f32[16,256]{1,0:T(8,128)S(1)}, f32[8,128]{1,0:T(8,128)S(1)}) custom-call(s32[6,40]{1,0:T(8,128)S(1)} %stack.2.lists.scalars, f32[16,128]{1,0:T(8,128)S(1)} %broadcast_in_dim.191.present, bf16[4,256,256]{2,1,0:T(8,128)(2,1)S(1)} %bitcast.27, bf16[4,256,256]{2,1,0:T(8,128)(2,1)S(1)} %collective-permute-done.2.core.refs_1_, ...), custom_call_target="tpu_custom_call" | custom-call | tf_op jit(solution)/shard_map/pallas_call | solution.py:449
  75.1 1.6 %collective-permute-start.14 = (f32[16,256]{1,0:T(8,128)S(1)}, f32[16,256]{1,0:T(8,128)S(1)}, u32[]{:S(2)}, u32[]{:S(2)}) collective-permute-start(f32[16,256]{1,0:T(8,128)S(1)} %get-tuple-element.30.refs_12_), channel_id=1, source_target_pairs={{0,2},{1,3},{2,0},{3,1},{4,6},{5,7},{6,4},{7,5},{8,10},{9,11},{10,... | collective-permute-start | bytes 49160 | tf_op jit(solution)/shard_map/ppermute | solution.py:460
  77.0 1.3 %collective-permute-done.15.refs_15_ = f32[16,256]{1,0:T(8,128)S(1)} collective-permute-done((f32[16,256]{1,0:T(8,128)S(1)}, f32[16,256]{1,0:T(8,128)S(1)}, u32[]{:S(2)}, u32[]{:S(2)}) %collective-permute-start.15) | collective-permute-done | bytes 16416 | tf_op jit(solution)/shard_map/ppermute | solution.py:460
  78.3 0.6 collective-permute-done.14.refs_14_
  78.9 3.6 %shard_map.73 = (f32[16,256]{1,0:T(8,128)S(1)}, f32[8,128]{1,0:T(8,128)}) custom-call(s32[6,40]{1,0:T(8,128)S(1)} %stack.2.lists.scalars, f32[16,128]{1,0:T(8,128)S(1)} %broadcast_in_dim.188.present, bf16[4,256,256]{2,1,0:T(8,128)(2,1)S(1)} %bitcast.28, bf16[4,256,256]{2,1,0:T(8,128)(2,1)S(1)} %collective-permute-done.2.core.refs_1_, ...), custom_call_target="tpu_custom_call" | custom-call | tf_op jit(solution)/shard_map/pallas_call | solution.py:449
  83.1 1.5 %collective-permute-start.18 = (f32[16,256]{1,0:T(8,128)S(1)}, f32[16,256]{1,0:T(8,128)S(1)}, u32[]{:S(2)}, u32[]{:S(2)}) collective-permute-start(f32[16,256]{1,0:T(8,128)S(1)} %get-tuple-element.33.columns), channel_id=1, source_target_pairs={{0,16},{8,24},{16,0},{24,8},{1,17},{9,25},{17,1},{25,9},{2,18},{10... | collective-permute-start | bytes 49160 | tf_op jit(solution)/shard_map/ppermute | solution.py:460
  84.6 1.5 %collective-permute-start.17 = (f32[16,256]{1,0:T(8,128)S(1)}, f32[16,256]{1,0:T(8,128)S(1)}, u32[]{:S(2)}, u32[]{:S(2)}) collective-permute-start(f32[16,256]{1,0:T(8,128)S(1)} %get-tuple-element.33.columns), channel_id=1, source_target_pairs={{0,8},{8,0},{16,24},{24,16},{1,9},{9,1},{17,25},{25,17},{2,10},{10... | collective-permute-start | bytes 49160 | tf_op jit(solution)/shard_map/ppermute | solution.py:460
  86.1 1.3 %collective-permute-start.16 = (f32[16,256]{1,0:T(8,128)S(1)}, f32[16,256]{1,0:T(8,128)S(1)}, u32[]{:S(2)}, u32[]{:S(2)}) collective-permute-start(f32[16,256]{1,0:T(8,128)S(1)} %get-tuple-element.33.columns), channel_id=1, source_target_pairs={{0,4},{1,5},{2,6},{3,7},{4,0},{5,1},{6,2},{7,3},{8,12},{9,13},{10,... | collective-permute-start | bytes 49160 | tf_op jit(solution)/shard_map/ppermute | solution.py:460
  87.4 0.9 %collective-permute-done.17.rest_0_ = f32[16,256]{1,0:T(8,128)S(1)} collective-permute-done((f32[16,256]{1,0:T(8,128)S(1)}, f32[16,256]{1,0:T(8,128)S(1)}, u32[]{:S(2)}, u32[]{:S(2)}) %collective-permute-start.17) | collective-permute-done | bytes 16416 | tf_op jit(solution)/shard_map/ppermute | solution.py:460
  88.3 2.4 %collective-permute-done.16.partner = f32[16,256]{1,0:T(8,128)S(1)} collective-permute-done((f32[16,256]{1,0:T(8,128)S(1)}, f32[16,256]{1,0:T(8,128)S(1)}, u32[]{:S(2)}, u32[]{:S(2)}) %collective-permute-start.16) | collective-permute-done | bytes 16416 | tf_op jit(solution)/shard_map/ppermute | solution.py:460
  90.7 1.2 %shard_map.74 = f32[8,128]{1,0:T(8,128)} custom-call(s32[6,40]{1,0:T(8,128)S(1)} %stack.2.lists.scalars, f32[16,256]{1,0:T(8,128)S(1)} %get-tuple-element.33.columns, f32[16,256]{1,0:T(8,128)S(1)} %collective-permute-done.16.partner, f32[16,256]{1,0:T(8,128)S(1)} %collective-permute-done.17.rest_0_, f32[16,256]{1,0:T(8,128)S(1)} %collective-permute-done.18.rest_1_, ...), custom_call_target="tpu_custom_call" | custom-call | tf_op jit(solution)/shard_map/pallas_call | solution.py:449
  (72 shorter events, 4.0 us)
Async XLA Ops:
  0.6 6.8 %collective-permute-start = (s32[4,8]{1,0:T(4,128)}, s32[4,8]{1,0:T(4,128)S(1)}, u32[]{:S(2)}, u32[]{:S(2)}) collective-permute-start(s32[4,8]{1,0:T(4,128)} %param.9), channel_id=1, source_target_pairs={{0,2},{1,3},{2,0},{3,1},{4,6},{5,7},{6,4},{7,5},{8,10},{9,11},{10,... | collective-permute-start | bytes 392 | tf_op jit(solution)/shard_map/ppermute | solution.py:460
  3.7 24.8 %collective-permute-start.3 = (bf16[4,256,256]{2,1,0:T(8,128)(2,1)}, bf16[4,256,256]{2,1,0:T(8,128)(2,1)S(1)}, u32[]{:S(2)}, u32[]{:S(2)}) collective-permute-start(bf16[4,256,256]{2,1,0:T(8,128)(2,1)} %bitcast.22), channel_id=1, source_target_pairs={{0,2},{1,3},{2,0},{3,1},{4,6},{5,7},{6,4},{7,5},{8,10},{9,11},{10,... | collective-permute-start | bytes 1572872 | tf_op jit(solution)/shard_map/ppermute | solution.py:460
  3.8 25.6 %collective-permute-start.5 = (bf16[4,256,256]{2,1,0:T(8,128)(2,1)}, bf16[4,256,256]{2,1,0:T(8,128)(2,1)S(1)}, u32[]{:S(2)}, u32[]{:S(2)}) collective-permute-start(bf16[4,256,256]{2,1,0:T(8,128)(2,1)} %bitcast.15), channel_id=1, source_target_pairs={{0,4},{1,5},{2,6},{3,7},{4,0},{5,1},{6,2},{7,3},{8,12},{9,13},{10,... | collective-permute-start | bytes 1572872 | tf_op jit(solution)/shard_map/ppermute | solution.py:460
  7.3 0.7 copy-start.4
  8.0 4.2 %collective-permute-start.1 = (s32[8,8]{1,0:T(8,128)S(1)}, s32[8,8]{1,0:T(8,128)S(1)}, u32[]{:S(2)}, u32[]{:S(2)}) collective-permute-start(s32[8,8]{1,0:T(8,128)S(1)} %pad_add_fusion.1), channel_id=1, source_target_pairs={{0,1},{1,0},{2,3},{3,2},{4,5},{5,4},{6,7},{7,6},{8,9},{9,8},{10,11... | collective-permute-start | bytes 776 | tf_op jit(solution)/shard_map/ppermute | solution.py:460
  8.0 3.9 %copy-start.1 = (bf16[1024,256]{1,0:T(8,128)(2,1)S(1)}, bf16[1024,256]{1,0:T(8,128)(2,1)}, u32[]{:S(2)}) copy-start(bf16[1024,256]{1,0:T(8,128)(2,1)} %param.5) | copy-start | bytes 1572868
  8.1 12.5 %copy-start = (bf16[1024,256]{1,0:T(8,128)(2,1)S(1)}, bf16[1024,256]{1,0:T(8,128)(2,1)}, u32[]{:S(2)}) copy-start(bf16[1024,256]{1,0:T(8,128)(2,1)} %param.6) | copy-start | bytes 1572868
  8.1 12.5 %all-to-all-start = ((bf16[4,256,256]{2,1,0:T(8,128)(2,1)}), bf16[4,256,256]{2,1,0:T(8,128)(2,1)S(1)}, u32[]{:S(2)}, u32[]{:S(2)}) async-start(bf16[4,256,256]{2,1,0:T(8,128)(2,1)} %bitcast.16), calls=%async_computation | async-start | bytes 1048576 | tf_op jit(solution)/shard_map/all_to_all | solution.py:539
  11.9 8.7 %collective-permute-start.2 = (bf16[4,256,256]{2,1,0:T(8,128)(2,1)S(1)}, bf16[4,256,256]{2,1,0:T(8,128)(2,1)S(1)}, u32[]{:S(2)}, u32[]{:S(2)}) collective-permute-start(bf16[4,256,256]{2,1,0:T(8,128)(2,1)S(1)} %bitcast.23), channel_id=1, source_target_pairs={{0,1},{1,0},{2,3},{3,2},{4,5},{5,4},{6,7},{7,6},{8,9},{9,8},{10,11... | collective-permute-start | bytes 1572872 | tf_op jit(solution)/shard_map/ppermute | solution.py:460
  20.6 8.0 %copy-start.2 = (f32[1024]{0:T(1024)S(1)}, f32[1024]{0:T(1024)}, u32[]{:S(2)}) copy-start(f32[1024]{0:T(1024)} %param.7) | copy-start | bytes 12292
  28.5 2.0 %collective-permute-start.4 = (bf16[4,256,256]{2,1,0:T(8,128)(2,1)S(1)}, bf16[4,256,256]{2,1,0:T(8,128)(2,1)}, u32[]{:S(2)}, u32[]{:S(2)}) collective-permute-start(bf16[4,256,256]{2,1,0:T(8,128)(2,1)S(1)} %collective-permute-done.3.refs_2_), channel_id=1, source_target_pairs={{0,1},{1,0},{2,3},{3,2},{4,5},{5,4},{6,7},{7,6},{8,9},{9,8},{10,11... | collective-permute-start | bytes 1572872 | tf_op jit(solution)/shard_map/ppermute | solution.py:460
  28.6 0.7 copy-start.3
  40.6 3.3 %collective-permute-start.8 = (f32[24,256]{1,0:T(8,128)S(1)}, f32[24,256]{1,0:T(8,128)S(1)}, u32[]{:S(2)}, u32[]{:S(2)}) collective-permute-start(f32[24,256]{1,0:T(8,128)S(1)} %shard_map.69.refs_7_), channel_id=1, source_target_pairs={{0,3},{1,2},{2,1},{3,0},{4,7},{5,6},{6,5},{7,4},{8,11},{9,10},{10,... | collective-permute-start | bytes 73736 | tf_op jit(solution)/shard_map/ppermute | solution.py:460
  40.7 4.0 %collective-permute-start.7 = (f32[24,256]{1,0:T(8,128)S(1)}, f32[24,256]{1,0:T(8,128)S(1)}, u32[]{:S(2)}, u32[]{:S(2)}) collective-permute-start(f32[24,256]{1,0:T(8,128)S(1)} %shard_map.69.refs_7_), channel_id=1, source_target_pairs={{0,2},{1,3},{2,0},{3,1},{4,6},{5,7},{6,4},{7,5},{8,10},{9,11},{10,... | collective-permute-start | bytes 73736 | tf_op jit(solution)/shard_map/ppermute | solution.py:460
  42.5 2.3 %collective-permute-start.6 = (f32[24,256]{1,0:T(8,128)S(1)}, f32[24,256]{1,0:T(8,128)S(1)}, u32[]{:S(2)}, u32[]{:S(2)}) collective-permute-start(f32[24,256]{1,0:T(8,128)S(1)} %shard_map.69.refs_7_), channel_id=1, source_target_pairs={{0,1},{1,0},{2,3},{3,2},{4,5},{5,4},{6,7},{7,6},{8,9},{9,8},{10,11... | collective-permute-start | bytes 73736 | tf_op jit(solution)/shard_map/ppermute | solution.py:460
  47.8 4.7 %collective-permute-start.9 = (f32[16,256]{1,0:T(8,128)S(1)}, f32[16,256]{1,0:T(8,128)S(1)}, u32[]{:S(2)}, u32[]{:S(2)}) collective-permute-start(f32[16,256]{1,0:T(8,128)S(1)} %get-tuple-element.26.columns.refs_8_), channel_id=1, source_target_pairs={{0,4},{1,5},{2,6},{3,7},{4,0},{5,1},{6,2},{7,3},{8,12},{9,13},{10,... | collective-permute-start | bytes 49160 | tf_op jit(solution)/shard_map/ppermute | solution.py:460
  53.2 3.7 %collective-permute-start.10 = (f32[4,256]{1,0:T(4,128)S(1)}, f32[4,256]{1,0:T(4,128)S(1)}, u32[]{:S(2)}, u32[]{:S(2)}) collective-permute-start(f32[4,256]{1,0:T(4,128)S(1)} %get-tuple-element.27), channel_id=1, source_target_pairs={{0,8},{8,0},{16,24},{24,16},{1,9},{9,1},{17,25},{25,17},{2,10},{10... | collective-permute-start | bytes 12296 | tf_op jit(solution)/shard_map/ppermute | solution.py:460
  54.7 3.6 %collective-permute-start.11 = (f32[4,256]{1,0:T(4,128)S(1)}, f32[4,256]{1,0:T(4,128)S(1)}, u32[]{:S(2)}, u32[]{:S(2)}) collective-permute-start(f32[4,256]{1,0:T(4,128)S(1)} %get-tuple-element.28), channel_id=1, source_target_pairs={{0,16},{8,24},{16,0},{24,8},{1,17},{9,25},{17,1},{25,9},{2,18},{10... | collective-permute-start | bytes 12296 | tf_op jit(solution)/shard_map/ppermute | solution.py:460
  56.2 4.5 %collective-permute-start.12 = (f32[4,256]{1,0:T(4,128)S(1)}, f32[4,256]{1,0:T(4,128)S(1)}, u32[]{:S(2)}, u32[]{:S(2)}) collective-permute-start(f32[4,256]{1,0:T(4,128)S(1)} %get-tuple-element.29), channel_id=1, source_target_pairs={{0,24},{8,16},{16,8},{24,0},{1,25},{9,17},{17,9},{25,1},{2,26},{10... | collective-permute-start | bytes 12296 | tf_op jit(solution)/shard_map/ppermute | solution.py:460
  75.0 3.3 %collective-permute-start.15 = (f32[16,256]{1,0:T(8,128)S(1)}, f32[16,256]{1,0:T(8,128)S(1)}, u32[]{:S(2)}, u32[]{:S(2)}) collective-permute-start(f32[16,256]{1,0:T(8,128)S(1)} %get-tuple-element.30.refs_12_), channel_id=1, source_target_pairs={{0,3},{1,2},{2,1},{3,0},{4,7},{5,6},{6,5},{7,4},{8,11},{9,10},{10,... | collective-permute-start | bytes 49160 | tf_op jit(solution)/shard_map/ppermute | solution.py:460
  75.1 3.8 %collective-permute-start.14 = (f32[16,256]{1,0:T(8,128)S(1)}, f32[16,256]{1,0:T(8,128)S(1)}, u32[]{:S(2)}, u32[]{:S(2)}) collective-permute-start(f32[16,256]{1,0:T(8,128)S(1)} %get-tuple-element.30.refs_12_), channel_id=1, source_target_pairs={{0,2},{1,3},{2,0},{3,1},{4,6},{5,7},{6,4},{7,5},{8,10},{9,11},{10,... | collective-permute-start | bytes 49160 | tf_op jit(solution)/shard_map/ppermute | solution.py:460
  76.8 2.2 %collective-permute-start.13 = (f32[16,256]{1,0:T(8,128)S(1)}, f32[16,256]{1,0:T(8,128)S(1)}, u32[]{:S(2)}, u32[]{:S(2)}) collective-permute-start(f32[16,256]{1,0:T(8,128)S(1)} %get-tuple-element.30.refs_12_), channel_id=1, source_target_pairs={{0,1},{1,0},{2,3},{3,2},{4,5},{5,4},{6,7},{7,6},{8,9},{9,8},{10,11... | collective-permute-start | bytes 49160 | tf_op jit(solution)/shard_map/ppermute | solution.py:460
  82.5 4.8 %collective-permute-start.19 = (f32[16,256]{1,0:T(8,128)S(1)}, f32[16,256]{1,0:T(8,128)S(1)}, u32[]{:S(2)}, u32[]{:S(2)}) collective-permute-start(f32[16,256]{1,0:T(8,128)S(1)} %get-tuple-element.33.columns), channel_id=1, source_target_pairs={{0,24},{8,16},{16,8},{24,0},{1,25},{9,17},{17,9},{25,1},{2,26},{10... | collective-permute-start | bytes 49160 | tf_op jit(solution)/shard_map/ppermute | solution.py:460
  83.1 4.3 %collective-permute-start.18 = (f32[16,256]{1,0:T(8,128)S(1)}, f32[16,256]{1,0:T(8,128)S(1)}, u32[]{:S(2)}, u32[]{:S(2)}) collective-permute-start(f32[16,256]{1,0:T(8,128)S(1)} %get-tuple-element.33.columns), channel_id=1, source_target_pairs={{0,16},{8,24},{16,0},{24,8},{1,17},{9,25},{17,1},{25,9},{2,18},{10... | collective-permute-start | bytes 49160 | tf_op jit(solution)/shard_map/ppermute | solution.py:460
  84.6 3.7 %collective-permute-start.17 = (f32[16,256]{1,0:T(8,128)S(1)}, f32[16,256]{1,0:T(8,128)S(1)}, u32[]{:S(2)}, u32[]{:S(2)}) collective-permute-start(f32[16,256]{1,0:T(8,128)S(1)} %get-tuple-element.33.columns), channel_id=1, source_target_pairs={{0,8},{8,0},{16,24},{24,16},{1,9},{9,1},{17,25},{25,17},{2,10},{10... | collective-permute-start | bytes 49160 | tf_op jit(solution)/shard_map/ppermute | solution.py:460
  86.1 4.6 %collective-permute-start.16 = (f32[16,256]{1,0:T(8,128)S(1)}, f32[16,256]{1,0:T(8,128)S(1)}, u32[]{:S(2)}, u32[]{:S(2)}) collective-permute-start(f32[16,256]{1,0:T(8,128)S(1)} %get-tuple-element.33.columns), channel_id=1, source_target_pairs={{0,4},{1,5},{2,6},{3,7},{4,0},{5,1},{6,2},{7,3},{8,12},{9,13},{10,... | collective-permute-start | bytes 49160 | tf_op jit(solution)/shard_map/ppermute | solution.py:460

commit v7 on v6

--- a/solution.py
+++ b/solution.py
@@ -359,9 +359,10 @@
     reference[...] = jnp.broadcast_to(-largest, reference.shape)
 
 
-def first_kernel(lists, present, *refs):
-    sources, targets = refs[0:4], refs[4:7]
-    reference, early, mass, out, total, *work = refs[7:]
+def first_kernel(lists, present, cross, *refs):
+    near_sources, targets = refs[0:3], refs[3:6]
+    reference, early, mass, out, far_source, total, *work = refs[6:]
+    far_source[...] = cross[...]
     out[16:20, :] = mass[...]
     out[20:24, :] = jnp.zeros((4, out.shape[1]), jnp.float32)
 
@@ -369,7 +370,17 @@
         out[0:16, :] = merge([early[...], result])
 
     guarded_pass(
-        lists, present, True, LATE, sources, targets, None, reference[0:1, 0:1], total, work, write
+        lists,
+        present,
+        True,
+        LATE,
+        (*near_sources, cross),
+        targets,
+        None,
+        reference[0:1, 0:1],
+        total,
+        work,
+        write,
     )
 
 
@@ -387,7 +398,7 @@
         for block in range(4):
             for half in range(2):
                 second[2 * block + half : 2 * block + half + 1, :] = (
-                    TO_POTENTIAL * rows[block : block + 1, 128 * half : 128 * (half + 1)]
+                    rows[block : block + 1, 128 * half : 128 * (half + 1)]
                 )
     else:
         second[...] = jnp.broadcast_to(middle([rows]), second.shape)
@@ -445,11 +456,10 @@
 
 def call(kernel, inputs, outs, scratch=()):
     whole = pl.BlockSpec(memory_space=VMEM)
-    scalar = pl.BlockSpec(memory_space=SMEM)
     return pl.pallas_call(
         kernel,
         out_shape=outs,
-        in_specs=[scalar] + [whole] * (len(inputs) - 1),
+        in_specs=[pl.BlockSpec(memory_space=SMEM)] + [whole] * (len(inputs) - 1),
         out_specs=[whole] * len(outs),
         scratch_shapes=list(scratch),
         compiler_params=pltpu.CompilerParams(vmem_limit_bytes=16 << 20),
@@ -561,13 +571,17 @@
     )
     source_near, early = lax.optimization_barrier((source_near, early))
     source_cross = member_swap(source_near, 1)
-    blocks = [source_own, source_core, source_near, source_cross, target_own, target_far, mirrors]
-    (parts,) = call(
+    sources, targets = [source_own, source_core, source_near], [target_own, target_far, mirrors]
+    parts, source_cross = call(
         first_kernel,
-        [lists, has_late, *blocks, reference, early, own_source_mass],
-        [jax.ShapeDtypeStruct((24, block_rows), jnp.float32)],
+        [lists, has_late, source_cross, *sources, *targets, reference, early, own_source_mass],
+        [
+            jax.ShapeDtypeStruct((24, block_rows), jnp.float32),
+            jax.ShapeDtypeStruct(blocked, source_vectors.dtype),
+        ],
         pass_buffers,
     )
+    blocks = [*sources, source_cross, *targets]
     masses, extra = [], []
     for step in range(ITERS):
         last_pass = step == ITERS - 1
@@ -602,7 +616,7 @@
         [flat],
         [VMEM((8, block_rows), jnp.float32)],
     )
-    return potential.reshape(source_mass.shape), final.reshape(target_mass.shape)
+    return (TO_POTENTIAL * potential).reshape(source_mass.shape), final.reshape(target_mass.shape)
 
 
 def shards(source_vectors, target_vectors, source_mass, target_mass, candidates):

time: 92.4 us -> 90.5 us (0.979)
  waiting for transfers between devices: 29.3 us -> 26.9 us
  Pallas kernels: 34.6 us -> 32.7 us
  starting transfers between devices: 23.8 us -> 25.7 us
    ppermute x20, waiting for transfers between devices: 21.8 us -> 19.5 us  [swap(): lax.ppermute(values, axis, [(index, index ^ bit) for index in range(size)])]
    ppermute x20, starting transfers between devices: 20 us -> 22 us  [swap(): lax.ppermute(values, axis, [(index, index ^ bit) for index in range(size)])]
    pallas_call x7, Pallas kernels: 34.6 us -> 32.7 us  [call(): pl.pallas_call(kernel, out_shape=outs, in_specs=[pl.BlockSpec(memory_spac...]
  transfers between devices with their start and end apart: 21 -> 21, of which waited for: 12 -> 11; matrix products, arithmetic and copies ran while one was open for 2% -> 3% of each run, Pallas kernels for 2% -> 2%
where the time goes in v7:
time: 90.5 us; the launch traced here: 90.2 us
  Pallas kernels  32.7 us (36%)
  waiting for transfers between devices  26.9 us (30%)
  starting transfers between devices  25.7 us (28%)
  local copies, waits for them, and re-layouts  2.53 us (3%)
  other arithmetic  1.41 us (2%)
    pallas_call x7, Pallas kernels, call(): pl.pallas_call(kernel, out_shape=outs, in_specs=[pl.BlockSpec(memory_spac...  32.7 us
    ppermute x20, starting transfers between devices, swap(): lax.ppermute(values, axis, [(index, index ^ bit) for index in range(size)])  22 us
    ppermute x20, waiting for transfers between devices, swap(): lax.ppermute(values, axis, [(index, index ^ bit) for index in range(size)])  19.5 us
    all_to_all x1, waiting for transfers between devices, shards_quad(): lax.all_to_all(target_late, 'group', split_axis=0, concat_axis=0, tiled=T...  7.42 us
    all_to_all x1, starting transfers between devices, shards_quad(): lax.all_to_all(target_late, 'group', split_axis=0, concat_axis=0, tiled=T...  3.72 us
  transfers between devices with their start and end apart: 21, of which 11 were waited for; matrix products, arithmetic and copies ran while one was open for 3% of the time, Pallas kernels for 2%

profile of v7, /device:TPU:0, one launch (start us, length us, event | category | flops | bytes accessed | tf_op | source)
XLA Modules:
  0.0 90.2 jit_solution(5564705757016667424)
XLA Ops:
  0.6 3.1 %collective-permute-start = (s32[4,8]{1,0:T(4,128)}, s32[4,8]{1,0:T(4,128)S(1)}, u32[]{:S(2)}, u32[]{:S(2)}) collective-permute-start(s32[4,8]{1,0:T(4,128)} %param.9), channel_id=1, source_target_pairs={{0,2},{1,3},{2,0},{3,1},{4,6},{5,7},{6,4},{7,5},{8,10},{9,11},{10,... | collective-permute-start | bytes 392 | tf_op jit(solution)/shard_map/ppermute | solution.py:470
  3.8 3.0 %collective-permute-start.5 = (bf16[4,256,256]{2,1,0:T(8,128)(2,1)}, bf16[4,256,256]{2,1,0:T(8,128)(2,1)S(1)}, u32[]{:S(2)}, u32[]{:S(2)}) collective-permute-start(bf16[4,256,256]{2,1,0:T(8,128)(2,1)} %bitcast.16), channel_id=1, source_target_pairs={{0,4},{1,5},{2,6},{3,7},{4,0},{5,1},{6,2},{7,3},{8,12},{9,13},{10,... | collective-permute-start | bytes 1572872 | tf_op jit(solution)/shard_map/ppermute | solution.py:470
  7.4 0.6 copy-done.4
  8.6 3.7 %all-to-all-start = ((bf16[4,256,256]{2,1,0:T(8,128)(2,1)}), bf16[4,256,256]{2,1,0:T(8,128)(2,1)S(1)}, u32[]{:S(2)}, u32[]{:S(2)}) async-start(bf16[4,256,256]{2,1,0:T(8,128)(2,1)} %bitcast.17), calls=%async_computation | async-start | bytes 1048576 | tf_op jit(solution)/shard_map/all_to_all | solution.py:549
  13.2 7.4 %all-to-all-done.mirrors.refs_5_.refs_6_ = bf16[4,256,256]{2,1,0:T(8,128)(2,1)S(1)} async-done(((bf16[4,256,256]{2,1,0:T(8,128)(2,1)}), bf16[4,256,256]{2,1,0:T(8,128)(2,1)S(1)}, u32[]{:S(2)}, u32[]{:S(2)}) %all-to-all-start) | async-done | bytes 524320 | tf_op jit(solution)/shard_map/all_to_all | solution.py:549
  20.7 2.0 %shard_map.68 = (f32[16,256]{1,0:T(8,128)S(1)}, f32[8,128]{1,0:T(8,128)S(1)}) custom-call(s32[6,40]{1,0:T(8,128)S(1)} %stack.2.lists.scalars, bf16[4,256,256]{2,1,0:T(8,128)(2,1)S(1)} %bitcast.25, bf16[4,256,256]{2,1,0:T(8,128)(2,1)S(1)} %collective-permute-done.2.core.refs_1_, bf16[4,256,256]{2,1,0:T(8,128)(2,1)S(1)} %bitcast.18, ...), custom_call_target="tpu_custom_call" | custom-call | tf_op jit(solution)/shard_map/pallas_call | solution.py:459
  22.7 5.8 %collective-permute-done.3.refs_2_ = bf16[4,256,256]{2,1,0:T(8,128)(2,1)S(1)} collective-permute-done((bf16[4,256,256]{2,1,0:T(8,128)(2,1)}, bf16[4,256,256]{2,1,0:T(8,128)(2,1)S(1)}, u32[]{:S(2)}, u32[]{:S(2)}) %collective-permute-start.3) | collective-permute-done | bytes 524320 | tf_op jit(solution)/shard_map/ppermute | solution.py:470
  28.6 0.7 copy-done.3
  29.4 1.2 %collective-permute-done.4.cross = bf16[4,256,256]{2,1,0:T(8,128)(2,1)} collective-permute-done((bf16[4,256,256]{2,1,0:T(8,128)(2,1)S(1)}, bf16[4,256,256]{2,1,0:T(8,128)(2,1)}, u32[]{:S(2)}, u32[]{:S(2)}) %collective-permute-start.4) | collective-permute-done | bytes 524320 | tf_op jit(solution)/shard_map/ppermute | solution.py:470
  30.7 10.0 %shard_map.69 = (f32[24,256]{1,0:T(8,128)S(1)}, bf16[4,256,256]{2,1,0:T(8,128)(2,1)S(1)}) custom-call(s32[6,40]{1,0:T(8,128)S(1)} %stack.2.lists.scalars, f32[16,128]{1,0:T(8,128)S(1)} %broadcast_in_dim.190.present, bf16[4,256,256]{2,1,0:T(8,128)(2,1)} %collective-permute-done.4.cross, bf16[4,256,256]{2,1,0:T(8,128)(2,1)S(1)} %bitcast.26, ...), custom_call_target="tpu_custom_call" | custom-call | tf_op jit(solution)/shard_map/pallas_call | solution.py:459
  41.4 1.2 %collective-permute-start.8 = (f32[24,256]{1,0:T(8,128)S(1)}, f32[24,256]{1,0:T(8,128)S(1)}, u32[]{:S(2)}, u32[]{:S(2)}) collective-permute-start(f32[24,256]{1,0:T(8,128)S(1)} %get-tuple-element.28.refs_7_), channel_id=1, source_target_pairs={{0,3},{1,2},{2,1},{3,0},{4,7},{5,6},{6,5},{7,4},{8,11},{9,10},{10,... | collective-permute-start | bytes 73736 | tf_op jit(solution)/shard_map/ppermute | solution.py:470
  42.7 2.2 %collective-permute-done.7.refs_9_ = f32[24,256]{1,0:T(8,128)S(1)} collective-permute-done((f32[24,256]{1,0:T(8,128)S(1)}, f32[24,256]{1,0:T(8,128)S(1)}, u32[]{:S(2)}, u32[]{:S(2)}) %collective-permute-start.7) | collective-permute-done | bytes 24608 | tf_op jit(solution)/shard_map/ppermute | solution.py:470
  45.0 2.5 %shard_map.70 = (f32[16,256]{1,0:T(8,128)S(1)}, f32[8,128]{1,0:T(8,128)S(1)}) custom-call(s32[6,40]{1,0:T(8,128)S(1)} %stack.2.lists.scalars, f32[16,128]{1,0:T(8,128)S(1)} %broadcast_in_dim.188.present, bf16[4,256,256]{2,1,0:T(8,128)(2,1)S(1)} %bitcast.27, bf16[4,256,256]{2,1,0:T(8,128)(2,1)S(1)} %collective-permute-done.2.core.refs_1_, ...), custom_call_target="tpu_custom_call" | custom-call | tf_op jit(solution)/shard_map/pallas_call | solution.py:459
  47.5 2.5 %collective-permute-start.9 = (f32[16,256]{1,0:T(8,128)S(1)}, f32[16,256]{1,0:T(8,128)S(1)}, u32[]{:S(2)}, u32[]{:S(2)}) collective-permute-start(f32[16,256]{1,0:T(8,128)S(1)} %get-tuple-element.30.columns.refs_8_), channel_id=1, source_target_pairs={{0,4},{1,5},{2,6},{3,7},{4,0},{5,1},{6,2},{7,3},{8,12},{9,13},{10,... | collective-permute-start | bytes 49160 | tf_op jit(solution)/shard_map/ppermute | solution.py:470
  50.0 2.2 %collective-permute-done.9.partner.refs_9_ = f32[16,256]{1,0:T(8,128)S(1)} collective-permute-done((f32[16,256]{1,0:T(8,128)S(1)}, f32[16,256]{1,0:T(8,128)S(1)}, u32[]{:S(2)}, u32[]{:S(2)}) %collective-permute-start.9) | collective-permute-done | bytes 16416 | tf_op jit(solution)/shard_map/ppermute | solution.py:470
  52.2 0.6 shard_map.71
  52.9 1.6 %collective-permute-start.10 = (f32[4,256]{1,0:T(4,128)S(1)}, f32[4,256]{1,0:T(4,128)S(1)}, u32[]{:S(2)}, u32[]{:S(2)}) collective-permute-start(f32[4,256]{1,0:T(4,128)S(1)} %get-tuple-element.31), channel_id=1, source_target_pairs={{0,8},{8,0},{16,24},{24,16},{1,9},{9,1},{17,25},{25,17},{2,10},{10... | collective-permute-start | bytes 12296 | tf_op jit(solution)/shard_map/ppermute | solution.py:470
  54.4 1.5 %collective-permute-start.11 = (f32[4,256]{1,0:T(4,128)S(1)}, f32[4,256]{1,0:T(4,128)S(1)}, u32[]{:S(2)}, u32[]{:S(2)}) collective-permute-start(f32[4,256]{1,0:T(4,128)S(1)} %get-tuple-element.32), channel_id=1, source_target_pairs={{0,16},{8,24},{16,0},{24,8},{1,17},{9,25},{17,1},{25,9},{2,18},{10... | collective-permute-start | bytes 12296 | tf_op jit(solution)/shard_map/ppermute | solution.py:470
  56.5 1.5 %collective-permute-done.11.refs_11_ = f32[4,256]{1,0:T(4,128)S(1)} collective-permute-done((f32[4,256]{1,0:T(4,128)S(1)}, f32[4,256]{1,0:T(4,128)S(1)}, u32[]{:S(2)}, u32[]{:S(2)}) %collective-permute-start.11) | collective-permute-done | bytes 4128 | tf_op jit(solution)/shard_map/ppermute | solution.py:470
  58.0 2.4 %collective-permute-done.12.refs_12_ = f32[4,256]{1,0:T(4,128)S(1)} collective-permute-done((f32[4,256]{1,0:T(4,128)S(1)}, f32[4,256]{1,0:T(4,128)S(1)}, u32[]{:S(2)}, u32[]{:S(2)}) %collective-permute-start.12) | collective-permute-done | bytes 4128 | tf_op jit(solution)/shard_map/ppermute | solution.py:470
  60.5 13.8 %shard_map.72 = (f32[16,256]{1,0:T(8,128)S(1)}, f32[8,128]{1,0:T(8,128)S(1)}) custom-call(s32[6,40]{1,0:T(8,128)S(1)} %stack.2.lists.scalars, f32[16,128]{1,0:T(8,128)S(1)} %broadcast_in_dim.191.present, bf16[4,256,256]{2,1,0:T(8,128)(2,1)S(1)} %bitcast.28, bf16[4,256,256]{2,1,0:T(8,128)(2,1)S(1)} %collective-permute-done.2.core.refs_1_, ...), custom_call_target="tpu_custom_call" | custom-call | tf_op jit(solution)/shard_map/pallas_call | solution.py:459
  74.4 1.3 %collective-permute-start.14 = (f32[16,256]{1,0:T(8,128)S(1)}, f32[16,256]{1,0:T(8,128)S(1)}, u32[]{:S(2)}, u32[]{:S(2)}) collective-permute-start(f32[16,256]{1,0:T(8,128)S(1)} %get-tuple-element.34.refs_12_), channel_id=1, source_target_pairs={{0,2},{1,3},{2,0},{3,1},{4,6},{5,7},{6,4},{7,5},{8,10},{9,11},{10,... | collective-permute-start | bytes 49160 | tf_op jit(solution)/shard_map/ppermute | solution.py:470
  75.7 0.6 collective-permute-start.15
  76.3 1.9 %collective-permute-done.14.refs_14_ = f32[16,256]{1,0:T(8,128)S(1)} collective-permute-done((f32[16,256]{1,0:T(8,128)S(1)}, f32[16,256]{1,0:T(8,128)S(1)}, u32[]{:S(2)}, u32[]{:S(2)}) %collective-permute-start.14) | collective-permute-done | bytes 16416 | tf_op jit(solution)/shard_map/ppermute | solution.py:470
  78.2 0.6 collective-permute-done.15.refs_15_
  78.9 2.5 %shard_map.73 = (f32[16,256]{1,0:T(8,128)S(1)}, f32[8,128]{1,0:T(8,128)S(1)}) custom-call(s32[6,40]{1,0:T(8,128)S(1)} %stack.2.lists.scalars, f32[16,128]{1,0:T(8,128)S(1)} %broadcast_in_dim.188.present, bf16[4,256,256]{2,1,0:T(8,128)(2,1)S(1)} %bitcast.29, bf16[4,256,256]{2,1,0:T(8,128)(2,1)S(1)} %collective-permute-done.2.core.refs_1_, ...), custom_call_target="tpu_custom_call" | custom-call | tf_op jit(solution)/shard_map/pallas_call | solution.py:459
  81.4 1.9 %collective-permute-start.16 = (f32[16,256]{1,0:T(8,128)S(1)}, f32[16,256]{1,0:T(8,128)S(1)}, u32[]{:S(2)}, u32[]{:S(2)}) collective-permute-start(f32[16,256]{1,0:T(8,128)S(1)} %get-tuple-element.37.columns), channel_id=1, source_target_pairs={{0,4},{1,5},{2,6},{3,7},{4,0},{5,1},{6,2},{7,3},{8,12},{9,13},{10,... | collective-permute-start | bytes 49160 | tf_op jit(solution)/shard_map/ppermute | solution.py:470
  83.3 0.6 collective-permute-start.17
  84.4 2.5 %collective-permute-start.19 = (f32[16,256]{1,0:T(8,128)S(1)}, f32[16,256]{1,0:T(8,128)S(1)}, u32[]{:S(2)}, u32[]{:S(2)}) collective-permute-start(f32[16,256]{1,0:T(8,128)S(1)} %get-tuple-element.37.columns), channel_id=1, source_target_pairs={{0,24},{8,16},{16,8},{24,0},{1,25},{9,17},{17,9},{25,1},{2,26},{10... | collective-permute-start | bytes 49160 | tf_op jit(solution)/shard_map/ppermute | solution.py:470
  86.8 0.6 multiply_bitcast_fusion
  87.6 1.4 %collective-permute-done.19.rest_2_ = f32[16,256]{1,0:T(8,128)S(1)} collective-permute-done((f32[16,256]{1,0:T(8,128)S(1)}, f32[16,256]{1,0:T(8,128)S(1)}, u32[]{:S(2)}, u32[]{:S(2)}) %collective-permute-start.19) | collective-permute-done | bytes 16416 | tf_op jit(solution)/shard_map/ppermute | solution.py:470
  89.0 1.2 %shard_map.74 = f32[8,128]{1,0:T(8,128)} custom-call(s32[6,40]{1,0:T(8,128)S(1)} %stack.2.lists.scalars, f32[16,256]{1,0:T(8,128)S(1)} %get-tuple-element.37.columns, f32[16,256]{1,0:T(8,128)S(1)} %collective-permute-done.16.partner, f32[16,256]{1,0:T(8,128)S(1)} %collective-permute-done.17.rest_0_, f32[16,256]{1,0:T(8,128)S(1)} %collective-permute-done.18.rest_1_, ...), custom_call_target="tpu_custom_call" | custom-call | tf_op jit(solution)/shard_map/pallas_call | solution.py:459
  (73 shorter events, 4.7 us)
Async XLA Ops:
  0.6 6.8 %collective-permute-start = (s32[4,8]{1,0:T(4,128)}, s32[4,8]{1,0:T(4,128)S(1)}, u32[]{:S(2)}, u32[]{:S(2)}) collective-permute-start(s32[4,8]{1,0:T(4,128)} %param.9), channel_id=1, source_target_pairs={{0,2},{1,3},{2,0},{3,1},{4,6},{5,7},{6,4},{7,5},{8,10},{9,11},{10,... | collective-permute-start | bytes 392 | tf_op jit(solution)/shard_map/ppermute | solution.py:470
  3.7 24.8 %collective-permute-start.3 = (bf16[4,256,256]{2,1,0:T(8,128)(2,1)}, bf16[4,256,256]{2,1,0:T(8,128)(2,1)S(1)}, u32[]{:S(2)}, u32[]{:S(2)}) collective-permute-start(bf16[4,256,256]{2,1,0:T(8,128)(2,1)} %bitcast.23), channel_id=1, source_target_pairs={{0,2},{1,3},{2,0},{3,1},{4,6},{5,7},{6,4},{7,5},{8,10},{9,11},{10,... | collective-permute-start | bytes 1572872 | tf_op jit(solution)/shard_map/ppermute | solution.py:470
  3.8 25.6 %collective-permute-start.5 = (bf16[4,256,256]{2,1,0:T(8,128)(2,1)}, bf16[4,256,256]{2,1,0:T(8,128)(2,1)S(1)}, u32[]{:S(2)}, u32[]{:S(2)}) collective-permute-start(bf16[4,256,256]{2,1,0:T(8,128)(2,1)} %bitcast.16), channel_id=1, source_target_pairs={{0,4},{1,5},{2,6},{3,7},{4,0},{5,1},{6,2},{7,3},{8,12},{9,13},{10,... | collective-permute-start | bytes 1572872 | tf_op jit(solution)/shard_map/ppermute | solution.py:470
  7.3 0.7 copy-start.4
  8.0 4.3 %collective-permute-start.1 = (s32[8,8]{1,0:T(8,128)S(1)}, s32[8,8]{1,0:T(8,128)S(1)}, u32[]{:S(2)}, u32[]{:S(2)}) collective-permute-start(s32[8,8]{1,0:T(8,128)S(1)} %pad_add_fusion.1), channel_id=1, source_target_pairs={{0,1},{1,0},{2,3},{3,2},{4,5},{5,4},{6,7},{7,6},{8,9},{9,8},{10,11... | collective-permute-start | bytes 776 | tf_op jit(solution)/shard_map/ppermute | solution.py:470
  8.0 12.6 %copy-start = (bf16[1024,256]{1,0:T(8,128)(2,1)S(1)}, bf16[1024,256]{1,0:T(8,128)(2,1)}, u32[]{:S(2)}) copy-start(bf16[1024,256]{1,0:T(8,128)(2,1)} %param.6) | copy-start | bytes 1572868
  8.0 12.6 %copy-start.1 = (bf16[1024,256]{1,0:T(8,128)(2,1)S(1)}, bf16[1024,256]{1,0:T(8,128)(2,1)}, u32[]{:S(2)}) copy-start(bf16[1024,256]{1,0:T(8,128)(2,1)} %param.5) | copy-start | bytes 1572868
  8.1 12.6 %collective-permute-start.2 = (bf16[4,256,256]{2,1,0:T(8,128)(2,1)}, bf16[4,256,256]{2,1,0:T(8,128)(2,1)S(1)}, u32[]{:S(2)}, u32[]{:S(2)}) collective-permute-start(bf16[4,256,256]{2,1,0:T(8,128)(2,1)} %bitcast.24), channel_id=1, source_target_pairs={{0,1},{1,0},{2,3},{3,2},{4,5},{5,4},{6,7},{7,6},{8,9},{9,8},{10,11... | collective-permute-start | bytes 1572872 | tf_op jit(solution)/shard_map/ppermute | solution.py:470
  8.6 12.1 %all-to-all-start = ((bf16[4,256,256]{2,1,0:T(8,128)(2,1)}), bf16[4,256,256]{2,1,0:T(8,128)(2,1)S(1)}, u32[]{:S(2)}, u32[]{:S(2)}) async-start(bf16[4,256,256]{2,1,0:T(8,128)(2,1)} %bitcast.17), calls=%async_computation | async-start | bytes 1048576 | tf_op jit(solution)/shard_map/all_to_all | solution.py:549
  20.7 7.9 %copy-start.2 = (f32[1024]{0:T(1024)S(1)}, f32[1024]{0:T(1024)}, u32[]{:S(2)}) copy-start(f32[1024]{0:T(1024)} %param.7) | copy-start | bytes 12292
  28.5 2.0 %collective-permute-start.4 = (bf16[4,256,256]{2,1,0:T(8,128)(2,1)S(1)}, bf16[4,256,256]{2,1,0:T(8,128)(2,1)}, u32[]{:S(2)}, u32[]{:S(2)}) collective-permute-start(bf16[4,256,256]{2,1,0:T(8,128)(2,1)S(1)} %collective-permute-done.3.refs_2_), channel_id=1, source_target_pairs={{0,1},{1,0},{2,3},{3,2},{4,5},{5,4},{6,7},{7,6},{8,9},{9,8},{10,11... | collective-permute-start | bytes 1572872 | tf_op jit(solution)/shard_map/ppermute | solution.py:470
  28.6 0.7 copy-start.3
  40.7 2.1 %collective-permute-start.6 = (f32[24,256]{1,0:T(8,128)S(1)}, f32[24,256]{1,0:T(8,128)S(1)}, u32[]{:S(2)}, u32[]{:S(2)}) collective-permute-start(f32[24,256]{1,0:T(8,128)S(1)} %get-tuple-element.28.refs_7_), channel_id=1, source_target_pairs={{0,1},{1,0},{2,3},{3,2},{4,5},{5,4},{6,7},{7,6},{8,9},{9,8},{10,11... | collective-permute-start | bytes 73736 | tf_op jit(solution)/shard_map/ppermute | solution.py:470
  40.9 4.0 %collective-permute-start.7 = (f32[24,256]{1,0:T(8,128)S(1)}, f32[24,256]{1,0:T(8,128)S(1)}, u32[]{:S(2)}, u32[]{:S(2)}) collective-permute-start(f32[24,256]{1,0:T(8,128)S(1)} %get-tuple-element.28.refs_7_), channel_id=1, source_target_pairs={{0,2},{1,3},{2,0},{3,1},{4,6},{5,7},{6,4},{7,5},{8,10},{9,11},{10,... | collective-permute-start | bytes 73736 | tf_op jit(solution)/shard_map/ppermute | solution.py:470
  41.4 3.5 %collective-permute-start.8 = (f32[24,256]{1,0:T(8,128)S(1)}, f32[24,256]{1,0:T(8,128)S(1)}, u32[]{:S(2)}, u32[]{:S(2)}) collective-permute-start(f32[24,256]{1,0:T(8,128)S(1)} %get-tuple-element.28.refs_7_), channel_id=1, source_target_pairs={{0,3},{1,2},{2,1},{3,0},{4,7},{5,6},{6,5},{7,4},{8,11},{9,10},{10,... | collective-permute-start | bytes 73736 | tf_op jit(solution)/shard_map/ppermute | solution.py:470
  47.5 4.7 %collective-permute-start.9 = (f32[16,256]{1,0:T(8,128)S(1)}, f32[16,256]{1,0:T(8,128)S(1)}, u32[]{:S(2)}, u32[]{:S(2)}) collective-permute-start(f32[16,256]{1,0:T(8,128)S(1)} %get-tuple-element.30.columns.refs_8_), channel_id=1, source_target_pairs={{0,4},{1,5},{2,6},{3,7},{4,0},{5,1},{6,2},{7,3},{8,12},{9,13},{10,... | collective-permute-start | bytes 49160 | tf_op jit(solution)/shard_map/ppermute | solution.py:470
  52.9 3.7 %collective-permute-start.10 = (f32[4,256]{1,0:T(4,128)S(1)}, f32[4,256]{1,0:T(4,128)S(1)}, u32[]{:S(2)}, u32[]{:S(2)}) collective-permute-start(f32[4,256]{1,0:T(4,128)S(1)} %get-tuple-element.31), channel_id=1, source_target_pairs={{0,8},{8,0},{16,24},{24,16},{1,9},{9,1},{17,25},{25,17},{2,10},{10... | collective-permute-start | bytes 12296 | tf_op jit(solution)/shard_map/ppermute | solution.py:470
  54.4 3.6 %collective-permute-start.11 = (f32[4,256]{1,0:T(4,128)S(1)}, f32[4,256]{1,0:T(4,128)S(1)}, u32[]{:S(2)}, u32[]{:S(2)}) collective-permute-start(f32[4,256]{1,0:T(4,128)S(1)} %get-tuple-element.32), channel_id=1, source_target_pairs={{0,16},{8,24},{16,0},{24,8},{1,17},{9,25},{17,1},{25,9},{2,18},{10... | collective-permute-start | bytes 12296 | tf_op jit(solution)/shard_map/ppermute | solution.py:470
  56.0 4.5 %collective-permute-start.12 = (f32[4,256]{1,0:T(4,128)S(1)}, f32[4,256]{1,0:T(4,128)S(1)}, u32[]{:S(2)}, u32[]{:S(2)}) collective-permute-start(f32[4,256]{1,0:T(4,128)S(1)} %get-tuple-element.33), channel_id=1, source_target_pairs={{0,24},{8,16},{16,8},{24,0},{1,25},{9,17},{17,9},{25,1},{2,26},{10... | collective-permute-start | bytes 12296 | tf_op jit(solution)/shard_map/ppermute | solution.py:470
  74.4 1.9 %collective-permute-start.13 = (f32[16,256]{1,0:T(8,128)S(1)}, f32[16,256]{1,0:T(8,128)S(1)}, u32[]{:S(2)}, u32[]{:S(2)}) collective-permute-start(f32[16,256]{1,0:T(8,128)S(1)} %get-tuple-element.34.refs_12_), channel_id=1, source_target_pairs={{0,1},{1,0},{2,3},{3,2},{4,5},{5,4},{6,7},{7,6},{8,9},{9,8},{10,11... | collective-permute-start | bytes 49160 | tf_op jit(solution)/shard_map/ppermute | solution.py:470
  74.4 3.8 %collective-permute-start.14 = (f32[16,256]{1,0:T(8,128)S(1)}, f32[16,256]{1,0:T(8,128)S(1)}, u32[]{:S(2)}, u32[]{:S(2)}) collective-permute-start(f32[16,256]{1,0:T(8,128)S(1)} %get-tuple-element.34.refs_12_), channel_id=1, source_target_pairs={{0,2},{1,3},{2,0},{3,1},{4,6},{5,7},{6,4},{7,5},{8,10},{9,11},{10,... | collective-permute-start | bytes 49160 | tf_op jit(solution)/shard_map/ppermute | solution.py:470
  75.7 3.2 %collective-permute-start.15 = (f32[16,256]{1,0:T(8,128)S(1)}, f32[16,256]{1,0:T(8,128)S(1)}, u32[]{:S(2)}, u32[]{:S(2)}) collective-permute-start(f32[16,256]{1,0:T(8,128)S(1)} %get-tuple-element.34.refs_12_), channel_id=1, source_target_pairs={{0,3},{1,2},{2,1},{3,0},{4,7},{5,6},{6,5},{7,4},{8,11},{9,10},{10,... | collective-permute-start | bytes 49160 | tf_op jit(solution)/shard_map/ppermute | solution.py:470
  81.4 6.0 %collective-permute-start.16 = (f32[16,256]{1,0:T(8,128)S(1)}, f32[16,256]{1,0:T(8,128)S(1)}, u32[]{:S(2)}, u32[]{:S(2)}) collective-permute-start(f32[16,256]{1,0:T(8,128)S(1)} %get-tuple-element.37.columns), channel_id=1, source_target_pairs={{0,4},{1,5},{2,6},{3,7},{4,0},{5,1},{6,2},{7,3},{8,12},{9,13},{10,... | collective-permute-start | bytes 49160 | tf_op jit(solution)/shard_map/ppermute | solution.py:470
  83.3 4.1 %collective-permute-start.17 = (f32[16,256]{1,0:T(8,128)S(1)}, f32[16,256]{1,0:T(8,128)S(1)}, u32[]{:S(2)}, u32[]{:S(2)}) collective-permute-start(f32[16,256]{1,0:T(8,128)S(1)} %get-tuple-element.37.columns), channel_id=1, source_target_pairs={{0,8},{8,0},{16,24},{24,16},{1,9},{9,1},{17,25},{25,17},{2,10},{10... | collective-permute-start | bytes 49160 | tf_op jit(solution)/shard_map/ppermute | solution.py:470
  83.9 3.7 %collective-permute-start.18 = (f32[16,256]{1,0:T(8,128)S(1)}, f32[16,256]{1,0:T(8,128)S(1)}, u32[]{:S(2)}, u32[]{:S(2)}) collective-permute-start(f32[16,256]{1,0:T(8,128)S(1)} %get-tuple-element.37.columns), channel_id=1, source_target_pairs={{0,16},{8,24},{16,0},{24,8},{1,17},{9,25},{17,1},{25,9},{2,18},{10... | collective-permute-start | bytes 49160 | tf_op jit(solution)/shard_map/ppermute | solution.py:470
  84.4 4.6 %collective-permute-start.19 = (f32[16,256]{1,0:T(8,128)S(1)}, f32[16,256]{1,0:T(8,128)S(1)}, u32[]{:S(2)}, u32[]{:S(2)}) collective-permute-start(f32[16,256]{1,0:T(8,128)S(1)} %get-tuple-element.37.columns), channel_id=1, source_target_pairs={{0,24},{8,16},{16,8},{24,0},{1,25},{9,17},{17,9},{25,1},{2,26},{10... | collective-permute-start | bytes 49160 | tf_op jit(solution)/shard_map/ppermute | solution.py:470

commit v8 on v7

--- a/solution.py
+++ b/solution.py
@@ -206,14 +206,14 @@
     return mass - merge([own, core, near, cross])
 
 
-def target_bias(scalars, columns, partner, mirrors, scratch):
-    group = scalars[0, GROUP_AT]
-    scratch[...] = jnp.full(scratch.shape, very_low, jnp.float32)
+def target_bias(chosen, columns, partner, mirrors):
+    own_across = far_across = jnp.full((4, columns.shape[1]), very_low, jnp.float32)
     for offset, ref in enumerate(mirrors, 1):
-        scratch[pl.ds(group ^ offset, 1), :] = ref[0:1]
-        scratch[pl.ds(4 + (group ^ offset), 1), :] = ref[1:2]
-    own = columns[12:16] - merge([columns[0:4], partner[8:12], scratch[0:4]])
-    far = partner[12:16] - merge([columns[8:12], partner[0:4], scratch[4:8]])
+        picked = chosen[8 * offset - 8 : 8 * offset - 4] > 0
+        own_across = jnp.where(picked, ref[0:1], own_across)
+        far_across = jnp.where(picked, ref[1:2], far_across)
+    own = columns[12:16] - merge([columns[0:4], partner[8:12], own_across])
+    far = partner[12:16] - merge([columns[8:12], partner[0:4], far_across])
     across = [
         ref[3:4] - merge([ref[2:3], columns[3 + offset : 4 + offset]])
         for offset, ref in enumerate(mirrors, 1)
@@ -352,14 +352,15 @@
     return 0.5 * (top + bottom)
 
 
-def early_kernel(lists, own, core, target, mirrors, out, reference, tops, sums, ids):
+def early_kernel(lists, wait, own, core, target, mirrors, out, reference, tops, sums, ids):
+    wait()
     result = exact_pass(lists, True, EARLY, (own, core), (target, None, mirrors), tops, sums, ids)
     out[...] = result
     largest = jnp.max(result, axis=(0, 1), keepdims=True)
     reference[...] = jnp.broadcast_to(-largest, reference.shape)
 
 
-def first_kernel(lists, present, cross, *refs):
+def first_kernel(lists, wait, present, cross, *refs):
     near_sources, targets = refs[0:3], refs[3:6]
     reference, early, mass, out, far_source, total, *work = refs[6:]
     far_source[...] = cross[...]
@@ -369,6 +370,7 @@
     def write(result):
         out[0:16, :] = merge([early[...], result])
 
+    wait()
     guarded_pass(
         lists,
         present,
@@ -384,7 +386,7 @@
     )
 
 
-def columns_kernel(last_pass, lists, present, *refs):
+def columns_kernel(last_pass, lists, wait, present, *refs):
     sources, targets = refs[0:4], refs[4:7]
     masses, target_mass, rest = refs[7:11], refs[11], refs[12:]
     parts, shift = masses, None
@@ -407,16 +409,17 @@
     def write(result):
         out[0:TARGET_SLOTS, :] = result
 
+    wait()
     guarded_pass(
         lists, present, False, SECTIONS, sources, targets, bias, shift, total, work, write
     )
 
 
-def rows_kernel(lists, present, *refs):
+def rows_kernel(lists, wait, present, *refs):
     sources, targets = refs[0:4], refs[4:7]
-    shift, columns, partner, *mirrors = refs[7:13]
-    out, second, bias, total, *work, scratch = refs[13:]
-    rows = target_bias(lists, columns, partner, mirrors, scratch)
+    chosen, shift, columns, partner, *mirrors = refs[7:14]
+    out, second, bias, total, *work = refs[14:]
+    rows = target_bias(chosen, columns, partner, mirrors)
     shift = shift[0:1, 0:1]
     spread(rows + shift, bias)
     second[...] = jnp.broadcast_to(middle([rows[0:7], rows[8:12]]), second.shape)
@@ -424,26 +427,28 @@
     def write(result):
         out[...] = result
 
+    wait()
     guarded_pass(lists, present, True, SECTIONS, sources, targets, bias, shift, total, work, write)
 
 
-def forward_kernel(scalars, columns, partner, *outs):
-    group = scalars[0, GROUP_AT]
+def forward_kernel(chosen, columns, partner, *outs):
+    totals = merge([columns[0:4], partner[8:12]])
+    masses = columns[12:16]
     for offset, out in enumerate(outs, 1):
-        block = group ^ offset
+        picked = chosen[8 * offset - 8 : 8 * offset - 4] > 0
         out[0:1, :] = columns[3 + offset : 4 + offset]
         out[1:2, :] = partner[3 + offset : 4 + offset]
-        out[2:3, :] = merge([columns[pl.ds(block, 1), :], partner[pl.ds(FAR + block, 1), :]])
-        out[3:4, :] = columns[pl.ds(12 + block, 1), :]
-
-
-def finish_kernel(scalars, columns, partner, *rest):
-    *mirrors, out, scratch = rest
-    group = scalars[0, GROUP_AT]
-    scratch[...] = jnp.full(scratch.shape, very_low, jnp.float32)
+        out[2:3, :] = jnp.sum(jnp.where(picked, totals, 0.0), axis=0, keepdims=True)
+        out[3:4, :] = jnp.sum(jnp.where(picked, masses, 0.0), axis=0, keepdims=True)
+
+
+def finish_kernel(chosen, columns, partner, *rest):
+    *mirrors, out = rest
+    across = jnp.full((4, columns.shape[1]), very_low, jnp.float32)
     for offset, ref in enumerate(mirrors, 1):
-        scratch[pl.ds(group ^ offset, 1), :] = ref[3 + offset : 4 + offset]
-    rows = columns[12:16] - merge([columns[0:4], partner[8:12], scratch[0:4]])
+        picked = chosen[8 * offset - 8 : 8 * offset - 4] > 0
+        across = jnp.where(picked, ref[3 + offset : 4 + offset], across)
+    rows = columns[12:16] - merge([columns[0:4], partner[8:12], across])
     for block in range(4):
         for half in range(2):
             out[2 * block + half : 2 * block + half + 1, :] = (
@@ -454,16 +459,33 @@
 SMEM, VMEM = pltpu.SMEM, pltpu.VMEM
 
 
-def call(kernel, inputs, outs, scratch=()):
+def call(kernel, inputs, outs, scratch=(), scalar=True):
     whole = pl.BlockSpec(memory_space=VMEM)
+    first = pl.BlockSpec(memory_space=SMEM) if scalar and inputs[0].dtype == jnp.int32 else whole
     return pl.pallas_call(
         kernel,
         out_shape=outs,
-        in_specs=[pl.BlockSpec(memory_space=SMEM)] + [whole] * (len(inputs) - 1),
+        in_specs=[first] + [whole] * (len(inputs) - 1),
         out_specs=[whole] * len(outs),
         scratch_shapes=list(scratch),
         compiler_params=pltpu.CompilerParams(vmem_limit_bytes=16 << 20),
     )(*inputs)
+
+
+def call_tiles(kernel, lists, inputs, outs, scratch=(), early=True):
+    def body(origin, *refs):
+        *refs, scalars, semaphore = refs
+        copy = pltpu.make_async_copy(origin, scalars, semaphore)
+        copy.start()
+        kernel(scalars, copy.wait, *refs)
+
+    def plain(scalars, *refs):
+        kernel(scalars, lambda: None, *refs)
+
+    if early:
+        return call(plain, [lists, *inputs], outs, scratch)
+    extra = [SMEM(lists.shape, lists.dtype), pltpu.SemaphoreType.DMA]
+    return call(body, [lists, *inputs], outs, [*scratch, *extra], False)
 
 
 def swap(values, axis, size, bit):
@@ -553,6 +575,9 @@
         own_member.astype(jnp.int32),
     )
     own_source_mass = LOG2E * source_mass.reshape(per_device, block_rows)
+    marked = jnp.arange(24, dtype=jnp.int32)
+    marked = (marked & 7) == (own_group.astype(jnp.int32) ^ ((marked >> 3) + 1))
+    chosen = jnp.broadcast_to(marked.astype(jnp.float32)[:, None], (24, block_rows))
     own_mass = LOG2E * target_mass.reshape(per_device, block_rows)
 
     side = jax.ShapeDtypeStruct((16, block_rows), jnp.float32)
@@ -566,15 +591,16 @@
     ]
     bias_buffer = VMEM((SOURCE_SLOTS, block_rows, 128), jnp.float32)
 
-    early, reference = call(
-        early_kernel, [lists, source_own, source_core, target_own, mirrors], [side, flat], tile_rows
+    early, reference = call_tiles(
+        early_kernel, lists, [source_own, source_core, target_own, mirrors], [side, flat], tile_rows
     )
     source_near, early = lax.optimization_barrier((source_near, early))
     source_cross = member_swap(source_near, 1)
     sources, targets = [source_own, source_core, source_near], [target_own, target_far, mirrors]
-    parts, source_cross = call(
+    parts, source_cross = call_tiles(
         first_kernel,
-        [lists, has_late, source_cross, *sources, *targets, reference, early, own_source_mass],
+        lists,
+        [has_late, source_cross, *sources, *targets, reference, early, own_source_mass],
         [
             jax.ShapeDtypeStruct((24, block_rows), jnp.float32),
             jax.ShapeDtypeStruct(blocked, source_vectors.dtype),
@@ -587,34 +613,37 @@
         last_pass = step == ITERS - 1
         parts = [parts] + [member_swap(parts, bit) for bit in (1, 2, 3)]
         masses = masses or parts
-        columns, potential = call(
+        columns, potential = call_tiles(
             functools.partial(columns_kernel, last_pass),
-            [lists, has_target, *blocks, *masses, own_mass, *(parts + extra if last_pass else [])],
+            lists,
+            [has_target, *blocks, *masses, own_mass, *(parts + extra if last_pass else [])],
             [side, flat],
             [bias_buffer, *pass_buffers],
+            early=not last_pass,
         )
         partner = member_swap(columns, 4)
         if last_pass:
             break
         sent = call(
             forward_kernel,
-            [lists, columns, partner],
+            [chosen, columns, partner],
             [jax.ShapeDtypeStruct((4, block_rows), jnp.float32)] * 3,
         )
         received = [group_swap(values, bit) for bit, values in enumerate(sent, 1)]
-        parts, shift = call(
+        parts, shift = call_tiles(
             rows_kernel,
-            [lists, has_source, *blocks, potential, columns, partner, *received],
+            lists,
+            [has_source, *blocks, chosen, potential, columns, partner, *received],
             [side, flat],
-            [bias_buffer, *pass_buffers, VMEM((8, block_rows), jnp.float32)],
+            [bias_buffer, *pass_buffers],
+            early=False,
         )
         extra = [shift]
     received = [group_swap(columns, bit) for bit in (1, 2, 3)]
     (final,) = call(
         finish_kernel,
-        [lists, columns, partner, *received],
+        [chosen, columns, partner, *received],
         [flat],
-        [VMEM((8, block_rows), jnp.float32)],
     )
     return (TO_POTENTIAL * potential).reshape(source_mass.shape), final.reshape(target_mass.shape)
 

time: 90.5 us -> 88.9 us (0.982)
  Pallas kernels: 32.7 us -> 31 us
    pallas_call x7, Pallas kernels: 32.7 us -> 31 us  [call(): pl.pallas_call(kernel, out_shape=outs, in_specs=[first] + [whole] * (len(...]
where the time goes in v8:
time: 88.9 us; the launch traced here: 88.6 us
  Pallas kernels  31 us (35%)
  waiting for transfers between devices  26.9 us (30%)
  starting transfers between devices  25.8 us (29%)
  local copies, waits for them, and re-layouts  2.6 us (3%)
  other arithmetic  1.42 us (2%)
  between operations  0.9 us (1%)
    pallas_call x7, Pallas kernels, call(): pl.pallas_call(kernel, out_shape=outs, in_specs=[first] + [whole] * (len(...  31 us
    ppermute x20, starting transfers between devices, swap(): lax.ppermute(values, axis, [(index, index ^ bit) for index in range(size)])  22 us
    ppermute x20, waiting for transfers between devices, swap(): lax.ppermute(values, axis, [(index, index ^ bit) for index in range(size)])  19.5 us
    all_to_all x1, waiting for transfers between devices, shards_quad(): lax.all_to_all(target_late, 'group', split_axis=0, concat_axis=0, tiled=T...  7.42 us
    all_to_all x1, starting transfers between devices, shards_quad(): lax.all_to_all(target_late, 'group', split_axis=0, concat_axis=0, tiled=T...  3.72 us
  transfers between devices with their start and end apart: 21, of which 11 were waited for; matrix products, arithmetic and copies ran while one was open for 3% of the time, Pallas kernels for 2%

profile of v8, /device:TPU:0, one launch (start us, length us, event | category | flops | bytes accessed | tf_op | source)
XLA Modules:
  0.0 88.6 jit_solution(14989647296022074070)
XLA Ops:
  0.6 3.1 %collective-permute-start = (s32[4,8]{1,0:T(4,128)}, s32[4,8]{1,0:T(4,128)S(1)}, u32[]{:S(2)}, u32[]{:S(2)}) collective-permute-start(s32[4,8]{1,0:T(4,128)} %param.9), channel_id=1, source_target_pairs={{0,2},{1,3},{2,0},{3,1},{4,6},{5,7},{6,4},{7,5},{8,10},{9,11},{10,... | collective-permute-start | bytes 392 | tf_op jit(solution)/shard_map/ppermute | solution.py:492
  3.8 3.0 %collective-permute-start.5 = (bf16[4,256,256]{2,1,0:T(8,128)(2,1)}, bf16[4,256,256]{2,1,0:T(8,128)(2,1)S(1)}, u32[]{:S(2)}, u32[]{:S(2)}) collective-permute-start(bf16[4,256,256]{2,1,0:T(8,128)(2,1)} %bitcast.16), channel_id=1, source_target_pairs={{0,4},{1,5},{2,6},{3,7},{4,0},{5,1},{6,2},{7,3},{8,12},{9,13},{10,... | collective-permute-start | bytes 1572872 | tf_op jit(solution)/shard_map/ppermute | solution.py:492
  7.4 0.6 copy-done.4
  8.1 0.5 collective-permute-start.2
  8.6 3.7 %all-to-all-start = ((bf16[4,256,256]{2,1,0:T(8,128)(2,1)}), bf16[4,256,256]{2,1,0:T(8,128)(2,1)S(1)}, u32[]{:S(2)}, u32[]{:S(2)}) async-start(bf16[4,256,256]{2,1,0:T(8,128)(2,1)} %bitcast.17), calls=%async_computation | async-start | bytes 1048576 | tf_op jit(solution)/shard_map/all_to_all | solution.py:571
  13.2 7.4 %all-to-all-done.refs_3_.refs_7_ = bf16[4,256,256]{2,1,0:T(8,128)(2,1)S(1)} async-done(((bf16[4,256,256]{2,1,0:T(8,128)(2,1)}), bf16[4,256,256]{2,1,0:T(8,128)(2,1)S(1)}, u32[]{:S(2)}, u32[]{:S(2)}) %all-to-all-start) | async-done | bytes 524320 | tf_op jit(solution)/shard_map/all_to_all | solution.py:571
  20.7 2.0 %shard_map.68 = (f32[16,256]{1,0:T(8,128)S(1)}, f32[8,128]{1,0:T(8,128)S(1)}) custom-call(s32[6,40]{1,0:T(8,128)S(1)} %stack.2.scalars.origin, bf16[4,256,256]{2,1,0:T(8,128)(2,1)S(1)} %bitcast.25, bf16[4,256,256]{2,1,0:T(8,128)(2,1)S(1)} %collective-permute-done.2.refs_1_.refs_3_.refs_2_, bf16[4,256,256]{2,1,0:T(8,128)(2,1)S(1)} %bitcast.18, ...), custom_call_target="tpu_custom_call" | custom-call | tf_op jit(solution)/shard_map/pallas_call | solution.py:465
  22.7 5.8 %collective-permute-done.3.refs_4_.refs_3_ = bf16[4,256,256]{2,1,0:T(8,128)(2,1)S(1)} collective-permute-done((bf16[4,256,256]{2,1,0:T(8,128)(2,1)}, bf16[4,256,256]{2,1,0:T(8,128)(2,1)S(1)}, u32[]{:S(2)}, u32[]{:S(2)}) %collective-permute-start.3) | collective-permute-done | bytes 524320 | tf_op jit(solution)/shard_map/ppermute | solution.py:492
  28.6 0.7 copy-done.3
  29.4 1.2 %collective-permute-done.4.refs_1_ = bf16[4,256,256]{2,1,0:T(8,128)(2,1)} collective-permute-done((bf16[4,256,256]{2,1,0:T(8,128)(2,1)S(1)}, bf16[4,256,256]{2,1,0:T(8,128)(2,1)}, u32[]{:S(2)}, u32[]{:S(2)}) %collective-permute-start.4) | collective-permute-done | bytes 524320 | tf_op jit(solution)/shard_map/ppermute | solution.py:492
  30.7 10.0 %shard_map.69 = (f32[24,256]{1,0:T(8,128)S(1)}, bf16[4,256,256]{2,1,0:T(8,128)(2,1)S(1)}) custom-call(s32[6,40]{1,0:T(8,128)S(1)} %stack.2.scalars.origin, f32[16,128]{1,0:T(8,128)S(1)} %broadcast_in_dim.196.refs_0_, bf16[4,256,256]{2,1,0:T(8,128)(2,1)} %collective-permute-done.4.refs_1_, bf16[4,256,256]{2,1,0:T(8,128)(2,1)S(1)} %bitcast.26, ...), custom_call_target="tpu_custom_call" | custom-call | tf_op jit(solution)/shard_map/pallas_call | solution.py:465
  41.4 1.2 %collective-permute-start.8 = (f32[24,256]{1,0:T(8,128)S(1)}, f32[24,256]{1,0:T(8,128)S(1)}, u32[]{:S(2)}, u32[]{:S(2)}) collective-permute-start(f32[24,256]{1,0:T(8,128)S(1)} %get-tuple-element.28.refs_8_), channel_id=1, source_target_pairs={{0,3},{1,2},{2,1},{3,0},{4,7},{5,6},{6,5},{7,4},{8,11},{9,10},{10,... | collective-permute-start | bytes 73736 | tf_op jit(solution)/shard_map/ppermute | solution.py:492
  42.7 2.1 %collective-permute-done.7.refs_10_ = f32[24,256]{1,0:T(8,128)S(1)} collective-permute-done((f32[24,256]{1,0:T(8,128)S(1)}, f32[24,256]{1,0:T(8,128)S(1)}, u32[]{:S(2)}, u32[]{:S(2)}) %collective-permute-start.7) | collective-permute-done | bytes 24608 | tf_op jit(solution)/shard_map/ppermute | solution.py:492
  45.0 2.5 %shard_map.70 = (f32[16,256]{1,0:T(8,128)S(1)}, f32[8,128]{1,0:T(8,128)S(1)}) custom-call(s32[6,40]{1,0:T(8,128)S(1)} %stack.2.scalars.origin, f32[16,128]{1,0:T(8,128)S(1)} %broadcast_in_dim.194.refs_0_, bf16[4,256,256]{2,1,0:T(8,128)(2,1)S(1)} %bitcast.27, bf16[4,256,256]{2,1,0:T(8,128)(2,1)S(1)} %collective-permute-done.2.refs_1_.refs_3_.refs_2_, ...), custom_call_target="tpu_custom_call" | custom-call | tf_op jit(solution)/shard_map/pallas_call | solution.py:465
  47.5 2.5 %collective-permute-start.9 = (f32[16,256]{1,0:T(8,128)S(1)}, f32[16,256]{1,0:T(8,128)S(1)}, u32[]{:S(2)}, u32[]{:S(2)}) collective-permute-start(f32[16,256]{1,0:T(8,128)S(1)} %get-tuple-element.30.columns.refs_10_), channel_id=1, source_target_pairs={{0,4},{1,5},{2,6},{3,7},{4,0},{5,1},{6,2},{7,3},{8,12},{9,13},{10,... | collective-permute-start | bytes 49160 | tf_op jit(solution)/shard_map/ppermute | solution.py:492
  50.0 2.3 %collective-permute-done.9.partner.refs_11_ = f32[16,256]{1,0:T(8,128)S(1)} collective-permute-done((f32[16,256]{1,0:T(8,128)S(1)}, f32[16,256]{1,0:T(8,128)S(1)}, u32[]{:S(2)}, u32[]{:S(2)}) %collective-permute-start.9) | collective-permute-done | bytes 16416 | tf_op jit(solution)/shard_map/ppermute | solution.py:492
  52.4 1.5 %collective-permute-start.10 = (f32[4,256]{1,0:T(4,128)S(1)}, f32[4,256]{1,0:T(4,128)S(1)}, u32[]{:S(2)}, u32[]{:S(2)}) collective-permute-start(f32[4,256]{1,0:T(4,128)S(1)} %get-tuple-element.31), channel_id=1, source_target_pairs={{0,8},{8,0},{16,24},{24,16},{1,9},{9,1},{17,25},{25,17},{2,10},{10... | collective-permute-start | bytes 12296 | tf_op jit(solution)/shard_map/ppermute | solution.py:492
  53.9 1.5 %collective-permute-start.11 = (f32[4,256]{1,0:T(4,128)S(1)}, f32[4,256]{1,0:T(4,128)S(1)}, u32[]{:S(2)}, u32[]{:S(2)}) collective-permute-start(f32[4,256]{1,0:T(4,128)S(1)} %get-tuple-element.32), channel_id=1, source_target_pairs={{0,16},{8,24},{16,0},{24,8},{1,17},{9,25},{17,1},{25,9},{2,18},{10... | collective-permute-start | bytes 12296 | tf_op jit(solution)/shard_map/ppermute | solution.py:492
  56.0 1.5 %collective-permute-done.11.refs_13_ = f32[4,256]{1,0:T(4,128)S(1)} collective-permute-done((f32[4,256]{1,0:T(4,128)S(1)}, f32[4,256]{1,0:T(4,128)S(1)}, u32[]{:S(2)}, u32[]{:S(2)}) %collective-permute-start.11) | collective-permute-done | bytes 4128 | tf_op jit(solution)/shard_map/ppermute | solution.py:492
  57.5 2.4 %collective-permute-done.12.refs_14_ = f32[4,256]{1,0:T(4,128)S(1)} collective-permute-done((f32[4,256]{1,0:T(4,128)S(1)}, f32[4,256]{1,0:T(4,128)S(1)}, u32[]{:S(2)}, u32[]{:S(2)}) %collective-permute-start.12) | collective-permute-done | bytes 4128 | tf_op jit(solution)/shard_map/ppermute | solution.py:492
  60.0 13.6 %shard_map.72 = (f32[16,256]{1,0:T(8,128)S(1)}, f32[8,128]{1,0:T(8,128)S(1)}) custom-call(s32[6,40]{1,0:T(8,128)S(1)} %stack.2.scalars.origin, f32[16,128]{1,0:T(8,128)S(1)} %broadcast_in_dim.197.refs_0_, bf16[4,256,256]{2,1,0:T(8,128)(2,1)S(1)} %bitcast.28, bf16[4,256,256]{2,1,0:T(8,128)(2,1)S(1)} %collective-permute-done.2.refs_1_.refs_3_.refs_2_, ...), custom_call_target="tpu_custom_call" | custom-call | tf_op jit(solution)/shard_map/pallas_call | solution.py:465
  73.7 1.3 %collective-permute-start.14 = (f32[16,256]{1,0:T(8,128)S(1)}, f32[16,256]{1,0:T(8,128)S(1)}, u32[]{:S(2)}, u32[]{:S(2)}) collective-permute-start(f32[16,256]{1,0:T(8,128)S(1)} %get-tuple-element.34.refs_13_), channel_id=1, source_target_pairs={{0,2},{1,3},{2,0},{3,1},{4,6},{5,7},{6,4},{7,5},{8,10},{9,11},{10,... | collective-permute-start | bytes 49160 | tf_op jit(solution)/shard_map/ppermute | solution.py:492
  74.9 0.6 collective-permute-start.15
  75.5 1.9 %collective-permute-done.14.refs_15_ = f32[16,256]{1,0:T(8,128)S(1)} collective-permute-done((f32[16,256]{1,0:T(8,128)S(1)}, f32[16,256]{1,0:T(8,128)S(1)}, u32[]{:S(2)}, u32[]{:S(2)}) %collective-permute-start.14) | collective-permute-done | bytes 16416 | tf_op jit(solution)/shard_map/ppermute | solution.py:492
  77.5 0.6 collective-permute-done.15.refs_16_
  78.1 2.2 %shard_map.73 = (f32[16,256]{1,0:T(8,128)S(1)}, f32[8,128]{1,0:T(8,128)S(1)}) custom-call(s32[6,40]{1,0:T(8,128)S(1)} %stack.2.scalars.origin, f32[16,128]{1,0:T(8,128)S(1)} %broadcast_in_dim.194.refs_0_, bf16[4,256,256]{2,1,0:T(8,128)(2,1)S(1)} %bitcast.29, bf16[4,256,256]{2,1,0:T(8,128)(2,1)S(1)} %collective-permute-done.2.refs_1_.refs_3_.refs_2_, ...), custom_call_target="tpu_custom_call" | custom-call | tf_op jit(solution)/shard_map/pallas_call | solution.py:465
  80.3 2.0 %collective-permute-start.16 = (f32[16,256]{1,0:T(8,128)S(1)}, f32[16,256]{1,0:T(8,128)S(1)}, u32[]{:S(2)}, u32[]{:S(2)}) collective-permute-start(f32[16,256]{1,0:T(8,128)S(1)} %get-tuple-element.37.columns), channel_id=1, source_target_pairs={{0,4},{1,5},{2,6},{3,7},{4,0},{5,1},{6,2},{7,3},{8,12},{9,13},{10,... | collective-permute-start | bytes 49160 | tf_op jit(solution)/shard_map/ppermute | solution.py:492
  82.8 0.5 collective-permute-start.18
  83.4 2.5 %collective-permute-start.19 = (f32[16,256]{1,0:T(8,128)S(1)}, f32[16,256]{1,0:T(8,128)S(1)}, u32[]{:S(2)}, u32[]{:S(2)}) collective-permute-start(f32[16,256]{1,0:T(8,128)S(1)} %get-tuple-element.37.columns), channel_id=1, source_target_pairs={{0,24},{8,16},{16,8},{24,0},{1,25},{9,17},{17,9},{25,1},{2,26},{10... | collective-permute-start | bytes 49160 | tf_op jit(solution)/shard_map/ppermute | solution.py:492
  85.8 0.6 multiply_bitcast_fusion
  86.6 1.4 %collective-permute-done.19.rest_2_ = f32[16,256]{1,0:T(8,128)S(1)} collective-permute-done((f32[16,256]{1,0:T(8,128)S(1)}, f32[16,256]{1,0:T(8,128)S(1)}, u32[]{:S(2)}, u32[]{:S(2)}) %collective-permute-start.19) | collective-permute-done | bytes 16416 | tf_op jit(solution)/shard_map/ppermute | solution.py:492
  88.0 0.6 shard_map.74
  (75 shorter events, 4.3 us)
Async XLA Ops:
  0.6 6.8 %collective-permute-start = (s32[4,8]{1,0:T(4,128)}, s32[4,8]{1,0:T(4,128)S(1)}, u32[]{:S(2)}, u32[]{:S(2)}) collective-permute-start(s32[4,8]{1,0:T(4,128)} %param.9), channel_id=1, source_target_pairs={{0,2},{1,3},{2,0},{3,1},{4,6},{5,7},{6,4},{7,5},{8,10},{9,11},{10,... | collective-permute-start | bytes 392 | tf_op jit(solution)/shard_map/ppermute | solution.py:492
  3.7 24.8 %collective-permute-start.3 = (bf16[4,256,256]{2,1,0:T(8,128)(2,1)}, bf16[4,256,256]{2,1,0:T(8,128)(2,1)S(1)}, u32[]{:S(2)}, u32[]{:S(2)}) collective-permute-start(bf16[4,256,256]{2,1,0:T(8,128)(2,1)} %bitcast.23), channel_id=1, source_target_pairs={{0,2},{1,3},{2,0},{3,1},{4,6},{5,7},{6,4},{7,5},{8,10},{9,11},{10,... | collective-permute-start | bytes 1572872 | tf_op jit(solution)/shard_map/ppermute | solution.py:492
  3.8 25.6 %collective-permute-start.5 = (bf16[4,256,256]{2,1,0:T(8,128)(2,1)}, bf16[4,256,256]{2,1,0:T(8,128)(2,1)S(1)}, u32[]{:S(2)}, u32[]{:S(2)}) collective-permute-start(bf16[4,256,256]{2,1,0:T(8,128)(2,1)} %bitcast.16), channel_id=1, source_target_pairs={{0,4},{1,5},{2,6},{3,7},{4,0},{5,1},{6,2},{7,3},{8,12},{9,13},{10,... | collective-permute-start | bytes 1572872 | tf_op jit(solution)/shard_map/ppermute | solution.py:492
  7.3 0.7 copy-start.4
  8.0 4.3 %collective-permute-start.1 = (s32[8,8]{1,0:T(8,128)S(1)}, s32[8,8]{1,0:T(8,128)S(1)}, u32[]{:S(2)}, u32[]{:S(2)}) collective-permute-start(s32[8,8]{1,0:T(8,128)S(1)} %pad_add_fusion.1), channel_id=1, source_target_pairs={{0,1},{1,0},{2,3},{3,2},{4,5},{5,4},{6,7},{7,6},{8,9},{9,8},{10,11... | collective-permute-start | bytes 776 | tf_op jit(solution)/shard_map/ppermute | solution.py:492
  8.0 12.6 %copy-start = (bf16[1024,256]{1,0:T(8,128)(2,1)S(1)}, bf16[1024,256]{1,0:T(8,128)(2,1)}, u32[]{:S(2)}) copy-start(bf16[1024,256]{1,0:T(8,128)(2,1)} %param.6) | copy-start | bytes 1572868
  8.0 12.6 %copy-start.1 = (bf16[1024,256]{1,0:T(8,128)(2,1)S(1)}, bf16[1024,256]{1,0:T(8,128)(2,1)}, u32[]{:S(2)}) copy-start(bf16[1024,256]{1,0:T(8,128)(2,1)} %param.5) | copy-start | bytes 1572868
  8.1 12.6 %collective-permute-start.2 = (bf16[4,256,256]{2,1,0:T(8,128)(2,1)}, bf16[4,256,256]{2,1,0:T(8,128)(2,1)S(1)}, u32[]{:S(2)}, u32[]{:S(2)}) collective-permute-start(bf16[4,256,256]{2,1,0:T(8,128)(2,1)} %bitcast.24), channel_id=1, source_target_pairs={{0,1},{1,0},{2,3},{3,2},{4,5},{5,4},{6,7},{7,6},{8,9},{9,8},{10,11... | collective-permute-start | bytes 1572872 | tf_op jit(solution)/shard_map/ppermute | solution.py:492
  8.6 12.1 %all-to-all-start = ((bf16[4,256,256]{2,1,0:T(8,128)(2,1)}), bf16[4,256,256]{2,1,0:T(8,128)(2,1)S(1)}, u32[]{:S(2)}, u32[]{:S(2)}) async-start(bf16[4,256,256]{2,1,0:T(8,128)(2,1)} %bitcast.17), calls=%async_computation | async-start | bytes 1048576 | tf_op jit(solution)/shard_map/all_to_all | solution.py:571
  20.7 7.9 %copy-start.2 = (f32[1024]{0:T(1024)S(1)}, f32[1024]{0:T(1024)}, u32[]{:S(2)}) copy-start(f32[1024]{0:T(1024)} %param.7) | copy-start | bytes 12292
  28.5 2.0 %collective-permute-start.4 = (bf16[4,256,256]{2,1,0:T(8,128)(2,1)S(1)}, bf16[4,256,256]{2,1,0:T(8,128)(2,1)}, u32[]{:S(2)}, u32[]{:S(2)}) collective-permute-start(bf16[4,256,256]{2,1,0:T(8,128)(2,1)S(1)} %collective-permute-done.3.refs_4_.refs_3_), channel_id=1, source_target_pairs={{0,1},{1,0},{2,3},{3,2},{4,5},{5,4},{6,7},{7,6},{8,9},{9,8},{10,11... | collective-permute-start | bytes 1572872 | tf_op jit(solution)/shard_map/ppermute | solution.py:492
  28.6 0.7 copy-start.3
  40.7 2.1 %collective-permute-start.6 = (f32[24,256]{1,0:T(8,128)S(1)}, f32[24,256]{1,0:T(8,128)S(1)}, u32[]{:S(2)}, u32[]{:S(2)}) collective-permute-start(f32[24,256]{1,0:T(8,128)S(1)} %get-tuple-element.28.refs_8_), channel_id=1, source_target_pairs={{0,1},{1,0},{2,3},{3,2},{4,5},{5,4},{6,7},{7,6},{8,9},{9,8},{10,11... | collective-permute-start | bytes 73736 | tf_op jit(solution)/shard_map/ppermute | solution.py:492
  40.9 4.0 %collective-permute-start.7 = (f32[24,256]{1,0:T(8,128)S(1)}, f32[24,256]{1,0:T(8,128)S(1)}, u32[]{:S(2)}, u32[]{:S(2)}) collective-permute-start(f32[24,256]{1,0:T(8,128)S(1)} %get-tuple-element.28.refs_8_), channel_id=1, source_target_pairs={{0,2},{1,3},{2,0},{3,1},{4,6},{5,7},{6,4},{7,5},{8,10},{9,11},{10,... | collective-permute-start | bytes 73736 | tf_op jit(solution)/shard_map/ppermute | solution.py:492
  41.4 3.5 %collective-permute-start.8 = (f32[24,256]{1,0:T(8,128)S(1)}, f32[24,256]{1,0:T(8,128)S(1)}, u32[]{:S(2)}, u32[]{:S(2)}) collective-permute-start(f32[24,256]{1,0:T(8,128)S(1)} %get-tuple-element.28.refs_8_), channel_id=1, source_target_pairs={{0,3},{1,2},{2,1},{3,0},{4,7},{5,6},{6,5},{7,4},{8,11},{9,10},{10,... | collective-permute-start | bytes 73736 | tf_op jit(solution)/shard_map/ppermute | solution.py:492
  47.5 4.8 %collective-permute-start.9 = (f32[16,256]{1,0:T(8,128)S(1)}, f32[16,256]{1,0:T(8,128)S(1)}, u32[]{:S(2)}, u32[]{:S(2)}) collective-permute-start(f32[16,256]{1,0:T(8,128)S(1)} %get-tuple-element.30.columns.refs_10_), channel_id=1, source_target_pairs={{0,4},{1,5},{2,6},{3,7},{4,0},{5,1},{6,2},{7,3},{8,12},{9,13},{10,... | collective-permute-start | bytes 49160 | tf_op jit(solution)/shard_map/ppermute | solution.py:492
  52.4 3.7 %collective-permute-start.10 = (f32[4,256]{1,0:T(4,128)S(1)}, f32[4,256]{1,0:T(4,128)S(1)}, u32[]{:S(2)}, u32[]{:S(2)}) collective-permute-start(f32[4,256]{1,0:T(4,128)S(1)} %get-tuple-element.31), channel_id=1, source_target_pairs={{0,8},{8,0},{16,24},{24,16},{1,9},{9,1},{17,25},{25,17},{2,10},{10... | collective-permute-start | bytes 12296 | tf_op jit(solution)/shard_map/ppermute | solution.py:492
  53.9 3.6 %collective-permute-start.11 = (f32[4,256]{1,0:T(4,128)S(1)}, f32[4,256]{1,0:T(4,128)S(1)}, u32[]{:S(2)}, u32[]{:S(2)}) collective-permute-start(f32[4,256]{1,0:T(4,128)S(1)} %get-tuple-element.32), channel_id=1, source_target_pairs={{0,16},{8,24},{16,0},{24,8},{1,17},{9,25},{17,1},{25,9},{2,18},{10... | collective-permute-start | bytes 12296 | tf_op jit(solution)/shard_map/ppermute | solution.py:492
  55.4 4.5 %collective-permute-start.12 = (f32[4,256]{1,0:T(4,128)S(1)}, f32[4,256]{1,0:T(4,128)S(1)}, u32[]{:S(2)}, u32[]{:S(2)}) collective-permute-start(f32[4,256]{1,0:T(4,128)S(1)} %get-tuple-element.33), channel_id=1, source_target_pairs={{0,24},{8,16},{16,8},{24,0},{1,25},{9,17},{17,9},{25,1},{2,26},{10... | collective-permute-start | bytes 12296 | tf_op jit(solution)/shard_map/ppermute | solution.py:492
  73.6 1.9 %collective-permute-start.13 = (f32[16,256]{1,0:T(8,128)S(1)}, f32[16,256]{1,0:T(8,128)S(1)}, u32[]{:S(2)}, u32[]{:S(2)}) collective-permute-start(f32[16,256]{1,0:T(8,128)S(1)} %get-tuple-element.34.refs_13_), channel_id=1, source_target_pairs={{0,1},{1,0},{2,3},{3,2},{4,5},{5,4},{6,7},{7,6},{8,9},{9,8},{10,11... | collective-permute-start | bytes 49160 | tf_op jit(solution)/shard_map/ppermute | solution.py:492
  73.7 3.8 %collective-permute-start.14 = (f32[16,256]{1,0:T(8,128)S(1)}, f32[16,256]{1,0:T(8,128)S(1)}, u32[]{:S(2)}, u32[]{:S(2)}) collective-permute-start(f32[16,256]{1,0:T(8,128)S(1)} %get-tuple-element.34.refs_13_), channel_id=1, source_target_pairs={{0,2},{1,3},{2,0},{3,1},{4,6},{5,7},{6,4},{7,5},{8,10},{9,11},{10,... | collective-permute-start | bytes 49160 | tf_op jit(solution)/shard_map/ppermute | solution.py:492
  74.9 3.2 %collective-permute-start.15 = (f32[16,256]{1,0:T(8,128)S(1)}, f32[16,256]{1,0:T(8,128)S(1)}, u32[]{:S(2)}, u32[]{:S(2)}) collective-permute-start(f32[16,256]{1,0:T(8,128)S(1)} %get-tuple-element.34.refs_13_), channel_id=1, source_target_pairs={{0,3},{1,2},{2,1},{3,0},{4,7},{5,6},{6,5},{7,4},{8,11},{9,10},{10,... | collective-permute-start | bytes 49160 | tf_op jit(solution)/shard_map/ppermute | solution.py:492
  80.3 6.1 %collective-permute-start.16 = (f32[16,256]{1,0:T(8,128)S(1)}, f32[16,256]{1,0:T(8,128)S(1)}, u32[]{:S(2)}, u32[]{:S(2)}) collective-permute-start(f32[16,256]{1,0:T(8,128)S(1)} %get-tuple-element.37.columns), channel_id=1, source_target_pairs={{0,4},{1,5},{2,6},{3,7},{4,0},{5,1},{6,2},{7,3},{8,12},{9,13},{10,... | collective-permute-start | bytes 49160 | tf_op jit(solution)/shard_map/ppermute | solution.py:492
  82.3 4.1 %collective-permute-start.17 = (f32[16,256]{1,0:T(8,128)S(1)}, f32[16,256]{1,0:T(8,128)S(1)}, u32[]{:S(2)}, u32[]{:S(2)}) collective-permute-start(f32[16,256]{1,0:T(8,128)S(1)} %get-tuple-element.37.columns), channel_id=1, source_target_pairs={{0,8},{8,0},{16,24},{24,16},{1,9},{9,1},{17,25},{25,17},{2,10},{10... | collective-permute-start | bytes 49160 | tf_op jit(solution)/shard_map/ppermute | solution.py:492
  82.8 3.7 %collective-permute-start.18 = (f32[16,256]{1,0:T(8,128)S(1)}, f32[16,256]{1,0:T(8,128)S(1)}, u32[]{:S(2)}, u32[]{:S(2)}) collective-permute-start(f32[16,256]{1,0:T(8,128)S(1)} %get-tuple-element.37.columns), channel_id=1, source_target_pairs={{0,16},{8,24},{16,0},{24,8},{1,17},{9,25},{17,1},{25,9},{2,18},{10... | collective-permute-start | bytes 49160 | tf_op jit(solution)/shard_map/ppermute | solution.py:492
  83.4 4.6 %collective-permute-start.19 = (f32[16,256]{1,0:T(8,128)S(1)}, f32[16,256]{1,0:T(8,128)S(1)}, u32[]{:S(2)}, u32[]{:S(2)}) collective-permute-start(f32[16,256]{1,0:T(8,128)S(1)} %get-tuple-element.37.columns), channel_id=1, source_target_pairs={{0,24},{8,16},{16,8},{24,0},{1,25},{9,17},{17,9},{25,1},{2,26},{10... | collective-permute-start | bytes 49160 | tf_op jit(solution)/shard_map/ppermute | solution.py:492

commit v9 on v8

--- a/solution.py
+++ b/solution.py
@@ -230,16 +230,16 @@
     return jnp.concatenate([high, middle, low], axis=0)
 
 
-def spread(rows, bias):
+def spread(rows, bias, used=SOURCE_SLOTS):
     count = rows.shape[0]
-    shape = (3 * count, count * 128)
+    shape = (3 * count, used * 128)
     slot = lax.broadcasted_iota(jnp.int32, shape, 0) & (count - 1)
     place = lax.broadcasted_iota(jnp.int32, shape, 1) >> 7
     chosen = jnp.where(slot == place, 1.0, 0.0).astype(jnp.bfloat16)
     turned = lax.dot_general(
         in_parts(rows), chosen, (((0,), (0,)), ((), ())), preferred_element_type=jnp.float32
     )
-    for index in range(count):
+    for index in range(used):
         bias[index] = turned[:, 128 * index : 128 * (index + 1)]
 
 
@@ -421,7 +421,7 @@
     out, second, bias, total, *work = refs[14:]
     rows = target_bias(chosen, columns, partner, mirrors)
     shift = shift[0:1, 0:1]
-    spread(rows + shift, bias)
+    spread(rows + shift, bias, TARGET_SLOTS)
     second[...] = jnp.broadcast_to(middle([rows[0:7], rows[8:12]]), second.shape)
 
     def write(result):
@@ -596,6 +596,8 @@
     )
     source_near, early = lax.optimization_barrier((source_near, early))
     source_cross = member_swap(source_near, 1)
+    nothing = jnp.minimum(candidates[0, 0], 0).astype(source_cross.dtype)
+    target_far, source_cross = lax.optimization_barrier((target_far, source_cross + nothing))
     sources, targets = [source_own, source_core, source_near], [target_own, target_far, mirrors]
     parts, source_cross = call_tiles(
         first_kernel,

time: 88.9 us -> 88.5 us (level)
  starting transfers between devices: 25.8 us -> 23.7 us
  other arithmetic: 1.42 us -> 2.5 us
    ppermute x20, starting transfers between devices: 22 us -> 20 us  [swap(): lax.ppermute(values, axis, [(index, index ^ bit) for index in range(size)])]
    add x0 -> x1, other arithmetic: none -> 1.08 us  [shards_quad(): source_cross + nothing]
  transfers between devices with their start and end apart: 21 -> 21, of which waited for: 11 -> 11; matrix products, arithmetic and copies ran while one was open for 3% -> 5% of each run, Pallas kernels for 2% -> 2%
where the time goes in v9:
time: 88.5 us; the launch traced here: 88.2 us
  Pallas kernels  30.5 us (34%)
  waiting for transfers between devices  26.6 us (30%)
  starting transfers between devices  23.7 us (27%)
  local copies, waits for them, and re-layouts  3.2 us (4%)
  other arithmetic  2.5 us (3%)
  between operations  1.58 us (2%)
    pallas_call x7, Pallas kernels, call(): pl.pallas_call(kernel, out_shape=outs, in_specs=[first] + [whole] * (len(...  30.5 us
    ppermute x20, starting transfers between devices, swap(): lax.ppermute(values, axis, [(index, index ^ bit) for index in range(size)])  20 us
    ppermute x20, waiting for transfers between devices, swap(): lax.ppermute(values, axis, [(index, index ^ bit) for index in range(size)])  19.2 us
    all_to_all x1, waiting for transfers between devices, shards_quad(): lax.all_to_all(target_late, 'group', split_axis=0, concat_axis=0, tiled=T...  7.43 us
    all_to_all x1, starting transfers between devices, shards_quad(): lax.all_to_all(target_late, 'group', split_axis=0, concat_axis=0, tiled=T...  3.72 us
  transfers between devices with their start and end apart: 21, of which 11 were waited for; matrix products, arithmetic and copies ran while one was open for 5% of the time, Pallas kernels for 2%

profile of v9, /device:TPU:0, one launch (start us, length us, event | category | flops | bytes accessed | tf_op | source)
XLA Modules:
  0.0 88.2 jit_solution(3810321909393236089)
XLA Ops:
  0.6 3.1 %collective-permute-start = (s32[4,8]{1,0:T(4,128)}, s32[4,8]{1,0:T(4,128)S(1)}, u32[]{:S(2)}, u32[]{:S(2)}) collective-permute-start(s32[4,8]{1,0:T(4,128)} %param.9), channel_id=1, source_target_pairs={{0,2},{1,3},{2,0},{3,1},{4,6},{5,7},{6,4},{7,5},{8,10},{9,11},{10,... | collective-permute-start | bytes 392 | tf_op jit(solution)/shard_map/ppermute | solution.py:492
  3.8 3.0 %collective-permute-start.4 = (bf16[4,256,256]{2,1,0:T(8,128)(2,1)}, bf16[4,256,256]{2,1,0:T(8,128)(2,1)S(1)}, u32[]{:S(2)}, u32[]{:S(2)}) collective-permute-start(bf16[4,256,256]{2,1,0:T(8,128)(2,1)} %bitcast.17), channel_id=1, source_target_pairs={{0,4},{1,5},{2,6},{3,7},{4,0},{5,1},{6,2},{7,3},{8,12},{9,13},{10,... | collective-permute-start | bytes 1572872 | tf_op jit(solution)/shard_map/ppermute | solution.py:492
  6.8 0.6 copy-done.4
  9.4 0.5 collective-permute-start.2
  9.9 3.7 %all-to-all-start = ((bf16[4,256,256]{2,1,0:T(8,128)(2,1)}), bf16[4,256,256]{2,1,0:T(8,128)(2,1)S(1)}, u32[]{:S(2)}, u32[]{:S(2)}) async-start(bf16[4,256,256]{2,1,0:T(8,128)(2,1)} %bitcast.18), calls=%async_computation | async-start | bytes 1048576 | tf_op jit(solution)/shard_map/all_to_all | solution.py:571
  14.6 7.4 %all-to-all-done.refs_3_.refs_7_ = bf16[4,256,256]{2,1,0:T(8,128)(2,1)S(1)} async-done(((bf16[4,256,256]{2,1,0:T(8,128)(2,1)}), bf16[4,256,256]{2,1,0:T(8,128)(2,1)S(1)}, u32[]{:S(2)}, u32[]{:S(2)}) %all-to-all-start) | async-done | bytes 524320 | tf_op jit(solution)/shard_map/all_to_all | solution.py:571
  22.0 2.0 %shard_map.68 = (f32[16,256]{1,0:T(8,128)S(1)}, f32[8,128]{1,0:T(8,128)S(1)}) custom-call(s32[6,40]{1,0:T(8,128)S(1)} %stack.2.scalars.origin, bf16[4,256,256]{2,1,0:T(8,128)(2,1)S(1)} %bitcast.26, bf16[4,256,256]{2,1,0:T(8,128)(2,1)S(1)} %collective-permute-done.2.refs_1_.refs_3_.refs_2_, bf16[4,256,256]{2,1,0:T(8,128)(2,1)S(1)} %bitcast.19, ...), custom_call_target="tpu_custom_call" | custom-call | tf_op jit(solution)/shard_map/pallas_call | solution.py:465
  24.0 4.5 %collective-permute-done.3.refs_4_.refs_3_ = bf16[4,256,256]{2,1,0:T(8,128)(2,1)S(1)} collective-permute-done((bf16[4,256,256]{2,1,0:T(8,128)(2,1)}, bf16[4,256,256]{2,1,0:T(8,128)(2,1)S(1)}, u32[]{:S(2)}, u32[]{:S(2)}) %collective-permute-start.3) | collective-permute-done | bytes 524320 | tf_op jit(solution)/shard_map/ppermute | solution.py:492
  28.6 0.7 copy-done.3
  29.4 1.2 %collective-permute-done.5 = bf16[4,256,256]{2,1,0:T(8,128)(2,1)} collective-permute-done((bf16[4,256,256]{2,1,0:T(8,128)(2,1)S(1)}, bf16[4,256,256]{2,1,0:T(8,128)(2,1)}, u32[]{:S(2)}, u32[]{:S(2)}) %collective-permute-start.5) | collective-permute-done | bytes 524320 | tf_op jit(solution)/shard_map/ppermute | solution.py:492
  30.6 1.1 %broadcast_add_fusion.refs_1_ = bf16[4,256,256]{2,1,0:T(8,128)(2,1)S(1)} fusion(bf16[4,256,256]{2,1,0:T(8,128)(2,1)} %collective-permute-done.5, bf16[]{:T(256)} %bitcast.7), kind=kLoop, calls=%fused_computation | loop fusion | flops 262144 | bytes 1048578 | tf_op jit(solution)/shard_map/add | solution.py:600
  31.8 9.5 %shard_map.69 = (f32[24,256]{1,0:T(8,128)S(1)}, bf16[4,256,256]{2,1,0:T(8,128)(2,1)S(1)}) custom-call(s32[6,40]{1,0:T(8,128)S(1)} %stack.2.scalars.origin, f32[16,128]{1,0:T(8,128)S(1)} %broadcast_in_dim.196.refs_0_, bf16[4,256,256]{2,1,0:T(8,128)(2,1)S(1)} %broadcast_add_fusion.refs_1_, bf16[4,256,256]{2,1,0:T(8,128)(2,1)S(1)} %bitcast.27, ...), custom_call_target="tpu_custom_call" | custom-call | tf_op jit(solution)/shard_map/pallas_call | solution.py:465
  41.5 1.7 %collective-permute-start.8 = (f32[24,256]{1,0:T(8,128)S(1)}, f32[24,256]{1,0:T(8,128)S(1)}, u32[]{:S(2)}, u32[]{:S(2)}) collective-permute-start(f32[24,256]{1,0:T(8,128)S(1)} %get-tuple-element.32.refs_8_), channel_id=1, source_target_pairs={{0,3},{1,2},{2,1},{3,0},{4,7},{5,6},{6,5},{7,4},{8,11},{9,10},{10,... | collective-permute-start | bytes 73736 | tf_op jit(solution)/shard_map/ppermute | solution.py:492
  43.4 2.0 %collective-permute-done.7.refs_10_ = f32[24,256]{1,0:T(8,128)S(1)} collective-permute-done((f32[24,256]{1,0:T(8,128)S(1)}, f32[24,256]{1,0:T(8,128)S(1)}, u32[]{:S(2)}, u32[]{:S(2)}) %collective-permute-start.7) | collective-permute-done | bytes 24608 | tf_op jit(solution)/shard_map/ppermute | solution.py:492
  45.4 2.5 %shard_map.70 = (f32[16,256]{1,0:T(8,128)S(1)}, f32[8,128]{1,0:T(8,128)S(1)}) custom-call(s32[6,40]{1,0:T(8,128)S(1)} %stack.2.scalars.origin, f32[16,128]{1,0:T(8,128)S(1)} %broadcast_in_dim.194.refs_0_, bf16[4,256,256]{2,1,0:T(8,128)(2,1)S(1)} %bitcast.28, bf16[4,256,256]{2,1,0:T(8,128)(2,1)S(1)} %collective-permute-done.2.refs_1_.refs_3_.refs_2_, ...), custom_call_target="tpu_custom_call" | custom-call | tf_op jit(solution)/shard_map/pallas_call | solution.py:465
  48.0 1.6 %collective-permute-start.9 = (f32[16,256]{1,0:T(8,128)S(1)}, f32[16,256]{1,0:T(8,128)S(1)}, u32[]{:S(2)}, u32[]{:S(2)}) collective-permute-start(f32[16,256]{1,0:T(8,128)S(1)} %get-tuple-element.34.columns.refs_10_), channel_id=1, source_target_pairs={{0,4},{1,5},{2,6},{3,7},{4,0},{5,1},{6,2},{7,3},{8,12},{9,13},{10,... | collective-permute-start | bytes 49160 | tf_op jit(solution)/shard_map/ppermute | solution.py:492
  49.5 3.3 %collective-permute-done.9.partner.refs_11_ = f32[16,256]{1,0:T(8,128)S(1)} collective-permute-done((f32[16,256]{1,0:T(8,128)S(1)}, f32[16,256]{1,0:T(8,128)S(1)}, u32[]{:S(2)}, u32[]{:S(2)}) %collective-permute-start.9) | collective-permute-done | bytes 16416 | tf_op jit(solution)/shard_map/ppermute | solution.py:492
  53.0 1.6 %collective-permute-start.10 = (f32[4,256]{1,0:T(4,128)S(1)}, f32[4,256]{1,0:T(4,128)S(1)}, u32[]{:S(2)}, u32[]{:S(2)}) collective-permute-start(f32[4,256]{1,0:T(4,128)S(1)} %get-tuple-element.35), channel_id=1, source_target_pairs={{0,8},{8,0},{16,24},{24,16},{1,9},{9,1},{17,25},{25,17},{2,10},{10... | collective-permute-start | bytes 12296 | tf_op jit(solution)/shard_map/ppermute | solution.py:492
  54.5 1.5 %collective-permute-start.11 = (f32[4,256]{1,0:T(4,128)S(1)}, f32[4,256]{1,0:T(4,128)S(1)}, u32[]{:S(2)}, u32[]{:S(2)}) collective-permute-start(f32[4,256]{1,0:T(4,128)S(1)} %get-tuple-element.36), channel_id=1, source_target_pairs={{0,16},{8,24},{16,0},{24,8},{1,17},{9,25},{17,1},{25,9},{2,18},{10... | collective-permute-start | bytes 12296 | tf_op jit(solution)/shard_map/ppermute | solution.py:492
  56.6 1.5 %collective-permute-done.11.refs_13_ = f32[4,256]{1,0:T(4,128)S(1)} collective-permute-done((f32[4,256]{1,0:T(4,128)S(1)}, f32[4,256]{1,0:T(4,128)S(1)}, u32[]{:S(2)}, u32[]{:S(2)}) %collective-permute-start.11) | collective-permute-done | bytes 4128 | tf_op jit(solution)/shard_map/ppermute | solution.py:492
  58.1 2.4 %collective-permute-done.12.refs_14_ = f32[4,256]{1,0:T(4,128)S(1)} collective-permute-done((f32[4,256]{1,0:T(4,128)S(1)}, f32[4,256]{1,0:T(4,128)S(1)}, u32[]{:S(2)}, u32[]{:S(2)}) %collective-permute-start.12) | collective-permute-done | bytes 4128 | tf_op jit(solution)/shard_map/ppermute | solution.py:492
  60.6 13.6 %shard_map.72 = (f32[16,256]{1,0:T(8,128)S(1)}, f32[8,128]{1,0:T(8,128)S(1)}) custom-call(s32[6,40]{1,0:T(8,128)S(1)} %stack.2.scalars.origin, f32[16,128]{1,0:T(8,128)S(1)} %broadcast_in_dim.197.refs_0_, bf16[4,256,256]{2,1,0:T(8,128)(2,1)S(1)} %bitcast.29, bf16[4,256,256]{2,1,0:T(8,128)(2,1)S(1)} %collective-permute-done.2.refs_1_.refs_3_.refs_2_, ...), custom_call_target="tpu_custom_call" | custom-call | tf_op jit(solution)/shard_map/pallas_call | solution.py:465
  74.3 1.4 %collective-permute-start.14 = (f32[16,256]{1,0:T(8,128)S(1)}, f32[16,256]{1,0:T(8,128)S(1)}, u32[]{:S(2)}, u32[]{:S(2)}) collective-permute-start(f32[16,256]{1,0:T(8,128)S(1)} %get-tuple-element.38.refs_13_), channel_id=1, source_target_pairs={{0,2},{1,3},{2,0},{3,1},{4,6},{5,7},{6,4},{7,5},{8,10},{9,11},{10,... | collective-permute-start | bytes 49160 | tf_op jit(solution)/shard_map/ppermute | solution.py:492
  76.1 1.9 %collective-permute-done.14.refs_15_ = f32[16,256]{1,0:T(8,128)S(1)} collective-permute-done((f32[16,256]{1,0:T(8,128)S(1)}, f32[16,256]{1,0:T(8,128)S(1)}, u32[]{:S(2)}, u32[]{:S(2)}) %collective-permute-start.14) | collective-permute-done | bytes 16416 | tf_op jit(solution)/shard_map/ppermute | solution.py:492
  78.1 0.7 collective-permute-done.15.refs_16_
  78.8 2.2 %shard_map.73 = (f32[16,256]{1,0:T(8,128)S(1)}, f32[8,128]{1,0:T(8,128)S(1)}) custom-call(s32[6,40]{1,0:T(8,128)S(1)} %stack.2.scalars.origin, f32[16,128]{1,0:T(8,128)S(1)} %broadcast_in_dim.194.refs_0_, bf16[4,256,256]{2,1,0:T(8,128)(2,1)S(1)} %bitcast.30, bf16[4,256,256]{2,1,0:T(8,128)(2,1)S(1)} %collective-permute-done.2.refs_1_.refs_3_.refs_2_, ...), custom_call_target="tpu_custom_call" | custom-call | tf_op jit(solution)/shard_map/pallas_call | solution.py:465
  81.0 0.8 collective-permute-start.16
  81.9 0.5 collective-permute-start.17
  82.9 2.5 %collective-permute-start.19 = (f32[16,256]{1,0:T(8,128)S(1)}, f32[16,256]{1,0:T(8,128)S(1)}, u32[]{:S(2)}, u32[]{:S(2)}) collective-permute-start(f32[16,256]{1,0:T(8,128)S(1)} %get-tuple-element.41.columns), channel_id=1, source_target_pairs={{0,24},{8,16},{16,8},{24,0},{1,25},{9,17},{17,9},{25,1},{2,26},{10... | collective-permute-start | bytes 49160 | tf_op jit(solution)/shard_map/ppermute | solution.py:492
  85.4 0.6 multiply_bitcast_fusion
  86.1 1.4 %collective-permute-done.19.rest_2_ = f32[16,256]{1,0:T(8,128)S(1)} collective-permute-done((f32[16,256]{1,0:T(8,128)S(1)}, f32[16,256]{1,0:T(8,128)S(1)}, u32[]{:S(2)}, u32[]{:S(2)}) %collective-permute-start.19) | collective-permute-done | bytes 16416 | tf_op jit(solution)/shard_map/ppermute | solution.py:492
  87.5 0.6 shard_map.74
  (77 shorter events, 4.8 us)
Async XLA Ops:
  0.6 8.6 %collective-permute-start = (s32[4,8]{1,0:T(4,128)}, s32[4,8]{1,0:T(4,128)S(1)}, u32[]{:S(2)}, u32[]{:S(2)}) collective-permute-start(s32[4,8]{1,0:T(4,128)} %param.9), channel_id=1, source_target_pairs={{0,2},{1,3},{2,0},{3,1},{4,6},{5,7},{6,4},{7,5},{8,10},{9,11},{10,... | collective-permute-start | bytes 392 | tf_op jit(solution)/shard_map/ppermute | solution.py:492
  3.7 24.8 %collective-permute-start.3 = (bf16[4,256,256]{2,1,0:T(8,128)(2,1)}, bf16[4,256,256]{2,1,0:T(8,128)(2,1)S(1)}, u32[]{:S(2)}, u32[]{:S(2)}) collective-permute-start(bf16[4,256,256]{2,1,0:T(8,128)(2,1)} %bitcast.24), channel_id=1, source_target_pairs={{0,2},{1,3},{2,0},{3,1},{4,6},{5,7},{6,4},{7,5},{8,10},{9,11},{10,... | collective-permute-start | bytes 1572872 | tf_op jit(solution)/shard_map/ppermute | solution.py:492
  3.8 27.9 %collective-permute-start.4 = (bf16[4,256,256]{2,1,0:T(8,128)(2,1)}, bf16[4,256,256]{2,1,0:T(8,128)(2,1)S(1)}, u32[]{:S(2)}, u32[]{:S(2)}) collective-permute-start(bf16[4,256,256]{2,1,0:T(8,128)(2,1)} %bitcast.17), channel_id=1, source_target_pairs={{0,4},{1,5},{2,6},{3,7},{4,0},{5,1},{6,2},{7,3},{8,12},{9,13},{10,... | collective-permute-start | bytes 1572872 | tf_op jit(solution)/shard_map/ppermute | solution.py:492
  6.8 0.7 copy-start.4
  9.3 4.4 %collective-permute-start.1 = (s32[8,8]{1,0:T(8,128)S(1)}, s32[8,8]{1,0:T(8,128)S(1)}, u32[]{:S(2)}, u32[]{:S(2)}) collective-permute-start(s32[8,8]{1,0:T(8,128)S(1)} %pad_add_fusion.1), channel_id=1, source_target_pairs={{0,1},{1,0},{2,3},{3,2},{4,5},{5,4},{6,7},{7,6},{8,9},{9,8},{10,11... | collective-permute-start | bytes 776 | tf_op jit(solution)/shard_map/ppermute | solution.py:492
  9.4 12.6 %copy-start = (bf16[1024,256]{1,0:T(8,128)(2,1)S(1)}, bf16[1024,256]{1,0:T(8,128)(2,1)}, u32[]{:S(2)}) copy-start(bf16[1024,256]{1,0:T(8,128)(2,1)} %param.6) | copy-start | bytes 1572868
  9.4 12.6 %copy-start.1 = (bf16[1024,256]{1,0:T(8,128)(2,1)S(1)}, bf16[1024,256]{1,0:T(8,128)(2,1)}, u32[]{:S(2)}) copy-start(bf16[1024,256]{1,0:T(8,128)(2,1)} %param.5) | copy-start | bytes 1572868
  9.4 12.6 %collective-permute-start.2 = (bf16[4,256,256]{2,1,0:T(8,128)(2,1)}, bf16[4,256,256]{2,1,0:T(8,128)(2,1)S(1)}, u32[]{:S(2)}, u32[]{:S(2)}) collective-permute-start(bf16[4,256,256]{2,1,0:T(8,128)(2,1)} %bitcast.25), channel_id=1, source_target_pairs={{0,1},{1,0},{2,3},{3,2},{4,5},{5,4},{6,7},{7,6},{8,9},{9,8},{10,11... | collective-permute-start | bytes 1572872 | tf_op jit(solution)/shard_map/ppermute | solution.py:492
  9.9 12.1 %all-to-all-start = ((bf16[4,256,256]{2,1,0:T(8,128)(2,1)}), bf16[4,256,256]{2,1,0:T(8,128)(2,1)S(1)}, u32[]{:S(2)}, u32[]{:S(2)}) async-start(bf16[4,256,256]{2,1,0:T(8,128)(2,1)} %bitcast.18), calls=%async_computation | async-start | bytes 1048576 | tf_op jit(solution)/shard_map/all_to_all | solution.py:571
  22.0 6.5 %copy-start.2 = (f32[1024]{0:T(1024)S(1)}, f32[1024]{0:T(1024)}, u32[]{:S(2)}) copy-start(f32[1024]{0:T(1024)} %param.7) | copy-start | bytes 12292
  28.5 2.0 %collective-permute-start.5 = (bf16[4,256,256]{2,1,0:T(8,128)(2,1)S(1)}, bf16[4,256,256]{2,1,0:T(8,128)(2,1)}, u32[]{:S(2)}, u32[]{:S(2)}) collective-permute-start(bf16[4,256,256]{2,1,0:T(8,128)(2,1)S(1)} %collective-permute-done.3.refs_4_.refs_3_), channel_id=1, source_target_pairs={{0,1},{1,0},{2,3},{3,2},{4,5},{5,4},{6,7},{7,6},{8,9},{9,8},{10,11... | collective-permute-start | bytes 1572872 | tf_op jit(solution)/shard_map/ppermute | solution.py:492
  28.6 0.7 copy-start.3
  41.3 2.1 %collective-permute-start.6 = (f32[24,256]{1,0:T(8,128)S(1)}, f32[24,256]{1,0:T(8,128)S(1)}, u32[]{:S(2)}, u32[]{:S(2)}) collective-permute-start(f32[24,256]{1,0:T(8,128)S(1)} %get-tuple-element.32.refs_8_), channel_id=1, source_target_pairs={{0,1},{1,0},{2,3},{3,2},{4,5},{5,4},{6,7},{7,6},{8,9},{9,8},{10,11... | collective-permute-start | bytes 73736 | tf_op jit(solution)/shard_map/ppermute | solution.py:492
  41.5 3.8 %collective-permute-start.7 = (f32[24,256]{1,0:T(8,128)S(1)}, f32[24,256]{1,0:T(8,128)S(1)}, u32[]{:S(2)}, u32[]{:S(2)}) collective-permute-start(f32[24,256]{1,0:T(8,128)S(1)} %get-tuple-element.32.refs_8_), channel_id=1, source_target_pairs={{0,2},{1,3},{2,0},{3,1},{4,6},{5,7},{6,4},{7,5},{8,10},{9,11},{10,... | collective-permute-start | bytes 73736 | tf_op jit(solution)/shard_map/ppermute | solution.py:492
  41.5 3.8 %collective-permute-start.8 = (f32[24,256]{1,0:T(8,128)S(1)}, f32[24,256]{1,0:T(8,128)S(1)}, u32[]{:S(2)}, u32[]{:S(2)}) collective-permute-start(f32[24,256]{1,0:T(8,128)S(1)} %get-tuple-element.32.refs_8_), channel_id=1, source_target_pairs={{0,3},{1,2},{2,1},{3,0},{4,7},{5,6},{6,5},{7,4},{8,11},{9,10},{10,... | collective-permute-start | bytes 73736 | tf_op jit(solution)/shard_map/ppermute | solution.py:492
  48.0 4.9 %collective-permute-start.9 = (f32[16,256]{1,0:T(8,128)S(1)}, f32[16,256]{1,0:T(8,128)S(1)}, u32[]{:S(2)}, u32[]{:S(2)}) collective-permute-start(f32[16,256]{1,0:T(8,128)S(1)} %get-tuple-element.34.columns.refs_10_), channel_id=1, source_target_pairs={{0,4},{1,5},{2,6},{3,7},{4,0},{5,1},{6,2},{7,3},{8,12},{9,13},{10,... | collective-permute-start | bytes 49160 | tf_op jit(solution)/shard_map/ppermute | solution.py:492
  53.0 3.7 %collective-permute-start.10 = (f32[4,256]{1,0:T(4,128)S(1)}, f32[4,256]{1,0:T(4,128)S(1)}, u32[]{:S(2)}, u32[]{:S(2)}) collective-permute-start(f32[4,256]{1,0:T(4,128)S(1)} %get-tuple-element.35), channel_id=1, source_target_pairs={{0,8},{8,0},{16,24},{24,16},{1,9},{9,1},{17,25},{25,17},{2,10},{10... | collective-permute-start | bytes 12296 | tf_op jit(solution)/shard_map/ppermute | solution.py:492
  54.5 3.6 %collective-permute-start.11 = (f32[4,256]{1,0:T(4,128)S(1)}, f32[4,256]{1,0:T(4,128)S(1)}, u32[]{:S(2)}, u32[]{:S(2)}) collective-permute-start(f32[4,256]{1,0:T(4,128)S(1)} %get-tuple-element.36), channel_id=1, source_target_pairs={{0,16},{8,24},{16,0},{24,8},{1,17},{9,25},{17,1},{25,9},{2,18},{10... | collective-permute-start | bytes 12296 | tf_op jit(solution)/shard_map/ppermute | solution.py:492
  56.0 4.5 %collective-permute-start.12 = (f32[4,256]{1,0:T(4,128)S(1)}, f32[4,256]{1,0:T(4,128)S(1)}, u32[]{:S(2)}, u32[]{:S(2)}) collective-permute-start(f32[4,256]{1,0:T(4,128)S(1)} %get-tuple-element.37), channel_id=1, source_target_pairs={{0,24},{8,16},{16,8},{24,0},{1,25},{9,17},{17,9},{25,1},{2,26},{10... | collective-permute-start | bytes 12296 | tf_op jit(solution)/shard_map/ppermute | solution.py:492
  74.2 1.9 %collective-permute-start.13 = (f32[16,256]{1,0:T(8,128)S(1)}, f32[16,256]{1,0:T(8,128)S(1)}, u32[]{:S(2)}, u32[]{:S(2)}) collective-permute-start(f32[16,256]{1,0:T(8,128)S(1)} %get-tuple-element.38.refs_13_), channel_id=1, source_target_pairs={{0,1},{1,0},{2,3},{3,2},{4,5},{5,4},{6,7},{7,6},{8,9},{9,8},{10,11... | collective-permute-start | bytes 49160 | tf_op jit(solution)/shard_map/ppermute | solution.py:492
  74.3 3.8 %collective-permute-start.14 = (f32[16,256]{1,0:T(8,128)S(1)}, f32[16,256]{1,0:T(8,128)S(1)}, u32[]{:S(2)}, u32[]{:S(2)}) collective-permute-start(f32[16,256]{1,0:T(8,128)S(1)} %get-tuple-element.38.refs_13_), channel_id=1, source_target_pairs={{0,2},{1,3},{2,0},{3,1},{4,6},{5,7},{6,4},{7,5},{8,10},{9,11},{10,... | collective-permute-start | bytes 49160 | tf_op jit(solution)/shard_map/ppermute | solution.py:492
  75.6 3.2 %collective-permute-start.15 = (f32[16,256]{1,0:T(8,128)S(1)}, f32[16,256]{1,0:T(8,128)S(1)}, u32[]{:S(2)}, u32[]{:S(2)}) collective-permute-start(f32[16,256]{1,0:T(8,128)S(1)} %get-tuple-element.38.refs_13_), channel_id=1, source_target_pairs={{0,3},{1,2},{2,1},{3,0},{4,7},{5,6},{6,5},{7,4},{8,11},{9,10},{10,... | collective-permute-start | bytes 49160 | tf_op jit(solution)/shard_map/ppermute | solution.py:492
  81.0 4.9 %collective-permute-start.16 = (f32[16,256]{1,0:T(8,128)S(1)}, f32[16,256]{1,0:T(8,128)S(1)}, u32[]{:S(2)}, u32[]{:S(2)}) collective-permute-start(f32[16,256]{1,0:T(8,128)S(1)} %get-tuple-element.41.columns), channel_id=1, source_target_pairs={{0,4},{1,5},{2,6},{3,7},{4,0},{5,1},{6,2},{7,3},{8,12},{9,13},{10,... | collective-permute-start | bytes 49160 | tf_op jit(solution)/shard_map/ppermute | solution.py:492
  81.9 4.1 %collective-permute-start.17 = (f32[16,256]{1,0:T(8,128)S(1)}, f32[16,256]{1,0:T(8,128)S(1)}, u32[]{:S(2)}, u32[]{:S(2)}) collective-permute-start(f32[16,256]{1,0:T(8,128)S(1)} %get-tuple-element.41.columns), channel_id=1, source_target_pairs={{0,8},{8,0},{16,24},{24,16},{1,9},{9,1},{17,25},{25,17},{2,10},{10... | collective-permute-start | bytes 49160 | tf_op jit(solution)/shard_map/ppermute | solution.py:492
  82.4 3.7 %collective-permute-start.18 = (f32[16,256]{1,0:T(8,128)S(1)}, f32[16,256]{1,0:T(8,128)S(1)}, u32[]{:S(2)}, u32[]{:S(2)}) collective-permute-start(f32[16,256]{1,0:T(8,128)S(1)} %get-tuple-element.41.columns), channel_id=1, source_target_pairs={{0,16},{8,24},{16,0},{24,8},{1,17},{9,25},{17,1},{25,9},{2,18},{10... | collective-permute-start | bytes 49160 | tf_op jit(solution)/shard_map/ppermute | solution.py:492
  82.9 4.6 %collective-permute-start.19 = (f32[16,256]{1,0:T(8,128)S(1)}, f32[16,256]{1,0:T(8,128)S(1)}, u32[]{:S(2)}, u32[]{:S(2)}) collective-permute-start(f32[16,256]{1,0:T(8,128)S(1)} %get-tuple-element.41.columns), channel_id=1, source_target_pairs={{0,24},{8,16},{16,8},{24,0},{1,25},{9,17},{17,9},{25,1},{2,26},{10... | collective-permute-start | bytes 49160 | tf_op jit(solution)/shard_map/ppermute | solution.py:492
